TPU v7x, 32 devices: a whole 2x2x4 slice. The times are simulated.
32 devices in a mesh: rep: 2 (over x), shard: 16 (over z, y, core).
Axes of the slice: x: 2, y: 2, z: 4, core: 2. Of those that a mesh axis runs over, the one named last changes fastest.
Arguments:
- tokens: bfloat16 [32, 1024, 1024], P(('rep', 'shard')), may hold values from -6 to 6
- enc_states: bfloat16 [32, 1024, 1024], P(('rep', 'shard')), may hold values from -6 to 6
- unit_ids: int32 [32, 1024], P(('rep', 'shard')), may hold values from 0 to 7, as said below
- enc_ids: int32 [32, 1024], P(('rep', 'shard')), may hold values from 0 to 7, as said below
- self_q: bfloat16 [1024, 1024], P('shard'), may hold values from -0.25 to 0.25
- self_k: bfloat16 [1024, 1024], P('shard'), may hold values from -0.25 to 0.25
- self_v: bfloat16 [1024, 1024], P('shard'), may hold values from -0.1875 to 0.1875
- self_o: bfloat16 [1024, 1024], P('shard'), may hold values from -0.75 to 0.75
- cross_q: bfloat16 [1024, 1024], P('shard'), may hold values from -0.25 to 0.25
- cross_k: bfloat16 [1024, 1024], P('shard'), may hold values from -0.25 to 0.25
- cross_v: bfloat16 [1024, 1024], P('shard'), may hold values from -0.1875 to 0.1875
- cross_o: bfloat16 [1024, 1024], P('shard'), may hold values from -0.75 to 0.75
- ffn_in: bfloat16 [1024, 4096], P('shard'), may hold values from -0.1875 to 0.1875
- ffn_out: bfloat16 [4096, 1024], P('shard'), may hold values from -0.125 to 0.125
- norm_gains: bfloat16 [4, 1024], P(None, 'shard'), may hold values from 0.25 to 1.75
- norm_biases: bfloat16 [4, 1024], P(None, 'shard'), may hold values from -1.5 to 1.5
- cotangent: bfloat16 [32, 1024, 1024], P(('rep', 'shard')), may hold values from -6 to 6
Outputs:
- layer_out: bfloat16 [32, 1024, 1024], P(('rep', 'shard'))
- grad_tokens: float32 [32, 1024, 1024], P(('rep', 'shard'))
- grad_enc_states: float32 [32, 1024, 1024], P(('rep', 'shard'))
- grad_self_q: float32 [1024, 1024], P('shard')
- grad_self_k: float32 [1024, 1024], P('shard')
- grad_self_v: float32 [1024, 1024], P('shard')
- grad_self_o: float32 [1024, 1024], P('shard')
- grad_cross_q: float32 [1024, 1024], P('shard')
- grad_cross_k: float32 [1024, 1024], P('shard')
- grad_cross_v: float32 [1024, 1024], P('shard')
- grad_cross_o: float32 [1024, 1024], P('shard')
- grad_ffn_in: float32 [1024, 4096], P('shard')
- grad_ffn_out: float32 [4096, 1024], P('shard')
- grad_norm_gains: float32 [4, 1024], P(None, 'shard')
- grad_norm_biases: float32 [4, 1024], P(None, 'shard')
Inputs may be any that keep to these rules, and one draw needn't show every extreme that they name: `unit_ids`: within each sequence the document number never falls from one unit to the next, and every number 0 to 7 labels one or more units; document lengths are uneven. `enc_ids`: within each sequence the document number never falls from one encoder state to the next, and every number 0 to 7 labels one or more encoder states, so each unit's document has encoder states in the same sequence.
All inputs are finite; a program needn't handle non-finite values.
Results may differ from a plain program's by a relative error of at most 0.025.
The roundings to bfloat16 on the way count: a program that leaves them out, or rounds other values in their place, can miss the bound.
Values may be sent and summed in bfloat16 or wider, within the bound.
No kernel may reach another device: no remote copies, remote signals or barrier semaphores. Data moves between devices by JAX's collectives and lax.ppermute only.
A program may use at most 512 MiB of HBM per device.

v0:
```python
import math

import jax
import jax.numpy as jnp
from jax import lax
from jax.sharding import PartitionSpec as P

HEADS = 16
HEAD = 64


eps_norm = 1e-05
big_negative = -1e30


def layer_norm(values_in, gain_row, bias_row):
    centre = values_in - jnp.mean(values_in, axis=-1, keepdims=True)
    spread = jnp.mean(centre * centre, axis=-1, keepdims=True)
    return centre * lax.rsqrt(spread + eps_norm) * gain_row + bias_row


def norm_backward(values_in, gain_row, bias_row, grad_out):
    result, pullback = jax.vjp(layer_norm, values_in, gain_row, bias_row)
    return pullback(grad_out)


def gelu_slope(values_in):
    return 0.5 * (1.0 + lax.erf(values_in * (1.0 / math.sqrt(2.0)))) + values_in * jnp.exp(
        -0.5 * values_in * values_in
    ) * (1.0 / math.sqrt(2.0 * math.pi))


def mask_for(query_ids, key_ids, first_row, block_rows, causal):
    allowed = query_ids[first_row : first_row + block_rows, None] == key_ids[None, :]
    if causal:
        allowed = allowed & (
            (first_row + jnp.arange(block_rows))[:, None] >= jnp.arange(key_ids.shape[0])[None, :]
        )
    return allowed


def block_scores(query_part, heads_k, allowed):
    raw_scores = jnp.einsum("qhe,khe->hqk", query_part, heads_k, preferred_element_type=jnp.float32)
    return jnp.where(allowed[None], raw_scores * (1.0 / math.sqrt(HEAD)), big_negative)


def attend_forward(queries, key_rows, value_rows, query_ids, key_ids, causal):
    row_count = queries.shape[0]
    key_count = key_rows.shape[0]
    block_rows = min(512, row_count)
    heads_k = key_rows.reshape(key_count, HEADS, HEAD)
    heads_v = value_rows.reshape(key_count, HEADS, HEAD)
    outputs = []
    log_parts = []
    for first_row in range(0, row_count, block_rows):
        query_part = queries[first_row : first_row + block_rows].reshape(block_rows, HEADS, HEAD)
        scores = block_scores(
            query_part, heads_k, mask_for(query_ids, key_ids, first_row, block_rows, causal)
        )
        top_score = jnp.max(scores, axis=-1, keepdims=True)
        exp_scores = jnp.exp(scores - top_score)
        row_total = jnp.sum(exp_scores, axis=-1, keepdims=True)
        soft_probs = (exp_scores / row_total).astype(jnp.bfloat16)
        attended = jnp.einsum(
            "hqk,khe->qhe", soft_probs, heads_v, preferred_element_type=jnp.float32
        )
        outputs.append(attended.reshape(block_rows, HEADS * HEAD).astype(jnp.bfloat16))
        log_parts.append(top_score + jnp.log(row_total))
    return (jnp.concatenate(outputs, axis=0), jnp.concatenate(log_parts, axis=1))


def attend_backward(
    queries, key_rows, value_rows, query_ids, key_ids, log_sums, grad_attended, causal
):
    row_count = queries.shape[0]
    key_count = key_rows.shape[0]
    block_rows = min(512, row_count)
    heads_k = key_rows.reshape(key_count, HEADS, HEAD)
    heads_v = value_rows.reshape(key_count, HEADS, HEAD)
    grad_query_parts = []
    grad_keys = jnp.zeros((key_count, HEADS, HEAD), jnp.float32)
    grad_values = jnp.zeros((key_count, HEADS, HEAD), jnp.float32)
    for first_row in range(0, row_count, block_rows):
        query_part = queries[first_row : first_row + block_rows].reshape(block_rows, HEADS, HEAD)
        scores = block_scores(
            query_part, heads_k, mask_for(query_ids, key_ids, first_row, block_rows, causal)
        )
        soft_probs = jnp.exp(scores - log_sums[:, first_row : first_row + block_rows])
        grad_part = grad_attended[first_row : first_row + block_rows].reshape(
            block_rows, HEADS, HEAD
        )
        grad_probs = jnp.einsum(
            "qhe,khe->hqk", grad_part, heads_v, preferred_element_type=jnp.float32
        )
        inner_sum = jnp.sum(soft_probs * grad_probs, axis=-1, keepdims=True)
        grad_raw = (soft_probs * (grad_probs - inner_sum) * (1.0 / math.sqrt(HEAD))).astype(
            jnp.bfloat16
        )
        grad_query = jnp.einsum(
            "hqk,khe->qhe", grad_raw, heads_k, preferred_element_type=jnp.float32
        )
        grad_query_parts.append(grad_query.reshape(block_rows, HEADS * HEAD))
        grad_keys = grad_keys + jnp.einsum(
            "hqk,qhe->khe", grad_raw, query_part, preferred_element_type=jnp.float32
        )
        grad_values = grad_values + jnp.einsum(
            "hqk,qhe->khe",
            soft_probs.astype(jnp.bfloat16),
            grad_part,
            preferred_element_type=jnp.float32,
        )
    grad_queries = jnp.concatenate(grad_query_parts, axis=0).astype(jnp.bfloat16)
    return (
        grad_queries,
        grad_keys.reshape(key_count, HEADS * HEAD).astype(jnp.bfloat16),
        grad_values.reshape(key_count, HEADS * HEAD).astype(jnp.bfloat16),
    )


def project(left, right):
    return jnp.dot(left, right, preferred_element_type=jnp.float32)


def weight_term(left, right):
    return jnp.einsum("ra,rb->ab", left, right, preferred_element_type=jnp.float32)


def back_project(grad_rows, weight):
    return jnp.einsum("rb,ab->ra", grad_rows, weight, preferred_element_type=jnp.float32)


def body(
    tokens,
    enc_states,
    unit_ids,
    enc_ids,
    self_q,
    self_k,
    self_v,
    self_o,
    cross_q,
    cross_k,
    cross_v,
    cross_o,
    ffn_in,
    ffn_out,
    norm_gains,
    norm_biases,
    cotangent,
):
    gathered = (
        lax.all_gather(self_q, "shard", axis=0, tiled=True),
        lax.all_gather(self_k, "shard", axis=0, tiled=True),
        lax.all_gather(self_v, "shard", axis=0, tiled=True),
        lax.all_gather(self_o, "shard", axis=0, tiled=True),
        lax.all_gather(cross_q, "shard", axis=0, tiled=True),
        lax.all_gather(cross_k, "shard", axis=0, tiled=True),
        lax.all_gather(cross_v, "shard", axis=0, tiled=True),
        lax.all_gather(cross_o, "shard", axis=0, tiled=True),
        lax.all_gather(ffn_in, "shard", axis=0, tiled=True),
        lax.all_gather(ffn_out, "shard", axis=0, tiled=True),
        lax.all_gather(norm_gains, "shard", axis=1, tiled=True),
        lax.all_gather(norm_biases, "shard", axis=1, tiled=True),
    )
    seq_count = tokens.shape[0]
    unit_count = tokens.shape[1]
    enc_count = enc_states.shape[1]
    row_count = seq_count * unit_count
    width = tokens.shape[2]
    w_sq, w_sk, w_sv, w_so, w_cq, w_ck, w_cv, w_co, w_in, w_out, gain_set, bias_set = gathered
    gain_rows = gain_set.astype(jnp.float32)
    bias_rows = bias_set.astype(jnp.float32)
    rows_in = tokens.reshape(row_count, width).astype(jnp.float32)
    enc_rows = enc_states.reshape(seq_count * enc_count, width)
    normed_one = layer_norm(rows_in, gain_rows[0], bias_rows[0]).astype(jnp.bfloat16)
    queries_one = project(normed_one, w_sq).astype(jnp.bfloat16)
    keys_one = project(normed_one, w_sk).astype(jnp.bfloat16)
    values_one = project(normed_one, w_sv).astype(jnp.bfloat16)

    def self_forward(seq_items):
        return attend_forward(
            seq_items[0], seq_items[1], seq_items[2], seq_items[3], seq_items[3], True
        )

    attended_one, log_one = lax.map(
        self_forward,
        (
            queries_one.reshape(seq_count, unit_count, width),
            keys_one.reshape(seq_count, unit_count, width),
            values_one.reshape(seq_count, unit_count, width),
            unit_ids,
        ),
    )
    attended_one = attended_one.reshape(row_count, width)
    after_self = rows_in + project(attended_one, w_so)
    normed_two = layer_norm(after_self, gain_rows[1], bias_rows[1]).astype(jnp.bfloat16)
    queries_two = project(normed_two, w_cq).astype(jnp.bfloat16)
    keys_two = project(enc_rows, w_ck).astype(jnp.bfloat16)
    values_two = project(enc_rows, w_cv).astype(jnp.bfloat16)

    def cross_forward(seq_items):
        return attend_forward(
            seq_items[0], seq_items[1], seq_items[2], seq_items[3], seq_items[4], False
        )

    attended_two, log_two = lax.map(
        cross_forward,
        (
            queries_two.reshape(seq_count, unit_count, width),
            keys_two.reshape(seq_count, enc_count, width),
            values_two.reshape(seq_count, enc_count, width),
            unit_ids,
            enc_ids,
        ),
    )
    attended_two = attended_two.reshape(row_count, width)
    after_cross = after_self + project(attended_two, w_co)
    normed_three = layer_norm(after_cross, gain_rows[2], bias_rows[2]).astype(jnp.bfloat16)
    pre_active = project(normed_three, w_in)
    hidden = jax.nn.gelu(pre_active, approximate=False).astype(jnp.bfloat16)
    after_ffn = after_cross + project(hidden, w_out)
    layer_out = (
        layer_norm(after_ffn, gain_rows[3], bias_rows[3])
        .astype(jnp.bfloat16)
        .reshape(seq_count, unit_count, width)
    )
    back_weights = (
        lax.all_gather(self_q, "shard", axis=0, tiled=True),
        lax.all_gather(self_k, "shard", axis=0, tiled=True),
        lax.all_gather(self_v, "shard", axis=0, tiled=True),
        lax.all_gather(self_o, "shard", axis=0, tiled=True),
        lax.all_gather(cross_q, "shard", axis=0, tiled=True),
        lax.all_gather(cross_k, "shard", axis=0, tiled=True),
        lax.all_gather(cross_v, "shard", axis=0, tiled=True),
        lax.all_gather(cross_o, "shard", axis=0, tiled=True),
        lax.all_gather(ffn_in, "shard", axis=0, tiled=True),
        lax.all_gather(ffn_out, "shard", axis=0, tiled=True),
        lax.all_gather(norm_gains, "shard", axis=1, tiled=True),
        lax.all_gather(norm_biases, "shard", axis=1, tiled=True),
    )
    b_sq, b_sk, b_sv, b_so, b_cq, b_ck, b_cv, b_co, b_in, b_out, back_gains, back_biases = (
        back_weights
    )
    gain_back = back_gains.astype(jnp.float32)
    bias_back = back_biases.astype(jnp.float32)
    grad_out = cotangent.reshape(row_count, width).astype(jnp.float32)
    grad_after_ffn, gain_four, bias_four = norm_backward(
        after_ffn, gain_back[3], bias_back[3], grad_out
    )
    grad_ffn_rows = grad_after_ffn.astype(jnp.bfloat16)
    grad_w_out = weight_term(hidden, grad_ffn_rows)
    grad_hidden = back_project(grad_ffn_rows, b_out)
    grad_pre = (grad_hidden * gelu_slope(pre_active)).astype(jnp.bfloat16)
    grad_w_in = weight_term(normed_three, grad_pre)
    grad_normed_three = back_project(grad_pre, b_in)
    grad_norm_three, gain_three, bias_three = norm_backward(
        after_cross, gain_back[2], bias_back[2], grad_normed_three
    )
    grad_after_cross = grad_after_ffn + grad_norm_three
    grad_cross_rows = grad_after_cross.astype(jnp.bfloat16)
    grad_w_co = weight_term(attended_two, grad_cross_rows)
    grad_attended_two = back_project(grad_cross_rows, b_co).astype(jnp.bfloat16)

    def cross_backward(seq_items):
        return attend_backward(
            seq_items[0],
            seq_items[1],
            seq_items[2],
            seq_items[3],
            seq_items[4],
            seq_items[5],
            seq_items[6],
            False,
        )

    grad_q_two, grad_k_two, grad_v_two = lax.map(
        cross_backward,
        (
            queries_two.reshape(seq_count, unit_count, width),
            keys_two.reshape(seq_count, enc_count, width),
            values_two.reshape(seq_count, enc_count, width),
            unit_ids,
            enc_ids,
            log_two,
            grad_attended_two.reshape(seq_count, unit_count, width),
        ),
    )
    grad_q_two = grad_q_two.reshape(row_count, width)
    grad_k_two = grad_k_two.reshape(seq_count * enc_count, width)
    grad_v_two = grad_v_two.reshape(seq_count * enc_count, width)
    grad_w_cq = weight_term(normed_two, grad_q_two)
    grad_w_ck = weight_term(enc_rows, grad_k_two)
    grad_w_cv = weight_term(enc_rows, grad_v_two)
    grad_enc = (back_project(grad_k_two, b_ck) + back_project(grad_v_two, b_cv)).reshape(
        seq_count, enc_count, width
    )
    grad_norm_two, gain_two, bias_two = norm_backward(
        after_self, gain_back[1], bias_back[1], back_project(grad_q_two, b_cq)
    )
    grad_after_self = grad_after_cross + grad_norm_two
    grad_self_rows = grad_after_self.astype(jnp.bfloat16)
    grad_w_so = weight_term(attended_one, grad_self_rows)
    grad_attended_one = back_project(grad_self_rows, b_so).astype(jnp.bfloat16)

    def self_backward(seq_items):
        return attend_backward(
            seq_items[0],
            seq_items[1],
            seq_items[2],
            seq_items[3],
            seq_items[3],
            seq_items[4],
            seq_items[5],
            True,
        )

    grad_q_one, grad_k_one, grad_v_one = lax.map(
        self_backward,
        (
            queries_one.reshape(seq_count, unit_count, width),
            keys_one.reshape(seq_count, unit_count, width),
            values_one.reshape(seq_count, unit_count, width),
            unit_ids,
            log_one,
            grad_attended_one.reshape(seq_count, unit_count, width),
        ),
    )
    grad_q_one = grad_q_one.reshape(row_count, width)
    grad_k_one = grad_k_one.reshape(row_count, width)
    grad_v_one = grad_v_one.reshape(row_count, width)
    grad_w_sq = weight_term(normed_one, grad_q_one)
    grad_w_sk = weight_term(normed_one, grad_k_one)
    grad_w_sv = weight_term(normed_one, grad_v_one)
    grad_normed_one = (
        back_project(grad_q_one, b_sq)
        + back_project(grad_k_one, b_sk)
        + back_project(grad_v_one, b_sv)
    )
    grad_norm_one, gain_one, bias_one = norm_backward(
        rows_in, gain_back[0], bias_back[0], grad_normed_one
    )
    grad_tokens = (grad_after_self + grad_norm_one).reshape(seq_count, unit_count, width)
    grad_gains = jnp.stack([gain_one, gain_two, gain_three, gain_four])
    grad_biases = jnp.stack([bias_one, bias_two, bias_three, bias_four])
    owned = (
        lax.psum_scatter(grad_w_sq, "shard", scatter_dimension=0, tiled=True),
        lax.psum_scatter(grad_w_sk, "shard", scatter_dimension=0, tiled=True),
        lax.psum_scatter(grad_w_sv, "shard", scatter_dimension=0, tiled=True),
        lax.psum_scatter(grad_w_so, "shard", scatter_dimension=0, tiled=True),
        lax.psum_scatter(grad_w_cq, "shard", scatter_dimension=0, tiled=True),
        lax.psum_scatter(grad_w_ck, "shard", scatter_dimension=0, tiled=True),
        lax.psum_scatter(grad_w_cv, "shard", scatter_dimension=0, tiled=True),
        lax.psum_scatter(grad_w_co, "shard", scatter_dimension=0, tiled=True),
        lax.psum_scatter(grad_w_in, "shard", scatter_dimension=0, tiled=True),
        lax.psum_scatter(grad_w_out, "shard", scatter_dimension=0, tiled=True),
        lax.psum_scatter(grad_gains, "shard", scatter_dimension=1, tiled=True),
        lax.psum_scatter(grad_biases, "shard", scatter_dimension=1, tiled=True),
    )
    summed = (
        lax.psum(owned[0].astype(jnp.bfloat16), "rep").astype(jnp.float32),
        lax.psum(owned[1].astype(jnp.bfloat16), "rep").astype(jnp.float32),
        lax.psum(owned[2].astype(jnp.bfloat16), "rep").astype(jnp.float32),
        lax.psum(owned[3].astype(jnp.bfloat16), "rep").astype(jnp.float32),
        lax.psum(owned[4].astype(jnp.bfloat16), "rep").astype(jnp.float32),
        lax.psum(owned[5].astype(jnp.bfloat16), "rep").astype(jnp.float32),
        lax.psum(owned[6].astype(jnp.bfloat16), "rep").astype(jnp.float32),
        lax.psum(owned[7].astype(jnp.bfloat16), "rep").astype(jnp.float32),
        lax.psum(owned[8].astype(jnp.bfloat16), "rep").astype(jnp.float32),
        lax.psum(owned[9].astype(jnp.bfloat16), "rep").astype(jnp.float32),
        lax.psum(owned[10].astype(jnp.bfloat16), "rep").astype(jnp.float32),
        lax.psum(owned[11].astype(jnp.bfloat16), "rep").astype(jnp.float32),
    )
    return (
        layer_out,
        grad_tokens,
        grad_enc,
        summed[0],
        summed[1],
        summed[2],
        summed[3],
        summed[4],
        summed[5],
        summed[6],
        summed[7],
        summed[8],
        summed[9],
        summed[10],
        summed[11],
    )


def solution(mesh):
    return jax.shard_map(
        body,
        mesh=mesh,
        in_specs=(
            P(("rep", "shard"), None, None),
            P(("rep", "shard"), None, None),
            P(("rep", "shard"), None),
            P(("rep", "shard"), None),
            P("shard", None),
            P("shard", None),
            P("shard", None),
            P("shard", None),
            P("shard", None),
            P("shard", None),
            P("shard", None),
            P("shard", None),
            P("shard", None),
            P("shard", None),
            P(None, "shard"),
            P(None, "shard"),
            P(("rep", "shard"), None, None),
        ),
        out_specs=(
            P(("rep", "shard"), None, None),
            P(("rep", "shard"), None, None),
            P(("rep", "shard"), None, None),
            P("shard", None),
            P("shard", None),
            P("shard", None),
            P("shard", None),
            P("shard", None),
            P("shard", None),
            P("shard", None),
            P("shard", None),
            P("shard", None),
            P("shard", None),
            P(None, "shard"),
            P(None, "shard"),
        ),
        check_vma=False,
    )
```

profile of v0, /device:TPU:0, one launch (start us, length us, event | category | flops | bytes accessed | tf_op | source)
XLA Modules:
  0.0 1966.8 jit_solution(9472068978425510376)
XLA Ops:
  14.7 23.3 %all-gather = bf16[16,64,4]{1,2,0:T(4,128)(2,1)S(1)} all-gather(bf16[1,64,4]{1,2,0:T(4,128)(2,1)} %bitcast.329), channel_id=1, replica_groups=mesh['rep'=2,'shard'=16] {'shard'}, dimensions={0}, use_global_device_ids=true | all-gather | bytes 8704 | tf_op jit(solution)/shard_map/all_gather | solution.py:162
  38.8 17.7 all-gather.1
  78.6 18.2 all-gather.17.cloned.1.call-done
  101.8 14.0 fusion.13
  115.8 14.3 fusion.12
  130.1 25.1 %fusion.8 = (f32[16,512]{1,0:T(8,128)S(1)}, f32[16,512]{1,0:T(8,128)S(1)}) fusion(f32[16,512,1024]{2,1,0:T(8,128)} %get-tuple-element.240, f32[16,512]{1,0:T(8,128)S(1)} %get-tuple-element.239, pred[512,1024]{1,0:T(8,128)(4,1)S(1)} %copy-done.32, f32[16,512]{1,0:T(8,128)S(1)} %get-tuple-element.237, f32[16,512,1024]{2,1,0:T(8,128)} %get-tuple-element.238, ...), kind=kLoop, calls=%fused_computation.32 | loop fusion | flops 67092480 | bytes 68288512 | tf_op jit(solution)/shard_map/while/body/eval_jaxpr/reduce_sum | solution.py:62
  160.4 16.2 fusion.210
  176.6 15.7 fusion.211
  192.3 5.3 fusion.311
  200.7 22.8 %all-gather.23.cloned.1.call-done = bf16[1024,1024]{1,0:T(8,128)(2,1)} async-done(((bf16[64,1024]{1,0:T(8,128)(2,1)}), bf16[1024,1024]{1,0:T(8,128)(2,1)}) %all-gather.23.cloned.1.call-update) | async-done | bytes 2097168 | tf_op jit(solution)/shard_map/all_gather | solution.py:156
  223.6 5.6 convolution_convert_fusion.2
  230.3 35.5 %all-gather.25.cloned.1.call-done = bf16[1024,1024]{1,0:T(8,128)(2,1)} async-done(((bf16[64,1024]{1,0:T(8,128)(2,1)}), bf16[1024,1024]{1,0:T(8,128)(2,1)}) %all-gather.25.cloned.1.call-update) | async-done | bytes 2097168 | tf_op jit(solution)/shard_map/all_gather | solution.py:157
  269.9 14.2 fusion.15
  284.1 15.1 fusion.11
  299.2 9.0 all-gather.21.cloned.1.call-done
  312.2 16.2 fusion.208
  328.4 14.1 fusion.14
  342.5 15.2 fusion.10
  358.4 15.7 fusion.209
  374.1 5.8 fusion.312
  383.9 42.4 %all-gather.29.cloned.1.call-done = bf16[1024,4096]{1,0:T(8,128)(2,1)} async-done(((bf16[64,4096]{1,0:T(8,128)(2,1)}), bf16[1024,4096]{1,0:T(8,128)(2,1)}) %all-gather.29.cloned.1.call-update) | async-done | bytes 8388624 | tf_op jit(solution)/shard_map/all_gather | solution.py:160
  426.3 48.0 %fusion.54 = (bf16[1024,4096]{1,0:T(8,128)(2,1)}, f32[1024,4096]{1,0:T(8,128)}) fusion(bf16[1024,4096]{1,0:T(8,128)(2,1)} %all-gather.29.cloned.1.call-done, bf16[1024,1024]{0,1:T(8,128)(2,1)} %add_convert_fusion.11.clone.4), kind=kOutput, calls=%fused_computation.56 | convolution fusion | flops 8862564352 | bytes 35651584 | tf_op jit(solution)/shard_map/dot_general | solution.py:121
  474.4 27.2 %all-gather.31.cloned.1.call-done = bf16[4096,1024]{1,0:T(8,128)(2,1)} async-done(((bf16[256,1024]{1,0:T(8,128)(2,1)}), bf16[4096,1024]{1,0:T(8,128)(2,1)}) %all-gather.31.cloned.1.call-update) | async-done | bytes 8388624 | tf_op jit(solution)/shard_map/all_gather | solution.py:161
  501.6 15.9 fusion.313
  524.2 22.1 %fusion.60 = bf16[1024,4096]{1,0:T(8,128)(2,1)} fusion(f32[1024,4096]{1,0:T(8,128)} %get-tuple-element.250, bf16[4096,1024]{1,0:T(8,128)(2,1)} %all-gather.31.cloned.1.call-done, f32[1024]{0:T(1024)S(1)} %negate_multiply_fusion.4, bf16[1,1024,1024]{1,2,0:T(8,128)(2,1)S(1)} %copy-done.5, f32[1024,1024]{0,1:T(8,128)} %get-tuple-element.252, ...), kind=kOutput, calls=%fused_computation.62 | convolution fusion | flops 8641314816 | bytes 39866368 | tf_op jit(solution)/shard_map/rb,ab->ra/dot_general | solution.py:129
  546.3 15.8 fusion.314
  562.1 5.4 copy.79
  588.2 5.2 convolution_convert_fusion.1
  594.5 17.8 fusion.119
  612.3 18.6 add_convert_fusion
  630.9 6.0 convolution_bitcast_fusion
  636.8 5.4 copy.95
  642.5 18.0 fusion.316
  660.5 61.0 %fusion.26 = f32[16,64,1024]{2,1,0:T(8,128)} fusion(bf16[512,16,64]{0,2,1:T(8,128)(2,1)S(1)} %bitcast.268, f32[16,512,1024]{2,1,0:T(8,128)} %fusion.316, f32[16,512,1024]{2,1,0:T(8,128)} %get-tuple-element.246, f32[16,512]{1,0:T(8,128)S(1)} %log_add_fusion.3, pred[512,1024]{1,0:T(8,128)(4,1)} %get-tuple-element.234), kind=kOutput, calls=%fused_computation.43 | convolution fusion | flops 1166025728 | bytes 72908800 | tf_op jit(solution)/shard_map/while/body/eval_jaxpr/hqk,qhe->khe/dot_general | solution.py:103
  721.4 17.8 fusion.317
  739.2 59.9 %add_convert_fusion.1 = bf16[16,64,1024]{2,1,0:T(8,128)(2,1)} fusion(f32[16,64,1024]{2,1,0:T(8,128)} %fusion.26, bf16[512,16,64]{0,2,1:T(8,128)(2,1)S(1)} %bitcast.266, f32[16,512,1024]{2,1,0:T(8,128)} %fusion.317, f32[16,512,1024]{2,1,0:T(8,128)} %get-tuple-element.244, f32[16,512]{1,0:T(8,128)S(1)} %log_add_fusion.2, ...), kind=kOutput, calls=%fused_computation.158 | convolution fusion | flops 1168122880 | bytes 75005952 | tf_op jit(solution)/shard_map/while/body/eval_jaxpr/hqk,qhe->khe/dot_general | solution.py:103
  799.1 6.0 convolution_bitcast_fusion.1
  805.0 5.3 copy.93
  810.5 62.2 %fusion.205 = bf16[16,64,512]{2,1,0:T(8,128)(2,1)} fusion(bf16[1024,16,64]{0,2,1:T(8,128)(2,1)} %bitcast.250, f32[16,512,1024]{2,1,0:T(8,128)} %fusion.316, f32[16,512,1024]{2,1,0:T(8,128)} %get-tuple-element.246, f32[16,512]{1,0:T(8,128)S(1)} %log_add_fusion.3, pred[512,1024]{1,0:T(8,128)(4,1)} %get-tuple-element.234), kind=kOutput, calls=%fused_computation.206 | convolution fusion | flops 1166550016 | bytes 70811648 | tf_op jit(solution)/shard_map/while/body/eval_jaxpr/hqk,khe->qhe/dot_general | solution.py:99
  872.7 61.8 %fusion.202 = bf16[16,64,512]{2,1,0:T(8,128)(2,1)} fusion(bf16[1024,16,64]{0,2,1:T(8,128)(2,1)} %bitcast.251, f32[16,512,1024]{2,1,0:T(8,128)} %fusion.317, f32[16,512,1024]{2,1,0:T(8,128)} %get-tuple-element.244, f32[16,512]{1,0:T(8,128)S(1)} %log_add_fusion.2, pred[512,1024]{1,0:T(8,128)(4,1)} %get-tuple-element.233), kind=kOutput, calls=%fused_computation.205 | convolution fusion | flops 1166550016 | bytes 70811648 | tf_op jit(solution)/shard_map/while/body/eval_jaxpr/hqk,khe->qhe/dot_general | solution.py:99
  934.6 7.2 fusion.214
  943.0 7.0 fusion.315
  950.0 5.6 copy.80
  955.6 5.8 multiply_reduce_fusion.5
  978.4 17.0 fusion.115
  995.4 18.3 add_convert_fusion.2
  1013.7 6.6 fusion.291
  1020.3 19.1 fusion.318
  1039.5 60.9 %fusion.40 = f32[16,64,1024]{2,1,0:T(8,128)} fusion(bf16[512,16,64]{0,2,1:T(8,128)(2,1)S(1)} %bitcast.264, f32[16,512,1024]{2,1,0:T(8,128)} %fusion.318, f32[16,512,1024]{2,1,0:T(8,128)} %get-tuple-element.240, f32[16,512]{1,0:T(8,128)S(1)} %log_add_fusion.1, pred[512,1024]{1,0:T(8,128)(4,1)} %get-tuple-element.231), kind=kOutput, calls=%fused_computation.49 | convolution fusion | flops 1166025728 | bytes 72908800 | tf_op jit(solution)/shard_map/while/body/eval_jaxpr/hqk,qhe->khe/dot_general | solution.py:103
  1100.3 18.5 fusion.319
  1118.9 60.4 %add_convert_fusion.3 = bf16[16,64,1024]{2,1,0:T(8,128)(2,1)} fusion(f32[16,64,1024]{2,1,0:T(8,128)} %fusion.40, bf16[512,16,64]{0,2,1:T(8,128)(2,1)S(1)} %bitcast.262, f32[16,512,1024]{2,1,0:T(8,128)} %fusion.319, f32[16,512,1024]{2,1,0:T(8,128)} %get-tuple-element.238, f32[16,512]{1,0:T(8,128)S(1)} %log_add_fusion, pred[512,1024]{1,0:T(8,128)(4,1)} %get-tuple-element.232), kind=kOutput, calls=%fused_computation.162 | convolution fusion | flops 1168122880 | bytes 75005952 | tf_op jit(solution)/shard_map/while/body/eval_jaxpr/hqk,qhe->khe/dot_general | solution.py:103
  1179.3 6.6 fusion.293
  1186.0 62.1 %fusion.199 = bf16[16,64,512]{2,1,0:T(8,128)(2,1)S(1)} fusion(bf16[1024,16,64]{0,2,1:T(8,128)(2,1)} %bitcast.247, f32[16,512,1024]{2,1,0:T(8,128)} %fusion.318, f32[16,512,1024]{2,1,0:T(8,128)} %get-tuple-element.240, f32[16,512]{1,0:T(8,128)S(1)} %log_add_fusion.1, pred[512,1024]{1,0:T(8,128)(4,1)} %get-tuple-element.231), kind=kOutput, calls=%fused_computation.204 | convolution fusion | flops 1166550016 | bytes 70811648 | tf_op jit(solution)/shard_map/while/body/eval_jaxpr/hqk,khe->qhe/dot_general | solution.py:99
  1248.0 61.9 %fusion.196 = bf16[16,64,512]{2,1,0:T(8,128)(2,1)} fusion(bf16[1024,16,64]{0,2,1:T(8,128)(2,1)} %bitcast.248, f32[16,512,1024]{2,1,0:T(8,128)} %fusion.319, f32[16,512,1024]{2,1,0:T(8,128)} %get-tuple-element.238, f32[16,512]{1,0:T(8,128)S(1)} %log_add_fusion, pred[512,1024]{1,0:T(8,128)(4,1)} %get-tuple-element.232), kind=kOutput, calls=%fused_computation.203 | convolution fusion | flops 1166550016 | bytes 70811648 | tf_op jit(solution)/shard_map/while/body/eval_jaxpr/hqk,khe->qhe/dot_general | solution.py:99
  1310.0 6.3 fusion.212
  1316.9 17.8 fusion.220
  1335.4 16.9 fusion.295
  1391.1 180.2 %reduce-scatter.35.cloned.1.call-done = f32[256,1024]{1,0:T(8,128)} async-done(((f32[4096,1024]{1,0:T(8,128)}), f32[256,1024]{1,0:T(8,128)}) %reduce-scatter.35.cloned.1.call-update) | async-done | bytes 1048592 | tf_op jit(solution)/shard_map/reduce_scatter | solution.py:355
  1573.3 179.5 %reduce-scatter.33.cloned.1.call-done = f32[64,4096]{1,0:T(8,128)} async-done(((f32[1024,4096]{1,0:T(8,128)}), f32[64,4096]{1,0:T(8,128)}) %reduce-scatter.33.cloned.1.call-update) | async-done | bytes 1048592 | tf_op jit(solution)/shard_map/reduce_scatter | solution.py:354
  1754.9 7.8 add_bitcast_fusion.1
  1762.7 5.4 copy.87
  1777.4 33.8 %reduce-scatter.41.cloned.1.call-done = f32[64,4]{1,0:T(8,128)} async-done(((f32[1024,4]{1,0:T(8,128)}), f32[64,4]{1,0:T(8,128)}) %reduce-scatter.41.cloned.1.call-update) | async-done | bytes 1040
  1812.0 58.0 %reduce-scatter.43.cloned.1.call-done = f32[64,4]{1,0:T(8,128)} async-done(((f32[1024,4]{1,0:T(8,128)}), f32[64,4]{1,0:T(8,128)}) %reduce-scatter.43.cloned.1.call-update) | async-done | bytes 1040
  1877.0 66.3 %all-reduce.4.cloned.1.call-done = (bf16[64,1024]{0,1:T(8,128)(2,1)}, bf16[64,1024]{0,1:T(8,128)(2,1)}, bf16[64,1024]{1,0:T(8,128)(2,1)}, bf16[64,1024]{1,0:T(8,...) async-done(((bf16[64,1024]{0,1:T(8,128)(2,1)}, ...) | async-done | bytes 2097168 | tf_op jit(solution)/shard_map/psum | solution.py:365
  (401 shorter events, 181.6 us)
Async XLA Ops:
  7.2 258.6 %copy-start = (bf16[1,1024,1024]{2,1,0:T(8,128)(2,1)S(1)}, bf16[1,1024,1024]{2,1,0:T(8,128)(2,1)}, u32[]{:S(2)}) copy-start(bf16[1,1024,1024]{2,1,0:T(8,128)(2,1)} %param.18) | copy-start | bytes 6291460
  7.2 65.4 %all-gather.15.cloned.1.call-start = ((), (), s32[]{:S(2)}) async-start(), calls=%async_computation.13 | async-start | bytes 2228224 | tf_op jit(solution)/shard_map/all_gather | solution.py:152
  7.9 88.8 %all-gather.17.cloned.1.call-start = ((), (), s32[]{:S(2)}) async-start(), calls=%async_computation.14 | async-start | bytes 2228224 | tf_op jit(solution)/shard_map/all_gather | solution.py:153
  8.7 146.6 %all-gather.13.cloned.1.call-start = ((), (), s32[]{:S(2)}) async-start(), calls=%async_computation.12 | async-start | bytes 2228224 | tf_op jit(solution)/shard_map/all_gather | solution.py:154
  9.4 182.9 %all-gather.19.cloned.1.call-start = ((), (), s32[]{:S(2)}) async-start(), calls=%async_computation.15 | async-start | bytes 2228224 | tf_op jit(solution)/shard_map/all_gather | solution.py:155
  10.0 213.6 %all-gather.23.cloned.1.call-start = ((), (), s32[]{:S(2)}) async-start(), calls=%async_computation.17 | async-start | bytes 2228224 | tf_op jit(solution)/shard_map/all_gather | solution.py:156
  10.6 255.2 %all-gather.25.cloned.1.call-start = ((), (), s32[]{:S(2)}) async-start(), calls=%async_computation.18 | async-start | bytes 2228224 | tf_op jit(solution)/shard_map/all_gather | solution.py:157
  11.2 297.0 %all-gather.21.cloned.1.call-start = ((), (), s32[]{:S(2)}) async-start(), calls=%async_computation.16 | async-start | bytes 2228224 | tf_op jit(solution)/shard_map/all_gather | solution.py:158
  11.9 362.2 %all-gather.27.cloned.1.call-start = ((), (), s32[]{:S(2)}) async-start(), calls=%async_computation.19 | async-start | bytes 2228224 | tf_op jit(solution)/shard_map/all_gather | solution.py:159
  12.7 413.7 %all-gather.29.cloned.1.call-start = ((), (), s32[]{:S(2)}) async-start(), calls=%async_computation.20 | async-start | bytes 8912896 | tf_op jit(solution)/shard_map/all_gather | solution.py:160
  13.4 488.2 %all-gather.31.cloned.1.call-start = ((), (), s32[]{:S(2)}) async-start(), calls=%async_computation.21 | async-start | bytes 8912896 | tf_op jit(solution)/shard_map/all_gather | solution.py:161
  14.0 1360.1 %reduce-scatter.31.cloned.1.call-start = ((), (), s32[]{:S(2)}) async-start(), calls=%async_computation.27 | async-start | bytes 4456448 | tf_op jit(solution)/shard_map/reduce_scatter | solution.py:353
  38.8 116.5 %copy-start.83 = (f32[1,1024]{1,0:T(1,128)}, f32[1,1024]{1,0:T(1,128)S(1)}, u32[]{:S(2)}) copy-start(f32[1,1024]{1,0:T(1,128)S(1)} %get-tuple-element.222) | copy-start | bytes 12292
  57.1 98.2 %copy-start.107 = (f32[1,1024]{1,0:T(1,128)}, f32[1,1024]{1,0:T(1,128)S(1)}, u32[]{:S(2)}) copy-start(f32[1,1024]{1,0:T(1,128)S(1)} %get-tuple-element.226) | copy-start | bytes 12292
  63.1 92.2 %copy-start.66 = (f32[1024]{0:T(1024)}, f32[1024]{0:T(1024)S(1)}, u32[]{:S(2)}) copy-start(f32[1024]{0:T(1024)S(1)} %broadcast_multiply_fusion.3) | copy-start | bytes 12292
  65.9 89.4 %copy-start.77 = (f32[1024]{0:T(1024)}, f32[1024]{0:T(1024)S(1)}, u32[]{:S(2)}) copy-start(f32[1024]{0:T(1024)S(1)} %fusion.222) | copy-start | bytes 12292
  78.6 23.1 %copy-start.21 = (bf16[512,1024]{0,1:T(8,128)(2,1)}, bf16[512,1024]{0,1:T(8,128)(2,1)S(1)}, u32[]{:S(2)}) copy-start(bf16[512,1024]{0,1:T(8,128)(2,1)S(1)} %get-tuple-element.218) | copy-start | bytes 3145732
  115.8 44.6 %copy-start.44 = (f32[16,512]{1,0:T(8,128)}, f32[16,512]{1,0:T(8,128)S(1)}, u32[]{:S(2)}) copy-start(f32[16,512]{1,0:T(8,128)S(1)} %get-tuple-element.237) | copy-start | bytes 98308
  130.1 46.5 %copy-start.46 = (f32[16,512]{1,0:T(8,128)}, f32[16,512]{1,0:T(8,128)S(1)}, u32[]{:S(2)}) copy-start(f32[16,512]{1,0:T(8,128)S(1)} %get-tuple-element.239) | copy-start | bytes 98308
  155.2 21.3 %copy-start.57 = (f32[16,512]{1,0:T(8,128)}, f32[16,512]{1,0:T(8,128)S(1)}, u32[]{:S(2)}) copy-start(f32[16,512]{1,0:T(8,128)S(1)} %get-tuple-element.258) | copy-start | bytes 98308
  160.3 16.2 copy-start.18
  197.7 25.9 %copy-start.85 = (f32[1,1024]{1,0:T(1,128)S(1)}, f32[1,1024]{1,0:T(1,128)}, u32[]{:S(2)}) copy-start(f32[1,1024]{1,0:T(1,128)} %get-tuple-element.221) | copy-start | bytes 12292
  197.7 25.9 %copy-start.110 = (f32[1,1024]{1,0:T(1,128)S(1)}, f32[1,1024]{1,0:T(1,128)}, u32[]{:S(2)}) copy-start(f32[1,1024]{1,0:T(1,128)} %get-tuple-element.225) | copy-start | bytes 12292
  197.7 25.9 %copy-start.68 = (f32[1024]{0:T(1024)}, f32[1024]{0:T(1024)S(1)}, u32[]{:S(2)}) copy-start(f32[1024]{0:T(1024)S(1)} %broadcast_multiply_fusion.2) | copy-start | bytes 12292
  200.7 22.9 %copy-start.81 = (f32[1024]{0:T(1024)}, f32[1024]{0:T(1024)S(1)}, u32[]{:S(2)}) copy-start(f32[1024]{0:T(1024)S(1)} %fusion.223) | copy-start | bytes 12292
  230.3 39.6 %copy-start.25 = (bf16[512,1024]{0,1:T(8,128)(2,1)}, bf16[512,1024]{0,1:T(8,128)(2,1)S(1)}, u32[]{:S(2)}) copy-start(bf16[512,1024]{0,1:T(8,128)(2,1)S(1)} %get-tuple-element.216) | copy-start | bytes 3145732
  284.1 28.0 %copy-start.48 = (f32[16,512]{1,0:T(8,128)}, f32[16,512]{1,0:T(8,128)S(1)}, u32[]{:S(2)}) copy-start(f32[16,512]{1,0:T(8,128)S(1)} %get-tuple-element.243) | copy-start | bytes 98308
  312.1 45.6 %copy-start.19 = (bf16[1024,1024]{0,1:T(8,128)(2,1)}, bf16[1024,1024]{0,1:T(8,128)(2,1)S(1)}, u32[]{:S(2)}) copy-start(bf16[1024,1024]{0,1:T(8,128)(2,1)S(1)} %fusion.189) | copy-start | bytes 6291460
  312.2 16.2 copy-start.17
  312.2 16.2 copy-start.27
  517.4 58.8 %copy-start.73 = (f32[1024]{0:T(1024)}, f32[1024]{0:T(1024)S(1)}, u32[]{:S(2)}) copy-start(f32[1024]{0:T(1024)S(1)} %broadcast_multiply_fusion) | copy-start | bytes 12292
  520.9 55.3 %copy-start.93 = (f32[1024]{0:T(1024)}, f32[1024]{0:T(1024)S(1)}, u32[]{:S(2)}) copy-start(f32[1024]{0:T(1024)S(1)} %get-tuple-element.227) | copy-start | bytes 12292
  520.9 55.3 %copy-start.95 = (f32[1024]{0:T(1024)}, f32[1024]{0:T(1024)S(1)}, u32[]{:S(2)}) copy-start(f32[1024]{0:T(1024)S(1)} %get-tuple-element.228) | copy-start | bytes 12292
  524.2 52.0 %copy-start.103 = (f32[1024]{0:T(1024)}, f32[1024]{0:T(1024)S(1)}, u32[]{:S(2)}) copy-start(f32[1024]{0:T(1024)S(1)} %negate_multiply_fusion.4) | copy-start | bytes 12292
  587.4 788.3 %reduce-scatter.39.cloned.1.call-start = ((), (), s32[]{:S(2)}) async-start(), calls=%async_computation.31 | async-start | bytes 4456448
  594.5 17.8 copy-start.40
  594.5 17.8 copy-start.39
  642.2 18.2 copy-start.28
  642.3 735.3 %reduce-scatter.37.cloned.1.call-start = ((), (), s32[]{:S(2)}) async-start(), calls=%async_computation.30 | async-start | bytes 4456448
  721.4 17.8 copy-start.26
  810.4 568.9 %reduce-scatter.29.cloned.1.call-start = ((), (), s32[]{:S(2)}) async-start(), calls=%async_computation.26 | async-start | bytes 4456448 | tf_op jit(solution)/shard_map/reduce_scatter | solution.py:350
  872.7 61.9 %copy-start.69 = (f32[1024]{0:T(1024)S(1)}, f32[1024]{0:T(1024)}, u32[]{:S(2)}) copy-start(f32[1024]{0:T(1024)} %copy-done.68) | copy-start | bytes 12292
  872.7 61.9 %copy-start.82 = (f32[1024]{0:T(1024)S(1)}, f32[1024]{0:T(1024)}, u32[]{:S(2)}) copy-start(f32[1024]{0:T(1024)} %copy-done.81) | copy-start | bytes 12292
  872.7 61.9 %copy-start.86 = (f32[1,1024]{1,0:T(1,128)S(1)}, f32[1,1024]{1,0:T(1,128)}, u32[]{:S(2)}) copy-start(f32[1,1024]{1,0:T(1,128)} %get-tuple-element.221) | copy-start | bytes 12292
  872.7 61.9 %copy-start.111 = (f32[1,1024]{1,0:T(1,128)S(1)}, f32[1,1024]{1,0:T(1,128)}, u32[]{:S(2)}) copy-start(f32[1,1024]{1,0:T(1,128)} %get-tuple-element.225) | copy-start | bytes 12292
  941.8 439.1 %reduce-scatter.27.cloned.1.call-start = ((), (), s32[]{:S(2)}) async-start(), calls=%async_computation.25 | async-start | bytes 4456448 | tf_op jit(solution)/shard_map/reduce_scatter | solution.py:349
  971.9 410.7 %reduce-scatter.25.cloned.1.call-start = ((), (), s32[]{:S(2)}) async-start(), calls=%async_computation.24 | async-start | bytes 4456448 | tf_op jit(solution)/shard_map/reduce_scatter | solution.py:348
  978.4 17.0 copy-start.41
  978.4 17.0 copy-start.34
  995.4 18.3 copy-start.67
  995.4 18.3 copy-start.78
  995.4 18.3 copy-start.84
  995.4 18.3 copy-start.108
  1020.3 19.2 copy-start.24
  1020.3 363.9 %reduce-scatter.23.cloned.1.call-start = ((), (), s32[]{:S(2)}) async-start(), calls=%async_computation.23 | async-start | bytes 4456448 | tf_op jit(solution)/shard_map/reduce_scatter | solution.py:347
  1100.3 18.5 copy-start.22
  1185.9 203.6 %reduce-scatter.21.cloned.1.call-start = ((), (), s32[]{:S(2)}) async-start(), calls=%async_computation.22 | async-start | bytes 4456448 | tf_op jit(solution)/shard_map/reduce_scatter | solution.py:346
  1248.0 61.9 %copy-start.124 = (bf16[16,64,512]{2,1,0:T(8,128)(2,1)}, bf16[16,64,512]{2,1,0:T(8,128)(2,1)S(1)}, u32[]{:S(2)}) copy-start(bf16[16,64,512]{2,1,0:T(8,128)(2,1)S(1)} %fusion.199) | copy-start | bytes 3145732
  1316.3 255.0 %reduce-scatter.35.cloned.1.call-start = ((), (), s32[]{:S(2)}) async-start(), calls=%async_computation.29 | async-start | bytes 17825792 | tf_op jit(solution)/shard_map/reduce_scatter | solution.py:355
  1334.7 418.1 %reduce-scatter.33.cloned.1.call-start = ((), (), s32[]{:S(2)}) async-start(), calls=%async_computation.28 | async-start | bytes 17825792 | tf_op jit(solution)/shard_map/reduce_scatter | solution.py:354
  1352.3 458.9 %reduce-scatter.41.cloned.1.call-start = ((), (), s32[]{:S(2)}) async-start(), calls=%async_computation.32 | async-start | bytes 557056
  1368.7 501.4 %reduce-scatter.43.cloned.1.call-start = ((), (), s32[]{:S(2)}) async-start(), calls=%async_computation.33 | async-start | bytes 557056
  1369.8 573.5 %all-reduce.4.cloned.1.call-start = ((), (), s32[]{:S(2)}) async-start(), calls=%async_computation.34 | async-start | bytes 4718592 | tf_op jit(solution)/shard_map/psum | solution.py:365
  1375.7 379.2 %copy-start.80 = (f32[1024]{0:T(1024)S(1)}, f32[1024]{0:T(1024)}, u32[]{:S(2)}) copy-start(f32[1024]{0:T(1024)} %copy-done.79) | copy-start | bytes 12292
  (85 other events, 396.9 us)
Sparse Core Ops, SparseCore 0:
  10.2 44.1 all-gather.14
  56.5 40.1 all-gather.16
  98.9 40.1 all-gather.12
  141.1 40.2 all-gather.18
  183.4 40.0 all-gather.22
  225.6 40.1 all-gather.24
  268.0 40.1 all-gather.20
  310.3 40.1 all-gather.26
  352.6 73.6 all-gather.28
  428.3 73.1 all-gather.30
  587.5 70.6 reduce-scatter.30
  662.4 71.8 reduce-scatter.38
  810.5 71.5 reduce-scatter.36
  941.9 71.5 reduce-scatter.28
  1017.2 71.8 reduce-scatter.26
  1093.3 71.2 reduce-scatter.24
  1186.0 72.7 reduce-scatter.22
  1316.4 73.0 reduce-scatter.20
  1393.6 177.6 reduce-scatter.34
  1575.2 177.5 reduce-scatter.32
  1756.4 54.7 reduce-scatter.40
  1815.2 54.8 reduce-scatter.42
  1874.1 69.1 all-reduce.3
where the time goes:
time: 1980 us; the launch traced here: 1970 us
  matrix products  1010 us (51%)
  waiting for transfers between devices  683 us (34%)
  other arithmetic  132 us (7%)
  local copies, waits for them, and re-layouts  73.4 us (4%)
  blocking collectives  45.9 us (2%)
    dot_general x4, matrix products, attend_backward(): jnp.einsum('hqk,khe->qhe', grad_raw, heads_k, preferred_element_type=jnp....  248 us
    dot_general x4, matrix products, attend_backward(): jnp.einsum('hqk,qhe->khe', grad_raw, query_part, preferred_element_type=j...  242 us
    reduce_scatter x1, waiting for transfers between devices, body(): lax.psum_scatter(grad_w_out, 'shard', scatter_dimension=0, tiled=True)  180 us
    reduce_scatter x1, waiting for transfers between devices, body(): lax.psum_scatter(grad_w_in, 'shard', scatter_dimension=0, tiled=True)  179 us
    dot_general x10, matrix products, project(): return jnp.dot(left, right, preferred_element_type=jnp.float32)  103 us
    unnamed x27, waiting for transfers between devices  98.3 us
    dot_general x10, matrix products, weight_term(): jnp.einsum('ra,rb->ab', left, right, preferred_element_type=jnp.float32)  82 us
    dot_general x10, matrix products, back_project(): jnp.einsum('rb,ab->ra', grad_rows, weight, preferred_element_type=jnp.flo...  73.8 us
  transfers between devices with their start and end apart: 23, of which 12 were waited for; matrix products, arithmetic and copies ran while one was open for 56% of the time, Pallas kernels for 0%

commit v1 on v0

v1 whole, which is shorter than its diff:
```python
import functools
import math

import jax
import jax.numpy as jnp
from jax import lax
from jax.experimental import pallas as pl
from jax.experimental.pallas import tpu as pltpu
from jax.sharding import PartitionSpec as P

HEADS = 16
HEAD = 64


eps_norm = 1e-05
big_negative = -1e30


def layer_norm(values_in, gain_row, bias_row):
    centre = values_in - jnp.mean(values_in, axis=-1, keepdims=True)
    spread = jnp.mean(centre * centre, axis=-1, keepdims=True)
    return centre * lax.rsqrt(spread + eps_norm) * gain_row + bias_row


def norm_backward(values_in, gain_row, bias_row, grad_out):
    result, pullback = jax.vjp(layer_norm, values_in, gain_row, bias_row)
    return pullback(grad_out)


def gelu_slope(values_in):
    return 0.5 * (1.0 + lax.erf(values_in * (1.0 / math.sqrt(2.0)))) + values_in * jnp.exp(
        -0.5 * values_in * values_in
    ) * (1.0 / math.sqrt(2.0 * math.pi))


BIG = 1e30
NT = (((1,), (1,)), ((), ()))
TN = (((0,), (0,)), ((), ()))


def key_extras(ids):
    lane = jnp.arange(128)[None, :] % 64
    return jnp.where(lane < 8, (ids[:, None] != lane).astype(jnp.bfloat16), ((lane >= 8) & (lane < 11)).astype(jnp.bfloat16))


def query_extras(ids):
    lane = jnp.arange(128)[None, :] % 64
    return jnp.where((lane < 8) & (ids[:, None] == lane), -BIG, 0.0).astype(jnp.bfloat16)


def windows(unit_ids, key_ids, bq, bk, causal):
    n = key_ids.shape[0]
    nq = unit_ids.shape[0] // bq
    blocks = unit_ids.reshape(nq, bq)
    low = jnp.sum((key_ids[None, :] < blocks[:, :1]).astype(jnp.int32), axis=1)
    if causal:
        end = (jnp.arange(nq, dtype=jnp.int32) + 1) * bq
        count = (end - low + bk - 1) // bk
        start = end - count * bk
    else:
        end = jnp.sum((key_ids[None, :] <= blocks[:, -1:]).astype(jnp.int32), axis=1)
        low = low // 16 * 16
        count = (end - low + bk - 1) // bk
        start = jnp.minimum(low, n - count * bk)
    return jnp.concatenate([start, count])


def attend_forward_kernel(bq, bk, causal, hp, norm, win_ref, q_ref, k_ref, v_ref, qx_ref, kx_ref, o_ref, qe_ref, ka):
    L, N = q_ref.shape[0], k_ref.shape[0]
    nq = L // bq
    lane = lax.broadcasted_iota(jnp.int32, (1, 128), 1)
    first = lane < 64
    part = lane % 64
    for g in range(hp):
        kp = k_ref[:, g*128:(g+1)*128]
        ka[2*g] = jnp.where(first, kp, kx_ref[...])
        ka[2*g+1] = jnp.where(first, kx_ref[...], kp)
    row = lax.broadcasted_iota(jnp.int32, (128, 1), 0)
    rpart = row % 64

    def one(i, W):
        rows = pl.ds(pl.multiple_of(i * bq, bq), bq)
        win = pl.ds(pl.multiple_of(win_ref[i], 16), W)
        xb = qx_ref[rows, :]
        ss = []
        for h in range(2*hp):
            g = h // 2
            qb = q_ref[rows, g*128:(g+1)*128]
            qa = jnp.where(first, qb, xb) if h % 2 == 0 else jnp.where(first, xb, qb)
            s = lax.dot_general(ka[h, win, :], qa, NT, preferred_element_type=jnp.float32)
            if causal:
                tri = lax.broadcasted_iota(jnp.int32, (bq, bq), 0) <= lax.broadcasted_iota(jnp.int32, (bq, bq), 1)
                d = jnp.where(tri, s[W - bq:, :], -BIG)
                s = d if W == bq else jnp.concatenate([s[: W - bq, :], d], axis=0)
            ss.append(s)
        outs, invs, lses = [], [], []
        for h in range(2*hp):
            g = h // 2
            s = ss[h]
            m = jnp.max(s, axis=0, keepdims=True)
            p = jnp.exp(s - m)
            l = jnp.sum(p, axis=0, keepdims=True)
            inv = 1.0 / l
            if norm: p = p * inv
            o = lax.dot_general(p.astype(jnp.bfloat16), v_ref[win, g*128:(g+1)*128], TN, preferred_element_type=jnp.float32)
            outs.append(o); invs.append(inv)
            neg = -(m + jnp.log(l))
            hi = neg.astype(jnp.bfloat16).astype(jnp.float32)
            mid = (neg - hi).astype(jnp.bfloat16).astype(jnp.float32)
            lo = neg - hi - mid
            lses.append((hi, mid, lo))
        for g in range(hp):
            o = jnp.where(first, outs[2*g], outs[2*g+1])
            if not norm:
                t = jnp.where(row < 64, invs[2*g], invs[2*g+1])
                o = o * jnp.transpose(t)
            o_ref[rows, g*128:(g+1)*128] = o.astype(jnp.bfloat16)
            a, b = lses[2*g], lses[2*g+1]
            e = jnp.where(row < 64, jnp.where(rpart == 8, b[0], jnp.where(rpart == 9, b[1], b[2])), jnp.where(rpart == 8, a[0], jnp.where(rpart == 9, a[1], a[2])))
            e = jnp.transpose(jnp.where((rpart >= 8) & (rpart < 11), e, 0.0))
            qe_ref[rows, g*128:(g+1)*128] = jnp.where(part < 8, xb.astype(jnp.float32), e).astype(jnp.bfloat16)

    def step(i, c):
        for j in range(1, N // bk + 1):
            @pl.when(win_ref[nq + i] == j)
            def _():
                one(i, j * bk)
        return c

    lax.fori_loop(0, nq, step, 0)

def attend_forward(q, k, v, qx, kx, win, causal, bq=256, bk=256, hp=1, norm=False):
    L, D = q.shape
    N = k.shape[0]
    w = 128*hp
    col = lambda n: pl.BlockSpec((n, w), lambda p, _: (0, p))
    fix = lambda n: pl.BlockSpec((n, 128), lambda p, _: (0, 0))
    return pl.pallas_call(
        functools.partial(attend_forward_kernel, bq, bk, causal, hp, norm),
        grid_spec=pltpu.PrefetchScalarGridSpec(
            num_scalar_prefetch=1, grid=(D // w,),
            in_specs=[col(L), col(N), col(N), fix(L), fix(N)],
            out_specs=[col(L), col(L)],
            scratch_shapes=[pltpu.VMEM((2*hp, N, 128), jnp.bfloat16)]),
        out_shape=[jax.ShapeDtypeStruct((L, D), jnp.bfloat16)] * 2,
        compiler_params=pltpu.CompilerParams(vmem_limit_bytes=56 << 20),
    )(win, q, k, v, qx, kx)


def attend_backward_kernel(bq, bk, causal, win_ref, q_ref, k_ref, v_ref, o_ref, do_ref, qe_ref, kx_ref, dq_ref, dk_ref, dv_ref, ka, va, dka, dva):
    L, N = q_ref.shape[0], k_ref.shape[0]
    nq = L // bq
    lane = lax.broadcasted_iota(jnp.int32, (1, 128), 1)
    first = lane < 64
    part = lane % 64
    ones = jnp.broadcast_to(jnp.where(part < 3, 1.0, 0.0).astype(jnp.bfloat16), (N, 128))
    ka[0] = jnp.where(first, k_ref[...], kx_ref[...])
    ka[1] = jnp.where(first, kx_ref[...], k_ref[...])
    va[0] = jnp.where(first, v_ref[...], ones)
    va[1] = jnp.where(first, ones, v_ref[...])
    dka[...] = jnp.zeros_like(dka)
    dva[...] = jnp.zeros_like(dva)
    zero = jnp.zeros((1, 128), jnp.bfloat16)

    def one(i, W):
        rows = pl.ds(pl.multiple_of(i * bq, bq), bq)
        win = pl.ds(pl.multiple_of(win_ref[i], 16), W)
        qb, xb, dob = q_ref[rows, :], qe_ref[rows, :], do_ref[rows, :]
        prod = dob.astype(jnp.float32) * o_ref[rows, :].astype(jnp.float32)
        ps, dss = [], []
        for h in range(2):
            mine = first if h == 0 else jnp.logical_not(first)
            neg = -jnp.sum(jnp.where(mine, prod, 0.0), axis=1, keepdims=True)
            hi = neg.astype(jnp.bfloat16).astype(jnp.float32)
            mid = (neg - hi).astype(jnp.bfloat16).astype(jnp.float32)
            lo = neg - hi - mid
            de = jnp.where(part == 0, hi, jnp.where(part == 1, mid, jnp.where(part == 2, lo, 0.0))).astype(jnp.bfloat16)
            qa = jnp.where(mine, qb, xb)
            da = jnp.where(mine, dob, de)
            s = lax.dot_general(ka[h, win, :], qa, NT, preferred_element_type=jnp.float32)
            if causal:
                tri = lax.broadcasted_iota(jnp.int32, (bq, bq), 0) <= lax.broadcasted_iota(jnp.int32, (bq, bq), 1)
                d = jnp.where(tri, s[W - bq:, :], -BIG)
                s = d if W == bq else jnp.concatenate([s[: W - bq, :], d], axis=0)
            p = jnp.exp(s)
            dp = lax.dot_general(va[h, win, :], da, NT, preferred_element_type=jnp.float32)
            dss.append((p * dp).astype(jnp.bfloat16))
            ps.append(p.astype(jnp.bfloat16))
        docat = jnp.concatenate([jnp.where(first, dob, zero), jnp.where(first, zero, dob)], axis=0)
        qcat = jnp.concatenate([jnp.where(first, qb, zero), jnp.where(first, zero, qb)], axis=0)
        dva[win, :] += jnp.dot(jnp.concatenate(ps, axis=1), docat, preferred_element_type=jnp.float32)
        dka[win, :] += jnp.dot(jnp.concatenate(dss, axis=1), qcat, preferred_element_type=jnp.float32)
        kw = k_ref[win, :]
        dq0 = lax.dot_general(dss[0], kw, TN, preferred_element_type=jnp.float32)
        dq1 = lax.dot_general(dss[1], kw, TN, preferred_element_type=jnp.float32)
        dq_ref[rows, :] = (jnp.where(first, dq0, dq1) * 0.125).astype(jnp.bfloat16)

    def step(i, c):
        for j in range(1, N // bk + 1):
            @pl.when(win_ref[nq + i] == j)
            def _():
                one(i, j * bk)
        return c

    lax.fori_loop(0, nq, step, 0)
    dk_ref[...] = dka[...].astype(jnp.bfloat16)
    dv_ref[...] = dva[...].astype(jnp.bfloat16)


def attend_backward(q, k, v, o, do, qe, kx, win, causal, bq=256, bk=256):
    L, D = q.shape
    N = k.shape[0]
    col = lambda n: pl.BlockSpec((n, 128), lambda p, w: (0, p))
    fix = lambda n: pl.BlockSpec((n, 128), lambda p, w: (0, 0))
    return pl.pallas_call(
        functools.partial(attend_backward_kernel, bq, bk, causal),
        grid_spec=pltpu.PrefetchScalarGridSpec(
            num_scalar_prefetch=1, grid=(D // 128,),
            in_specs=[col(L), col(N), col(N), col(L), col(L), col(L), fix(N)],
            out_specs=[col(L), col(N), col(N)],
            scratch_shapes=[pltpu.VMEM((2, N, 128), jnp.bfloat16)] * 2 + [pltpu.VMEM((N, 128), jnp.float32)] * 2),
        out_shape=[jax.ShapeDtypeStruct((L, D), jnp.bfloat16)] + [jax.ShapeDtypeStruct((N, D), jnp.bfloat16)] * 2,
        compiler_params=pltpu.CompilerParams(vmem_limit_bytes=48 << 20),
        cost_estimate=pl.CostEstimate(flops=5 * 2 * L * N * D, bytes_accessed=16 * L * D, transcendentals=0),
    )(win, q, k, v, o, do, qe, kx)


def project(left, right):
    return jnp.dot(left, right, preferred_element_type=jnp.float32)


def weight_term(left, right):
    return jnp.einsum("ra,rb->ab", left, right, preferred_element_type=jnp.float32)


def back_project(grad_rows, weight):
    return jnp.einsum("rb,ab->ra", grad_rows, weight, preferred_element_type=jnp.float32)


def ring_place(chips):
    half = chips // 2
    walk = [2 * i for i in range(half)] + [2 * i + 1 for i in reversed(range(half))]
    place = [0] * chips
    for at, chip in enumerate(walk):
        place[chip] = at
    return walk, place


def ring_moves(count):
    walk, place = ring_place(count // 2)
    chips = len(walk)
    up = [(2 * walk[i] + c, 2 * walk[(i + 1) % chips] + c) for i in range(chips) for c in range(2)]
    down = [(b, a) for a, b in up]
    swap = [(i, i ^ 1) for i in range(count)]
    return up, down, swap


def gather_rows(piece, count):
    if count != 16:
        return lax.all_gather(piece, "shard", axis=0, tiled=True)
    walk, place = ring_place(count // 2)
    up, down, swap = ring_moves(count)
    chips = count // 2
    me = lax.axis_index("shard")
    core = me % 2
    walk_at = jnp.array(walk, jnp.int32)
    at = jnp.array(place, jnp.int32)[me // 2]
    rows = piece.shape[0]
    pieces = {0: piece}
    upward = downward = piece
    for step in range(1, chips // 2 + 1):
        upward = lax.ppermute(upward, "shard", up)
        pieces[-step] = upward
        if step < chips // 2:
            downward = lax.ppermute(downward, "shard", down)
            pieces[step] = downward
    whole = jnp.zeros((count * rows,) + piece.shape[1:], piece.dtype)
    for step, part in pieces.items():
        chip = walk_at[(at + step) % chips]
        other = lax.ppermute(part, "shard", swap)
        whole = lax.dynamic_update_slice_in_dim(whole, part, (2 * chip + core) * rows, 0)
        whole = lax.dynamic_update_slice_in_dim(whole, other, (2 * chip + 1 - core) * rows, 0)
    return whole


def add_pair(left, right):
    return (left.astype(jnp.float32) + right.astype(jnp.float32)).astype(jnp.bfloat16)


def reduce_rows(term, count, flip):
    rows = term.shape[0] // count
    term = term.astype(jnp.bfloat16)
    if count != 16:
        owned = lax.psum_scatter(term, "shard", scatter_dimension=0, tiled=True)
        return lax.psum(owned, "rep").astype(jnp.float32)
    walk, place = ring_place(count // 2)
    up, down, swap = ring_moves(count)
    if flip:
        up, down = down, up
    sign = -1 if flip else 1
    chips = count // 2
    me = lax.axis_index("shard")
    core = me % 2
    walk_at = jnp.array(walk, jnp.int32)
    at = jnp.array(place, jnp.int32)[me // 2]
    split = term.reshape((chips, 2, rows) + term.shape[1:])
    mine = lax.dynamic_index_in_dim(split, core, 1, keepdims=False)
    other = lax.dynamic_index_in_dim(split, 1 - core, 1, keepdims=False)
    both = add_pair(mine, lax.ppermute(other, "shard", swap))

    def part(step):
        return lax.dynamic_index_in_dim(both, walk_at[(at + sign * step) % chips], 0, keepdims=False)

    half = chips // 2
    upward = part(half)
    downward = part(-(half - 1))
    for step in range(half, 0, -1):
        upward = lax.ppermute(upward, "shard", up)
        if step > 1:
            upward = add_pair(upward, part(step - 1))
    for step in range(half - 1, 0, -1):
        downward = lax.ppermute(downward, "shard", down)
        if step > 1:
            downward = add_pair(downward, part(-(step - 1)))
    owned = (part(0).astype(jnp.float32) + upward.astype(jnp.float32) + downward.astype(jnp.float32)).astype(jnp.bfloat16)
    partner = lax.ppermute(owned, "rep", [(0, 1), (1, 0)])
    return owned.astype(jnp.float32) + partner.astype(jnp.float32)


def body(
    tokens,
    enc_states,
    unit_ids,
    enc_ids,
    self_q,
    self_k,
    self_v,
    self_o,
    cross_q,
    cross_k,
    cross_v,
    cross_o,
    ffn_in,
    ffn_out,
    norm_gains,
    norm_biases,
    cotangent,
):
    count = lax.axis_size("shard")
    norm_piece = jnp.concatenate([norm_gains, norm_biases], axis=0)
    own_width = norm_piece.shape[1]
    norm_rows = jnp.pad(norm_piece.reshape(1, -1), ((0, 15), (0, self_q.shape[1] - 8 * own_width)))
    first_set = gather_rows(jnp.concatenate([self_q, self_k, self_v, norm_rows], axis=0), count)
    own_rows = self_q.shape[0]
    first_set = first_set.reshape(count, 3 * own_rows + 16, -1)
    w_sq, w_sk, w_sv = (
        first_set[:, i * own_rows : (i + 1) * own_rows].reshape(count * own_rows, -1) for i in range(3)
    )
    norm_set = first_set[:, 3 * own_rows, : 8 * own_width].reshape(count, 8, own_width)
    norm_set = jnp.transpose(norm_set, (1, 0, 2)).reshape(8, count * own_width).astype(jnp.float32)
    gain_rows, bias_rows = norm_set[:4], norm_set[4:]
    w_so = gather_rows(self_o, count)
    w_cq = gather_rows(cross_q, count)
    w_ck = gather_rows(cross_k, count)
    w_cv = gather_rows(cross_v, count)
    w_co = gather_rows(cross_o, count)
    w_in = gather_rows(ffn_in, count)
    w_out = gather_rows(ffn_out, count)
    seq_count = tokens.shape[0]
    unit_count = tokens.shape[1]
    enc_count = enc_states.shape[1]
    row_count = seq_count * unit_count
    width = tokens.shape[2]
    rows_in = tokens.reshape(row_count, width).astype(jnp.float32)
    enc_rows = enc_states.reshape(seq_count * enc_count, width)
    normed_one = layer_norm(rows_in, gain_rows[0], bias_rows[0]).astype(jnp.bfloat16)
    queries_one = (project(normed_one, w_sq) * 0.125).astype(jnp.bfloat16)
    keys_one = project(normed_one, w_sk).astype(jnp.bfloat16)
    values_one = project(normed_one, w_sv).astype(jnp.bfloat16)

    unit_extra, enc_extra = key_extras(unit_ids[0]), key_extras(enc_ids[0])
    query_extra = query_extras(unit_ids[0])
    self_windows = windows(unit_ids[0], unit_ids[0], 256, 256, True)
    cross_windows = windows(unit_ids[0], enc_ids[0], 256, 256, False)
    attended_one, log_one = attend_forward(
        queries_one, keys_one, values_one, query_extra, unit_extra, self_windows, True, hp=2, norm=True
    )
    after_self = rows_in + project(attended_one, w_so)
    normed_two = layer_norm(after_self, gain_rows[1], bias_rows[1]).astype(jnp.bfloat16)
    queries_two = (project(normed_two, w_cq) * 0.125).astype(jnp.bfloat16)
    keys_two = project(enc_rows, w_ck).astype(jnp.bfloat16)
    values_two = project(enc_rows, w_cv).astype(jnp.bfloat16)

    attended_two, log_two = attend_forward(
        queries_two, keys_two, values_two, query_extra, enc_extra, cross_windows, False, hp=2, norm=True
    )
    after_cross = after_self + project(attended_two, w_co)
    normed_three = layer_norm(after_cross, gain_rows[2], bias_rows[2]).astype(jnp.bfloat16)
    pre_active = project(normed_three, w_in)
    hidden = jax.nn.gelu(pre_active, approximate=False).astype(jnp.bfloat16)
    after_ffn = after_cross + project(hidden, w_out)
    layer_out = (
        layer_norm(after_ffn, gain_rows[3], bias_rows[3])
        .astype(jnp.bfloat16)
        .reshape(seq_count, unit_count, width)
    )
    b_sq, b_sk, b_sv, b_so, b_cq, b_ck, b_cv, b_co, b_in, b_out = (
        w_sq, w_sk, w_sv, w_so, w_cq, w_ck, w_cv, w_co, w_in, w_out
    )
    gain_back, bias_back = gain_rows, bias_rows
    grad_out = cotangent.reshape(row_count, width).astype(jnp.float32)
    grad_after_ffn, gain_four, bias_four = norm_backward(
        after_ffn, gain_back[3], bias_back[3], grad_out
    )
    grad_ffn_rows = grad_after_ffn.astype(jnp.bfloat16)
    grad_w_out = weight_term(hidden, grad_ffn_rows)
    grad_hidden = back_project(grad_ffn_rows, b_out)
    grad_pre = (grad_hidden * gelu_slope(pre_active)).astype(jnp.bfloat16)
    grad_w_in = weight_term(normed_three, grad_pre)
    grad_normed_three = back_project(grad_pre, b_in)
    grad_norm_three, gain_three, bias_three = norm_backward(
        after_cross, gain_back[2], bias_back[2], grad_normed_three
    )
    grad_after_cross = grad_after_ffn + grad_norm_three
    grad_cross_rows = grad_after_cross.astype(jnp.bfloat16)
    grad_w_co = weight_term(attended_two, grad_cross_rows)
    grad_attended_two = back_project(grad_cross_rows, b_co).astype(jnp.bfloat16)

    grad_q_two, grad_k_two, grad_v_two = attend_backward(
        queries_two, keys_two, values_two, attended_two, grad_attended_two, log_two, enc_extra, cross_windows, False
    )
    grad_w_cq = weight_term(normed_two, grad_q_two)
    grad_w_ck = weight_term(enc_rows, grad_k_two)
    grad_w_cv = weight_term(enc_rows, grad_v_two)
    grad_enc = (back_project(grad_k_two, b_ck) + back_project(grad_v_two, b_cv)).reshape(
        seq_count, enc_count, width
    )
    grad_norm_two, gain_two, bias_two = norm_backward(
        after_self, gain_back[1], bias_back[1], back_project(grad_q_two, b_cq)
    )
    grad_after_self = grad_after_cross + grad_norm_two
    grad_self_rows = grad_after_self.astype(jnp.bfloat16)
    grad_w_so = weight_term(attended_one, grad_self_rows)
    grad_attended_one = back_project(grad_self_rows, b_so).astype(jnp.bfloat16)

    grad_q_one, grad_k_one, grad_v_one = attend_backward(
        queries_one, keys_one, values_one, attended_one, grad_attended_one, log_one, unit_extra, self_windows, True
    )
    grad_w_sq = weight_term(normed_one, grad_q_one)
    grad_w_sk = weight_term(normed_one, grad_k_one)
    grad_w_sv = weight_term(normed_one, grad_v_one)
    grad_normed_one = (
        back_project(grad_q_one, b_sq)
        + back_project(grad_k_one, b_sk)
        + back_project(grad_v_one, b_sv)
    )
    grad_norm_one, gain_one, bias_one = norm_backward(
        rows_in, gain_back[0], bias_back[0], grad_normed_one
    )
    grad_tokens = (grad_after_self + grad_norm_one).reshape(seq_count, unit_count, width)
    grad_gains = jnp.stack([gain_one, gain_two, gain_three, gain_four])
    grad_biases = jnp.stack([bias_one, bias_two, bias_three, bias_four])
    norm_term = jnp.concatenate([grad_gains, grad_biases], axis=0).reshape(8, count, own_width)
    norm_term = jnp.transpose(norm_term, (1, 0, 2)).reshape(count, 1, 8 * own_width)
    norm_term = jnp.pad(norm_term, ((0, 0), (0, 15), (0, width - 8 * own_width)))
    last_set = jnp.concatenate(
        [w.reshape(count, own_rows, width) for w in (grad_w_sq, grad_w_sk, grad_w_sv)] + [norm_term], axis=1
    )
    last_set = reduce_rows(last_set.reshape(count * (3 * own_rows + 16), width), count, False)
    norm_sum = last_set[3 * own_rows, : 8 * own_width].reshape(8, own_width)
    summed = (
        last_set[:own_rows],
        last_set[own_rows : 2 * own_rows],
        last_set[2 * own_rows : 3 * own_rows],
        reduce_rows(grad_w_so, count, True),
        reduce_rows(grad_w_cq, count, False),
        reduce_rows(grad_w_ck, count, True),
        reduce_rows(grad_w_cv, count, False),
        reduce_rows(grad_w_co, count, True),
        reduce_rows(grad_w_in, count, False),
        reduce_rows(grad_w_out, count, True),
        norm_sum[:4],
        norm_sum[4:],
    )
    return (
        layer_out,
        grad_tokens,
        grad_enc,
        summed[0],
        summed[1],
        summed[2],
        summed[3],
        summed[4],
        summed[5],
        summed[6],
        summed[7],
        summed[8],
        summed[9],
        summed[10],
        summed[11],
    )


def solution(mesh):
    return jax.shard_map(
        body,
        mesh=mesh,
        in_specs=(
            P(("rep", "shard"), None, None),
            P(("rep", "shard"), None, None),
            P(("rep", "shard"), None),
            P(("rep", "shard"), None),
            P("shard", None),
            P("shard", None),
            P("shard", None),
            P("shard", None),
            P("shard", None),
            P("shard", None),
            P("shard", None),
            P("shard", None),
            P("shard", None),
            P("shard", None),
            P(None, "shard"),
            P(None, "shard"),
            P(("rep", "shard"), None, None),
        ),
        out_specs=(
            P(("rep", "shard"), None, None),
            P(("rep", "shard"), None, None),
            P(("rep", "shard"), None, None),
            P("shard", None),
            P("shard", None),
            P("shard", None),
            P("shard", None),
            P("shard", None),
            P("shard", None),
            P("shard", None),
            P("shard", None),
            P("shard", None),
            P("shard", None),
            P(None, "shard"),
            P(None, "shard"),
        ),
        check_vma=False,
    )
```

time: 1980 us -> 1110 us (0.56)
  matrix products: 1010 us -> 249 us
  waiting for transfers between devices: 683 us -> 280 us
  Pallas kernels: 0 us -> 132 us
  starting transfers between devices: 2.13 us -> 132 us
  local copies, waits for them, and re-layouts: 73.4 us -> 187 us
  blocking collectives: 45.9 us -> 0 us
  other arithmetic: 132 us -> 91.9 us
    dot_general x24 -> x0, matrix products: 756 us -> none  [the longest x4 248 us: attend_backward(): jnp.einsum('hqk,khe->qhe', grad_raw, heads_k, preferred_element_type=jnp....]
    reduce_scatter x8 -> x0, waiting for transfers between devices: 363 us -> none  [the longest x1 180 us: body(): lax.psum_scatter(grad_w_out, 'shard', scatter_dimension=0, tiled=True)]
    ppermute x0 -> x192, waiting for transfers between devices: none -> 280 us  [the longest x32 91.4 us: gather_rows(): upward = lax.ppermute(upward, 'shard', up)]
    all_gather x10 -> x0, waiting for transfers between devices: 155 us -> none  [the longest x1 42.4 us: body(): lax.all_gather(ffn_in, 'shard', axis=0, tiled=True)]
    pallas_call x0 -> x4, Pallas kernels: none -> 132 us  [the longest x2 83.9 us: attend_backward(): pl.pallas_call(functools.partial(attend_backward_kernel, bq, bk, causal),...]
    ppermute x0 -> x192, starting transfers between devices: none -> 132 us  [the longest x32 32.1 us: gather_rows(): upward = lax.ppermute(upward, 'shard', up)]
    dynamic_update_slice x0 -> x126, local copies, waits for them, and re-layouts: none -> 100 us  [the longest x63 50.7 us: gather_rows(): lax.dynamic_update_slice_in_dim(whole, other, (2 * chip + 1 - core) * row...]
    unnamed x27 -> x0, waiting for transfers between devices: 98.3 us -> none
  transfers between devices with their start and end apart: 23 -> 192, of which waited for: 12 -> 93; matrix products, arithmetic and copies ran while one was open for 56% -> 27% of each run, Pallas kernels for 0% -> 4%
where the time goes in v1:
time: 1110 us; the launch traced here: 1100 us
  waiting for transfers between devices  280 us (25%)
  matrix products  249 us (22%)
  local copies, waits for them, and re-layouts  187 us (17%)
  starting transfers between devices  132 us (12%)
  Pallas kernels  132 us (12%)
  other arithmetic  91.9 us (8%)
  between operations  32.7 us (3%)
    dot_general x10, matrix products, project(): return jnp.dot(left, right, preferred_element_type=jnp.float32)  106 us
    ppermute x32, waiting for transfers between devices, gather_rows(): upward = lax.ppermute(upward, 'shard', up)  91.4 us
    pallas_call x2, Pallas kernels, attend_backward(): pl.pallas_call(functools.partial(attend_backward_kernel, bq, bk, causal),...  83.9 us
    dot_general x10, matrix products, back_project(): jnp.einsum('rb,ab->ra', grad_rows, weight, preferred_element_type=jnp.flo...  83.4 us
    ppermute x32, waiting for transfers between devices, reduce_rows(): upward = lax.ppermute(upward, 'shard', up)  77.6 us
    dot_general x10, matrix products, weight_term(): jnp.einsum('ra,rb->ab', left, right, preferred_element_type=jnp.float32)  59.7 us
    ppermute x24, waiting for transfers between devices, reduce_rows(): downward = lax.ppermute(downward, 'shard', down)  55.6 us
    dynamic_update_slice x63, local copies, waits for them, and re-layouts, gather_rows(): lax.dynamic_update_slice_in_dim(whole, other, (2 * chip + 1 - core) * row...  50.7 us
  transfers between devices with their start and end apart: 192, of which 93 were waited for; matrix products, arithmetic and copies ran while one was open for 27% of the time, Pallas kernels for 4%

profile of v1, /device:TPU:0, one launch (start us, length us, event | category | flops | bytes accessed | tf_op | source)
XLA Modules:
  0.0 1105.0 jit_solution(10065632721845646650)
XLA Ops:
  26.9 4.3 broadcast_in_dim.86
  45.8 4.3 broadcast_in_dim.87
  122.5 4.3 collective-permute-done.80
  220.1 4.8 collective-permute-done.88
  254.0 5.3 convert_bitcast_fusion.2.k_ref
  260.5 5.3 convert_bitcast_fusion.1.v_ref
  273.7 6.9 collective-permute-done.93
  286.3 5.5 collective-permute-done.108
  295.6 5.3 collective-permute-done.7
  318.7 4.7 collective-permute-done.112
  334.3 5.0 collective-permute-done.114
  343.9 8.2 collective-permute-done.13
  355.4 8.0 collective-permute-done.103
  363.9 9.4 collective-permute-done.118
  382.1 5.8 fusion.160
  389.3 6.4 multiply_convert_fusion.1.q_ref
  395.7 4.1 convolution_convert_fusion.8.k_ref
  399.9 4.2 convolution_convert_fusion.7.v_ref
  404.2 25.5 %shard_map.568 = (bf16[1024,1024]{1,0:T(8,128)(2,1)}, bf16[1024,1024]{1,0:T(8,128)(2,1)}) custom-call(s32[8]{0:T(128)} %pad_add_fusion.win_ref, bf16[1024,1024]{1,0:T(8,128)(2,1)} %multiply_convert_fusion.1.q_ref, bf16[1024,1024]{1,0:T(8,128)(2,1)} %convolution_convert_fusion.8.k_ref, bf16[1024,1024]{1,0:T(8,128)(2,1)} %convolution_convert_fusion.7.v_ref, ...), custom_call_target="tpu_custom_call" | custom-call | tf_op jit(solution)/shard_map/pallas_call | solution.py:138
  429.7 4.7 fusion.164
  437.6 6.9 multiply_convert_fusion.q_ref
  444.6 22.9 %shard_map.569 = (bf16[1024,1024]{1,0:T(8,128)(2,1)}, bf16[1024,1024]{1,0:T(8,128)(2,1)}) custom-call(s32[8]{0:T(128)} %pad_add_fusion.1.win_ref, bf16[1024,1024]{1,0:T(8,128)(2,1)} %multiply_convert_fusion.q_ref, bf16[1024,1024]{1,0:T(8,128)(2,1)} %convert_bitcast_fusion.2.k_ref, bf16[1024,1024]{1,0:T(8,128)(2,1)} %convert_bitcast_fusion.1.v_ref, ...), custom_call_target="tpu_custom_call" | custom-call | tf_op jit(solution)/shard_map/pallas_call | solution.py:138
  467.5 6.6 fusion.165
  481.5 47.0 %fusion.2 = (bf16[1024,4096]{1,0:T(8,128)(2,1)}, f32[1024,4096]{1,0:T(8,128)}) fusion(bf16[1024,4096]{1,0:T(8,128)(2,1)} %constant_dynamic-update-slice_fusion.91, bf16[1024,1024]{0,1:T(8,128)(2,1)S(1)} %add_convert_fusion.7.clone.4), kind=kOutput, calls=%fused_computation.4 | convolution fusion | flops 8862564352 | bytes 35651584 | tf_op jit(solution)/shard_map/dot_general | solution.py:229
  530.4 15.1 %fusion.166 = (f32[1024]{0:T(1024)S(1)}, f32[1024,1024]{0,1:T(8,128)}) fusion(f32[1024,1024]{0,1:T(8,128)S(1)} %copy-done.9, bf16[1024,4096]{1,0:T(8,128)(2,1)} %get-tuple-element.190, bf16[4096,1024]{1,0:T(8,128)(2,1)} %constant_dynamic-update-slice_fusion.1), kind=kOutput, calls=%fused_computation.479 | convolution fusion | flops 8592030720 | bytes 25169920 | tf_op jit(solution)/shard_map/dot_general | solution.py:229
  553.5 21.0 %fusion.8 = bf16[1024,4096]{1,0:T(8,128)(2,1)} fusion(f32[1024,4096]{1,0:T(8,128)} %get-tuple-element.191, bf16[4096,1024]{1,0:T(8,128)(2,1)} %constant_dynamic-update-slice_fusion.1, f32[1024]{0:T(1024)S(1)} %negate_multiply_fusion.4, f32[1024,1024]{0,1:T(8,128)S(1)} %copy-done.20, bf16[1,1024,1024]{1,2,0:T(8,128)(2,1)S(1)} %copy-done.26, ...), kind=kOutput, calls=%fused_computation.10 | convolution fusion | flops 8641314816 | bytes 39866368 | tf_op jit(solution)/shard_map/rb,ab->ra/dot_general | solution.py:237
  574.6 15.7 %fusion.168 = (bf16[1024]{0:T(1024)(128)(2,1)}, f32[1024,1024]{1,0:T(8,128)}) fusion(bf16[1024,4096]{1,0:T(8,128)(2,1)} %fusion.8, bf16[1024,4096]{1,0:T(8,128)(2,1)} %constant_dynamic-update-slice_fusion.91), kind=kOutput, calls=%fused_computation.481 | convolution fusion | flops 8590982144 | bytes 20973568 | tf_op jit(solution)/shard_map/rb,ab->ra/dot_general | solution.py:237
  590.2 5.4 copy.118
  595.7 4.2 multiply_reduce_fusion.3
  604.4 4.4 add_add_fusion.6
  608.8 6.9 convolution_convert_fusion.6.do_ref
  615.7 39.2 %shard_map.570 = (bf16[1024,1024]{1,0:T(8,128)(2,1)S(1)}, bf16[1024,1024]{1,0:T(8,128)(2,1)S(1)}, bf16[1024,1024]{1,0:T(8,128)(2,1)}) custom-call(s32[8]{0:T(128)S(1)} %copy-done.4, bf16[1024,1024]{1,0:T(8,128)(2,1)} %multiply_convert_fusion.q_ref, bf16[1024,1024]{1,0:T(8,128)(2,1)} %convert_bitcast_fusion.2.k_ref, ...), custom_call_target="tpu_custom_call" | custom-call | flops 10737418240 | bytes 16777216 | tf_op jit(solution)/shard_map/pallas_call | solution.py:215
  654.9 8.0 fusion.167
  663.0 5.7 copy.119
  668.8 5.4 multiply_reduce_fusion.1
  678.0 6.1 convolution_convert_fusion.5.do_ref
  684.1 44.7 %shard_map.571 = (bf16[1024,1024]{1,0:T(8,128)(2,1)S(1)}, bf16[1024,1024]{1,0:T(8,128)(2,1)S(1)}, bf16[1024,1024]{1,0:T(8,128)(2,1)}) custom-call(s32[8]{0:T(128)S(1)} %copy-done.3, bf16[1024,1024]{1,0:T(8,128)(2,1)} %multiply_convert_fusion.1.q_ref, bf16[1024,1024]{1,0:T(8,128)(2,1)} %convolution_convert_fusion.8.k_ref, ...), custom_call_target="tpu_custom_call" | custom-call | flops 10737418240 | bytes 16777216 | tf_op jit(solution)/shard_map/pallas_call | solution.py:215
  728.8 4.1 fusion.169
  733.0 4.4 fusion.170
  737.4 5.3 fusion.158
  767.6 5.9 fusion.171
  773.6 4.2 fusion.70
  781.5 15.0 %convolution_convert_fusion.1 = bf16[1024,4096]{1,0:T(8,128)(2,1)} fusion(bf16[1024,4096]{1,0:T(8,128)(2,1)} %fusion.8, f32[1024,1024]{0,1:T(8,128)S(1)} %copy-done.11, f32[1024]{0:T(1024)S(1)} %copy-done.82, f32[1024]{0:T(1024)S(1)} %copy-done.58, f32[1024]{0:T(1024)S(1)} %copy-done.66, f32[1024]{0:T(1024)S(1)} %copy-done.47), kind=kOutput, calls=%fused_computation.33 | convolution fusion | flops 8599371776 | bytes 20987904 | tf_op jit(solution)/shard_map/ra,rb->ab/dot_general | solution.py:233
  796.5 12.7 %convolution_convert_fusion = bf16[4096,1024]{1,0:T(8,128)(2,1)} fusion(bf16[1024,4096]{1,0:T(8,128)(2,1)S(1)} %bitcast.454, f32[1024]{0:T(1024)S(1)} %negate_multiply_fusion.4, f32[1024,1024]{0,1:T(8,128)S(1)} %copy-done.22, bf16[1,1024,1024]{1,2,0:T(8,128)(2,1)S(1)} %copy-done.28, f32[1024]{0:T(1024)S(1)} %get-tuple-element.171, f32[1024]{0:T(1024)S(1)} %copy-done.64, ...), kind=kOutput, calls=%fused_computation.32 | convolution fusion | flops 8603566080 | bytes 23089152 | tf_op jit(solution)/shard_map/ra,rb->ab/dot_general | solution.py:233
  813.2 5.5 copy.136
  818.7 5.5 fusion.67
  824.2 6.0 add_bitcast_fusion
  831.0 4.2 fusion.19
  837.4 13.0 %collective-permute-start.120 = (bf16[8,208,1024]{2,1,0:T(8,128)(2,1)}, bf16[8,208,1024]{2,1,0:T(8,128)(2,1)}, u32[]{:S(2)}, u32[]{:S(2)}) collective-permute-start(bf16[8,208,1024]{2,1,0:T(8,128)(2,1)} %dynamic-slice_bitcast_fusion.2), channel_id=1, source_target_pairs={{0,1},{1,0},{2,3},{3,2},{4,5},{5,4},{6,7},{7,6},{8,9},{9,8},{10,11... | collective-permute-start | bytes 10223624 | tf_op jit(solution)/shard_map/ppermute | solution.py:309
  874.1 4.9 collective-permute-done.139
  879.5 4.6 collective-permute-done.148
  889.4 5.9 collective-permute-done.166
  895.8 4.5 collective-permute-done.131
  969.3 4.3 collective-permute-done.172
  990.7 7.5 collective-permute-done.121
  999.6 5.0 fusion.18
  1007.7 4.3 fusion.17
  1015.7 7.7 collective-permute-done.175
  1027.4 5.0 collective-permute-done.123
  1033.0 8.2 collective-permute-done.126
  1047.3 7.1 collective-permute-done.127
  1056.2 7.8 collective-permute-done.124
  1068.6 6.7 collective-permute-done.177
  1098.3 5.2 collective-permute-done.191
  (859 shorter events, 500.5 us)
Async XLA Ops:
  0.7 85.1 %collective-permute-start.75 = (bf16[64,1024]{1,0:T(8,128)(2,1)}, bf16[64,1024]{1,0:T(8,128)(2,1)}, u32[]{:S(2)}, u32[]{:S(2)}) collective-permute-start(bf16[64,1024]{1,0:T(8,128)(2,1)} %param.60), channel_id=1, source_target_pairs={{0,1},{1,0},{2,3},{3,2},{4,5},{5,4},{6,7},{7,6},{8,9},{9,8},{10,11... | collective-permute-start | bytes 393224 | tf_op jit(solution)/shard_map/ppermute | solution.py:280
  1.2 89.8 %collective-permute-start.76 = (bf16[64,1024]{1,0:T(8,128)(2,1)}, bf16[64,1024]{1,0:T(8,128)(2,1)}, u32[]{:S(2)}, u32[]{:S(2)}) collective-permute-start(bf16[64,1024]{1,0:T(8,128)(2,1)} %param.60), channel_id=1, source_target_pairs={{0,4},{1,5},{4,8},{5,9},{8,12},{9,13},{12,14},{13,15},{14,10},{15,... | collective-permute-start | bytes 393224 | tf_op jit(solution)/shard_map/ppermute | solution.py:272
  3.8 108.2 %collective-permute-start.78 = (bf16[64,1024]{1,0:T(8,128)(2,1)}, bf16[64,1024]{1,0:T(8,128)(2,1)}, u32[]{:S(2)}, u32[]{:S(2)}) collective-permute-start(bf16[64,1024]{1,0:T(8,128)(2,1)} %param.60), channel_id=1, source_target_pairs={{4,0},{5,1},{8,4},{9,5},{12,8},{13,9},{14,12},{15,13},{10,14},{11,... | collective-permute-start | bytes 393224 | tf_op jit(solution)/shard_map/ppermute | solution.py:275
  3.8 194.8 %collective-permute-start.90 = (bf16[64,4096]{1,0:T(8,128)(2,1)}, bf16[64,4096]{1,0:T(8,128)(2,1)}, u32[]{:S(2)}, u32[]{:S(2)}) collective-permute-start(bf16[64,4096]{1,0:T(8,128)(2,1)} %param.61), channel_id=1, source_target_pairs={{0,1},{1,0},{2,3},{3,2},{4,5},{5,4},{6,7},{7,6},{8,9},{9,8},{10,11... | collective-permute-start | bytes 1572872 | tf_op jit(solution)/shard_map/ppermute | solution.py:280
  4.0 85.3 %collective-permute-start.15 = (bf16[64,1024]{1,0:T(8,128)(2,1)}, bf16[64,1024]{1,0:T(8,128)(2,1)}, u32[]{:S(2)}, u32[]{:S(2)}) collective-permute-start(bf16[64,1024]{1,0:T(8,128)(2,1)} %param.56), channel_id=1, source_target_pairs={{0,1},{1,0},{2,3},{3,2},{4,5},{5,4},{6,7},{7,6},{8,9},{9,8},{10,11... | collective-permute-start | bytes 393224 | tf_op jit(solution)/shard_map/ppermute | solution.py:280
  89.3 25.8 %collective-permute-start.18 = (bf16[64,1024]{1,0:T(8,128)(2,1)S(1)}, bf16[64,1024]{1,0:T(8,128)(2,1)S(1)}, u32[]{:S(2)}, u32[]{:S(2)}) collective-permute-start(bf16[64,1024]{1,0:T(8,128)(2,1)S(1)} %copy-done.52), channel_id=1, source_target_pairs={{4,0},{5,1},{8,4},{9,5},{12,8},{13,9},{14,12},{15,13},{10,14},{11,... | collective-permute-start | bytes 393224 | tf_op jit(solution)/shard_map/ppermute | solution.py:275
  112.1 23.4 %collective-permute-start.48 = (bf16[64,1024]{1,0:T(8,128)(2,1)S(1)}, bf16[64,1024]{1,0:T(8,128)(2,1)S(1)}, u32[]{:S(2)}, u32[]{:S(2)}) collective-permute-start(bf16[64,1024]{1,0:T(8,128)(2,1)S(1)} %copy-done.55), channel_id=1, source_target_pairs={{4,0},{5,1},{8,4},{9,5},{12,8},{13,9},{14,12},{15,13},{10,14},{11,... | collective-permute-start | bytes 393224 | tf_op jit(solution)/shard_map/ppermute | solution.py:275
  117.9 20.4 %collective-permute-start.63 = (bf16[64,1024]{1,0:T(8,128)(2,1)}, bf16[64,1024]{1,0:T(8,128)(2,1)S(1)}, u32[]{:S(2)}, u32[]{:S(2)}) collective-permute-start(bf16[64,1024]{1,0:T(8,128)(2,1)} %param.59), channel_id=1, source_target_pairs={{4,0},{5,1},{8,4},{9,5},{12,8},{13,9},{14,12},{15,13},{10,14},{11,... | collective-permute-start | bytes 393224 | tf_op jit(solution)/shard_map/ppermute | solution.py:275
  133.6 63.1 %collective-permute-start = (bf16[208,1024]{1,0:T(8,128)(2,1)S(1)}, bf16[208,1024]{1,0:T(8,128)(2,1)S(1)}, u32[]{:S(2)}, u32[]{:S(2)}) collective-permute-start(bf16[208,1024]{1,0:T(8,128)(2,1)S(1)} %copy-done.45), channel_id=1, source_target_pairs={{0,1},{1,0},{2,3},{3,2},{4,5},{5,4},{6,7},{7,6},{8,9},{9,8},{10,11... | collective-permute-start | bytes 1277960 | tf_op jit(solution)/shard_map/ppermute | solution.py:280
  135.5 15.7 %collective-permute-start.82 = (bf16[64,1024]{1,0:T(8,128)(2,1)}, bf16[64,1024]{1,0:T(8,128)(2,1)S(1)}, u32[]{:S(2)}, u32[]{:S(2)}) collective-permute-start(bf16[64,1024]{1,0:T(8,128)(2,1)} %collective-permute-done.78), channel_id=1, source_target_pairs={{4,0},{5,1},{8,4},{9,5},{12,8},{13,9},{14,12},{15,13},{10,14},{11,... | collective-permute-start | bytes 393224 | tf_op jit(solution)/shard_map/ppermute | solution.py:275
  151.2 46.3 %collective-permute-start.1 = (bf16[208,1024]{1,0:T(8,128)(2,1)S(1)}, bf16[208,1024]{1,0:T(8,128)(2,1)S(1)}, u32[]{:S(2)}, u32[]{:S(2)}) collective-permute-start(bf16[208,1024]{1,0:T(8,128)(2,1)S(1)} %copy-done.45), channel_id=1, source_target_pairs={{0,4},{1,5},{4,8},{5,9},{8,12},{9,13},{12,14},{13,15},{14,10},{15,... | collective-permute-start | bytes 1277960 | tf_op jit(solution)/shard_map/ppermute | solution.py:272
  191.5 12.9 %collective-permute-start.91 = (bf16[64,4096]{1,0:T(8,128)(2,1)S(1)}, bf16[64,4096]{1,0:T(8,128)(2,1)S(1)}, u32[]{:S(2)}, u32[]{:S(2)}) collective-permute-start(bf16[64,4096]{1,0:T(8,128)(2,1)S(1)} %copy-done.43), channel_id=1, source_target_pairs={{0,4},{1,5},{4,8},{5,9},{8,12},{9,13},{12,14},{13,15},{14,10},{15,... | collective-permute-start | bytes 1572872 | tf_op jit(solution)/shard_map/ppermute | solution.py:272
  195.7 70.1 %collective-permute-start.3 = (bf16[208,1024]{1,0:T(8,128)(2,1)S(1)}, bf16[208,1024]{1,0:T(8,128)(2,1)S(1)}, u32[]{:S(2)}, u32[]{:S(2)}) collective-permute-start(bf16[208,1024]{1,0:T(8,128)(2,1)S(1)} %copy-done.45), channel_id=1, source_target_pairs={{4,0},{5,1},{8,4},{9,5},{12,8},{13,9},{14,12},{15,13},{10,14},{11,... | collective-permute-start | bytes 1277960 | tf_op jit(solution)/shard_map/ppermute | solution.py:275
  196.7 51.6 %collective-permute-start.105 = (bf16[256,1024]{1,0:T(8,128)(2,1)S(1)}, bf16[256,1024]{1,0:T(8,128)(2,1)S(1)}, u32[]{:S(2)}, u32[]{:S(2)}) collective-permute-start(bf16[256,1024]{1,0:T(8,128)(2,1)S(1)} %copy-done.44), channel_id=1, source_target_pairs={{0,1},{1,0},{2,3},{3,2},{4,5},{5,4},{6,7},{7,6},{8,9},{9,8},{10,11... | collective-permute-start | bytes 1572872 | tf_op jit(solution)/shard_map/ppermute | solution.py:280
  208.1 44.0 %collective-permute-start.106 = (bf16[256,1024]{1,0:T(8,128)(2,1)S(1)}, bf16[256,1024]{1,0:T(8,128)(2,1)S(1)}, u32[]{:S(2)}, u32[]{:S(2)}) collective-permute-start(bf16[256,1024]{1,0:T(8,128)(2,1)S(1)} %copy-done.44), channel_id=1, source_target_pairs={{0,4},{1,5},{4,8},{5,9},{8,12},{9,13},{12,14},{13,15},{14,10},{15,... | collective-permute-start | bytes 1572872 | tf_op jit(solution)/shard_map/ppermute | solution.py:272
  247.6 22.1 %collective-permute-start.2 = (bf16[208,1024]{1,0:T(8,128)(2,1)S(1)}, bf16[208,1024]{1,0:T(8,128)(2,1)S(1)}, u32[]{:S(2)}, u32[]{:S(2)}) collective-permute-start(bf16[208,1024]{1,0:T(8,128)(2,1)S(1)} %collective-permute-done.1), channel_id=1, source_target_pairs={{0,1},{1,0},{2,3},{3,2},{4,5},{5,4},{6,7},{7,6},{8,9},{9,8},{10,11... | collective-permute-start | bytes 1277960 | tf_op jit(solution)/shard_map/ppermute | solution.py:280
  248.3 18.5 %collective-permute-start.89 = (bf16[64,1024]{1,0:T(8,128)(2,1)S(1)}, bf16[64,1024]{1,0:T(8,128)(2,1)S(1)}, u32[]{:S(2)}, u32[]{:S(2)}) collective-permute-start(bf16[64,1024]{1,0:T(8,128)(2,1)S(1)} %collective-permute-done.88), channel_id=1, source_target_pairs={{0,1},{1,0},{2,3},{3,2},{4,5},{5,4},{6,7},{7,6},{8,9},{9,8},{10,11... | collective-permute-start | bytes 393224 | tf_op jit(solution)/shard_map/ppermute | solution.py:280
  252.0 15.8 %collective-permute-start.29 = (bf16[64,1024]{1,0:T(8,128)(2,1)S(1)}, bf16[64,1024]{1,0:T(8,128)(2,1)S(1)}, u32[]{:S(2)}, u32[]{:S(2)}) collective-permute-start(bf16[64,1024]{1,0:T(8,128)(2,1)S(1)} %collective-permute-done.28), channel_id=1, source_target_pairs={{0,1},{1,0},{2,3},{3,2},{4,5},{5,4},{6,7},{7,6},{8,9},{9,8},{10,11... | collective-permute-start | bytes 393224 | tf_op jit(solution)/shard_map/ppermute | solution.py:280
  265.8 14.8 %collective-permute-start.93 = (bf16[64,4096]{1,0:T(8,128)(2,1)S(1)}, bf16[64,4096]{1,0:T(8,128)(2,1)S(1)}, u32[]{:S(2)}, u32[]{:S(2)}) collective-permute-start(bf16[64,4096]{1,0:T(8,128)(2,1)S(1)} %copy-done.43), channel_id=1, source_target_pairs={{4,0},{5,1},{8,4},{9,5},{12,8},{13,9},{14,12},{15,13},{10,14},{11,... | collective-permute-start | bytes 1572872 | tf_op jit(solution)/shard_map/ppermute | solution.py:275
  266.8 14.3 %collective-permute-start.5 = (bf16[208,1024]{1,0:T(8,128)(2,1)S(1)}, bf16[208,1024]{1,0:T(8,128)(2,1)S(1)}, u32[]{:S(2)}, u32[]{:S(2)}) collective-permute-start(bf16[208,1024]{1,0:T(8,128)(2,1)S(1)} %collective-permute-done.1), channel_id=1, source_target_pairs={{0,4},{1,5},{4,8},{5,9},{8,12},{9,13},{12,14},{13,15},{14,10},{15,... | collective-permute-start | bytes 1277960 | tf_op jit(solution)/shard_map/ppermute | solution.py:272
  268.6 13.4 %collective-permute-start.92 = (bf16[64,4096]{1,0:T(8,128)(2,1)S(1)}, bf16[64,4096]{1,0:T(8,128)(2,1)S(1)}, u32[]{:S(2)}, u32[]{:S(2)}) collective-permute-start(bf16[64,4096]{1,0:T(8,128)(2,1)S(1)} %collective-permute-done.91), channel_id=1, source_target_pairs={{0,1},{1,0},{2,3},{3,2},{4,5},{5,4},{6,7},{7,6},{8,9},{9,8},{10,11... | collective-permute-start | bytes 1572872 | tf_op jit(solution)/shard_map/ppermute | solution.py:280
  269.7 22.1 %collective-permute-start.108 = (bf16[256,1024]{1,0:T(8,128)(2,1)S(1)}, bf16[256,1024]{1,0:T(8,128)(2,1)S(1)}, u32[]{:S(2)}, u32[]{:S(2)}) collective-permute-start(bf16[256,1024]{1,0:T(8,128)(2,1)S(1)} %copy-done.44), channel_id=1, source_target_pairs={{4,0},{5,1},{8,4},{9,5},{12,8},{13,9},{14,12},{15,13},{10,14},{11,... | collective-permute-start | bytes 1572872 | tf_op jit(solution)/shard_map/ppermute | solution.py:275
  272.3 28.6 %collective-permute-start.7 = (bf16[208,1024]{1,0:T(8,128)(2,1)S(1)}, bf16[208,1024]{1,0:T(8,128)(2,1)S(1)}, u32[]{:S(2)}, u32[]{:S(2)}) collective-permute-start(bf16[208,1024]{1,0:T(8,128)(2,1)S(1)} %collective-permute-done.3), channel_id=1, source_target_pairs={{4,0},{5,1},{8,4},{9,5},{12,8},{13,9},{14,12},{15,13},{10,14},{11,... | collective-permute-start | bytes 1277960 | tf_op jit(solution)/shard_map/ppermute | solution.py:275
  281.9 31.9 %collective-permute-start.97 = (bf16[64,4096]{1,0:T(8,128)(2,1)S(1)}, bf16[64,4096]{1,0:T(8,128)(2,1)S(1)}, u32[]{:S(2)}, u32[]{:S(2)}) collective-permute-start(bf16[64,4096]{1,0:T(8,128)(2,1)S(1)} %collective-permute-done.93), channel_id=1, source_target_pairs={{4,0},{5,1},{8,4},{9,5},{12,8},{13,9},{14,12},{15,13},{10,14},{11,... | collective-permute-start | bytes 1572872 | tf_op jit(solution)/shard_map/ppermute | solution.py:275
  291.8 14.1 %collective-permute-start.110 = (bf16[256,1024]{1,0:T(8,128)(2,1)S(1)}, bf16[256,1024]{1,0:T(8,128)(2,1)S(1)}, u32[]{:S(2)}, u32[]{:S(2)}) collective-permute-start(bf16[256,1024]{1,0:T(8,128)(2,1)S(1)} %collective-permute-done.106), channel_id=1, source_target_pairs={{0,4},{1,5},{4,8},{5,9},{8,12},{9,13},{12,14},{13,15},{14,10},{15,... | collective-permute-start | bytes 1572872 | tf_op jit(solution)/shard_map/ppermute | solution.py:272
  293.4 13.3 %collective-permute-start.6 = (bf16[208,1024]{1,0:T(8,128)(2,1)S(1)}, bf16[208,1024]{1,0:T(8,128)(2,1)S(1)}, u32[]{:S(2)}, u32[]{:S(2)}) collective-permute-start(bf16[208,1024]{1,0:T(8,128)(2,1)S(1)} %collective-permute-done.5), channel_id=1, source_target_pairs={{0,1},{1,0},{2,3},{3,2},{4,5},{5,4},{6,7},{7,6},{8,9},{9,8},{10,11... | collective-permute-start | bytes 1277960 | tf_op jit(solution)/shard_map/ppermute | solution.py:280
  306.7 16.7 %collective-permute-start.112 = (bf16[256,1024]{1,0:T(8,128)(2,1)S(1)}, bf16[256,1024]{1,0:T(8,128)(2,1)S(1)}, u32[]{:S(2)}, u32[]{:S(2)}) collective-permute-start(bf16[256,1024]{1,0:T(8,128)(2,1)S(1)} %collective-permute-done.108), channel_id=1, source_target_pairs={{4,0},{5,1},{8,4},{9,5},{12,8},{13,9},{14,12},{15,13},{10,14},{11,... | collective-permute-start | bytes 1572872 | tf_op jit(solution)/shard_map/ppermute | solution.py:275
  309.5 23.1 %collective-permute-start.11 = (bf16[208,1024]{1,0:T(8,128)(2,1)S(1)}, bf16[208,1024]{1,0:T(8,128)(2,1)S(1)}, u32[]{:S(2)}, u32[]{:S(2)}) collective-permute-start(bf16[208,1024]{1,0:T(8,128)(2,1)S(1)} %collective-permute-done.7), channel_id=1, source_target_pairs={{4,0},{5,1},{8,4},{9,5},{12,8},{13,9},{14,12},{15,13},{10,14},{11,... | collective-permute-start | bytes 1277960 | tf_op jit(solution)/shard_map/ppermute | solution.py:275
  313.8 14.7 %collective-permute-start.99 = (bf16[64,4096]{1,0:T(8,128)(2,1)S(1)}, bf16[64,4096]{1,0:T(8,128)(2,1)S(1)}, u32[]{:S(2)}, u32[]{:S(2)}) collective-permute-start(bf16[64,4096]{1,0:T(8,128)(2,1)S(1)} %collective-permute-done.95), channel_id=1, source_target_pairs={{0,4},{1,5},{4,8},{5,9},{8,12},{9,13},{12,14},{13,15},{14,10},{15,... | collective-permute-start | bytes 1572872 | tf_op jit(solution)/shard_map/ppermute | solution.py:272
  315.4 28.3 %collective-permute-start.101 = (bf16[64,4096]{1,0:T(8,128)(2,1)S(1)}, bf16[64,4096]{1,0:T(8,128)(2,1)S(1)}, u32[]{:S(2)}, u32[]{:S(2)}) collective-permute-start(bf16[64,4096]{1,0:T(8,128)(2,1)S(1)} %collective-permute-done.97), channel_id=1, source_target_pairs={{4,0},{5,1},{8,4},{9,5},{12,8},{13,9},{14,12},{15,13},{10,14},{11,... | collective-permute-start | bytes 1572872 | tf_op jit(solution)/shard_map/ppermute | solution.py:275
  323.4 15.9 %collective-permute-start.114 = (bf16[256,1024]{1,0:T(8,128)(2,1)S(1)}, bf16[256,1024]{1,0:T(8,128)(2,1)S(1)}, u32[]{:S(2)}, u32[]{:S(2)}) collective-permute-start(bf16[256,1024]{1,0:T(8,128)(2,1)S(1)} %collective-permute-done.110), channel_id=1, source_target_pairs={{0,4},{1,5},{4,8},{5,9},{8,12},{9,13},{12,14},{13,15},{14,10},{15,... | collective-permute-start | bytes 1572872 | tf_op jit(solution)/shard_map/ppermute | solution.py:272
  332.5 21.5 %collective-permute-start.116 = (bf16[256,1024]{1,0:T(8,128)(2,1)S(1)}, bf16[256,1024]{1,0:T(8,128)(2,1)S(1)}, u32[]{:S(2)}, u32[]{:S(2)}) collective-permute-start(bf16[256,1024]{1,0:T(8,128)(2,1)S(1)} %collective-permute-done.112), channel_id=1, source_target_pairs={{4,0},{5,1},{8,4},{9,5},{12,8},{13,9},{14,12},{15,13},{10,14},{11,... | collective-permute-start | bytes 1572872 | tf_op jit(solution)/shard_map/ppermute | solution.py:275
  339.9 14.1 %collective-permute-start.100 = (bf16[64,4096]{1,0:T(8,128)(2,1)S(1)}, bf16[64,4096]{1,0:T(8,128)(2,1)S(1)}, u32[]{:S(2)}, u32[]{:S(2)}) collective-permute-start(bf16[64,4096]{1,0:T(8,128)(2,1)S(1)} %collective-permute-done.99), channel_id=1, source_target_pairs={{0,1},{1,0},{2,3},{3,2},{4,5},{5,4},{6,7},{7,6},{8,9},{9,8},{10,11... | collective-permute-start | bytes 1572872 | tf_op jit(solution)/shard_map/ppermute | solution.py:280
  342.4 21.0 %collective-permute-start.103 = (bf16[64,4096]{1,0:T(8,128)(2,1)S(1)}, bf16[64,4096]{1,0:T(8,128)(2,1)}, u32[]{:S(2)}, u32[]{:S(2)}) collective-permute-start(bf16[64,4096]{1,0:T(8,128)(2,1)S(1)} %collective-permute-done.99), channel_id=1, source_target_pairs={{0,4},{1,5},{4,8},{5,9},{8,12},{9,13},{12,14},{13,15},{14,10},{15,... | collective-permute-start | bytes 1572872 | tf_op jit(solution)/shard_map/ppermute | solution.py:272
  343.8 19.6 %collective-permute-start.115 = (bf16[256,1024]{1,0:T(8,128)(2,1)S(1)}, bf16[256,1024]{1,0:T(8,128)(2,1)S(1)}, u32[]{:S(2)}, u32[]{:S(2)}) collective-permute-start(bf16[256,1024]{1,0:T(8,128)(2,1)S(1)} %collective-permute-done.114), channel_id=1, source_target_pairs={{0,1},{1,0},{2,3},{3,2},{4,5},{5,4},{6,7},{7,6},{8,9},{9,8},{10,11... | collective-permute-start | bytes 1572872 | tf_op jit(solution)/shard_map/ppermute | solution.py:280
  352.1 21.2 %collective-permute-start.118 = (bf16[256,1024]{1,0:T(8,128)(2,1)S(1)}, bf16[256,1024]{1,0:T(8,128)(2,1)}, u32[]{:S(2)}, u32[]{:S(2)}) collective-permute-start(bf16[256,1024]{1,0:T(8,128)(2,1)S(1)} %collective-permute-done.114), channel_id=1, source_target_pairs={{0,4},{1,5},{4,8},{5,9},{8,12},{9,13},{12,14},{13,15},{14,10},{15,... | collective-permute-start | bytes 1572872 | tf_op jit(solution)/shard_map/ppermute | solution.py:272
  354.0 21.8 %collective-permute-start.102 = (bf16[64,4096]{1,0:T(8,128)(2,1)S(1)}, bf16[64,4096]{1,0:T(8,128)(2,1)S(1)}, u32[]{:S(2)}, u32[]{:S(2)}) collective-permute-start(bf16[64,4096]{1,0:T(8,128)(2,1)S(1)} %collective-permute-done.101), channel_id=1, source_target_pairs={{0,1},{1,0},{2,3},{3,2},{4,5},{5,4},{6,7},{7,6},{8,9},{9,8},{10,11... | collective-permute-start | bytes 1572872 | tf_op jit(solution)/shard_map/ppermute | solution.py:280
  354.0 22.6 %collective-permute-start.117 = (bf16[256,1024]{1,0:T(8,128)(2,1)S(1)}, bf16[256,1024]{1,0:T(8,128)(2,1)S(1)}, u32[]{:S(2)}, u32[]{:S(2)}) collective-permute-start(bf16[256,1024]{1,0:T(8,128)(2,1)S(1)} %collective-permute-done.116), channel_id=1, source_target_pairs={{0,1},{1,0},{2,3},{3,2},{4,5},{5,4},{6,7},{7,6},{8,9},{9,8},{10,11... | collective-permute-start | bytes 1572872 | tf_op jit(solution)/shard_map/ppermute | solution.py:280
  363.4 17.8 %collective-permute-start.14 = (bf16[208,1024]{1,0:T(8,128)(2,1)S(1)}, bf16[208,1024]{1,0:T(8,128)(2,1)S(1)}, u32[]{:S(2)}, u32[]{:S(2)}) collective-permute-start(bf16[208,1024]{1,0:T(8,128)(2,1)S(1)} %collective-permute-done.13), channel_id=1, source_target_pairs={{0,1},{1,0},{2,3},{3,2},{4,5},{5,4},{6,7},{7,6},{8,9},{9,8},{10,11... | collective-permute-start | bytes 1277960 | tf_op jit(solution)/shard_map/ppermute | solution.py:280
  363.4 116.1 %collective-permute-start.104 = (bf16[64,4096]{1,0:T(8,128)(2,1)}, bf16[64,4096]{1,0:T(8,128)(2,1)}, u32[]{:S(2)}, u32[]{:S(2)}) collective-permute-start(bf16[64,4096]{1,0:T(8,128)(2,1)} %collective-permute-done.103), channel_id=1, source_target_pairs={{0,1},{1,0},{2,3},{3,2},{4,5},{5,4},{6,7},{7,6},{8,9},{9,8},{10,11... | collective-permute-start | bytes 1572872 | tf_op jit(solution)/shard_map/ppermute | solution.py:280
  373.3 155.2 %collective-permute-start.119 = (bf16[256,1024]{1,0:T(8,128)(2,1)}, bf16[256,1024]{1,0:T(8,128)(2,1)}, u32[]{:S(2)}, u32[]{:S(2)}) collective-permute-start(bf16[256,1024]{1,0:T(8,128)(2,1)} %collective-permute-done.118), channel_id=1, source_target_pairs={{0,1},{1,0},{2,3},{3,2},{4,5},{5,4},{6,7},{7,6},{8,9},{9,8},{10,11... | collective-permute-start | bytes 1572872 | tf_op jit(solution)/shard_map/ppermute | solution.py:280
  837.4 144.6 %collective-permute-start.120 = (bf16[8,208,1024]{2,1,0:T(8,128)(2,1)}, bf16[8,208,1024]{2,1,0:T(8,128)(2,1)}, u32[]{:S(2)}, u32[]{:S(2)}) collective-permute-start(bf16[8,208,1024]{2,1,0:T(8,128)(2,1)} %dynamic-slice_bitcast_fusion.2), channel_id=1, source_target_pairs={{0,1},{1,0},{2,3},{3,2},{4,5},{5,4},{6,7},{7,6},{8,9},{9,8},{10,11... | collective-permute-start | bytes 10223624 | tf_op jit(solution)/shard_map/ppermute | solution.py:309
  852.6 13.8 %collective-permute-start.138 = (bf16[8,64,1024]{2,1,0:T(8,128)(2,1)}, bf16[8,64,1024]{2,1,0:T(8,128)(2,1)}, u32[]{:S(2)}, u32[]{:S(2)}) collective-permute-start(bf16[8,64,1024]{2,1,0:T(8,128)(2,1)} %dynamic-slice_bitcast_fusion.6), channel_id=1, source_target_pairs={{0,1},{1,0},{2,3},{3,2},{4,5},{5,4},{6,7},{7,6},{8,9},{9,8},{10,11... | collective-permute-start | bytes 3145736 | tf_op jit(solution)/shard_map/ppermute | solution.py:309
  854.2 14.2 %collective-permute-start.156 = (bf16[8,64,1024]{2,1,0:T(8,128)(2,1)S(1)}, bf16[8,64,1024]{2,1,0:T(8,128)(2,1)}, u32[]{:S(2)}, u32[]{:S(2)}) collective-permute-start(bf16[8,64,1024]{2,1,0:T(8,128)(2,1)S(1)} %dynamic-slice_bitcast_fusion.4), channel_id=1, source_target_pairs={{0,1},{1,0},{2,3},{3,2},{4,5},{5,4},{6,7},{7,6},{8,9},{9,8},{10,11... | collective-permute-start | bytes 3145736 | tf_op jit(solution)/shard_map/ppermute | solution.py:309
  864.1 135.5 %collective-permute-start.174 = (bf16[8,64,4096]{2,1,0:T(8,128)(2,1)}, bf16[8,64,4096]{2,1,0:T(8,128)(2,1)}, u32[]{:S(2)}, u32[]{:S(2)}) collective-permute-start(bf16[8,64,4096]{2,1,0:T(8,128)(2,1)} %dynamic-slice_bitcast_fusion.1), channel_id=1, source_target_pairs={{0,1},{1,0},{2,3},{3,2},{4,5},{5,4},{6,7},{7,6},{8,9},{9,8},{10,11... | collective-permute-start | bytes 12582920 | tf_op jit(solution)/shard_map/ppermute | solution.py:309
  866.4 139.7 %collective-permute-start.183 = (bf16[8,256,1024]{2,1,0:T(8,128)(2,1)}, bf16[8,256,1024]{2,1,0:T(8,128)(2,1)}, u32[]{:S(2)}, u32[]{:S(2)}) collective-permute-start(bf16[8,256,1024]{2,1,0:T(8,128)(2,1)} %dynamic-slice_bitcast_fusion), channel_id=1, source_target_pairs={{0,1},{1,0},{2,3},{3,2},{4,5},{5,4},{6,7},{7,6},{8,9},{9,8},{10,11... | collective-permute-start | bytes 12582920 | tf_op jit(solution)/shard_map/ppermute | solution.py:309
  870.2 25.6 %collective-permute-start.134 = (bf16[64,1024]{1,0:T(8,128)(2,1)S(1)}, bf16[64,1024]{1,0:T(8,128)(2,1)S(1)}, u32[]{:S(2)}, u32[]{:S(2)}) collective-permute-start(bf16[64,1024]{1,0:T(8,128)(2,1)S(1)} %get-tuple-element.165), channel_id=1, source_target_pairs={{0,4},{1,5},{4,8},{5,9},{8,12},{9,13},{12,14},{13,15},{14,10},{15,... | collective-permute-start | bytes 393224 | tf_op jit(solution)/shard_map/ppermute | solution.py:322
  982.0 43.6 %collective-permute-start.173 = (bf16[64,1024]{1,0:T(8,128)(2,1)S(1)}, bf16[64,1024]{1,0:T(8,128)(2,1)S(1)}, u32[]{:S(2)}, u32[]{:S(2)}) collective-permute-start(bf16[64,1024]{1,0:T(8,128)(2,1)S(1)} %fusion.117), channel_id=1, source_target_pairs={{0,16},{16,0},{1,17},{17,1},{2,18},{18,2},{3,19},{19,3},{4,20},{20... | collective-permute-start | bytes 393224 | tf_op jit(solution)/shard_map/ppermute | solution.py:326
  990.3 21.8 %collective-permute-start.125 = (bf16[208,1024]{1,0:T(8,128)(2,1)}, bf16[208,1024]{1,0:T(8,128)(2,1)}, u32[]{:S(2)}, u32[]{:S(2)}) collective-permute-start(bf16[208,1024]{1,0:T(8,128)(2,1)} %get-tuple-element.133), channel_id=1, source_target_pairs={{4,0},{5,1},{8,4},{9,5},{12,8},{13,9},{14,12},{15,13},{10,14},{11,... | collective-permute-start | bytes 1277960 | tf_op jit(solution)/shard_map/ppermute | solution.py:322
  999.1 14.6 %collective-permute-start.122 = (bf16[208,1024]{1,0:T(8,128)(2,1)}, bf16[208,1024]{1,0:T(8,128)(2,1)}, u32[]{:S(2)}, u32[]{:S(2)}) collective-permute-start(bf16[208,1024]{1,0:T(8,128)(2,1)} %fusion.103), channel_id=1, source_target_pairs={{0,4},{1,5},{4,8},{5,9},{8,12},{9,13},{12,14},{13,15},{14,10},{15,... | collective-permute-start | bytes 1277960 | tf_op jit(solution)/shard_map/ppermute | solution.py:318
  1005.7 17.7 %collective-permute-start.175 = (bf16[64,4096]{1,0:T(8,128)(2,1)}, bf16[64,4096]{1,0:T(8,128)(2,1)}, u32[]{:S(2)}, u32[]{:S(2)}) collective-permute-start(bf16[64,4096]{1,0:T(8,128)(2,1)} %get-tuple-element.126), channel_id=1, source_target_pairs={{0,4},{1,5},{4,8},{5,9},{8,12},{9,13},{12,14},{13,15},{14,10},{15,... | collective-permute-start | bytes 1572872 | tf_op jit(solution)/shard_map/ppermute | solution.py:318
  1006.1 37.7 %collective-permute-start.179 = (bf16[64,4096]{1,0:T(8,128)(2,1)}, bf16[64,4096]{1,0:T(8,128)(2,1)}, u32[]{:S(2)}, u32[]{:S(2)}) collective-permute-start(bf16[64,4096]{1,0:T(8,128)(2,1)} %get-tuple-element.127), channel_id=1, source_target_pairs={{4,0},{5,1},{8,4},{9,5},{12,8},{13,9},{14,12},{15,13},{10,14},{11,... | collective-permute-start | bytes 1572872 | tf_op jit(solution)/shard_map/ppermute | solution.py:322
  1012.1 31.3 %collective-permute-start.184 = (bf16[256,1024]{1,0:T(8,128)(2,1)S(1)}, bf16[256,1024]{1,0:T(8,128)(2,1)S(1)}, u32[]{:S(2)}, u32[]{:S(2)}) collective-permute-start(bf16[256,1024]{1,0:T(8,128)(2,1)S(1)} %get-tuple-element.120), channel_id=1, source_target_pairs={{4,0},{5,1},{8,4},{9,5},{12,8},{13,9},{14,12},{15,13},{10,14},{11,... | collective-permute-start | bytes 1572872 | tf_op jit(solution)/shard_map/ppermute | solution.py:318
  1015.1 17.3 %collective-permute-start.123 = (bf16[208,1024]{1,0:T(8,128)(2,1)S(1)}, bf16[208,1024]{1,0:T(8,128)(2,1)S(1)}, u32[]{:S(2)}, u32[]{:S(2)}) collective-permute-start(bf16[208,1024]{1,0:T(8,128)(2,1)S(1)} %get-tuple-element.130), channel_id=1, source_target_pairs={{0,4},{1,5},{4,8},{5,9},{8,12},{9,13},{12,14},{13,15},{14,10},{15,... | collective-permute-start | bytes 1277960 | tf_op jit(solution)/shard_map/ppermute | solution.py:318
  1023.4 17.8 %collective-permute-start.126 = (bf16[208,1024]{1,0:T(8,128)(2,1)S(1)}, bf16[208,1024]{1,0:T(8,128)(2,1)S(1)}, u32[]{:S(2)}, u32[]{:S(2)}) collective-permute-start(bf16[208,1024]{1,0:T(8,128)(2,1)S(1)} %get-tuple-element.131), channel_id=1, source_target_pairs={{4,0},{5,1},{8,4},{9,5},{12,8},{13,9},{14,12},{15,13},{10,14},{11,... | collective-permute-start | bytes 1277960 | tf_op jit(solution)/shard_map/ppermute | solution.py:322
  1025.7 20.1 %collective-permute-start.176 = (bf16[64,4096]{1,0:T(8,128)(2,1)S(1)}, bf16[64,4096]{1,0:T(8,128)(2,1)S(1)}, u32[]{:S(2)}, u32[]{:S(2)}) collective-permute-start(bf16[64,4096]{1,0:T(8,128)(2,1)S(1)} %fusion.94), channel_id=1, source_target_pairs={{0,4},{1,5},{4,8},{5,9},{8,12},{9,13},{12,14},{13,15},{14,10},{15,... | collective-permute-start | bytes 1572872 | tf_op jit(solution)/shard_map/ppermute | solution.py:318
  1032.4 33.6 %collective-permute-start.188 = (bf16[256,1024]{1,0:T(8,128)(2,1)S(1)}, bf16[256,1024]{1,0:T(8,128)(2,1)S(1)}, u32[]{:S(2)}, u32[]{:S(2)}) collective-permute-start(bf16[256,1024]{1,0:T(8,128)(2,1)S(1)} %get-tuple-element.121), channel_id=1, source_target_pairs={{0,4},{1,5},{4,8},{5,9},{8,12},{9,13},{12,14},{13,15},{14,10},{15,... | collective-permute-start | bytes 1572872 | tf_op jit(solution)/shard_map/ppermute | solution.py:322
  1043.5 20.6 %collective-permute-start.124 = (bf16[208,1024]{1,0:T(8,128)(2,1)S(1)}, bf16[208,1024]{1,0:T(8,128)(2,1)S(1)}, u32[]{:S(2)}, u32[]{:S(2)}) collective-permute-start(bf16[208,1024]{1,0:T(8,128)(2,1)S(1)} %get-tuple-element.128), channel_id=1, source_target_pairs={{0,4},{1,5},{4,8},{5,9},{8,12},{9,13},{12,14},{13,15},{14,10},{15,... | collective-permute-start | bytes 1277960 | tf_op jit(solution)/shard_map/ppermute | solution.py:318
  1043.8 22.2 %collective-permute-start.185 = (bf16[256,1024]{1,0:T(8,128)(2,1)S(1)}, bf16[256,1024]{1,0:T(8,128)(2,1)S(1)}, u32[]{:S(2)}, u32[]{:S(2)}) collective-permute-start(bf16[256,1024]{1,0:T(8,128)(2,1)S(1)} %fusion.87), channel_id=1, source_target_pairs={{4,0},{5,1},{8,4},{9,5},{12,8},{13,9},{14,12},{15,13},{10,14},{11,... | collective-permute-start | bytes 1572872 | tf_op jit(solution)/shard_map/ppermute | solution.py:318
  1047.1 28.2 %collective-permute-start.177 = (bf16[64,4096]{1,0:T(8,128)(2,1)S(1)}, bf16[64,4096]{1,0:T(8,128)(2,1)S(1)}, u32[]{:S(2)}, u32[]{:S(2)}) collective-permute-start(bf16[64,4096]{1,0:T(8,128)(2,1)S(1)} %get-tuple-element.124), channel_id=1, source_target_pairs={{0,4},{1,5},{4,8},{5,9},{8,12},{9,13},{12,14},{13,15},{14,10},{15,... | collective-permute-start | bytes 1572872 | tf_op jit(solution)/shard_map/ppermute | solution.py:318
  1054.4 20.9 %collective-permute-start.180 = (bf16[64,4096]{1,0:T(8,128)(2,1)S(1)}, bf16[64,4096]{1,0:T(8,128)(2,1)S(1)}, u32[]{:S(2)}, u32[]{:S(2)}) collective-permute-start(bf16[64,4096]{1,0:T(8,128)(2,1)S(1)} %get-tuple-element.125), channel_id=1, source_target_pairs={{4,0},{5,1},{8,4},{9,5},{12,8},{13,9},{14,12},{15,13},{10,14},{11,... | collective-permute-start | bytes 1572872 | tf_op jit(solution)/shard_map/ppermute | solution.py:322
  1064.3 13.3 %collective-permute-start.128 = (bf16[208,1024]{1,0:T(8,128)(2,1)S(1)}, bf16[208,1024]{1,0:T(8,128)(2,1)S(1)}, u32[]{:S(2)}, u32[]{:S(2)}) collective-permute-start(bf16[208,1024]{1,0:T(8,128)(2,1)S(1)} %fusion.105), channel_id=1, source_target_pairs={{0,16},{16,0},{1,17},{17,1},{2,18},{18,2},{3,19},{19,3},{4,20},{20... | collective-permute-start | bytes 1277960 | tf_op jit(solution)/shard_map/ppermute | solution.py:326
  1066.5 13.3 %collective-permute-start.186 = (bf16[256,1024]{1,0:T(8,128)(2,1)S(1)}, bf16[256,1024]{1,0:T(8,128)(2,1)S(1)}, u32[]{:S(2)}, u32[]{:S(2)}) collective-permute-start(bf16[256,1024]{1,0:T(8,128)(2,1)S(1)} %get-tuple-element.118), channel_id=1, source_target_pairs={{4,0},{5,1},{8,4},{9,5},{12,8},{13,9},{14,12},{15,13},{10,14},{11,... | collective-permute-start | bytes 1572872 | tf_op jit(solution)/shard_map/ppermute | solution.py:318
  1067.9 13.1 %collective-permute-start.189 = (bf16[256,1024]{1,0:T(8,128)(2,1)S(1)}, bf16[256,1024]{1,0:T(8,128)(2,1)S(1)}, u32[]{:S(2)}, u32[]{:S(2)}) collective-permute-start(bf16[256,1024]{1,0:T(8,128)(2,1)S(1)} %get-tuple-element.119), channel_id=1, source_target_pairs={{0,4},{1,5},{4,8},{5,9},{8,12},{9,13},{12,14},{13,15},{14,10},{15,... | collective-permute-start | bytes 1572872 | tf_op jit(solution)/shard_map/ppermute | solution.py:322
  (234 other events, 2783.1 us)

commit v2 on v1

v2 whole, which is shorter than its diff:
```python
import functools
import math

import jax
import jax.numpy as jnp
from jax import lax
from jax.experimental import pallas as pl
from jax.experimental.pallas import tpu as pltpu
from jax.sharding import PartitionSpec as P

HEADS = 16
HEAD = 64


eps_norm = 1e-05


COST = 4
BIG = 1e30
NT = (((1,), (1,)), ((), ()))
TN = (((0,), (0,)), ((), ()))


def key_extras(ids):
    lane = jnp.arange(128)[None, :] % 64
    return jnp.where(lane < 8, (ids[:, None] != lane).astype(jnp.bfloat16), ((lane >= 8) & (lane < 11)).astype(jnp.bfloat16))


def query_extras(ids):
    lane = jnp.arange(128)[None, :] % 64
    return jnp.where((lane < 8) & (ids[:, None] == lane), -BIG, 0.0).astype(jnp.bfloat16)


def windows(unit_ids, key_ids, bq, bk, causal):
    n = key_ids.shape[0]
    nq = unit_ids.shape[0] // bq
    blocks = unit_ids.reshape(nq, bq)
    low = jnp.sum((key_ids[None, :] < blocks[:, :1]).astype(jnp.int32), axis=1)
    if causal:
        end = (jnp.arange(nq, dtype=jnp.int32) + 1) * bq
        count = (end - low + bk - 1) // bk
        start = end - count * bk
    else:
        end = jnp.sum((key_ids[None, :] <= blocks[:, -1:]).astype(jnp.int32), axis=1)
        low = low // 16 * 16
        count = (end - low + bk - 1) // bk
        start = jnp.minimum(low, n - count * bk)
    return jnp.concatenate([start, count])


def attend_forward_kernel(bq, bk, causal, hp, norm, win_ref, q_ref, k_ref, v_ref, qx_ref, kx_ref, o_ref, qe_ref, ka):
    L, N = q_ref.shape[0], k_ref.shape[0]
    nq = L // bq
    lane = lax.broadcasted_iota(jnp.int32, (1, 128), 1)
    first = lane < 64
    part = lane % 64
    for g in range(hp):
        kp = k_ref[:, g*128:(g+1)*128]
        ka[2*g] = jnp.where(first, kp, kx_ref[...])
        ka[2*g+1] = jnp.where(first, kx_ref[...], kp)
    row = lax.broadcasted_iota(jnp.int32, (128, 1), 0)
    rpart = row % 64

    def one(i, W):
        rows = pl.ds(pl.multiple_of(i * bq, bq), bq)
        win = pl.ds(pl.multiple_of(win_ref[i], 16), W)
        xb = qx_ref[rows, :]
        ss = []
        for h in range(2*hp):
            g = h // 2
            qb = q_ref[rows, g*128:(g+1)*128]
            qa = jnp.where(first, qb, xb) if h % 2 == 0 else jnp.where(first, xb, qb)
            s = lax.dot_general(ka[h, win, :], qa, NT, preferred_element_type=jnp.float32)
            if causal:
                tri = lax.broadcasted_iota(jnp.int32, (bq, bq), 0) <= lax.broadcasted_iota(jnp.int32, (bq, bq), 1)
                d = jnp.where(tri, s[W - bq:, :], -BIG)
                s = d if W == bq else jnp.concatenate([s[: W - bq, :], d], axis=0)
            ss.append(s)
        outs, invs, lses = [], [], []
        for h in range(2*hp):
            g = h // 2
            s = ss[h]
            m = jnp.max(s, axis=0, keepdims=True)
            p = jnp.exp(s - m)
            l = jnp.sum(p, axis=0, keepdims=True)
            inv = 1.0 / l
            if norm: p = p * inv
            o = lax.dot_general(p.astype(jnp.bfloat16), v_ref[win, g*128:(g+1)*128], TN, preferred_element_type=jnp.float32)
            outs.append(o); invs.append(inv)
            neg = -(m + jnp.log(l))
            hi = neg.astype(jnp.bfloat16).astype(jnp.float32)
            mid = (neg - hi).astype(jnp.bfloat16).astype(jnp.float32)
            lo = neg - hi - mid
            lses.append((hi, mid, lo))
        for g in range(hp):
            o = jnp.where(first, outs[2*g], outs[2*g+1])
            if not norm:
                t = jnp.where(row < 64, invs[2*g], invs[2*g+1])
                o = o * jnp.transpose(t)
            o_ref[rows, g*128:(g+1)*128] = o.astype(jnp.bfloat16)
            a, b = lses[2*g], lses[2*g+1]
            e = jnp.where(row < 64, jnp.where(rpart == 8, b[0], jnp.where(rpart == 9, b[1], b[2])), jnp.where(rpart == 8, a[0], jnp.where(rpart == 9, a[1], a[2])))
            e = jnp.transpose(jnp.where((rpart >= 8) & (rpart < 11), e, 0.0))
            qe_ref[rows, g*128:(g+1)*128] = jnp.where(part < 8, xb.astype(jnp.float32), e).astype(jnp.bfloat16)

    def step(i, c):
        for j in range(1, N // bk + 1):
            @pl.when(win_ref[nq + i] == j)
            def _():
                one(i, j * bk)
        return c

    lax.fori_loop(0, nq, step, 0)

def attend_forward(q, k, v, qx, kx, win, causal, bq=256, bk=256, hp=1, norm=False):
    L, D = q.shape
    N = k.shape[0]
    w = 128*hp
    col = lambda n: pl.BlockSpec((n, w), lambda p, _: (0, p))
    fix = lambda n: pl.BlockSpec((n, 128), lambda p, _: (0, 0))
    return pl.pallas_call(
        functools.partial(attend_forward_kernel, bq, bk, causal, hp, norm),
        grid_spec=pltpu.PrefetchScalarGridSpec(
            num_scalar_prefetch=1, grid=(D // w,),
            in_specs=[col(L), col(N), col(N), fix(L), fix(N)],
            out_specs=[col(L), col(L)],
            scratch_shapes=[pltpu.VMEM((2*hp, N, 128), jnp.bfloat16)]),
        out_shape=[jax.ShapeDtypeStruct((L, D), jnp.bfloat16)] * 2,
        compiler_params=pltpu.CompilerParams(vmem_limit_bytes=56 << 20),
        cost_estimate=pl.CostEstimate(flops=COST * 2 * 2 * L * N * D, bytes_accessed=10 * L * D, transcendentals=0),
    )(win, q, k, v, qx, kx)


def attend_backward_kernel(bq, bk, causal, win_ref, q_ref, k_ref, v_ref, o_ref, do_ref, qe_ref, kx_ref, dq_ref, dk_ref, dv_ref, ka, va, dka, dva):
    L, N = q_ref.shape[0], k_ref.shape[0]
    nq = L // bq
    lane = lax.broadcasted_iota(jnp.int32, (1, 128), 1)
    first = lane < 64
    part = lane % 64
    ones = jnp.broadcast_to(jnp.where(part < 3, 1.0, 0.0).astype(jnp.bfloat16), (N, 128))
    ka[0] = jnp.where(first, k_ref[...], kx_ref[...])
    ka[1] = jnp.where(first, kx_ref[...], k_ref[...])
    va[0] = jnp.where(first, v_ref[...], ones)
    va[1] = jnp.where(first, ones, v_ref[...])
    dka[...] = jnp.zeros_like(dka)
    dva[...] = jnp.zeros_like(dva)
    zero = jnp.zeros((1, 128), jnp.bfloat16)

    def one(i, W):
        rows = pl.ds(pl.multiple_of(i * bq, bq), bq)
        win = pl.ds(pl.multiple_of(win_ref[i], 16), W)
        qb, xb, dob = q_ref[rows, :], qe_ref[rows, :], do_ref[rows, :]
        prod = dob.astype(jnp.float32) * o_ref[rows, :].astype(jnp.float32)
        ps, dss = [], []
        for h in range(2):
            mine = first if h == 0 else jnp.logical_not(first)
            neg = -jnp.sum(jnp.where(mine, prod, 0.0), axis=1, keepdims=True)
            hi = neg.astype(jnp.bfloat16).astype(jnp.float32)
            mid = (neg - hi).astype(jnp.bfloat16).astype(jnp.float32)
            lo = neg - hi - mid
            de = jnp.where(part == 0, hi, jnp.where(part == 1, mid, jnp.where(part == 2, lo, 0.0))).astype(jnp.bfloat16)
            qa = jnp.where(mine, qb, xb)
            da = jnp.where(mine, dob, de)
            s = lax.dot_general(ka[h, win, :], qa, NT, preferred_element_type=jnp.float32)
            if causal:
                tri = lax.broadcasted_iota(jnp.int32, (bq, bq), 0) <= lax.broadcasted_iota(jnp.int32, (bq, bq), 1)
                d = jnp.where(tri, s[W - bq:, :], -BIG)
                s = d if W == bq else jnp.concatenate([s[: W - bq, :], d], axis=0)
            p = jnp.exp(s)
            dp = lax.dot_general(va[h, win, :], da, NT, preferred_element_type=jnp.float32)
            dss.append((p * dp).astype(jnp.bfloat16))
            ps.append(p.astype(jnp.bfloat16))
        docat = jnp.concatenate([jnp.where(first, dob, zero), jnp.where(first, zero, dob)], axis=0)
        qcat = jnp.concatenate([jnp.where(first, qb, zero), jnp.where(first, zero, qb)], axis=0)
        dva[win, :] += jnp.dot(jnp.concatenate(ps, axis=1), docat, preferred_element_type=jnp.float32)
        dka[win, :] += jnp.dot(jnp.concatenate(dss, axis=1), qcat, preferred_element_type=jnp.float32)
        kw = k_ref[win, :]
        dq0 = lax.dot_general(dss[0], kw, TN, preferred_element_type=jnp.float32)
        dq1 = lax.dot_general(dss[1], kw, TN, preferred_element_type=jnp.float32)
        dq_ref[rows, :] = (jnp.where(first, dq0, dq1) * 0.125).astype(jnp.bfloat16)

    def step(i, c):
        for j in range(1, N // bk + 1):
            @pl.when(win_ref[nq + i] == j)
            def _():
                one(i, j * bk)
        return c

    lax.fori_loop(0, nq, step, 0)
    dk_ref[...] = dka[...].astype(jnp.bfloat16)
    dv_ref[...] = dva[...].astype(jnp.bfloat16)


def attend_backward(q, k, v, o, do, qe, kx, win, causal, bq=256, bk=256):
    L, D = q.shape
    N = k.shape[0]
    col = lambda n: pl.BlockSpec((n, 128), lambda p, w: (0, p))
    fix = lambda n: pl.BlockSpec((n, 128), lambda p, w: (0, 0))
    return pl.pallas_call(
        functools.partial(attend_backward_kernel, bq, bk, causal),
        grid_spec=pltpu.PrefetchScalarGridSpec(
            num_scalar_prefetch=1, grid=(D // 128,),
            in_specs=[col(L), col(N), col(N), col(L), col(L), col(L), fix(N)],
            out_specs=[col(L), col(N), col(N)],
            scratch_shapes=[pltpu.VMEM((2, N, 128), jnp.bfloat16)] * 2 + [pltpu.VMEM((N, 128), jnp.float32)] * 2),
        out_shape=[jax.ShapeDtypeStruct((L, D), jnp.bfloat16)] + [jax.ShapeDtypeStruct((N, D), jnp.bfloat16)] * 2,
        compiler_params=pltpu.CompilerParams(vmem_limit_bytes=48 << 20),
        cost_estimate=pl.CostEstimate(flops=COST * 5 * 2 * L * N * D, bytes_accessed=16 * L * D, transcendentals=0),
    )(win, q, k, v, o, do, qe, kx)


def fetch(plan, refs, order_ref, dst, sem):
    kind, offset, rows, flat, piece_rows, count = plan
    if kind == "flat":
        pltpu.make_async_copy(refs[0].at[pl.ds(flat, rows * count)], dst, sem).start()
        return
    for j in range(count):
        if kind == "ring":
            src = refs[j].at[pl.ds(offset, rows)]
            at = pl.multiple_of(order_ref[j] * rows, 16)
        else:
            src = refs[0].at[pl.ds(j * piece_rows + offset, rows)]
            at = j * rows
        pltpu.make_async_copy(src, dst.at[pl.ds(at, rows)], sem).start()


def arrived(dst, sem):
    pltpu.make_async_copy(dst, dst, sem).wait()


def normed(values_in):
    centre = values_in - jnp.mean(values_in, axis=-1, keepdims=True)
    spread = jnp.mean(centre * centre, axis=-1, keepdims=True)
    scale = lax.rsqrt(spread + eps_norm)
    return centre * scale, scale


def normed_back(unit, scale, gain, grad_out):
    grad_unit = grad_out * gain
    inner = jnp.mean(grad_unit * unit, axis=-1, keepdims=True)
    return (grad_unit - jnp.mean(grad_unit, axis=-1, keepdims=True) - unit * inner) * scale


def mm(left, right):
    return jnp.dot(left, right, preferred_element_type=jnp.float32)


def mm_back(left, right):
    return lax.dot_general(left, right, NT, preferred_element_type=jnp.float32)


def low(values_in):
    return values_in.astype(jnp.bfloat16)


def term_rows(refs, at, values_in):
    refs[at : at + 1, :] += jnp.sum(values_in, axis=0, keepdims=True)


def first_kernel(plans, n_refs, order_ref, x_ref, norm_ref, *rest):
    refs, (a_ref, q_ref, k_ref, v_ref, w, sem) = rest[:n_refs], rest[n_refs:]

    @pl.when(pl.program_id(0) == 0)
    def _():
        for i in range(3):
            fetch(plans[i], refs, order_ref, w.at[i], sem.at[i])
        for i in range(3):
            arrived(w.at[i], sem.at[i])

    unit, _ = normed(x_ref[...].astype(jnp.float32))
    a = low(unit * norm_ref[0:1, :] + norm_ref[4:5, :])
    a_ref[...] = a
    q_ref[...] = low(mm(a, w[0]) * 0.125)
    k_ref[...] = low(mm(a, w[1]))
    v_ref[...] = low(mm(a, w[2]))


def second_kernel(plans, n_refs, order_ref, o_ref, x_ref, e_ref, norm_ref, *rest):
    refs, (r_ref, a_ref, q_ref, k_ref, v_ref, w, sem) = rest[:n_refs], rest[n_refs:]

    @pl.when(pl.program_id(0) == 0)
    def _():
        for i in range(4):
            fetch(plans[i], refs, order_ref, w.at[i], sem.at[i])
        for i in range(4):
            arrived(w.at[i], sem.at[i])

    r = x_ref[...].astype(jnp.float32) + mm(o_ref[...], w[0])
    r_ref[...] = r
    k_ref[...] = low(mm(e_ref[...], w[2]))
    v_ref[...] = low(mm(e_ref[...], w[3]))
    unit, _ = normed(r)
    a = low(unit * norm_ref[1:2, :] + norm_ref[5:6, :])
    a_ref[...] = a
    q_ref[...] = low(mm(a, w[1]) * 0.125)


def third_kernel(plans, n_b, n_c, order_ref, o_ref, r_ref, cot_ref, norm_ref, *rest):
    refs_b, refs_c = rest[:n_b], rest[n_b : n_b + n_c]
    (out_ref, a_ref, h_ref, df_ref, du_ref, dr_ref, dc_ref, do_ref, term_ref, wc, wi, wo, slope, sem) = rest[n_b + n_c :]
    parts = wi.shape[0]
    first = pl.program_id(0) == 0

    @pl.when(first)
    def _():
        fetch(plans[0], refs_b, order_ref, wc, sem.at[0])
        for i in range(parts):
            fetch(plans[1 + i], refs_c, order_ref, wi.at[i], sem.at[1 + i])
        fetch(plans[1 + parts], refs_c, order_ref, wo, sem.at[1 + parts])
        term_ref[...] = jnp.zeros_like(term_ref)
        arrived(wc, sem.at[0])

    r2 = r_ref[...] + mm(o_ref[...], wc[...])
    unit2, scale2 = normed(r2)
    a3 = low(unit2 * norm_ref[2:3, :] + norm_ref[6:7, :])
    a_ref[...] = a3

    @pl.when(first)
    def _():
        for i in range(parts):
            arrived(wi.at[i], sem.at[1 + i])
        arrived(wo, sem.at[1 + parts])

    width = wi.shape[2]
    r3 = r2
    for i in range(parts):
        cols = slice(i * width, (i + 1) * width)
        u = mm(a3, wi[i])
        half = 0.5 * (1.0 + lax.erf(u * (1.0 / math.sqrt(2.0))))
        h = low(u * half)
        h_ref[:, cols] = h
        slope[:, cols] = half + u * jnp.exp(-0.5 * u * u) * (1.0 / math.sqrt(2.0 * math.pi))
        r3 = r3 + mm(h, wo[cols, :])
    unit3, scale3 = normed(r3)
    out_ref[...] = low(unit3 * norm_ref[3:4, :] + norm_ref[7:8, :])
    cot = cot_ref[...].astype(jnp.float32)
    term_rows(term_ref, 3, cot * unit3)
    term_rows(term_ref, 7, cot)
    dr3 = normed_back(unit3, scale3, norm_ref[3:4, :], cot)
    df = low(dr3)
    df_ref[...] = df
    da3 = jnp.zeros_like(dr3)
    for i in range(parts):
        cols = slice(i * width, (i + 1) * width)
        du = low(mm_back(df, wo[cols, :]) * slope[:, cols])
        du_ref[:, cols] = du
        da3 = da3 + mm_back(du, wi[i])
    term_rows(term_ref, 2, da3 * unit2)
    term_rows(term_ref, 6, da3)
    dr2 = dr3 + normed_back(unit2, scale2, norm_ref[2:3, :], da3)
    dr_ref[...] = dr2
    dc = low(dr2)
    dc_ref[...] = dc
    do_ref[...] = low(mm_back(dc, wc[...]))


def fourth_kernel(plans, n_refs, order_ref, dq_ref, r_ref, dr_ref, dk_ref, dv_ref, norm_ref, *rest):
    refs, (dx_ref, dc_ref, do_ref, de_ref, term_ref, w, sem) = rest[:n_refs], rest[n_refs:]

    @pl.when(pl.program_id(0) == 0)
    def _():
        for i in range(4):
            fetch(plans[i], refs, order_ref, w.at[i], sem.at[i])
        for i in range(4):
            arrived(w.at[i], sem.at[i])
        term_ref[...] = jnp.zeros_like(term_ref)

    da = mm_back(dq_ref[...], w[1])
    unit, scale = normed(r_ref[...])
    term_rows(term_ref, 1, da * unit)
    term_rows(term_ref, 5, da)
    dx = dr_ref[...] + normed_back(unit, scale, norm_ref[1:2, :], da)
    dx_ref[...] = dx
    dc = low(dx)
    dc_ref[...] = dc
    do_ref[...] = low(mm_back(dc, w[0]))
    de_ref[...] = mm_back(dk_ref[...], w[2]) + mm_back(dv_ref[...], w[3])


def fifth_kernel(plans, n_refs, order_ref, dq_ref, dk_ref, dv_ref, x_ref, dr_ref, norm_ref, *rest):
    refs, (dx_ref, term_ref, w, sem) = rest[:n_refs], rest[n_refs:]

    @pl.when(pl.program_id(0) == 0)
    def _():
        for i in range(3):
            fetch(plans[i], refs, order_ref, w.at[i], sem.at[i])
        for i in range(3):
            arrived(w.at[i], sem.at[i])
        term_ref[...] = jnp.zeros_like(term_ref)

    da = mm_back(dq_ref[...], w[0]) + mm_back(dk_ref[...], w[1]) + mm_back(dv_ref[...], w[2])
    unit, scale = normed(x_ref[...].astype(jnp.float32))
    term_rows(term_ref, 0, da * unit)
    term_rows(term_ref, 4, da)
    dx_ref[...] = dr_ref[...] + normed_back(unit, scale, norm_ref[0:1, :], da)


def by_rows(kernel, order, row_inputs, norms, piece_refs, row_outputs, terms, scratch, flops, block=256):
    rows = row_inputs[0].shape[0]

    def spec(width):
        return pl.BlockSpec((block, width), lambda i, _: (i, 0))

    def fixed(shape):
        return pl.BlockSpec(shape, lambda i, _: (0, 0))

    out_shape = [jax.ShapeDtypeStruct((rows, w), t) for w, t in row_outputs]
    out_specs = [spec(w) for w, _ in row_outputs]
    if terms:
        out_shape.append(jax.ShapeDtypeStruct(norms.shape, jnp.float32))
        out_specs.append(fixed(norms.shape))
    moved = sum(x.size * x.dtype.itemsize for x in row_inputs) + sum(rows * w * t.dtype.itemsize if hasattr(t, "dtype") else rows * w * jnp.dtype(t).itemsize for w, t in row_outputs)
    return pl.pallas_call(
        kernel,
        grid_spec=pltpu.PrefetchScalarGridSpec(
            num_scalar_prefetch=1,
            grid=(rows // block,),
            in_specs=[spec(x.shape[1]) for x in row_inputs]
            + [fixed(norms.shape)]
            + [pl.BlockSpec(memory_space=pl.ANY)] * len(piece_refs),
            out_specs=out_specs,
            scratch_shapes=scratch,
        ),
        out_shape=out_shape,
        compiler_params=pltpu.CompilerParams(vmem_limit_bytes=58 << 20),
        cost_estimate=pl.CostEstimate(flops=flops, bytes_accessed=moved, transcendentals=0),
    )(order, *row_inputs, norms, *piece_refs)


def term_kernel(pairs, chips, rank_ref, *rest):
    lefts, rights = rest[: len(pairs)], rest[len(pairs) : 2 * len(pairs)]
    mine_ref, other_ref, turned = rest[2 * len(pairs) :]
    weight = pl.program_id(0)
    rows = mine_ref.shape[1]
    for i in range(len(pairs)):
        new_left = i == 0 or pairs[i] != pairs[i - 1]

        @pl.when(weight == i)
        def _():
            if new_left:

                @pl.when(pl.program_id(1) == 0)
                def _():
                    turned[...] = jnp.transpose(lefts[i][...])

            total = low(mm(turned[...], rights[i][...]))
            core = rank_ref[chips]
            for chip in range(chips):
                one = total[2 * chip * rows : (2 * chip + 1) * rows]
                two = total[(2 * chip + 1) * rows : (2 * chip + 2) * rows]
                mine_ref[rank_ref[chip]] = jnp.where(core == 0, one, two)
                other_ref[rank_ref[chip]] = jnp.where(core == 0, two, one)


def term_sets(rank, lefts, rights, pairs, count, block=256):
    total, width = lefts[0].shape[1], rights[0].shape[1]
    rows = total // count
    chips = count // 2
    number = len(lefts)

    def right_spec(i):
        return pl.BlockSpec(
            (rights[i].shape[0], block),
            lambda w, n, _: (0, jnp.where(w == i, n, jnp.where(w < i, 0, width // block - 1))),
        )

    return pl.pallas_call(
        functools.partial(term_kernel, pairs, chips),
        grid_spec=pltpu.PrefetchScalarGridSpec(
            num_scalar_prefetch=1,
            grid=(number, width // block),
            in_specs=[pl.BlockSpec(x.shape, lambda w, n, _: (0, 0)) for x in lefts] + [right_spec(i) for i in range(number)],
            out_specs=[pl.BlockSpec((chips, rows, block), lambda w, n, _: (0, w, n))] * 2,
            scratch_shapes=[pltpu.VMEM((total, lefts[0].shape[0]), jnp.bfloat16)],
        ),
        out_shape=[jax.ShapeDtypeStruct((chips, number * rows, width), jnp.bfloat16)] * 2,
        compiler_params=pltpu.CompilerParams(vmem_limit_bytes=58 << 20),
        cost_estimate=pl.CostEstimate(flops=2 * number * total * width * lefts[0].shape[0], bytes_accessed=6 * number * total * width, transcendentals=0),
    )(rank, *lefts, *rights)


def ring_walk(chips):
    half = chips // 2
    return [2 * i for i in range(half)] + [2 * i + 1 for i in reversed(range(half))]


def ring_moves(count):
    walk = ring_walk(count // 2)
    chips = len(walk)
    up = [(2 * walk[i] + c, 2 * walk[(i + 1) % chips] + c) for i in range(chips) for c in range(2)]
    down = [(b, a) for a, b in up]
    swap = [(i, i ^ 1) for i in range(count)]
    return up, down, swap


def ring_tables(count):
    chips = count // 2
    walk = ring_walk(chips)
    place = [0] * chips
    for at, chip in enumerate(walk):
        place[chip] = at
    order, rank = [], []
    for shard in range(count):
        at, core = place[shard // 2], shard % 2
        near = [walk[(at + k) % chips] for k in range(chips)]
        order.append([2 * c + core for c in near] + [2 * c + 1 - core for c in near])
        rank.append([(place[c] - at) % chips for c in range(chips)] + [core])
    me = lax.axis_index("shard")
    return jnp.array(order, jnp.int32)[me], jnp.array(rank, jnp.int32)[me]


def gather_pieces(piece, count):
    up, down, swap = ring_moves(count)
    chips = count // 2
    pieces = [piece] + [None] * (chips - 1)
    upward = downward = piece
    for step in range(1, chips // 2 + 1):
        upward = lax.ppermute(upward, "shard", up)
        pieces[chips - step] = upward
        if step < chips // 2:
            downward = lax.ppermute(downward, "shard", down)
            pieces[step] = downward
    return pieces + [lax.ppermute(p, "shard", swap) for p in pieces]


def add_low(*values_in):
    return low(sum(v.astype(jnp.float32) for v in values_in))


def over_rep(owned):
    partner = lax.ppermute(owned, "rep", [(0, 1), (1, 0)])
    return owned.astype(jnp.float32) + partner.astype(jnp.float32)


def ring_sum(mine, other, count):
    up, down, swap = ring_moves(count)
    chips = count // 2
    half = chips // 2
    came = lax.ppermute(other, "shard", swap)
    upward = add_low(mine[half], came[half])
    downward = add_low(mine[chips - half + 1], came[chips - half + 1])
    for step in range(half - 1, -1, -1):
        upward = lax.ppermute(upward, "shard", up)
        if step:
            upward = add_low(upward, mine[step], came[step])
    for step in range(half - 2, -1, -1):
        downward = lax.ppermute(downward, "shard", down)
        if step:
            downward = add_low(downward, mine[chips - step], came[chips - step])
    return over_rep(add_low(mine[0], came[0], upward, downward))


def scatter_sum(term):
    return over_rep(lax.psum_scatter(low(term), "shard", scatter_dimension=0, tiled=True))


def total_sum(values_in, count):
    step = 1
    while step < count:
        values_in = values_in + lax.ppermute(values_in, "shard", [(i, i ^ step) for i in range(count)])
        step *= 2
    return values_in + lax.ppermute(values_in, "rep", [(0, 1), (1, 0)])


def weight_term(left, right):
    return jnp.einsum("ra,rb->ab", left, right, preferred_element_type=jnp.float32)


def body(
    tokens,
    enc_states,
    unit_ids,
    enc_ids,
    self_q,
    self_k,
    self_v,
    self_o,
    cross_q,
    cross_k,
    cross_v,
    cross_o,
    ffn_in,
    ffn_out,
    norm_gains,
    norm_biases,
    cotangent,
):
    count = lax.axis_size("shard")
    ring = count == 16
    own, width = self_q.shape
    own_out = ffn_out.shape[0]
    parts = ffn_in.shape[1] // width
    hidden = parts * width
    own_width = norm_gains.shape[1]
    x = tokens.reshape(-1, width)
    enc = enc_states.reshape(-1, width)
    cot = cotangent.reshape(-1, width)
    row_count = x.shape[0]
    bf16, f32 = jnp.bfloat16, jnp.float32

    norm_piece = jnp.concatenate([norm_gains, norm_biases], axis=0)
    in_parts = [ffn_in[:, i * width : (i + 1) * width] for i in range(parts)]
    if ring:
        order, rank = ring_tables(count)
        norm_row = jnp.pad(norm_piece.reshape(1, -1), ((0, 15), (0, width - 8 * own_width)))
        set_a = gather_pieces(jnp.concatenate([self_q, self_k, self_v, norm_row], axis=0), count)
        set_b = gather_pieces(jnp.concatenate([self_o, cross_q, cross_k, cross_v, cross_o], axis=0), count)
        set_c = [lax.all_gather(jnp.concatenate(in_parts + [ffn_out], axis=0), "shard", axis=0, tiled=True)]
        norm_rows = jnp.concatenate([p[3 * own : 3 * own + 1, : 8 * own_width] for p in set_a], axis=0)
        place = (jnp.arange(count, dtype=jnp.int32)[:, None] == order[None, :]).astype(bf16)
        norms = mm(place, norm_rows)
        norms = jnp.transpose(norms.reshape(count, 8, own_width), (1, 0, 2)).reshape(8, width)
        kinds = ("ring", "ring", "tiled")
    else:
        order = jnp.zeros((1,), jnp.int32)

        def whole(part):
            return lax.all_gather(part, "shard", axis=0, tiled=True)

        set_a = [jnp.concatenate([whole(w) for w in (self_q, self_k, self_v)], axis=0)]
        set_b = [jnp.concatenate([whole(w) for w in (self_o, cross_q, cross_k, cross_v, cross_o)], axis=0)]
        set_c = [jnp.concatenate([whole(w) for w in in_parts + [ffn_out]], axis=0)]
        norms = lax.all_gather(norm_piece, "shard", axis=1, tiled=True).astype(f32)
        kinds = ("flat", "flat", "flat")
    plan_a = [(kinds[0], i * own, own, i * width, 0, count) for i in range(3)]
    plan_b = [(kinds[1], i * own, own, i * width, 0, count) for i in range(5)]
    piece_c = parts * own + own_out
    plan_c = [(kinds[2], i * own, own, i * width, piece_c, count) for i in range(parts)]
    plan_c.append((kinds[2], parts * own, own_out, parts * width, piece_c, count))
    sems = pltpu.SemaphoreType.DMA
    square = 2 * row_count * width * width

    unit_extra, enc_extra = key_extras(unit_ids[0]), key_extras(enc_ids[0])
    query_extra = query_extras(unit_ids[0])
    self_windows = windows(unit_ids[0], unit_ids[0], 256, 256, True)
    cross_windows = windows(unit_ids[0], enc_ids[0], 256, 256, False)
    a1, q1, k1, v1 = by_rows(
        functools.partial(first_kernel, plan_a, len(set_a)), order, [x], norms, set_a,
        [(width, bf16)] * 4, False,
        [pltpu.VMEM((3, width, width), bf16), sems((3,))], 3 * square,
    )
    o1, log1 = attend_forward(q1, k1, v1, query_extra, unit_extra, self_windows, True, hp=2, norm=True)
    r1, a2, q2, k2, v2 = by_rows(
        functools.partial(second_kernel, plan_b[:4], len(set_b)), order, [o1, x, enc], norms, set_b,
        [(width, f32)] + [(width, bf16)] * 4, False,
        [pltpu.VMEM((4, width, width), bf16), sems((4,))], 4 * square,
    )
    o2, log2 = attend_forward(q2, k2, v2, query_extra, enc_extra, cross_windows, False, hp=2, norm=True)
    out, a3, h, df, du, dr2, dc2, do2, terms_three = by_rows(
        functools.partial(third_kernel, plan_b[4:] + plan_c, len(set_b), len(set_c)), order, [o2, r1, cot], norms, set_b + set_c,
        [(width, bf16), (width, bf16), (hidden, bf16), (width, bf16), (hidden, bf16), (width, f32), (width, bf16), (width, bf16)], True,
        [
            pltpu.VMEM((width, width), bf16),
            pltpu.VMEM((parts, width, width), bf16),
            pltpu.VMEM((hidden, width), bf16),
            pltpu.VMEM((256, hidden), f32),
            sems((parts + 2,)),
        ],
        (2 + 4 * parts) * square,
    )

    grad_out = scatter_sum(weight_term(h, df))
    grad_in = scatter_sum(weight_term(a3, du))
    dq2, dk2, dv2 = attend_backward(q2, k2, v2, o2, do2, log2, enc_extra, cross_windows, False)
    dr1, dc1, do1, grad_enc, terms_two = by_rows(
        functools.partial(fourth_kernel, plan_b[:4], len(set_b)), order, [dq2, r1, dr2, dk2, dv2], norms, set_b,
        [(width, f32), (width, bf16), (width, bf16), (width, f32)], True,
        [pltpu.VMEM((4, width, width), bf16), sems((4,))], 4 * square,
    )
    lefts, rights = [o2, a2, enc, enc, o1], [dc2, dq2, dk2, dv2, dc1]
    if ring:
        mine, other = term_sets(rank, lefts, rights, (0, 1, 2, 2, 3), count)
        grad_b = ring_sum(mine, other, count)
        grad_co, grad_cq, grad_ck, grad_cv, grad_so = (grad_b[i * own : (i + 1) * own] for i in range(5))
    else:
        grad_co, grad_cq, grad_ck, grad_cv, grad_so = (scatter_sum(weight_term(a, b)) for a, b in zip(lefts, rights))
    dq1, dk1, dv1 = attend_backward(q1, k1, v1, o1, do1, log1, unit_extra, self_windows, True)
    lefts, rights = [a1, a1, a1], [dq1, dk1, dv1]
    if ring:
        mine, other = term_sets(rank, lefts, rights, (0, 0, 0), count)
        grad_a = ring_sum(mine, other, count)
        grad_sq, grad_sk, grad_sv = (grad_a[i * own : (i + 1) * own] for i in range(3))
    else:
        grad_sq, grad_sk, grad_sv = (scatter_sum(weight_term(a, b)) for a, b in zip(lefts, rights))
    grad_x, terms_one = by_rows(
        functools.partial(fifth_kernel, plan_a, len(set_a)), order, [dq1, dk1, dv1, x, dr1], norms, set_a,
        [(width, f32)], True,
        [pltpu.VMEM((3, width, width), bf16), sems((3,))], 3 * square,
    )
    norm_sum = total_sum(terms_one + terms_two + terms_three, count)
    norm_sum = lax.dynamic_slice_in_dim(norm_sum, lax.axis_index("shard") * own_width, own_width, 1)
    return (
        out.reshape(tokens.shape),
        grad_x.reshape(tokens.shape),
        grad_enc.reshape(enc_states.shape),
        grad_sq,
        grad_sk,
        grad_sv,
        grad_so,
        grad_cq,
        grad_ck,
        grad_cv,
        grad_co,
        grad_in,
        grad_out,
        norm_sum[:4],
        norm_sum[4:],
    )


def solution(mesh):
    return jax.shard_map(
        body,
        mesh=mesh,
        in_specs=(
            P(("rep", "shard"), None, None),
            P(("rep", "shard"), None, None),
            P(("rep", "shard"), None),
            P(("rep", "shard"), None),
            P("shard", None),
            P("shard", None),
            P("shard", None),
            P("shard", None),
            P("shard", None),
            P("shard", None),
            P("shard", None),
            P("shard", None),
            P("shard", None),
            P("shard", None),
            P(None, "shard"),
            P(None, "shard"),
            P(("rep", "shard"), None, None),
        ),
        out_specs=(
            P(("rep", "shard"), None, None),
            P(("rep", "shard"), None, None),
            P(("rep", "shard"), None, None),
            P("shard", None),
            P("shard", None),
            P("shard", None),
            P("shard", None),
            P("shard", None),
            P("shard", None),
            P("shard", None),
            P("shard", None),
            P("shard", None),
            P("shard", None),
            P(None, "shard"),
            P(None, "shard"),
        ),
        check_vma=False,
    )
```

time: 1110 us -> 722 us (0.65)
  matrix products: 249 us -> 29.9 us
  Pallas kernels: 132 us -> 298 us
  local copies, waits for them, and re-layouts: 187 us -> 23.1 us
  other arithmetic: 91.9 us -> 28.6 us
  starting transfers between devices: 132 us -> 84.4 us
  waiting for transfers between devices: 280 us -> 234 us
  between operations: 32.7 us -> 14.9 us
    dot_general x20 -> x1, matrix products: 189 us -> 0.12 us  [mm(): return jnp.dot(left, right, preferred_element_type=jnp.float32)]
    pallas_call x0 -> x7, Pallas kernels: none -> 170 us  [the longest x5 123 us: by_rows(): pl.pallas_call(kernel, grid_spec=pltpu.PrefetchScalarGridSpec(num_scalar_...]
    dynamic_update_slice x126 -> x0, local copies, waits for them, and re-layouts: 100 us -> none  [the longest x63 50.7 us: gather_rows(): lax.dynamic_update_slice_in_dim(whole, other, (2 * chip + 1 - core) * row...]
    ppermute x192 -> x55, starting transfers between devices: 132 us -> 84.3 us  [the longest x8 29.7 us: gather_pieces(): upward = lax.ppermute(upward, 'shard', up)]
    ppermute x192 -> x55, waiting for transfers between devices: 280 us -> 234 us  [the longest x6 72.7 us: gather_pieces(): downward = lax.ppermute(downward, 'shard', down)]
    reduce_sum x12 -> x0, other arithmetic: 32.3 us -> none  [the longest x7 23.8 us: layer_norm(): return centre * lax.rsqrt(spread + eps_norm) * gain_row + bias_row]
    dot_general x10 -> x2, matrix products: 59.7 us -> 29.8 us  [weight_term(): jnp.einsum('ra,rb->ab', left, right, preferred_element_type=jnp.float32)]
    convert_element_type x44 -> x10, other arithmetic: 37.4 us -> 21.7 us  [low(): return values_in.astype(jnp.bfloat16)]
  transfers between devices with their start and end apart: 192 -> 58, of which waited for: 93 -> 20; matrix products, arithmetic and copies ran while one was open for 27% -> 7% of each run, Pallas kernels for 4% -> 34%
where the time goes in v2:
time: 722 us; the launch traced here: 713 us
  Pallas kernels  298 us (41%)
  waiting for transfers between devices  234 us (32%)
  starting transfers between devices  84.4 us (12%)
  matrix products  29.9 us (4%)
  other arithmetic  28.6 us (4%)
  local copies, waits for them, and re-layouts  23.1 us (3%)
  between operations  14.9 us (2%)
    pallas_call x5, Pallas kernels, by_rows(): pl.pallas_call(kernel, grid_spec=pltpu.PrefetchScalarGridSpec(num_scalar_...  123 us
    pallas_call x2, Pallas kernels, attend_backward(): pl.pallas_call(functools.partial(attend_backward_kernel, bq, bk, causal),...  81.1 us
    ppermute x6, waiting for transfers between devices, gather_pieces(): downward = lax.ppermute(downward, 'shard', down)  72.7 us
    ppermute x8, waiting for transfers between devices, gather_pieces(): upward = lax.ppermute(upward, 'shard', up)  51.3 us
    ppermute x8, waiting for transfers between devices, ring_sum(): upward = lax.ppermute(upward, 'shard', up)  49.3 us
    pallas_call x2, Pallas kernels, attend_forward(): pl.pallas_call(functools.partial(attend_forward_kernel, bq, bk, causal, h...  47.2 us
    pallas_call x2, Pallas kernels, term_sets(): pl.pallas_call(functools.partial(term_kernel, pairs, chips), grid_spec=pl...  46.3 us
    ppermute x4, waiting for transfers between devices, over_rep(): partner = lax.ppermute(owned, 'rep', [(0, 1), (1, 0)])  30.9 us
  transfers between devices with their start and end apart: 58, of which 20 were waited for; matrix products, arithmetic and copies ran while one was open for 7% of the time, Pallas kernels for 34%

profile of v2, /device:TPU:0, one launch (start us, length us, event | category | flops | bytes accessed | tf_op | source)
XLA Modules:
  0.0 712.8 jit_solution(2491709754357116214)
XLA Ops:
  14.1 2.6 collective-permute-start.3
  16.9 1.6 collective-permute-start.18
  19.0 9.0 %collective-permute-done.3.rest_7_ = bf16[208,1024]{1,0:T(8,128)(2,1)S(1)} collective-permute-done((bf16[208,1024]{1,0:T(8,128)(2,1)S(1)}, bf16[208,1024]{1,0:T(8,128)(2,1)S(1)}, u32[]{:S(2)}, u32[]{:S(2)}) %collective-permute-start.3) | collective-permute-done | bytes 426016 | tf_op jit(solution)/shard_map/ppermute | solution.py:518
  28.0 2.5 collective-permute-start.4
  32.0 45.7 %collective-permute-done.rest_1_ = bf16[208,1024]{1,0:T(8,128)(2,1)S(1)} collective-permute-done((bf16[208,1024]{1,0:T(8,128)(2,1)S(1)}, bf16[208,1024]{1,0:T(8,128)(2,1)S(1)}, u32[]{:S(2)}, u32[]{:S(2)}) %collective-permute-start) | collective-permute-done | bytes 426016 | tf_op jit(solution)/shard_map/ppermute | solution.py:521
  77.8 2.0 collective-permute-start.19
  79.8 5.4 collective-permute-start.5
  86.9 3.0 collective-permute-done.1.rest_2_
  90.3 27.4 %collective-permute-done.5.rest_5_ = bf16[208,1024]{1,0:T(8,128)(2,1)S(1)} collective-permute-done((bf16[208,1024]{1,0:T(8,128)(2,1)S(1)}, bf16[208,1024]{1,0:T(8,128)(2,1)S(1)}, u32[]{:S(2)}, u32[]{:S(2)}) %collective-permute-start.5) | collective-permute-done | bytes 426016 | tf_op jit(solution)/shard_map/ppermute | solution.py:518
  117.7 12.7 %collective-permute-start.6 = (bf16[208,1024]{1,0:T(8,128)(2,1)S(1)}, bf16[208,1024]{1,0:T(8,128)(2,1)S(1)}, u32[]{:S(2)}, u32[]{:S(2)}) collective-permute-start(bf16[208,1024]{1,0:T(8,128)(2,1)S(1)} %collective-permute-done.5.rest_5_), channel_id=1, source_target_pairs={{0,4},{1,5},{4,8},{5,9},{8,12},{9,13},{12,14},{13,15},{14,10},{15,... | collective-permute-start | bytes 1277960 | tf_op jit(solution)/shard_map/ppermute | solution.py:518
  130.6 2.5 collective-permute-start.20
  134.8 14.9 %collective-permute-done.6.rest_4_ = bf16[208,1024]{1,0:T(8,128)(2,1)S(1)} collective-permute-done((bf16[208,1024]{1,0:T(8,128)(2,1)S(1)}, bf16[208,1024]{1,0:T(8,128)(2,1)S(1)}, u32[]{:S(2)}, u32[]{:S(2)}) %collective-permute-start.6) | collective-permute-done | bytes 426016 | tf_op jit(solution)/shard_map/ppermute | solution.py:518
  153.3 23.9 %collective-permute-done.16.rest_2_ = bf16[320,1024]{1,0:T(8,128)(2,1)} collective-permute-done((bf16[320,1024]{1,0:T(8,128)(2,1)}, bf16[320,1024]{1,0:T(8,128)(2,1)}, u32[]{:S(2)}, u32[]{:S(2)}) %collective-permute-start.16) | collective-permute-done | bytes 655392 | tf_op jit(solution)/shard_map/ppermute | solution.py:521
  177.2 21.8 %collective-permute-start.17 = (bf16[320,1024]{1,0:T(8,128)(2,1)}, bf16[320,1024]{1,0:T(8,128)(2,1)}, u32[]{:S(2)}, u32[]{:S(2)}) collective-permute-start(bf16[320,1024]{1,0:T(8,128)(2,1)} %collective-permute-done.16.rest_2_), channel_id=1, source_target_pairs={{4,0},{5,1},{8,4},{9,5},{12,8},{13,9},{14,12},{15,13},{10,14},{11,... | collective-permute-start | bytes 1966088 | tf_op jit(solution)/shard_map/ppermute | solution.py:521
  200.9 13.9 %shard_map.298 = (bf16[1024,1024]{1,0:T(8,128)(2,1)}, bf16[1024,1024]{1,0:T(8,128)(2,1)}, bf16[1024,1024]{1,0:T(8,128)(2,1)}, bf16[1024,1024]{1,0:T(8,128)(2,1)}) custom-call(s32[16]{0:T(128)} %copy-done.30, bf16[1024,1024]{1,0:T(8,128)(2,1)} %bitcast.136, f32[8,1024]{1,0:T(8,128)} %reshape.151.norm_ref, bf16[208,1024]{1,0:T(8,128)(2,1)} %copy-done.13, ...), custom_call_target="tpu_custom_call" | custom-call | flops 6442450944 | bytes 10485760 | tf_op jit(solution)/shard_map/pallas_call | solution.py:413
  216.1 22.2 %shard_map.299 = (bf16[1024,1024]{1,0:T(8,128)(2,1)}, bf16[1024,1024]{1,0:T(8,128)(2,1)}) custom-call(s32[8]{0:T(128)} %pad_add_fusion.1.win_ref, bf16[1024,1024]{1,0:T(8,128)(2,1)} %get-tuple-element.54.q_ref, bf16[1024,1024]{1,0:T(8,128)(2,1)} %get-tuple-element.55.k_ref, bf16[1024,1024]{1,0:T(8,128)(2,1)} %get-tuple-element.56.v_ref, ...), custom_call_target="tpu_custom_call" | custom-call | flops 17179869184 | bytes 10485760 | tf_op jit(solution)/shard_map/pallas_call | solution.py:121
  240.1 16.3 %shard_map.300 = (f32[1024,1024]{1,0:T(8,128)}, bf16[1024,1024]{1,0:T(8,128)(2,1)}, bf16[1024,1024]{1,0:T(8,128)(2,1)}, bf16[1024,1024]{1,0:T(8,128)(2,1)}, bf16[1024,1024]{1,0:T(8,128)(2,1)}) custom-call(s32[16]{0:T(128)} %copy-done.30, bf16[1024,1024]{1,0:T(8,128)(2,1)} %get-tuple-element.57.o_ref.rest_4_, bf16[1024,1024]{1,0:T(8,128)(2,1)} %bitcast.137, ...), custom_call_target="tpu_custom_call" | custom-call | flops 8589934592 | bytes 18874368 | tf_op jit(solution)/shard_map/pallas_call | solution.py:413
  256.4 25.0 %shard_map.301 = (bf16[1024,1024]{1,0:T(8,128)(2,1)}, bf16[1024,1024]{1,0:T(8,128)(2,1)}) custom-call(s32[8]{0:T(128)} %pad_add_fusion.win_ref, bf16[1024,1024]{1,0:T(8,128)(2,1)} %get-tuple-element.58.q_ref, bf16[1024,1024]{1,0:T(8,128)(2,1)} %get-tuple-element.59.k_ref, bf16[1024,1024]{1,0:T(8,128)(2,1)} %get-tuple-element.60.v_ref, ...), custom_call_target="tpu_custom_call" | custom-call | flops 17179869184 | bytes 10485760 | tf_op jit(solution)/shard_map/pallas_call | solution.py:121
  281.4 57.9 %shard_map.302 = (bf16[1024,1024]{1,0:T(8,128)(2,1)}, bf16[1024,1024]{1,0:T(8,128)(2,1)}, bf16[1024,4096]{1,0:T(8,128)(2,1)}, bf16[1024,1024]{1,0:T(8,128)(2,1)}...) custom-call(s32[16]{0:T(128)} %copy-done.30, ...), custom_call_target="tpu_custom_call" | custom-call | flops 38654705664 | bytes 39845888 | tf_op jit(solution)/shard_map/pallas_call | solution.py:413
  339.3 15.1 %convolution_convert_fusion.1 = bf16[1024,4096]{1,0:T(8,128)(2,1)} fusion(bf16[1024,1024]{1,0:T(8,128)(2,1)} %get-tuple-element.86, bf16[1024,4096]{1,0:T(8,128)(2,1)} %get-tuple-element.87), kind=kOutput, calls=%fused_computation.1 | convolution fusion | flops 8594128896 | bytes 18874368 | tf_op jit(solution)/shard_map/ra,rb->ab/dot_general | solution.py:566
  355.7 41.7 %shard_map.303 = (bf16[1024,1024]{1,0:T(8,128)(2,1)S(1)}, bf16[1024,1024]{1,0:T(8,128)(2,1)S(1)}, bf16[1024,1024]{1,0:T(8,128)(2,1)}) custom-call(s32[8]{0:T(128)S(1)} %copy-done.3, bf16[1024,1024]{1,0:T(8,128)(2,1)} %get-tuple-element.58.q_ref, bf16[1024,1024]{1,0:T(8,128)(2,1)} %get-tuple-element.59.k_ref, bf16[1024,1024]{1,0:T(8,128)(2,1)} %get-tuple-element.60.v_ref, ...), custom_call_target="tpu_custom_call" | custom-call | flops 42949672960 | bytes 16777216 | tf_op jit(solution)/shard_map/pallas_call | solution.py:199
  398.6 1.3 copy-done.7
  400.0 19.0 %shard_map.304 = (f32[1024,1024]{1,0:T(8,128)}, bf16[1024,1024]{1,0:T(8,128)(2,1)}, bf16[1024,1024]{1,0:T(8,128)(2,1)}, f32[1024,1024]{1,0:T(8,128)}, f32[8,1024]{1,0:T(8,128)}) custom-call(s32[16]{0:T(128)} %copy-done.30, bf16[1024,1024]{1,0:T(8,128)(2,1)} %copy-done.6, f32[1024,1024]{1,0:T(8,128)} %get-tuple-element.62.r_ref, ...), custom_call_target="tpu_custom_call" | custom-call | flops 8589934592 | bytes 27262976 | tf_op jit(solution)/shard_map/pallas_call | solution.py:413
  419.0 28.7 %shard_map.308 = (bf16[8,320,1024]{2,1,0:T(8,128)(2,1)}, bf16[8,320,1024]{2,1,0:T(8,128)(2,1)}) custom-call(s32[9]{0:T(128)} %fusion.25.rank_ref, bf16[1024,1024]{1,0:T(8,128)(2,1)} %get-tuple-element.61.o_ref.rest_0_, bf16[1024,1024]{1,0:T(8,128)(2,1)} %get-tuple-element.81.rest_1_, bf16[1024,1024]{1,0:T(8,128)(2,1)} %bitcast.134, ...), custom_call_target="tpu_custom_call" | custom-call | flops 10737418240 | bytes 31457280 | tf_op jit(solution)/shard_map/pallas_call | solution.py:467
  447.8 14.7 %convolution_convert_fusion = bf16[4096,1024]{1,0:T(8,128)(2,1)} fusion(bf16[1024,4096]{1,0:T(8,128)(2,1)} %get-tuple-element.88, bf16[1024,1024]{1,0:T(8,128)(2,1)S(1)} %copy-done.53), kind=kOutput, calls=%fused_computation | convolution fusion | flops 8594128896 | bytes 18874368 | tf_op jit(solution)/shard_map/ra,rb->ab/dot_general | solution.py:566
  463.4 39.4 %shard_map.305 = (bf16[1024,1024]{1,0:T(8,128)(2,1)S(1)}, bf16[1024,1024]{1,0:T(8,128)(2,1)S(1)}, bf16[1024,1024]{1,0:T(8,128)(2,1)}) custom-call(s32[8]{0:T(128)S(1)} %copy-done.2, bf16[1024,1024]{1,0:T(8,128)(2,1)} %get-tuple-element.54.q_ref, bf16[1024,1024]{1,0:T(8,128)(2,1)} %get-tuple-element.55.k_ref, bf16[1024,1024]{1,0:T(8,128)(2,1)} %get-tuple-element.56.v_ref, ...), custom_call_target="tpu_custom_call" | custom-call | flops 42949672960 | bytes 16777216 | tf_op jit(solution)/shard_map/pallas_call | solution.py:199
  502.8 1.3 copy-done.4
  505.4 17.6 %shard_map.307 = (bf16[8,192,1024]{2,1,0:T(8,128)(2,1)}, bf16[8,192,1024]{2,1,0:T(8,128)(2,1)}) custom-call(s32[9]{0:T(128)} %fusion.25.rank_ref, bf16[1024,1024]{1,0:T(8,128)(2,1)} %get-tuple-element.78.rest_0_.rest_1_.rest_2_, bf16[1024,1024]{1,0:T(8,128)(2,1)} %get-tuple-element.78.rest_0_.rest_1_.rest_2_, ...), custom_call_target="tpu_custom_call" | custom-call | flops 6442450944 | bytes 18874368 | tf_op jit(solution)/shard_map/pallas_call | solution.py:467
  523.5 5.5 collective-permute-done.30
  529.0 2.0 fusion.18
  531.0 2.3 collective-permute-start.31
  533.3 1.8 fusion.15
  535.2 2.0 collective-permute-start.35
  537.2 13.1 %collective-permute-done.31 = bf16[192,1024]{1,0:T(8,128)(2,1)S(1)} collective-permute-done((bf16[192,1024]{1,0:T(8,128)(2,1)S(1)}, bf16[192,1024]{1,0:T(8,128)(2,1)S(1)}, u32[]{:S(2)}, u32[]{:S(2)}) %collective-permute-start.31) | collective-permute-done | bytes 393248 | tf_op jit(solution)/shard_map/ppermute | solution.py:543
  551.6 2.0 collective-permute-start.44
  553.6 11.9 %collective-permute-done.40 = bf16[320,1024]{1,0:T(8,128)(2,1)S(1)} collective-permute-done((bf16[320,1024]{1,0:T(8,128)(2,1)S(1)}, bf16[320,1024]{1,0:T(8,128)(2,1)S(1)}, u32[]{:S(2)}, u32[]{:S(2)}) %collective-permute-start.40) | collective-permute-done | bytes 655392 | tf_op jit(solution)/shard_map/ppermute | solution.py:543
  565.5 1.4 fusion.4
  567.0 11.4 %collective-permute-done.32 = bf16[192,1024]{1,0:T(8,128)(2,1)S(1)} collective-permute-done((bf16[192,1024]{1,0:T(8,128)(2,1)S(1)}, bf16[192,1024]{1,0:T(8,128)(2,1)S(1)}, u32[]{:S(2)}, u32[]{:S(2)}) %collective-permute-start.32) | collective-permute-done | bytes 393248 | tf_op jit(solution)/shard_map/ppermute | solution.py:543
  578.4 2.5 fusion.11
  580.9 2.0 collective-permute-start.36
  582.9 12.9 %collective-permute-done.41 = bf16[320,1024]{1,0:T(8,128)(2,1)S(1)} collective-permute-done((bf16[320,1024]{1,0:T(8,128)(2,1)S(1)}, bf16[320,1024]{1,0:T(8,128)(2,1)S(1)}, u32[]{:S(2)}, u32[]{:S(2)}) %collective-permute-start.41) | collective-permute-done | bytes 655392 | tf_op jit(solution)/shard_map/ppermute | solution.py:543
  595.8 3.2 fusion.3
  599.0 2.5 collective-permute-start.42
  601.5 16.2 %shard_map.306 = (f32[1024,1024]{1,0:T(8,128)}, f32[8,1024]{1,0:T(8,128)}) custom-call(s32[16]{0:T(128)} %copy-done.30, bf16[1024,1024]{1,0:T(8,128)(2,1)} %copy-done.4, bf16[1024,1024]{1,0:T(8,128)(2,1)} %copy-done.5, bf16[1024,1024]{1,0:T(8,128)(2,1)} %get-tuple-element.74.dv_ref.rest_5_, bf16[1024,1024]{1,0:T(8,128)(2,1)} %bitcast.138, ...), custom_call_target="tpu_custom_call" | custom-call | flops 6442450944 | bytes 16777216 | tf_op jit(solution)/shard_map/pallas_call | solution.py:413
  617.7 3.0 fusion.10
  620.7 2.0 collective-permute-start.34
  623.6 3.4 fusion.2
  626.9 2.0 collective-permute-start.43
  630.3 2.0 collective-permute-start.51
  632.3 14.0 %collective-permute-done.51 = f32[8,1024]{1,0:T(8,128)S(1)} collective-permute-done((f32[8,1024]{1,0:T(8,128)S(1)}, f32[8,1024]{1,0:T(8,128)S(1)}, u32[]{:S(2)}, u32[]{:S(2)}) %collective-permute-start.51) | collective-permute-done | bytes 32800 | tf_op jit(solution)/shard_map/ppermute | solution.py:560
  646.3 3.9 collective-permute-done.52
  650.2 1.9 collective-permute-start.53
  652.0 2.9 collective-permute-done.53
  655.0 3.1 collective-permute-start.54
  658.1 2.2 collective-permute-done.54
  660.5 1.6 fusion.14
  662.1 2.1 collective-permute-start.38
  664.2 1.8 fusion.6
  666.6 7.6 %collective-permute-done.38 = bf16[192,1024]{1,0:T(8,128)(2,1)S(1)} collective-permute-done((bf16[192,1024]{1,0:T(8,128)(2,1)S(1)}, bf16[192,1024]{1,0:T(8,128)(2,1)S(1)}, u32[]{:S(2)}, u32[]{:S(2)}) %collective-permute-start.38) | collective-permute-done | bytes 393248 | tf_op jit(solution)/shard_map/ppermute | solution.py:531
  675.2 2.0 collective-permute-start.48
  677.2 11.0 %collective-permute-done.47 = bf16[320,1024]{1,0:T(8,128)(2,1)S(1)} collective-permute-done((bf16[320,1024]{1,0:T(8,128)(2,1)S(1)}, bf16[320,1024]{1,0:T(8,128)(2,1)S(1)}, u32[]{:S(2)}, u32[]{:S(2)}) %collective-permute-start.47) | collective-permute-done | bytes 655392 | tf_op jit(solution)/shard_map/ppermute | solution.py:531
  689.5 2.0 collective-permute-start.49
  691.6 7.8 %collective-permute-done.48 = bf16[64,4096]{1,0:T(8,128)(2,1)S(1)} collective-permute-done((bf16[64,4096]{1,0:T(8,128)(2,1)}, bf16[64,4096]{1,0:T(8,128)(2,1)S(1)}, u32[]{:S(2)}, u32[]{:S(2)}) %collective-permute-start.48) | collective-permute-done | bytes 524320 | tf_op jit(solution)/shard_map/ppermute | solution.py:531
  700.4 4.5 collective-permute-done.49
  (254 shorter events, 35.1 us)
Async XLA Ops:
  7.3 274.1 %all-gather.2.cloned.1.call-start = ((), (), s32[]{:S(2)}) async-start(), calls=%async_computation.2 | async-start | bytes 17825792 | tf_op jit(solution)/shard_map/all_gather | solution.py:608
  13.4 661.8 %reduce-scatter.3.cloned.1.call-start = ((), (), s32[]{:S(2)}) async-start(), calls=%async_computation.3 | async-start | bytes 8912896 | tf_op jit(solution)/shard_map/reduce_scatter | solution.py:554
  13.6 187.3 %copy-start.13 = (bf16[208,1024]{1,0:T(8,128)(2,1)}, bf16[208,1024]{1,0:T(8,128)(2,1)S(1)}, u32[]{:S(2)}) copy-start(bf16[208,1024]{1,0:T(8,128)(2,1)S(1)} %fusion.17.rest_0_) | copy-start | bytes 1277956
  13.6 18.1 %collective-permute-start.7 = (bf16[208,1024]{1,0:T(8,128)(2,1)S(1)}, bf16[208,1024]{1,0:T(8,128)(2,1)S(1)}, u32[]{:S(2)}, u32[]{:S(2)}) collective-permute-start(bf16[208,1024]{1,0:T(8,128)(2,1)S(1)} %fusion.17.rest_0_), channel_id=1, source_target_pairs={{0,1},{1,0},{2,3},{3,2},{4,5},{5,4},{6,7},{7,6},{8,9},{9,8},{10,11... | collective-permute-start | bytes 1277960 | tf_op jit(solution)/shard_map/ppermute | solution.py:523
  14.1 13.9 %collective-permute-start.3 = (bf16[208,1024]{1,0:T(8,128)(2,1)S(1)}, bf16[208,1024]{1,0:T(8,128)(2,1)S(1)}, u32[]{:S(2)}, u32[]{:S(2)}) collective-permute-start(bf16[208,1024]{1,0:T(8,128)(2,1)S(1)} %fusion.17.rest_0_), channel_id=1, source_target_pairs={{0,4},{1,5},{4,8},{5,9},{8,12},{9,13},{12,14},{13,15},{14,10},{15,... | collective-permute-start | bytes 1277960 | tf_op jit(solution)/shard_map/ppermute | solution.py:518
  16.9 198.0 %copy-start.26 = (bf16[320,1024]{1,0:T(8,128)(2,1)}, bf16[320,1024]{1,0:T(8,128)(2,1)S(1)}, u32[]{:S(2)}) copy-start(bf16[320,1024]{1,0:T(8,128)(2,1)S(1)} %constant_dynamic-update-slice_fusion.rest_0_) | copy-start | bytes 1966084
  16.9 60.8 %collective-permute-start.18 = (bf16[320,1024]{1,0:T(8,128)(2,1)S(1)}, bf16[320,1024]{1,0:T(8,128)(2,1)}, u32[]{:S(2)}, u32[]{:S(2)}) collective-permute-start(bf16[320,1024]{1,0:T(8,128)(2,1)S(1)} %constant_dynamic-update-slice_fusion.rest_0_), channel_id=1, source_target_pairs={{0,4},{1,5},{4,8},{5,9},{8,12},{9,13},{12,14},{13,15},{14,10},{15,... | collective-permute-start | bytes 1966088 | tf_op jit(solution)/shard_map/ppermute | solution.py:518
  18.5 59.3 %collective-permute-start.15 = (bf16[320,1024]{1,0:T(8,128)(2,1)S(1)}, bf16[320,1024]{1,0:T(8,128)(2,1)}, u32[]{:S(2)}, u32[]{:S(2)}) collective-permute-start(bf16[320,1024]{1,0:T(8,128)(2,1)S(1)} %constant_dynamic-update-slice_fusion.rest_0_), channel_id=1, source_target_pairs={{4,0},{5,1},{8,4},{9,5},{12,8},{13,9},{14,12},{15,13},{10,14},{11,... | collective-permute-start | bytes 1966088 | tf_op jit(solution)/shard_map/ppermute | solution.py:521
  19.0 58.7 %collective-permute-start = (bf16[208,1024]{1,0:T(8,128)(2,1)S(1)}, bf16[208,1024]{1,0:T(8,128)(2,1)S(1)}, u32[]{:S(2)}, u32[]{:S(2)}) collective-permute-start(bf16[208,1024]{1,0:T(8,128)(2,1)S(1)} %fusion.17.rest_0_), channel_id=1, source_target_pairs={{4,0},{5,1},{8,4},{9,5},{12,8},{13,9},{14,12},{15,13},{10,14},{11,... | collective-permute-start | bytes 1277960 | tf_op jit(solution)/shard_map/ppermute | solution.py:521
  28.0 172.9 %copy-start.32 = (bf16[208,1024]{1,0:T(8,128)(2,1)}, bf16[208,1024]{1,0:T(8,128)(2,1)S(1)}, u32[]{:S(2)}) copy-start(bf16[208,1024]{1,0:T(8,128)(2,1)S(1)} %collective-permute-done.3.rest_7_) | copy-start | bytes 1277956
  28.0 51.8 %collective-permute-start.4 = (bf16[208,1024]{1,0:T(8,128)(2,1)S(1)}, bf16[208,1024]{1,0:T(8,128)(2,1)S(1)}, u32[]{:S(2)}, u32[]{:S(2)}) collective-permute-start(bf16[208,1024]{1,0:T(8,128)(2,1)S(1)} %collective-permute-done.3.rest_7_), channel_id=1, source_target_pairs={{0,4},{1,5},{4,8},{5,9},{8,12},{9,13},{12,14},{13,15},{14,10},{15,... | collective-permute-start | bytes 1277960 | tf_op jit(solution)/shard_map/ppermute | solution.py:518
  31.7 169.2 %copy-start.31 = (bf16[208,1024]{1,0:T(8,128)(2,1)}, bf16[208,1024]{1,0:T(8,128)(2,1)S(1)}, u32[]{:S(2)}) copy-start(bf16[208,1024]{1,0:T(8,128)(2,1)S(1)} %collective-permute-done.7.rest_8_) | copy-start | bytes 1277956
  31.7 53.5 %collective-permute-start.14 = (bf16[208,1024]{1,0:T(8,128)(2,1)S(1)}, bf16[208,1024]{1,0:T(8,128)(2,1)S(1)}, u32[]{:S(2)}, u32[]{:S(2)}) collective-permute-start(bf16[208,1024]{1,0:T(8,128)(2,1)S(1)} %collective-permute-done.3.rest_7_), channel_id=1, source_target_pairs={{0,1},{1,0},{2,3},{3,2},{4,5},{5,4},{6,7},{7,6},{8,9},{9,8},{10,11... | collective-permute-start | bytes 1277960 | tf_op jit(solution)/shard_map/ppermute | solution.py:523
  77.7 123.1 %copy-start.33 = (bf16[208,1024]{1,0:T(8,128)(2,1)}, bf16[208,1024]{1,0:T(8,128)(2,1)S(1)}, u32[]{:S(2)}) copy-start(bf16[208,1024]{1,0:T(8,128)(2,1)S(1)} %collective-permute-done.rest_1_) | copy-start | bytes 1277956
  77.7 12.2 %collective-permute-start.8 = (bf16[208,1024]{1,0:T(8,128)(2,1)S(1)}, bf16[208,1024]{1,0:T(8,128)(2,1)S(1)}, u32[]{:S(2)}, u32[]{:S(2)}) collective-permute-start(bf16[208,1024]{1,0:T(8,128)(2,1)S(1)} %collective-permute-done.rest_1_), channel_id=1, source_target_pairs={{0,1},{1,0},{2,3},{3,2},{4,5},{5,4},{6,7},{7,6},{8,9},{9,8},{10,11... | collective-permute-start | bytes 1277960 | tf_op jit(solution)/shard_map/ppermute | solution.py:523
  77.7 12.2 %collective-permute-start.1 = (bf16[208,1024]{1,0:T(8,128)(2,1)S(1)}, bf16[208,1024]{1,0:T(8,128)(2,1)S(1)}, u32[]{:S(2)}, u32[]{:S(2)}) collective-permute-start(bf16[208,1024]{1,0:T(8,128)(2,1)S(1)} %collective-permute-done.rest_1_), channel_id=1, source_target_pairs={{4,0},{5,1},{8,4},{9,5},{12,8},{13,9},{14,12},{15,13},{10,14},{11,... | collective-permute-start | bytes 1277960 | tf_op jit(solution)/shard_map/ppermute | solution.py:521
  77.8 52.7 %collective-permute-start.19 = (bf16[320,1024]{1,0:T(8,128)(2,1)}, bf16[320,1024]{1,0:T(8,128)(2,1)S(1)}, u32[]{:S(2)}, u32[]{:S(2)}) collective-permute-start(bf16[320,1024]{1,0:T(8,128)(2,1)} %collective-permute-done.18.rest_7_), channel_id=1, source_target_pairs={{0,4},{1,5},{4,8},{5,9},{8,12},{9,13},{12,14},{13,15},{14,10},{15,... | collective-permute-start | bytes 1966088 | tf_op jit(solution)/shard_map/ppermute | solution.py:518
  79.8 121.1 %copy-start.34 = (bf16[208,1024]{1,0:T(8,128)(2,1)}, bf16[208,1024]{1,0:T(8,128)(2,1)S(1)}, u32[]{:S(2)}) copy-start(bf16[208,1024]{1,0:T(8,128)(2,1)S(1)} %collective-permute-done.4.rest_6_) | copy-start | bytes 1277956
  79.8 37.9 %collective-permute-start.5 = (bf16[208,1024]{1,0:T(8,128)(2,1)S(1)}, bf16[208,1024]{1,0:T(8,128)(2,1)S(1)}, u32[]{:S(2)}, u32[]{:S(2)}) collective-permute-start(bf16[208,1024]{1,0:T(8,128)(2,1)S(1)} %collective-permute-done.4.rest_6_), channel_id=1, source_target_pairs={{0,4},{1,5},{4,8},{5,9},{8,12},{9,13},{12,14},{13,15},{14,10},{15,... | collective-permute-start | bytes 1277960 | tf_op jit(solution)/shard_map/ppermute | solution.py:518
  86.0 44.5 %collective-permute-start.13 = (bf16[208,1024]{1,0:T(8,128)(2,1)S(1)}, bf16[208,1024]{1,0:T(8,128)(2,1)S(1)}, u32[]{:S(2)}, u32[]{:S(2)}) collective-permute-start(bf16[208,1024]{1,0:T(8,128)(2,1)S(1)} %collective-permute-done.4.rest_6_), channel_id=1, source_target_pairs={{0,1},{1,0},{2,3},{3,2},{4,5},{5,4},{6,7},{7,6},{8,9},{9,8},{10,11... | collective-permute-start | bytes 1277960 | tf_op jit(solution)/shard_map/ppermute | solution.py:523
  90.0 44.3 %collective-permute-start.9 = (bf16[208,1024]{1,0:T(8,128)(2,1)S(1)}, bf16[208,1024]{1,0:T(8,128)(2,1)S(1)}, u32[]{:S(2)}, u32[]{:S(2)}) collective-permute-start(bf16[208,1024]{1,0:T(8,128)(2,1)S(1)} %collective-permute-done.1.rest_2_), channel_id=1, source_target_pairs={{0,1},{1,0},{2,3},{3,2},{4,5},{5,4},{6,7},{7,6},{8,9},{9,8},{10,11... | collective-permute-start | bytes 1277960 | tf_op jit(solution)/shard_map/ppermute | solution.py:523
  90.0 44.3 %collective-permute-start.2 = (bf16[208,1024]{1,0:T(8,128)(2,1)S(1)}, bf16[208,1024]{1,0:T(8,128)(2,1)S(1)}, u32[]{:S(2)}, u32[]{:S(2)}) collective-permute-start(bf16[208,1024]{1,0:T(8,128)(2,1)S(1)} %collective-permute-done.1.rest_2_), channel_id=1, source_target_pairs={{4,0},{5,1},{8,4},{9,5},{12,8},{13,9},{14,12},{15,13},{10,14},{11,... | collective-permute-start | bytes 1277960 | tf_op jit(solution)/shard_map/ppermute | solution.py:521
  117.7 32.0 %collective-permute-start.6 = (bf16[208,1024]{1,0:T(8,128)(2,1)S(1)}, bf16[208,1024]{1,0:T(8,128)(2,1)S(1)}, u32[]{:S(2)}, u32[]{:S(2)}) collective-permute-start(bf16[208,1024]{1,0:T(8,128)(2,1)S(1)} %collective-permute-done.5.rest_5_), channel_id=1, source_target_pairs={{0,4},{1,5},{4,8},{5,9},{8,12},{9,13},{12,14},{13,15},{14,10},{15,... | collective-permute-start | bytes 1277960 | tf_op jit(solution)/shard_map/ppermute | solution.py:518
  130.5 46.8 %collective-permute-start.16 = (bf16[320,1024]{1,0:T(8,128)(2,1)}, bf16[320,1024]{1,0:T(8,128)(2,1)}, u32[]{:S(2)}, u32[]{:S(2)}) collective-permute-start(bf16[320,1024]{1,0:T(8,128)(2,1)} %collective-permute-done.15.rest_1_), channel_id=1, source_target_pairs={{4,0},{5,1},{8,4},{9,5},{12,8},{13,9},{14,12},{15,13},{10,14},{11,... | collective-permute-start | bytes 1966088 | tf_op jit(solution)/shard_map/ppermute | solution.py:521
  130.6 46.7 %collective-permute-start.20 = (bf16[320,1024]{1,0:T(8,128)(2,1)S(1)}, bf16[320,1024]{1,0:T(8,128)(2,1)}, u32[]{:S(2)}, u32[]{:S(2)}) collective-permute-start(bf16[320,1024]{1,0:T(8,128)(2,1)S(1)} %collective-permute-done.19.rest_6_), channel_id=1, source_target_pairs={{0,4},{1,5},{4,8},{5,9},{8,12},{9,13},{12,14},{13,15},{14,10},{15,... | collective-permute-start | bytes 1966088 | tf_op jit(solution)/shard_map/ppermute | solution.py:518
  134.3 18.3 %collective-permute-start.12 = (bf16[208,1024]{1,0:T(8,128)(2,1)S(1)}, bf16[208,1024]{1,0:T(8,128)(2,1)S(1)}, u32[]{:S(2)}, u32[]{:S(2)}) collective-permute-start(bf16[208,1024]{1,0:T(8,128)(2,1)S(1)} %collective-permute-done.5.rest_5_), channel_id=1, source_target_pairs={{0,1},{1,0},{2,3},{3,2},{4,5},{5,4},{6,7},{7,6},{8,9},{9,8},{10,11... | collective-permute-start | bytes 1277960 | tf_op jit(solution)/shard_map/ppermute | solution.py:523
  134.3 18.9 %collective-permute-start.10 = (bf16[208,1024]{1,0:T(8,128)(2,1)S(1)}, bf16[208,1024]{1,0:T(8,128)(2,1)S(1)}, u32[]{:S(2)}, u32[]{:S(2)}) collective-permute-start(bf16[208,1024]{1,0:T(8,128)(2,1)S(1)} %collective-permute-done.2.rest_3_), channel_id=1, source_target_pairs={{0,1},{1,0},{2,3},{3,2},{4,5},{5,4},{6,7},{7,6},{8,9},{9,8},{10,11... | collective-permute-start | bytes 1277960 | tf_op jit(solution)/shard_map/ppermute | solution.py:523
  149.7 49.4 %collective-permute-start.11 = (bf16[208,1024]{1,0:T(8,128)(2,1)S(1)}, bf16[208,1024]{1,0:T(8,128)(2,1)S(1)}, u32[]{:S(2)}, u32[]{:S(2)}) collective-permute-start(bf16[208,1024]{1,0:T(8,128)(2,1)S(1)} %collective-permute-done.6.rest_4_), channel_id=1, source_target_pairs={{0,1},{1,0},{2,3},{3,2},{4,5},{5,4},{6,7},{7,6},{8,9},{9,8},{10,11... | collective-permute-start | bytes 1277960 | tf_op jit(solution)/shard_map/ppermute | solution.py:523
  152.6 62.3 %collective-permute-start.22 = (bf16[320,1024]{1,0:T(8,128)(2,1)S(1)}, bf16[320,1024]{1,0:T(8,128)(2,1)}, u32[]{:S(2)}, u32[]{:S(2)}) collective-permute-start(bf16[320,1024]{1,0:T(8,128)(2,1)S(1)} %constant_dynamic-update-slice_fusion.rest_0_), channel_id=1, source_target_pairs={{0,1},{1,0},{2,3},{3,2},{4,5},{5,4},{6,7},{7,6},{8,9},{9,8},{10,11... | collective-permute-start | bytes 1966088 | tf_op jit(solution)/shard_map/ppermute | solution.py:523
  153.2 61.8 %collective-permute-start.29 = (bf16[320,1024]{1,0:T(8,128)(2,1)}, bf16[320,1024]{1,0:T(8,128)(2,1)}, u32[]{:S(2)}, u32[]{:S(2)}) collective-permute-start(bf16[320,1024]{1,0:T(8,128)(2,1)} %collective-permute-done.18.rest_7_), channel_id=1, source_target_pairs={{0,1},{1,0},{2,3},{3,2},{4,5},{5,4},{6,7},{7,6},{8,9},{9,8},{10,11... | collective-permute-start | bytes 1966088 | tf_op jit(solution)/shard_map/ppermute | solution.py:523
  177.2 38.2 %collective-permute-start.23 = (bf16[320,1024]{1,0:T(8,128)(2,1)}, bf16[320,1024]{1,0:T(8,128)(2,1)}, u32[]{:S(2)}, u32[]{:S(2)}) collective-permute-start(bf16[320,1024]{1,0:T(8,128)(2,1)} %collective-permute-done.15.rest_1_), channel_id=1, source_target_pairs={{0,1},{1,0},{2,3},{3,2},{4,5},{5,4},{6,7},{7,6},{8,9},{9,8},{10,11... | collective-permute-start | bytes 1966088 | tf_op jit(solution)/shard_map/ppermute | solution.py:523
  177.2 38.3 %collective-permute-start.17 = (bf16[320,1024]{1,0:T(8,128)(2,1)}, bf16[320,1024]{1,0:T(8,128)(2,1)}, u32[]{:S(2)}, u32[]{:S(2)}) collective-permute-start(bf16[320,1024]{1,0:T(8,128)(2,1)} %collective-permute-done.16.rest_2_), channel_id=1, source_target_pairs={{4,0},{5,1},{8,4},{9,5},{12,8},{13,9},{14,12},{15,13},{10,14},{11,... | collective-permute-start | bytes 1966088 | tf_op jit(solution)/shard_map/ppermute | solution.py:521
  199.1 16.9 %collective-permute-start.21 = (bf16[320,1024]{1,0:T(8,128)(2,1)}, bf16[320,1024]{1,0:T(8,128)(2,1)}, u32[]{:S(2)}, u32[]{:S(2)}) collective-permute-start(bf16[320,1024]{1,0:T(8,128)(2,1)} %collective-permute-done.20.rest_5_), channel_id=1, source_target_pairs={{0,4},{1,5},{4,8},{5,9},{8,12},{9,13},{12,14},{13,15},{14,10},{15,... | collective-permute-start | bytes 1966088 | tf_op jit(solution)/shard_map/ppermute | solution.py:518
  214.9 23.4 %collective-permute-start.28 = (bf16[320,1024]{1,0:T(8,128)(2,1)S(1)}, bf16[320,1024]{1,0:T(8,128)(2,1)S(1)}, u32[]{:S(2)}, u32[]{:S(2)}) collective-permute-start(bf16[320,1024]{1,0:T(8,128)(2,1)S(1)} %copy-done.47), channel_id=1, source_target_pairs={{0,1},{1,0},{2,3},{3,2},{4,5},{5,4},{6,7},{7,6},{8,9},{9,8},{10,11... | collective-permute-start | bytes 1966088 | tf_op jit(solution)/shard_map/ppermute | solution.py:523
  215.0 23.3 %collective-permute-start.24 = (bf16[320,1024]{1,0:T(8,128)(2,1)}, bf16[320,1024]{1,0:T(8,128)(2,1)S(1)}, u32[]{:S(2)}, u32[]{:S(2)}) collective-permute-start(bf16[320,1024]{1,0:T(8,128)(2,1)} %collective-permute-done.16.rest_2_), channel_id=1, source_target_pairs={{0,1},{1,0},{2,3},{3,2},{4,5},{5,4},{6,7},{7,6},{8,9},{9,8},{10,11... | collective-permute-start | bytes 1966088 | tf_op jit(solution)/shard_map/ppermute | solution.py:523
  215.5 22.8 %collective-permute-start.27 = (bf16[320,1024]{1,0:T(8,128)(2,1)}, bf16[320,1024]{1,0:T(8,128)(2,1)S(1)}, u32[]{:S(2)}, u32[]{:S(2)}) collective-permute-start(bf16[320,1024]{1,0:T(8,128)(2,1)} %collective-permute-done.20.rest_5_), channel_id=1, source_target_pairs={{0,1},{1,0},{2,3},{3,2},{4,5},{5,4},{6,7},{7,6},{8,9},{9,8},{10,11... | collective-permute-start | bytes 1966088 | tf_op jit(solution)/shard_map/ppermute | solution.py:523
  215.5 22.8 %collective-permute-start.25 = (bf16[320,1024]{1,0:T(8,128)(2,1)}, bf16[320,1024]{1,0:T(8,128)(2,1)S(1)}, u32[]{:S(2)}, u32[]{:S(2)}) collective-permute-start(bf16[320,1024]{1,0:T(8,128)(2,1)} %collective-permute-done.17.rest_3_), channel_id=1, source_target_pairs={{0,1},{1,0},{2,3},{3,2},{4,5},{5,4},{6,7},{7,6},{8,9},{9,8},{10,11... | collective-permute-start | bytes 1966088 | tf_op jit(solution)/shard_map/ppermute | solution.py:523
  216.0 22.4 %collective-permute-start.26 = (bf16[320,1024]{1,0:T(8,128)(2,1)}, bf16[320,1024]{1,0:T(8,128)(2,1)S(1)}, u32[]{:S(2)}, u32[]{:S(2)}) collective-permute-start(bf16[320,1024]{1,0:T(8,128)(2,1)} %collective-permute-done.21.rest_4_), channel_id=1, source_target_pairs={{0,1},{1,0},{2,3},{3,2},{4,5},{5,4},{6,7},{7,6},{8,9},{9,8},{10,11... | collective-permute-start | bytes 1966088 | tf_op jit(solution)/shard_map/ppermute | solution.py:523
  354.4 335.2 %reduce-scatter.5.cloned.1.call-start = ((), (), s32[]{:S(2)}) async-start(), calls=%async_computation.4 | async-start | bytes 8912896 | tf_op jit(solution)/shard_map/reduce_scatter | solution.py:554
  447.8 85.6 %collective-permute-start.39 = (bf16[8,320,1024]{2,1,0:T(8,128)(2,1)}, bf16[8,320,1024]{2,1,0:T(8,128)(2,1)}, u32[]{:S(2)}, u32[]{:S(2)}) collective-permute-start(bf16[8,320,1024]{2,1,0:T(8,128)(2,1)} %get-tuple-element.85), channel_id=1, source_target_pairs={{0,1},{1,0},{2,3},{3,2},{4,5},{5,4},{6,7},{7,6},{8,9},{9,8},{10,11... | collective-permute-start | bytes 15728648 | tf_op jit(solution)/shard_map/ppermute | solution.py:539
  523.0 6.0 collective-permute-start.30
  531.0 19.3 %collective-permute-start.31 = (bf16[192,1024]{1,0:T(8,128)(2,1)S(1)}, bf16[192,1024]{1,0:T(8,128)(2,1)S(1)}, u32[]{:S(2)}, u32[]{:S(2)}) collective-permute-start(bf16[192,1024]{1,0:T(8,128)(2,1)S(1)} %get-tuple-element.110), channel_id=1, source_target_pairs={{0,4},{1,5},{4,8},{5,9},{8,12},{9,13},{12,14},{13,15},{14,10},{15,... | collective-permute-start | bytes 1179656 | tf_op jit(solution)/shard_map/ppermute | solution.py:543
  535.2 30.4 %collective-permute-start.40 = (bf16[320,1024]{1,0:T(8,128)(2,1)S(1)}, bf16[320,1024]{1,0:T(8,128)(2,1)S(1)}, u32[]{:S(2)}, u32[]{:S(2)}) collective-permute-start(bf16[320,1024]{1,0:T(8,128)(2,1)S(1)} %get-tuple-element.104), channel_id=1, source_target_pairs={{0,4},{1,5},{4,8},{5,9},{8,12},{9,13},{12,14},{13,15},{14,10},{15,... | collective-permute-start | bytes 1966088 | tf_op jit(solution)/shard_map/ppermute | solution.py:543
  535.2 31.8 %collective-permute-start.35 = (bf16[192,1024]{1,0:T(8,128)(2,1)S(1)}, bf16[192,1024]{1,0:T(8,128)(2,1)S(1)}, u32[]{:S(2)}, u32[]{:S(2)}) collective-permute-start(bf16[192,1024]{1,0:T(8,128)(2,1)S(1)} %get-tuple-element.111), channel_id=1, source_target_pairs={{4,0},{5,1},{8,4},{9,5},{12,8},{13,9},{14,12},{15,13},{10,14},{11,... | collective-permute-start | bytes 1179656 | tf_op jit(solution)/shard_map/ppermute | solution.py:547
  551.5 26.9 %collective-permute-start.32 = (bf16[192,1024]{1,0:T(8,128)(2,1)S(1)}, bf16[192,1024]{1,0:T(8,128)(2,1)S(1)}, u32[]{:S(2)}, u32[]{:S(2)}) collective-permute-start(bf16[192,1024]{1,0:T(8,128)(2,1)S(1)} %fusion.12), channel_id=1, source_target_pairs={{0,4},{1,5},{4,8},{5,9},{8,12},{9,13},{12,14},{13,15},{14,10},{15,... | collective-permute-start | bytes 1179656 | tf_op jit(solution)/shard_map/ppermute | solution.py:543
  551.6 31.3 %collective-permute-start.44 = (bf16[320,1024]{1,0:T(8,128)(2,1)S(1)}, bf16[320,1024]{1,0:T(8,128)(2,1)S(1)}, u32[]{:S(2)}, u32[]{:S(2)}) collective-permute-start(bf16[320,1024]{1,0:T(8,128)(2,1)S(1)} %get-tuple-element.105), channel_id=1, source_target_pairs={{4,0},{5,1},{8,4},{9,5},{12,8},{13,9},{14,12},{15,13},{10,14},{11,... | collective-permute-start | bytes 1966088 | tf_op jit(solution)/shard_map/ppermute | solution.py:547
  566.9 28.9 %collective-permute-start.41 = (bf16[320,1024]{1,0:T(8,128)(2,1)S(1)}, bf16[320,1024]{1,0:T(8,128)(2,1)S(1)}, u32[]{:S(2)}, u32[]{:S(2)}) collective-permute-start(bf16[320,1024]{1,0:T(8,128)(2,1)S(1)} %fusion.4), channel_id=1, source_target_pairs={{0,4},{1,5},{4,8},{5,9},{8,12},{9,13},{12,14},{13,15},{14,10},{15,... | collective-permute-start | bytes 1966088 | tf_op jit(solution)/shard_map/ppermute | solution.py:543
  580.9 36.8 %collective-permute-start.33 = (bf16[192,1024]{1,0:T(8,128)(2,1)}, bf16[192,1024]{1,0:T(8,128)(2,1)}, u32[]{:S(2)}, u32[]{:S(2)}) collective-permute-start(bf16[192,1024]{1,0:T(8,128)(2,1)} %get-tuple-element.108), channel_id=1, source_target_pairs={{0,4},{1,5},{4,8},{5,9},{8,12},{9,13},{12,14},{13,15},{14,10},{15,... | collective-permute-start | bytes 1179656 | tf_op jit(solution)/shard_map/ppermute | solution.py:543
  580.9 36.8 %collective-permute-start.36 = (bf16[192,1024]{1,0:T(8,128)(2,1)}, bf16[192,1024]{1,0:T(8,128)(2,1)}, u32[]{:S(2)}, u32[]{:S(2)}) collective-permute-start(bf16[192,1024]{1,0:T(8,128)(2,1)} %get-tuple-element.109), channel_id=1, source_target_pairs={{4,0},{5,1},{8,4},{9,5},{12,8},{13,9},{14,12},{15,13},{10,14},{11,... | collective-permute-start | bytes 1179656 | tf_op jit(solution)/shard_map/ppermute | solution.py:547
  599.0 23.7 %collective-permute-start.42 = (bf16[320,1024]{1,0:T(8,128)(2,1)}, bf16[320,1024]{1,0:T(8,128)(2,1)S(1)}, u32[]{:S(2)}, u32[]{:S(2)}) collective-permute-start(bf16[320,1024]{1,0:T(8,128)(2,1)} %get-tuple-element.102), channel_id=1, source_target_pairs={{0,4},{1,5},{4,8},{5,9},{8,12},{9,13},{12,14},{13,15},{14,10},{15,... | collective-permute-start | bytes 1966088 | tf_op jit(solution)/shard_map/ppermute | solution.py:543
  601.5 22.1 %collective-permute-start.45 = (bf16[320,1024]{1,0:T(8,128)(2,1)}, bf16[320,1024]{1,0:T(8,128)(2,1)}, u32[]{:S(2)}, u32[]{:S(2)}) collective-permute-start(bf16[320,1024]{1,0:T(8,128)(2,1)} %get-tuple-element.103), channel_id=1, source_target_pairs={{4,0},{5,1},{8,4},{9,5},{12,8},{13,9},{14,12},{15,13},{10,14},{11,... | collective-permute-start | bytes 1966088 | tf_op jit(solution)/shard_map/ppermute | solution.py:547
  620.7 39.8 %collective-permute-start.34 = (bf16[192,1024]{1,0:T(8,128)(2,1)}, bf16[192,1024]{1,0:T(8,128)(2,1)}, u32[]{:S(2)}, u32[]{:S(2)}) collective-permute-start(bf16[192,1024]{1,0:T(8,128)(2,1)} %get-tuple-element.106), channel_id=1, source_target_pairs={{0,4},{1,5},{4,8},{5,9},{8,12},{9,13},{12,14},{13,15},{14,10},{15,... | collective-permute-start | bytes 1179656 | tf_op jit(solution)/shard_map/ppermute | solution.py:543
  622.7 37.8 %collective-permute-start.37 = (bf16[192,1024]{1,0:T(8,128)(2,1)}, bf16[192,1024]{1,0:T(8,128)(2,1)}, u32[]{:S(2)}, u32[]{:S(2)}) collective-permute-start(bf16[192,1024]{1,0:T(8,128)(2,1)} %get-tuple-element.107), channel_id=1, source_target_pairs={{4,0},{5,1},{8,4},{9,5},{12,8},{13,9},{14,12},{15,13},{10,14},{11,... | collective-permute-start | bytes 1179656 | tf_op jit(solution)/shard_map/ppermute | solution.py:547
  626.9 37.2 %collective-permute-start.43 = (bf16[320,1024]{1,0:T(8,128)(2,1)}, bf16[320,1024]{1,0:T(8,128)(2,1)S(1)}, u32[]{:S(2)}, u32[]{:S(2)}) collective-permute-start(bf16[320,1024]{1,0:T(8,128)(2,1)} %get-tuple-element.100), channel_id=1, source_target_pairs={{0,4},{1,5},{4,8},{5,9},{8,12},{9,13},{12,14},{13,15},{14,10},{15,... | collective-permute-start | bytes 1966088 | tf_op jit(solution)/shard_map/ppermute | solution.py:543
  628.9 35.2 %collective-permute-start.46 = (bf16[320,1024]{1,0:T(8,128)(2,1)S(1)}, bf16[320,1024]{1,0:T(8,128)(2,1)S(1)}, u32[]{:S(2)}, u32[]{:S(2)}) collective-permute-start(bf16[320,1024]{1,0:T(8,128)(2,1)S(1)} %get-tuple-element.101), channel_id=1, source_target_pairs={{4,0},{5,1},{8,4},{9,5},{12,8},{13,9},{14,12},{15,13},{10,14},{11,... | collective-permute-start | bytes 1966088 | tf_op jit(solution)/shard_map/ppermute | solution.py:547
  629.0 1.3 collective-permute-start.50
  630.3 16.0 %collective-permute-start.51 = (f32[8,1024]{1,0:T(8,128)S(1)}, f32[8,1024]{1,0:T(8,128)S(1)}, u32[]{:S(2)}, u32[]{:S(2)}) collective-permute-start(f32[8,1024]{1,0:T(8,128)S(1)} %add.238), channel_id=1, source_target_pairs={{0,2},{1,3},{2,0},{3,1},{4,6},{5,7},{6,4},{7,5},{8,10},{9,11},{10,... | collective-permute-start | bytes 98312 | tf_op jit(solution)/shard_map/ppermute | solution.py:560
  646.2 3.9 collective-permute-start.52
  650.2 4.8 collective-permute-start.53
  655.0 5.4 collective-permute-start.54
  662.1 12.1 %collective-permute-start.38 = (bf16[192,1024]{1,0:T(8,128)(2,1)S(1)}, bf16[192,1024]{1,0:T(8,128)(2,1)S(1)}, u32[]{:S(2)}, u32[]{:S(2)}) collective-permute-start(bf16[192,1024]{1,0:T(8,128)(2,1)S(1)} %fusion.14), channel_id=1, source_target_pairs={{0,16},{16,0},{1,17},{17,1},{2,18},{18,2},{3,19},{19,3},{4,20},{20... | collective-permute-start | bytes 1179656 | tf_op jit(solution)/shard_map/ppermute | solution.py:531
  665.9 22.3 %collective-permute-start.47 = (bf16[320,1024]{1,0:T(8,128)(2,1)S(1)}, bf16[320,1024]{1,0:T(8,128)(2,1)S(1)}, u32[]{:S(2)}, u32[]{:S(2)}) collective-permute-start(bf16[320,1024]{1,0:T(8,128)(2,1)S(1)} %fusion.6), channel_id=1, source_target_pairs={{0,16},{16,0},{1,17},{17,1},{2,18},{18,2},{3,19},{19,3},{4,20},{20... | collective-permute-start | bytes 1966088 | tf_op jit(solution)/shard_map/ppermute | solution.py:531
  675.2 24.1 %collective-permute-start.48 = (bf16[64,4096]{1,0:T(8,128)(2,1)}, bf16[64,4096]{1,0:T(8,128)(2,1)S(1)}, u32[]{:S(2)}, u32[]{:S(2)}) collective-permute-start(bf16[64,4096]{1,0:T(8,128)(2,1)} %reduce-scatter.3.cloned.1.call-done), channel_id=1, source_target_pairs={{0,16},{16,0},{1,17},{17,1},{2,18},{18,2},{3,19},{19,3},{4,20},{20... | collective-permute-start | bytes 1572872 | tf_op jit(solution)/shard_map/ppermute | solution.py:531
  689.5 15.4 %collective-permute-start.49 = (bf16[256,1024]{1,0:T(8,128)(2,1)}, bf16[256,1024]{1,0:T(8,128)(2,1)S(1)}, u32[]{:S(2)}, u32[]{:S(2)}) collective-permute-start(bf16[256,1024]{1,0:T(8,128)(2,1)} %reduce-scatter.5.cloned.1.call-done), channel_id=1, source_target_pairs={{0,16},{16,0},{1,17},{17,1},{2,18},{18,2},{3,19},{19,3},{4,20},{20... | collective-permute-start | bytes 1572872 | tf_op jit(solution)/shard_map/ppermute | solution.py:531
  (50 other events, 1219.7 us)
Sparse Core Ops, SparseCore 0:
  13.5 183.9 all-gather.1
  354.5 106.6 reduce-scatter.2
  465.3 130.2 reduce-scatter.4

commit v3 on v2

--- a/solution.py
+++ b/solution.py
@@ -16,6 +16,10 @@
 
 
 COST = 4
+
+
+def estimate(flops, bytes_accessed, transcendentals):
+    return pl.CostEstimate(flops=flops // 8, bytes_accessed=bytes_accessed // 8, transcendentals=0)
 BIG = 1e30
 NT = (((1,), (1,)), ((), ()))
 TN = (((0,), (0,)), ((), ()))
@@ -48,7 +52,8 @@
     return jnp.concatenate([start, count])
 
 
-def attend_forward_kernel(bq, bk, causal, hp, norm, win_ref, q_ref, k_ref, v_ref, qx_ref, kx_ref, o_ref, qe_ref, ka):
+def attend_forward_kernel(bq, bk, causal, hp, norm, win_ref, q_ref, k_ref, v_ref, qx_ref, kx_ref, *rest):
+    o_ref, qe_ref, ka = rest[-3:]
     L, N = q_ref.shape[0], k_ref.shape[0]
     nq = L // bq
     lane = lax.broadcasted_iota(jnp.int32, (1, 128), 1)
@@ -112,26 +117,32 @@
 
     lax.fori_loop(0, nq, step, 0)
 
-def attend_forward(q, k, v, qx, kx, win, causal, bq=256, bk=256, hp=1, norm=False):
-    L, D = q.shape
-    N = k.shape[0]
-    w = 128*hp
-    col = lambda n: pl.BlockSpec((n, w), lambda p, _: (0, p))
+def attend_forward(q, k, v, qx, kx, win, causal, pairs, after=(), bq=256, bk=256, hp=2):
+    L, N = q.shape[0], k.shape[0]
+    w = 128 * hp
+    start, number = pairs[0] // hp, (pairs[1] - pairs[0]) // hp
+    col = lambda n: pl.BlockSpec((n, w), lambda p, _: (0, start + p))
+    own = lambda n: pl.BlockSpec((n, w), lambda p, _: (0, p))
     fix = lambda n: pl.BlockSpec((n, 128), lambda p, _: (0, 0))
     return pl.pallas_call(
-        functools.partial(attend_forward_kernel, bq, bk, causal, hp, norm),
+        functools.partial(attend_forward_kernel, bq, bk, causal, hp, True),
         grid_spec=pltpu.PrefetchScalarGridSpec(
-            num_scalar_prefetch=1, grid=(D // w,),
-            in_specs=[col(L), col(N), col(N), fix(L), fix(N)],
-            out_specs=[col(L), col(L)],
-            scratch_shapes=[pltpu.VMEM((2*hp, N, 128), jnp.bfloat16)]),
-        out_shape=[jax.ShapeDtypeStruct((L, D), jnp.bfloat16)] * 2,
+            num_scalar_prefetch=1,
+            grid=(number,),
+            in_specs=[col(L), col(N), col(N), fix(L), fix(N)] + [pl.BlockSpec(memory_space=pl.ANY)] * len(after),
+            out_specs=[own(L), own(L)],
+            scratch_shapes=[pltpu.VMEM((2 * hp, N, 128), jnp.bfloat16)],
+        ),
+        out_shape=[jax.ShapeDtypeStruct((L, number * w), jnp.bfloat16)] * 2,
         compiler_params=pltpu.CompilerParams(vmem_limit_bytes=56 << 20),
-        cost_estimate=pl.CostEstimate(flops=COST * 2 * 2 * L * N * D, bytes_accessed=10 * L * D, transcendentals=0),
-    )(win, q, k, v, qx, kx)
-
-
-def attend_backward_kernel(bq, bk, causal, win_ref, q_ref, k_ref, v_ref, o_ref, do_ref, qe_ref, kx_ref, dq_ref, dk_ref, dv_ref, ka, va, dka, dva):
+        cost_estimate=estimate(
+            flops=COST * 2 * 2 * L * N * number * w, bytes_accessed=10 * L * number * w, transcendentals=0
+        ),
+    )(win, q, k, v, qx, kx, *after)
+
+
+def attend_backward_kernel(bq, bk, causal, win_ref, q_ref, k_ref, v_ref, o_ref, do_ref, qe_ref, kx_ref, *rest):
+    dq_ref, dk_ref, dv_ref, ka, va, dka, dva = rest[-7:]
     L, N = q_ref.shape[0], k_ref.shape[0]
     nq = L // bq
     lane = lax.broadcasted_iota(jnp.int32, (1, 128), 1)
@@ -191,28 +202,38 @@
     dv_ref[...] = dva[...].astype(jnp.bfloat16)
 
 
-def attend_backward(q, k, v, o, do, qe, kx, win, causal, bq=256, bk=256):
-    L, D = q.shape
-    N = k.shape[0]
-    col = lambda n: pl.BlockSpec((n, 128), lambda p, w: (0, p))
-    fix = lambda n: pl.BlockSpec((n, 128), lambda p, w: (0, 0))
+def attend_backward(q, k, v, o, do, qe, kx, win, causal, pairs, base=0, after=(), bq=256, bk=256):
+    L, N = q.shape[0], k.shape[0]
+    start, number = pairs[0], pairs[1] - pairs[0]
+    col = lambda n: pl.BlockSpec((n, 128), lambda p, _: (0, start + p))
+    own = lambda n: pl.BlockSpec((n, 128), lambda p, _: (0, p))
+    held = pl.BlockSpec((L, 128), lambda p, _: (0, start - base + p))
+    fix = lambda n: pl.BlockSpec((n, 128), lambda p, _: (0, 0))
     return pl.pallas_call(
         functools.partial(attend_backward_kernel, bq, bk, causal),
         grid_spec=pltpu.PrefetchScalarGridSpec(
-            num_scalar_prefetch=1, grid=(D // 128,),
-            in_specs=[col(L), col(N), col(N), col(L), col(L), col(L), fix(N)],
-            out_specs=[col(L), col(N), col(N)],
-            scratch_shapes=[pltpu.VMEM((2, N, 128), jnp.bfloat16)] * 2 + [pltpu.VMEM((N, 128), jnp.float32)] * 2),
-        out_shape=[jax.ShapeDtypeStruct((L, D), jnp.bfloat16)] + [jax.ShapeDtypeStruct((N, D), jnp.bfloat16)] * 2,
+            num_scalar_prefetch=1,
+            grid=(number,),
+            in_specs=[col(L), col(N), col(N), held, col(L), held, fix(N)]
+            + [pl.BlockSpec(memory_space=pl.ANY)] * len(after),
+            out_specs=[own(L), own(N), own(N)],
+            scratch_shapes=[pltpu.VMEM((2, N, 128), jnp.bfloat16)] * 2 + [pltpu.VMEM((N, 128), jnp.float32)] * 2,
+        ),
+        out_shape=[jax.ShapeDtypeStruct((L, number * 128), jnp.bfloat16)]
+        + [jax.ShapeDtypeStruct((N, number * 128), jnp.bfloat16)] * 2,
         compiler_params=pltpu.CompilerParams(vmem_limit_bytes=48 << 20),
-        cost_estimate=pl.CostEstimate(flops=COST * 5 * 2 * L * N * D, bytes_accessed=16 * L * D, transcendentals=0),
-    )(win, q, k, v, o, do, qe, kx)
+        cost_estimate=estimate(
+            flops=COST * 5 * 2 * L * N * number * 128, bytes_accessed=16 * L * number * 128, transcendentals=0
+        ),
+    )(win, q, k, v, o, do, qe, kx, *after)
 
 
 def fetch(plan, refs, order_ref, dst, sem):
     kind, offset, rows, flat, piece_rows, count = plan
     if kind == "flat":
-        pltpu.make_async_copy(refs[0].at[pl.ds(flat, rows * count)], dst, sem).start()
+        part = rows * count // 16
+        for j in range(16):
+            pltpu.make_async_copy(refs[0].at[pl.ds(flat + j * part, part)], dst.at[pl.ds(j * part, part)], sem).start()
         return
     for j in range(count):
         if kind == "ring":
@@ -258,7 +279,7 @@
 
 
 def first_kernel(plans, n_refs, order_ref, x_ref, norm_ref, *rest):
-    refs, (a_ref, q_ref, k_ref, v_ref, w, sem) = rest[:n_refs], rest[n_refs:]
+    refs, (a_ref, q_ref, k_ref, v_ref, w, sem) = rest[:n_refs], rest[-6:]
 
     @pl.when(pl.program_id(0) == 0)
     def _():
@@ -275,8 +296,13 @@
     v_ref[...] = low(mm(a, w[2]))
 
 
-def second_kernel(plans, n_refs, order_ref, o_ref, x_ref, e_ref, norm_ref, *rest):
-    refs, (r_ref, a_ref, q_ref, k_ref, v_ref, w, sem) = rest[:n_refs], rest[n_refs:]
+def joined(refs):
+    return refs[0][...] if len(refs) == 1 else jnp.concatenate([r[...] for r in refs], axis=1)
+
+
+def second_kernel(plans, n_refs, n_o, order_ref, *rest):
+    o_refs, (x_ref, e_ref, norm_ref), rest = rest[:n_o], rest[n_o : n_o + 3], rest[n_o + 3 :]
+    refs, (r_ref, a_ref, q_ref, k_ref, v_ref, w, sem) = rest[:n_refs], rest[-7:]
 
     @pl.when(pl.program_id(0) == 0)
     def _():
@@ -285,7 +311,7 @@
         for i in range(4):
             arrived(w.at[i], sem.at[i])
 
-    r = x_ref[...].astype(jnp.float32) + mm(o_ref[...], w[0])
+    r = x_ref[...].astype(jnp.float32) + mm(joined(o_refs), w[0])
     r_ref[...] = r
     k_ref[...] = low(mm(e_ref[...], w[2]))
     v_ref[...] = low(mm(e_ref[...], w[3]))
@@ -295,9 +321,10 @@
     q_ref[...] = low(mm(a, w[1]) * 0.125)
 
 
-def third_kernel(plans, n_b, n_c, order_ref, o_ref, r_ref, cot_ref, norm_ref, *rest):
+def third_kernel(plans, n_b, n_c, n_o, order_ref, *rest):
+    o_refs, (r_ref, cot_ref, norm_ref), rest = rest[:n_o], rest[n_o : n_o + 3], rest[n_o + 3 :]
     refs_b, refs_c = rest[:n_b], rest[n_b : n_b + n_c]
-    (out_ref, a_ref, h_ref, df_ref, du_ref, dr_ref, dc_ref, do_ref, term_ref, wc, wi, wo, slope, sem) = rest[n_b + n_c :]
+    (out_ref, a_ref, h_ref, df_ref, du_ref, dr_ref, dc_ref, do_ref, term_ref, wc, wi, wo, slope, sem) = rest[-14:]
     parts = wi.shape[0]
     first = pl.program_id(0) == 0
 
@@ -310,7 +337,7 @@
         term_ref[...] = jnp.zeros_like(term_ref)
         arrived(wc, sem.at[0])
 
-    r2 = r_ref[...] + mm(o_ref[...], wc[...])
+    r2 = r_ref[...] + mm(joined(o_refs), wc[...])
     unit2, scale2 = normed(r2)
     a3 = low(unit2 * norm_ref[2:3, :] + norm_ref[6:7, :])
     a_ref[...] = a3
@@ -354,8 +381,10 @@
     do_ref[...] = low(mm_back(dc, wc[...]))
 
 
-def fourth_kernel(plans, n_refs, order_ref, dq_ref, r_ref, dr_ref, dk_ref, dv_ref, norm_ref, *rest):
-    refs, (dx_ref, dc_ref, do_ref, de_ref, term_ref, w, sem) = rest[:n_refs], rest[n_refs:]
+def fourth_kernel(plans, n_refs, n_g, order_ref, *rest):
+    dq_refs, dk_refs, dv_refs = (rest[i * n_g : (i + 1) * n_g] for i in range(3))
+    (r_ref, dr_ref, norm_ref), rest = rest[3 * n_g : 3 * n_g + 3], rest[3 * n_g + 3 :]
+    refs, (dx_ref, dc_ref, do_ref, de_ref, term_ref, w, sem) = rest[:n_refs], rest[-7:]
 
     @pl.when(pl.program_id(0) == 0)
     def _():
@@ -365,7 +394,7 @@
             arrived(w.at[i], sem.at[i])
         term_ref[...] = jnp.zeros_like(term_ref)
 
-    da = mm_back(dq_ref[...], w[1])
+    da = mm_back(joined(dq_refs), w[1])
     unit, scale = normed(r_ref[...])
     term_rows(term_ref, 1, da * unit)
     term_rows(term_ref, 5, da)
@@ -374,11 +403,13 @@
     dc = low(dx)
     dc_ref[...] = dc
     do_ref[...] = low(mm_back(dc, w[0]))
-    de_ref[...] = mm_back(dk_ref[...], w[2]) + mm_back(dv_ref[...], w[3])
-
-
-def fifth_kernel(plans, n_refs, order_ref, dq_ref, dk_ref, dv_ref, x_ref, dr_ref, norm_ref, *rest):
-    refs, (dx_ref, term_ref, w, sem) = rest[:n_refs], rest[n_refs:]
+    de_ref[...] = mm_back(joined(dk_refs), w[2]) + mm_back(joined(dv_refs), w[3])
+
+
+def fifth_kernel(plans, n_refs, n_g, order_ref, *rest):
+    dq_refs, dk_refs, dv_refs = (rest[i * n_g : (i + 1) * n_g] for i in range(3))
+    (x_ref, dr_ref, norm_ref), rest = rest[3 * n_g : 3 * n_g + 3], rest[3 * n_g + 3 :]
+    refs, (dx_ref, term_ref, w, sem) = rest[:n_refs], rest[-4:]
 
     @pl.when(pl.program_id(0) == 0)
     def _():
@@ -388,18 +419,22 @@
             arrived(w.at[i], sem.at[i])
         term_ref[...] = jnp.zeros_like(term_ref)
 
-    da = mm_back(dq_ref[...], w[0]) + mm_back(dk_ref[...], w[1]) + mm_back(dv_ref[...], w[2])
+    da = mm_back(joined(dq_refs), w[0]) + mm_back(joined(dk_refs), w[1]) + mm_back(joined(dv_refs), w[2])
     unit, scale = normed(x_ref[...].astype(jnp.float32))
     term_rows(term_ref, 0, da * unit)
     term_rows(term_ref, 4, da)
     dx_ref[...] = dr_ref[...] + normed_back(unit, scale, norm_ref[0:1, :], da)
 
 
-def by_rows(kernel, order, row_inputs, norms, piece_refs, row_outputs, terms, scratch, flops, block=256):
+def by_rows(kernel, order, row_inputs, norms, piece_refs, row_outputs, terms, scratch, flops, after=(), block=256, part=(0, 1), into=None):
     rows = row_inputs[0].shape[0]
+    steps = rows // block // part[1]
+    first = part[0] * steps
+    piece_refs = list(piece_refs) + list(after) + ([] if into is None else [into])
+    aliases = {} if into is None else {1 + len(row_inputs) + len(piece_refs): 0}
 
     def spec(width):
-        return pl.BlockSpec((block, width), lambda i, _: (i, 0))
+        return pl.BlockSpec((block, width), lambda i, _: (first + i, 0))
 
     def fixed(shape):
         return pl.BlockSpec(shape, lambda i, _: (0, 0))
@@ -414,7 +449,7 @@
         kernel,
         grid_spec=pltpu.PrefetchScalarGridSpec(
             num_scalar_prefetch=1,
-            grid=(rows // block,),
+            grid=(steps,),
             in_specs=[spec(x.shape[1]) for x in row_inputs]
             + [fixed(norms.shape)]
             + [pl.BlockSpec(memory_space=pl.ANY)] * len(piece_refs),
@@ -422,28 +457,26 @@
             scratch_shapes=scratch,
         ),
         out_shape=out_shape,
+        input_output_aliases=aliases,
         compiler_params=pltpu.CompilerParams(vmem_limit_bytes=58 << 20),
-        cost_estimate=pl.CostEstimate(flops=flops, bytes_accessed=moved, transcendentals=0),
+        cost_estimate=estimate(flops=flops, bytes_accessed=moved, transcendentals=0),
     )(order, *row_inputs, norms, *piece_refs)
 
 
-def term_kernel(pairs, chips, rank_ref, *rest):
-    lefts, rights = rest[: len(pairs)], rest[len(pairs) : 2 * len(pairs)]
-    mine_ref, other_ref, turned = rest[2 * len(pairs) :]
-    weight = pl.program_id(0)
+def term_kernel(names, chips, n_left, n_right, rank_ref, *rest):
+    parts = len(names)
+    flat, rest = rest[: sum(n_left)], rest[sum(n_left) :]
+    lefts = [flat[sum(n_left[:i]) : sum(n_left[: i + 1])] for i in range(len(n_left))]
+    rights = [rest[sum(n_right[:i]) : sum(n_right[: i + 1])] for i in range(parts)]
+    mine_ref, other_ref, turned = rest[-3:]
     rows = mine_ref.shape[1]
-    for i in range(len(pairs)):
-        new_left = i == 0 or pairs[i] != pairs[i - 1]
-
-        @pl.when(weight == i)
+    for i in range(parts):
+
+        @pl.when(pl.program_id(0) == i)
         def _():
-            if new_left:
-
-                @pl.when(pl.program_id(1) == 0)
-                def _():
-                    turned[...] = jnp.transpose(lefts[i][...])
-
-            total = low(mm(turned[...], rights[i][...]))
+            if i == 0 or names[i] != names[i - 1]:
+                turned[...] = jnp.transpose(joined(lefts[names[i]]))
+            total = low(mm(turned[...], joined(rights[i])))
             core = rank_ref[chips]
             for chip in range(chips):
                 one = total[2 * chip * rows : (2 * chip + 1) * rows]
@@ -452,31 +485,204 @@
                 other_ref[rank_ref[chip]] = jnp.where(core == 0, two, one)
 
 
-def term_sets(rank, lefts, rights, pairs, count, block=256):
-    total, width = lefts[0].shape[1], rights[0].shape[1]
+def term_sets(rank, lefts, parts, count, after=()):
+    total, depth = sum(x.shape[1] for x in lefts[0]), lefts[0][0].shape[0]
+    flat = [x for left in lefts for x in left]
     rows = total // count
     chips = count // 2
-    number = len(lefts)
-
-    def right_spec(i):
-        return pl.BlockSpec(
-            (rights[i].shape[0], block),
-            lambda w, n, _: (0, jnp.where(w == i, n, jnp.where(w < i, 0, width // block - 1))),
-        )
-
+    number = len(parts)
+    rights, specs = [], []
+    for _, given in parts:
+        for x, c in given:
+            rights.append(x)
+            specs.append(pl.BlockSpec((depth, 512 // len(given)), lambda n, _, c=c: (0, c)))
     return pl.pallas_call(
-        functools.partial(term_kernel, pairs, chips),
+        functools.partial(term_kernel, [p[0] for p in parts], chips, [len(left) for left in lefts], [len(p[1]) for p in parts]),
         grid_spec=pltpu.PrefetchScalarGridSpec(
             num_scalar_prefetch=1,
-            grid=(number, width // block),
-            in_specs=[pl.BlockSpec(x.shape, lambda w, n, _: (0, 0)) for x in lefts] + [right_spec(i) for i in range(number)],
-            out_specs=[pl.BlockSpec((chips, rows, block), lambda w, n, _: (0, w, n))] * 2,
-            scratch_shapes=[pltpu.VMEM((total, lefts[0].shape[0]), jnp.bfloat16)],
+            grid=(number,),
+            in_specs=[pl.BlockSpec(x.shape, lambda n, _: (0, 0)) for x in flat]
+            + specs
+            + [pl.BlockSpec(memory_space=pl.ANY)] * len(after),
+            out_specs=[pl.BlockSpec((chips, rows, 512), lambda n, _: (0, n, 0))] * 2,
+            scratch_shapes=[pltpu.VMEM((total, depth), jnp.bfloat16)],
         ),
-        out_shape=[jax.ShapeDtypeStruct((chips, number * rows, width), jnp.bfloat16)] * 2,
+        out_shape=[jax.ShapeDtypeStruct((chips, number * rows, 512), jnp.bfloat16)] * 2,
         compiler_params=pltpu.CompilerParams(vmem_limit_bytes=58 << 20),
-        cost_estimate=pl.CostEstimate(flops=2 * number * total * width * lefts[0].shape[0], bytes_accessed=6 * number * total * width, transcendentals=0),
-    )(rank, *lefts, *rights)
+        cost_estimate=estimate(
+            flops=2 * number * total * 512 * depth, bytes_accessed=6 * number * total * 512, transcendentals=0
+        ),
+    )(rank, *flat, *rights, *after)
+
+
+def ffn_term_kernel(parts, a_ref, du_ref, h_ref, df_ref, *rest):
+    out_ref = rest[-1]
+    step = pl.program_id(1)
+    width = a_ref.shape[1]
+    rows_in = width // out_ref.shape[0]
+    rows_out = parts * rows_in
+    owners = width // rows_out
+
+    def deal(total, rows, first, at):
+        for i in range(width // rows):
+            out_ref[first + i, pl.ds(at, rows)] = total[i * rows : (i + 1) * rows]
+
+    for i in range(parts):
+
+        @pl.when(step == i)
+        def _():
+            total = low(lax.dot_general(a_ref[...], du_ref[...], TN, preferred_element_type=jnp.float32))
+            deal(total, rows_in, 0, i * rows_in)
+
+        @pl.when(step == parts + i)
+        def _():
+            total = low(lax.dot_general(h_ref[...], df_ref[...], TN, preferred_element_type=jnp.float32))
+            deal(total, rows_out, i * owners, parts * rows_in)
+
+
+def ffn_terms(a, du, h, df, count, block=512):
+    depth, width = a.shape
+    parts = du.shape[1] // width
+    rows = (parts * width + h.shape[1]) // count
+    per = width // block
+    return pl.pallas_call(
+        functools.partial(ffn_term_kernel, parts),
+        grid=(per, 2 * parts),
+        in_specs=[
+            pl.BlockSpec((depth, width), lambda n, s: (0, 0)),
+            pl.BlockSpec((depth, block), lambda n, s: (0, jnp.minimum(s, parts - 1) * per + n)),
+            pl.BlockSpec((depth, width), lambda n, s: (0, jnp.maximum(s - parts, 0))),
+            pl.BlockSpec((depth, block), lambda n, s: (0, n)),
+        ],
+        out_specs=pl.BlockSpec((count, rows, block), lambda n, s: (0, 0, n)),
+        out_shape=jax.ShapeDtypeStruct((count, rows, width), jnp.bfloat16),
+        compiler_params=pltpu.CompilerParams(vmem_limit_bytes=58 << 20),
+        cost_estimate=estimate(
+            flops=4 * parts * depth * width * width, bytes_accessed=12 * parts * width * width, transcendentals=0
+        ),
+    )(a, du, h, df)
+
+
+def halve_kernel(split, rep_ref, mine_ref, came_ref, *rest):
+    keep_ref, soon_ref, late_ref = rest[-3:]
+    total = low(mine_ref[...].astype(jnp.float32) + came_ref[...].astype(jnp.float32))
+    half = total.shape[1] // 2
+    one, two = total[:, :half], total[:, half:]
+    keep_ref[...] = jnp.where(rep_ref[0] == 0, one, two)
+    send = jnp.where(rep_ref[0] == 0, two, one)
+
+    @pl.when(pl.program_id(0) < split)
+    def _():
+        soon_ref[...] = send
+
+    @pl.when(pl.program_id(0) >= split)
+    def _():
+        late_ref[...] = send
+
+
+def halve(rep, mine, came, split, after=()):
+    chips, rows, width = mine.shape
+    pairs = chips // 2
+    spec = pl.BlockSpec((2, rows, width), lambda i, _: (i, 0, 0))
+    block = (2, rows // 2, width)
+    half = rows // 2
+    return pl.pallas_call(
+        functools.partial(halve_kernel, split),
+        grid_spec=pltpu.PrefetchScalarGridSpec(
+            num_scalar_prefetch=1,
+            grid=(pairs,),
+            in_specs=[spec, spec] + [pl.BlockSpec(memory_space=pl.ANY)] * len(after),
+            out_specs=[
+                pl.BlockSpec(block, lambda i, _: (i, 0, 0)),
+                pl.BlockSpec(block, lambda i, _: (jnp.minimum(i, split - 1), 0, 0)),
+                pl.BlockSpec(block, lambda i, _: (jnp.maximum(i - split, 0), 0, 0)),
+            ],
+        ),
+        out_shape=[
+            jax.ShapeDtypeStruct((chips, half, width), jnp.bfloat16),
+            jax.ShapeDtypeStruct((2 * split, half, width), jnp.bfloat16),
+            jax.ShapeDtypeStruct((chips - 2 * split, half, width), jnp.bfloat16),
+        ],
+        compiler_params=pltpu.CompilerParams(vmem_limit_bytes=32 << 20),
+        cost_estimate=estimate(flops=2 * mine.size, bytes_accessed=6 * mine.size, transcendentals=0),
+    )(rep, mine, came, *after)
+
+
+def pair_kernel(split, one_ref, soon_ref, late_ref, *rest):
+    two = jnp.where(pl.program_id(0) < split, soon_ref[...], late_ref[...])
+    rest[-1][...] = low(one_ref[...].astype(jnp.float32) + two.astype(jnp.float32))
+
+
+def pair_sum(one, soon, late, after=()):
+    chips, rows, width = one.shape
+    split = soon.shape[0] // 2
+    block = (2, rows, width)
+    spec = pl.BlockSpec(block, lambda i: (i, 0, 0))
+    return pl.pallas_call(
+        functools.partial(pair_kernel, split),
+        grid=(chips // 2,),
+        in_specs=[
+            spec,
+            pl.BlockSpec(block, lambda i: (jnp.minimum(i, split - 1), 0, 0)),
+            pl.BlockSpec(block, lambda i: (jnp.maximum(i - split, 0), 0, 0)),
+        ]
+        + [pl.BlockSpec(memory_space=pl.ANY)] * len(after),
+        out_specs=spec,
+        out_shape=jax.ShapeDtypeStruct(one.shape, jnp.bfloat16),
+        compiler_params=pltpu.CompilerParams(vmem_limit_bytes=32 << 20),
+        cost_estimate=estimate(flops=one.size, bytes_accessed=6 * one.size, transcendentals=0),
+    )(one, soon, late, *after)
+
+
+def hop_kernel(first, second, *rest):
+    if first:
+        mine_up, came_up, mine_down, came_down = rest[:4]
+        up = mine_up[0].astype(jnp.float32) + came_up[0].astype(jnp.float32)
+        down = mine_down[0].astype(jnp.float32) + came_down[0].astype(jnp.float32)
+        rest[-2][...] = low(up)
+        rest[-1][...] = low(down)
+        return
+    up_ref, mine_up, came_up = rest[:3]
+    up = up_ref[...].astype(jnp.float32) + mine_up[0].astype(jnp.float32) + came_up[0].astype(jnp.float32)
+    if not second:
+        rest[-1][...] = low(up)
+        return
+    down_ref, mine_down, came_down = rest[3:6]
+    down = down_ref[...].astype(jnp.float32) + mine_down[0].astype(jnp.float32) + came_down[0].astype(jnp.float32)
+    rest[-2][...] = low(up)
+    rest[-1][...] = low(down)
+
+
+def hop(mine, came, up, down, up_at, down_at, after=()):
+    rows, width = mine.shape[1:]
+    blocks = 2 if rows % 32 == 0 else 1
+    part = rows // blocks
+
+    def pick(at):
+        return pl.BlockSpec((1, part, width), lambda i: (at, i, 0))
+
+    flat = pl.BlockSpec((part, width), lambda i: (i, 0))
+    args, specs = [], []
+    if up is not None:
+        args.append(up)
+        specs.append(flat)
+    args += [mine, came]
+    specs += [pick(up_at)] * 2
+    if down_at is not None:
+        if down is not None:
+            args.append(down)
+            specs.append(flat)
+        args += [mine, came]
+        specs += [pick(down_at)] * 2
+    number = 1 if down_at is None else 2
+    return pl.pallas_call(
+        functools.partial(hop_kernel, up is None, down_at is not None),
+        grid=(blocks,),
+        in_specs=specs + [pl.BlockSpec(memory_space=pl.ANY)] * len(after),
+        out_specs=[flat] * number,
+        out_shape=[jax.ShapeDtypeStruct((rows, width), jnp.bfloat16)] * number,
+        cost_estimate=estimate(flops=4 * rows * width, bytes_accessed=16 * rows * width, transcendentals=0),
+    )(*args, *after)
 
 
 def ring_walk(chips):
@@ -523,6 +729,31 @@
     return pieces + [lax.ppermute(p, "shard", swap) for p in pieces]
 
 
+class RingGather:
+    def __init__(self, piece, count):
+        self.up, self.down, self.swap = ring_moves(count)
+        self.chips = count // 2
+        self.pieces = [piece] + [None] * (self.chips - 1)
+        self.step = 0
+
+    def hop(self, after):
+        def held(part):
+            return part + after[:1, :1] * 0
+
+        last, half = self.step, self.chips // 2
+        self.step += 1
+        up = lax.ppermute(held(self.pieces[-last % self.chips]), "shard", self.up)
+        self.pieces[self.chips - self.step] = up
+        if self.step == half:
+            return [up]
+        down = lax.ppermute(held(self.pieces[last]), "shard", self.down)
+        self.pieces[self.step] = down
+        return [up, down]
+
+    def finish(self):
+        return self.pieces + [lax.ppermute(p, "shard", self.swap) for p in self.pieces]
+
+
 def add_low(*values_in):
     return low(sum(v.astype(jnp.float32) for v in values_in))
 
@@ -532,34 +763,84 @@
     return owned.astype(jnp.float32) + partner.astype(jnp.float32)
 
 
-def ring_sum(mine, other, count):
-    up, down, swap = ring_moves(count)
-    chips = count // 2
-    half = chips // 2
-    came = lax.ppermute(other, "shard", swap)
-    upward = add_low(mine[half], came[half])
-    downward = add_low(mine[chips - half + 1], came[chips - half + 1])
-    for step in range(half - 1, -1, -1):
-        upward = lax.ppermute(upward, "shard", up)
-        if step:
-            upward = add_low(upward, mine[step], came[step])
-    for step in range(half - 2, -1, -1):
-        downward = lax.ppermute(downward, "shard", down)
-        if step:
-            downward = add_low(downward, mine[chips - step], came[chips - step])
-    return over_rep(add_low(mine[0], came[0], upward, downward))
+class RingSum:
+    def __init__(self, mine, other, count, flip=False):
+        self.up, self.down, swap = ring_moves(count)
+        self.chips = count // 2
+        self.sign = 1
+        if flip:
+            self.up, self.down, self.sign = self.down, self.up, -1
+        self.mine = mine
+        self.came = lax.ppermute(other, "shard", swap)
+        self.step = self.chips // 2
+        self.upward = self.downward = None
+
+    def at(self, distance):
+        return (self.sign * distance) % self.chips
+
+    def hop(self, after=()):
+        half = self.chips // 2
+        down_at = 1 - self.step if self.step > 1 else None
+        sums = hop(
+            self.mine, self.came, self.upward, self.downward if down_at is not None else None,
+            self.at(self.step), None if down_at is None else self.at(down_at), after,
+        )
+        self.upward = lax.ppermute(sums[0], "shard", self.up)
+        if down_at is not None:
+            self.downward = lax.ppermute(sums[1], "shard", self.down)
+        self.step -= 1
+        return [sums[0]]
+
+    def finish(self):
+        owned = add_low(self.mine[0], self.came[0], self.upward, self.downward)
+        return over_rep(owned)
+
+
+class HalfSum:
+    def __init__(self, rep, mine, other, count):
+        self.rep, self.count, self.mine = rep, count, mine
+        self.came = lax.ppermute(other, "shard", ring_moves(count)[2])
+
+    def over_rep(self, split, after=()):
+        swap = [(0, 1), (1, 0)]
+        self.keep, soon, late = halve(self.rep, self.mine, self.came, split, after)
+        self.soon, self.late = lax.ppermute(soon, "rep", swap), lax.ppermute(late, "rep", swap)
+        return [self.keep]
+
+    def over_chips(self, after=()):
+        both = pair_sum(self.keep, self.soon, self.late, after).reshape(-1, self.keep.shape[2])
+        groups = [list(range(core, self.count, 2)) for core in range(2)]
+        self.owned = lax.psum_scatter(both, "shard", scatter_dimension=0, axis_index_groups=groups, tiled=True)
+        return [both]
+
+    def finish(self):
+        partner = lax.ppermute(self.owned, "rep", [(0, 1), (1, 0)])
+        first = self.rep[0] == 0
+        return jnp.concatenate(
+            [jnp.where(first, self.owned, partner), jnp.where(first, partner, self.owned)], axis=0
+        ).astype(jnp.float32)
 
 
 def scatter_sum(term):
     return over_rep(lax.psum_scatter(low(term), "shard", scatter_dimension=0, tiled=True))
 
 
-def total_sum(values_in, count):
-    step = 1
-    while step < count:
-        values_in = values_in + lax.ppermute(values_in, "shard", [(i, i ^ step) for i in range(count)])
-        step *= 2
-    return values_in + lax.ppermute(values_in, "rep", [(0, 1), (1, 0)])
+class TotalSum:
+    def __init__(self, values_in, count):
+        self.value, self.count, self.step = values_in, count, 1
+
+    def phase(self):
+        if self.step < self.count:
+            radix = min(4, self.count // self.step)
+            came = [
+                lax.ppermute(self.value, "shard", [(i, i ^ (k * self.step)) for i in range(self.count)])
+                for k in range(1, radix)
+            ]
+            self.step *= radix
+        else:
+            came = [lax.ppermute(self.value, "rep", [(0, 1), (1, 0)])]
+        self.value = self.value + sum(came[1:], came[0])
+        return [self.value]
 
 
 def weight_term(left, right):
@@ -604,8 +885,11 @@
         order, rank = ring_tables(count)
         norm_row = jnp.pad(norm_piece.reshape(1, -1), ((0, 15), (0, width - 8 * own_width)))
         set_a = gather_pieces(jnp.concatenate([self_q, self_k, self_v, norm_row], axis=0), count)
-        set_b = gather_pieces(jnp.concatenate([self_o, cross_q, cross_k, cross_v, cross_o], axis=0), count)
-        set_c = [lax.all_gather(jnp.concatenate(in_parts + [ffn_out], axis=0), "shard", axis=0, tiled=True)]
+        ring_b = RingGather(jnp.concatenate([self_o, cross_q, cross_k, cross_v, cross_o], axis=0), count)
+        ring_b.hop(set_a[count // 4])
+        rep = lax.axis_index("rep").astype(jnp.int32).reshape(1)
+        half_c = jnp.where(rep[0] == 0, jnp.concatenate(in_parts, axis=0), ffn_out)
+        set_c = [lax.all_gather(half_c, ("rep", "shard"), axis=0, tiled=True)]
         norm_rows = jnp.concatenate([p[3 * own : 3 * own + 1, : 8 * own_width] for p in set_a], axis=0)
         place = (jnp.arange(count, dtype=jnp.int32)[:, None] == order[None, :]).astype(bf16)
         norms = mm(place, norm_rows)
@@ -624,9 +908,8 @@
         kinds = ("flat", "flat", "flat")
     plan_a = [(kinds[0], i * own, own, i * width, 0, count) for i in range(3)]
     plan_b = [(kinds[1], i * own, own, i * width, 0, count) for i in range(5)]
-    piece_c = parts * own + own_out
-    plan_c = [(kinds[2], i * own, own, i * width, piece_c, count) for i in range(parts)]
-    plan_c.append((kinds[2], parts * own, own_out, parts * width, piece_c, count))
+    plan_c = [(kinds[2], i * own, own, i * width, parts * own, count) for i in range(parts)]
+    plan_c.append(("flat", 0, own_out, parts * width, 0, count))
     sems = pltpu.SemaphoreType.DMA
     square = 2 * row_count * width * width
 
@@ -639,15 +922,27 @@
         [(width, bf16)] * 4, False,
         [pltpu.VMEM((3, width, width), bf16), sems((3,))], 3 * square,
     )
-    o1, log1 = attend_forward(q1, k1, v1, query_extra, unit_extra, self_windows, True, hp=2, norm=True)
+    pairs = width // 128
+    self_args = (q1, k1, v1, query_extra, unit_extra, self_windows, True)
+    if ring:
+        o1_low, log1_low = attend_forward(*self_args, (0, pairs // 2))
+        ring_b.hop(o1_low)
+        o1_high, log1_high = attend_forward(*self_args, (pairs // 2, pairs), [o1_low])
+        ring_b.hop(o1_high)
+        ring_b.hop(o1_high)
+        set_b = ring_b.finish()
+    else:
+        o1_low, log1_low = attend_forward(*self_args, (0, pairs // 2))
+        o1_high, log1_high = attend_forward(*self_args, (pairs // 2, pairs))
+    o1 = [o1_low, o1_high]
     r1, a2, q2, k2, v2 = by_rows(
-        functools.partial(second_kernel, plan_b[:4], len(set_b)), order, [o1, x, enc], norms, set_b,
+        functools.partial(second_kernel, plan_b[:4], len(set_b), 2), order, o1 + [x, enc], norms, set_b,
         [(width, f32)] + [(width, bf16)] * 4, False,
         [pltpu.VMEM((4, width, width), bf16), sems((4,))], 4 * square,
     )
-    o2, log2 = attend_forward(q2, k2, v2, query_extra, enc_extra, cross_windows, False, hp=2, norm=True)
+    o2, log2 = attend_forward(q2, k2, v2, query_extra, enc_extra, cross_windows, False, (0, pairs))
     out, a3, h, df, du, dr2, dc2, do2, terms_three = by_rows(
-        functools.partial(third_kernel, plan_b[4:] + plan_c, len(set_b), len(set_c)), order, [o2, r1, cot], norms, set_b + set_c,
+        functools.partial(third_kernel, plan_b[4:] + plan_c, len(set_b), len(set_c), 1), order, [o2, r1, cot], norms, set_b + set_c,
         [(width, bf16), (width, bf16), (hidden, bf16), (width, bf16), (hidden, bf16), (width, f32), (width, bf16), (width, bf16)], True,
         [
             pltpu.VMEM((width, width), bf16),
@@ -659,35 +954,86 @@
         (2 + 4 * parts) * square,
     )
 
-    grad_out = scatter_sum(weight_term(h, df))
-    grad_in = scatter_sum(weight_term(a3, du))
-    dq2, dk2, dv2 = attend_backward(q2, k2, v2, o2, do2, log2, enc_extra, cross_windows, False)
-    dr1, dc1, do1, grad_enc, terms_two = by_rows(
-        functools.partial(fourth_kernel, plan_b[:4], len(set_b)), order, [dq2, r1, dr2, dk2, dv2], norms, set_b,
+    cross_args = (q2, k2, v2, o2, do2, log2, enc_extra, cross_windows, False)
+    if ring:
+        plain = jnp.concatenate([jnp.arange(count // 2, dtype=jnp.int32), rank[-1:]])
+        ffn_set = ffn_terms(a3, du, h, df, count)
+        ffn_set = lax.psum_scatter(ffn_set.reshape(-1, width), "shard", scatter_dimension=0, tiled=True)
+    else:
+        grad_in, grad_out = scatter_sum(weight_term(a3, du)), scatter_sum(weight_term(h, df))
+    dq2, dk2, dv2 = attend_backward(*cross_args, (0, pairs))
+    fourth = functools.partial(
+        by_rows, functools.partial(fourth_kernel, plan_b[:4], len(set_b), 1), order, [dq2, dk2, dv2, r1, dr2], norms, set_b,
         [(width, f32), (width, bf16), (width, bf16), (width, f32)], True,
         [pltpu.VMEM((4, width, width), bf16), sems((4,))], 4 * square,
     )
-    lefts, rights = [o2, a2, enc, enc, o1], [dc2, dq2, dk2, dv2, dc1]
+
+    half = pairs // 2
+
+    def self_backward(i, after):
+        return attend_backward(
+            q1, k1, v1, o1[i], do1, (log1_low, log1_high)[i], unit_extra, self_windows, True,
+            (i * half, (i + 1) * half), i * half, after,
+        )
+
+    def fifth(groups, after, part=(0, 1), into=None):
+        dq1, dk1, dv1 = ([g[i] for g in groups] for i in range(3))
+        return by_rows(
+            functools.partial(fifth_kernel, plan_a, len(set_a), len(groups)), order, dq1 + dk1 + dv1 + [x, dr1], norms, set_a,
+            [(width, f32)], True,
+            [pltpu.VMEM((3, width, width), bf16), sems((3,))], 3 * square // part[1], after, part=part, into=into,
+        )
+
     if ring:
-        mine, other = term_sets(rank, lefts, rights, (0, 1, 2, 2, 3), count)
-        grad_b = ring_sum(mine, other, count)
-        grad_co, grad_cq, grad_ck, grad_cv, grad_so = (grad_b[i * own : (i + 1) * own] for i in range(5))
+        sums_b = HalfSum(
+            rep,
+            *term_sets(
+                plain, [(o2,), (a2,), (enc,)],
+                [(i, [(g, c)]) for i, g in ((0, dc2), (1, dq2), (2, dk2), (2, dv2)) for c in range(2)], count,
+            ),
+            count,
+        )
+        dr1, dc1, do1, grad_enc, terms_two = fourth([sums_b.mine])
+        groups = [self_backward(0, sums_b.over_rep(2, [dc1]))]
+        groups.append(self_backward(1, [groups[0][0], sums_b.soon]))
+        sums_a = RingSum(
+            *term_sets(
+                rank, [tuple(o1), (a1,)],
+                [(0, [(dc1, c)]) for c in range(2)] + [(1, [(g[i], 0)]) for i in range(3) for g in groups], count, [sums_b.late],
+            ),
+            count, True,
+        )
+        grad_x, terms_one = fifth(groups, [sums_a.mine])
+        norm_sum = TotalSum(terms_one + terms_two + terms_three, count)
+        last = sums_b.over_chips(sums_a.hop([grad_x]) + [ffn_set])
+        for _ in range(count // 4 - 1):
+            last = sums_a.hop(last + norm_sum.phase())
+        ffn_set = over_rep(ffn_set)
+        grad_in = jnp.concatenate([ffn_set[i * own : (i + 1) * own] for i in range(parts)], axis=1)
+        grad_out = ffn_set[parts * own :]
+        grad_a, grad_b = sums_a.finish(), sums_b.finish()
+
+        def columns(array, places):
+            return jnp.concatenate([array[i * own : (i + 1) * own] for i in places], axis=1)
+
+        grad_co, grad_cq, grad_ck, grad_cv = (columns(grad_b, (2 * w, 2 * w + 1)) for w in range(4))
+        grad_so, grad_sq, grad_sk, grad_sv = (columns(grad_a, (2 * w, 2 * w + 1)) for w in range(4))
     else:
-        grad_co, grad_cq, grad_ck, grad_cv, grad_so = (scatter_sum(weight_term(a, b)) for a, b in zip(lefts, rights))
-    dq1, dk1, dv1 = attend_backward(q1, k1, v1, o1, do1, log1, unit_extra, self_windows, True)
-    lefts, rights = [a1, a1, a1], [dq1, dk1, dv1]
-    if ring:
-        mine, other = term_sets(rank, lefts, rights, (0, 0, 0), count)
-        grad_a = ring_sum(mine, other, count)
-        grad_sq, grad_sk, grad_sv = (grad_a[i * own : (i + 1) * own] for i in range(3))
-    else:
-        grad_sq, grad_sk, grad_sv = (scatter_sum(weight_term(a, b)) for a, b in zip(lefts, rights))
-    grad_x, terms_one = by_rows(
-        functools.partial(fifth_kernel, plan_a, len(set_a)), order, [dq1, dk1, dv1, x, dr1], norms, set_a,
-        [(width, f32)], True,
-        [pltpu.VMEM((3, width, width), bf16), sems((3,))], 3 * square,
-    )
-    norm_sum = total_sum(terms_one + terms_two + terms_three, count)
+        dr1, dc1, do1, grad_enc, terms_two = fourth()
+        groups = [self_backward(i, ()) for i in range(2)]
+        dq1, dk1, dv1 = (jnp.concatenate([g[i] for g in groups], axis=1) for i in range(3))
+        grad_x, terms_one = fifth(groups, ())
+        norm_sum = TotalSum(terms_one + terms_two + terms_three, count)
+        while norm_sum.step < count:
+            norm_sum.phase()
+        norm_sum.phase()
+        grad_co, grad_cq, grad_ck, grad_cv, grad_so, grad_sq, grad_sk, grad_sv = (
+            scatter_sum(weight_term(a, b))
+            for a, b in (
+                (o2, dc2), (a2, dq2), (enc, dk2), (enc, dv2), (jnp.concatenate(o1, axis=1), dc1), (a1, dq1), (a1, dk1), (a1, dv1)
+            )
+        )
+    norm_sum = norm_sum.value
     norm_sum = lax.dynamic_slice_in_dim(norm_sum, lax.axis_index("shard") * own_width, own_width, 1)
     return (
         out.reshape(tokens.shape),

time: 722 us -> 656 us (0.909)
  waiting for transfers between devices: 234 us -> 165 us
  Pallas kernels: 298 us -> 335 us
  matrix products: 29.9 us -> 0.12 us
  local copies, waits for them, and re-layouts: 23.1 us -> 36.3 us
  other arithmetic: 28.6 us -> 18.8 us
    ppermute x6 -> x3, waiting for transfers between devices: 72.7 us -> 3.2 us  [gather_pieces(): downward = lax.ppermute(downward, 'shard', down)]
    pallas_call x2 -> x9, Pallas kernels: 46.3 us -> 82 us  [the longest x2 34.7 us: term_sets(): pl.pallas_call(functools.partial(term_kernel, [p[0] for p in parts], chip...]
    ppermute x21 -> x34, starting transfers between devices: 22.7 us -> 54.1 us  [the longest x4 21 us: hop(): up = lax.ppermute(held(self.pieces[-last % self.chips]), 'shard', self.up)]
    dot_general x2 -> x0, matrix products: 29.8 us -> none  [weight_term(): jnp.einsum('ra,rb->ab', left, right, preferred_element_type=jnp.float32)]
    ppermute x4 -> x2, waiting for transfers between devices: 30.9 us -> 7.83 us  [over_rep(): partner = lax.ppermute(owned, 'rep', [(0, 1), (1, 0)])]
    ppermute x21 -> x34, waiting for transfers between devices: 79.1 us -> 101 us  [the longest x4 36 us: hop(): up = lax.ppermute(held(self.pieces[-last % self.chips]), 'shard', self.up)]
    ppermute x6 -> x3, starting transfers between devices: 22.8 us -> 0.91 us  [gather_pieces(): downward = lax.ppermute(downward, 'shard', down)]
    convert_element_type x10 -> x1, other arithmetic: 21.7 us -> 1.47 us  [low(): return values_in.astype(jnp.bfloat16)]
  transfers between devices with their start and end apart: 58 -> 54, of which waited for: 20 -> 22; matrix products, arithmetic and copies ran while one was open for 7% -> 4% of each run, Pallas kernels for 34% -> 37%
where the time goes in v3:
time: 656 us; the launch traced here: 650 us
  Pallas kernels  335 us (51%)
  waiting for transfers between devices  165 us (25%)
  starting transfers between devices  78 us (12%)
  local copies, waits for them, and re-layouts  36.3 us (6%)
  other arithmetic  18.8 us (3%)
  between operations  17.2 us (3%)
    pallas_call x5, Pallas kernels, by_rows(): pl.pallas_call(kernel, grid_spec=pltpu.PrefetchScalarGridSpec(num_scalar_...  124 us
    pallas_call x3, Pallas kernels, attend_backward(): pl.pallas_call(functools.partial(attend_backward_kernel, bq, bk, causal),...  80.1 us
    ppermute x4, waiting for transfers between devices, gather_pieces(): upward = lax.ppermute(upward, 'shard', up)  51.8 us
    pallas_call x3, Pallas kernels, attend_forward(): pl.pallas_call(functools.partial(attend_forward_kernel, bq, bk, causal, h...  48.7 us
    ppermute x4, waiting for transfers between devices, hop(): up = lax.ppermute(held(self.pieces[-last % self.chips]), 'shard', self.up)  36 us
    pallas_call x2, Pallas kernels, term_sets(): pl.pallas_call(functools.partial(term_kernel, [p[0] for p in parts], chip...  34.7 us
    pallas_call x1, Pallas kernels, ffn_terms(): pl.pallas_call(functools.partial(ffn_term_kernel, parts), grid=(per, 2 *...  31.2 us
    ppermute x6, waiting for transfers between devices, phase(): lax.ppermute(self.value, 'shard', [(i, i ^ k * self.step) for i in range(...  30.9 us
  transfers between devices with their start and end apart: 54, of which 22 were waited for; matrix products, arithmetic and copies ran while one was open for 4% of the time, Pallas kernels for 37%

profile of v3, /device:TPU:0, one launch (start us, length us, event | category | flops | bytes accessed | tf_op | source)
XLA Modules:
  0.0 650.0 jit_solution(8786487758494077280)
XLA Ops:
  9.9 3.1 collective-permute-start.3
  14.5 8.3 %collective-permute-done.3.rest_7_.rest_16_ = bf16[208,1024]{1,0:T(8,128)(2,1)S(1)} collective-permute-done((bf16[208,1024]{1,0:T(8,128)(2,1)S(1)}, bf16[208,1024]{1,0:T(8,128)(2,1)S(1)}, u32[]{:S(2)}, u32[]{:S(2)}) %collective-permute-start.3) | collective-permute-done | bytes 426016 | tf_op jit(solution)/shard_map/ppermute | solution.py:724
  22.8 1.8 collective-permute-start.4
  24.7 18.4 %collective-permute-done.4.rest_6_.rest_15_ = bf16[208,1024]{1,0:T(8,128)(2,1)S(1)} collective-permute-done((bf16[208,1024]{1,0:T(8,128)(2,1)S(1)}, bf16[208,1024]{1,0:T(8,128)(2,1)S(1)}, u32[]{:S(2)}, u32[]{:S(2)}) %collective-permute-start.4) | collective-permute-done | bytes 426016 | tf_op jit(solution)/shard_map/ppermute | solution.py:724
  43.1 2.5 collective-permute-start.5
  46.8 10.0 %collective-permute-done.5.rest_5_.rest_14_ = bf16[208,1024]{1,0:T(8,128)(2,1)S(1)} collective-permute-done((bf16[208,1024]{1,0:T(8,128)(2,1)S(1)}, bf16[208,1024]{1,0:T(8,128)(2,1)S(1)}, u32[]{:S(2)}, u32[]{:S(2)}) %collective-permute-start.5) | collective-permute-done | bytes 426016 | tf_op jit(solution)/shard_map/ppermute | solution.py:724
  56.8 9.5 %collective-permute-start.6 = (bf16[208,1024]{1,0:T(8,128)(2,1)S(1)}, bf16[208,1024]{1,0:T(8,128)(2,1)S(1)}, u32[]{:S(2)}, u32[]{:S(2)}) collective-permute-start(bf16[208,1024]{1,0:T(8,128)(2,1)S(1)} %collective-permute-done.5.rest_5_.rest_14_), channel_id=1, source_target_pairs={{0,4},{1,5},{4,8},{5,9},{8,12},{9,13},{12,14},{13,15},{14,10},{15,... | collective-permute-start | bytes 1277960 | tf_op jit(solution)/shard_map/ppermute | solution.py:724
  67.7 15.0 %collective-permute-done.6.rest_4_.rest_13_ = bf16[208,1024]{1,0:T(8,128)(2,1)S(1)} collective-permute-done((bf16[208,1024]{1,0:T(8,128)(2,1)S(1)}, bf16[208,1024]{1,0:T(8,128)(2,1)S(1)}, u32[]{:S(2)}, u32[]{:S(2)}) %collective-permute-start.6) | collective-permute-done | bytes 426016 | tf_op jit(solution)/shard_map/ppermute | solution.py:724
  85.4 3.2 collective-permute-done.2.rest_3_.rest_12_
  90.0 2.1 collective-permute-start.18
  96.8 13.9 %shard_map.298 = (bf16[1024,1024]{1,0:T(8,128)(2,1)}, bf16[1024,1024]{1,0:T(8,128)(2,1)}, bf16[1024,1024]{1,0:T(8,128)(2,1)}, bf16[1024,1024]{1,0:T(8,128)(2,1)}) custom-call(s32[16]{0:T(128)} %copy-done.81, bf16[1024,1024]{1,0:T(8,128)(2,1)} %bitcast.32, f32[8,1024]{1,0:T(8,128)} %reshape.102.norm_ref.rest_4_.rest_3_.rest_5_.rest_8_, ...), custom_call_target="tpu_custom_call" | custom-call | flops 805306368 | bytes 1310720 | tf_op jit(solution)/shard_map/pallas_call | solution.py:448
  110.6 12.8 %shard_map.299 = (bf16[1024,512]{1,0:T(8,128)(2,1)}, bf16[1024,512]{1,0:T(8,128)(2,1)}) custom-call(s32[8]{0:T(128)} %pad_add_fusion.1.win_ref, bf16[1024,1024]{1,0:T(8,128)(2,1)} %get-tuple-element.68.q_ref, bf16[1024,1024]{1,0:T(8,128)(2,1)} %get-tuple-element.69.k_ref, bf16[1024,1024]{1,0:T(8,128)(2,1)} %get-tuple-element.70.v_ref, ...), custom_call_target="tpu_custom_call" | custom-call | flops 1073741824 | bytes 655360 | tf_op jit(solution)/shard_map/pallas_call | solution.py:127
  125.3 13.0 %collective-permute-start.19 = (bf16[320,1024]{1,0:T(8,128)(2,1)S(1)}, bf16[320,1024]{1,0:T(8,128)(2,1)S(1)}, u32[]{:S(2)}, u32[]{:S(2)}) collective-permute-start(bf16[320,1024]{1,0:T(8,128)(2,1)S(1)} %broadcast_add_fusion.3), channel_id=1, source_target_pairs={{0,4},{1,5},{4,8},{5,9},{8,12},{9,13},{12,14},{13,15},{14,10},{15,... | collective-permute-start | bytes 1966088 | tf_op jit(solution)/shard_map/ppermute | solution.py:745
  138.3 12.8 %shard_map.300 = (bf16[1024,512]{1,0:T(8,128)(2,1)}, bf16[1024,512]{1,0:T(8,128)(2,1)}) custom-call(s32[8]{0:T(128)} %pad_add_fusion.1.win_ref, bf16[1024,1024]{1,0:T(8,128)(2,1)} %get-tuple-element.68.q_ref, bf16[1024,1024]{1,0:T(8,128)(2,1)} %get-tuple-element.69.k_ref, bf16[1024,1024]{1,0:T(8,128)(2,1)} %get-tuple-element.70.v_ref, ...), custom_call_target="tpu_custom_call" | custom-call | flops 1073741824 | bytes 655360 | tf_op jit(solution)/shard_map/pallas_call | solution.py:127
  153.1 10.6 %collective-permute-done.19.rest_11_.rest_10_.rest_12_ = bf16[320,1024]{1,0:T(8,128)(2,1)S(1)} collective-permute-done((bf16[320,1024]{1,0:T(8,128)(2,1)S(1)}, bf16[320,1024]{1,0:T(8,128)(2,1)S(1)}, u32[]{:S(2)}, u32[]{:S(2)}) %collective-permute-start.19) | collective-permute-done | bytes 655392 | tf_op jit(solution)/shard_map/ppermute | solution.py:745
  163.7 4.1 collective-permute-start.20
  168.4 1.7 collective-permute-done.16.rest_7_.rest_6_.rest_8_
  170.2 12.8 %collective-permute-done.20.rest_10_.rest_9_.rest_11_ = bf16[320,1024]{1,0:T(8,128)(2,1)S(1)} collective-permute-done((bf16[320,1024]{1,0:T(8,128)(2,1)S(1)}, bf16[320,1024]{1,0:T(8,128)(2,1)S(1)}, u32[]{:S(2)}, u32[]{:S(2)}) %collective-permute-start.20) | collective-permute-done | bytes 655392 | tf_op jit(solution)/shard_map/ppermute | solution.py:745
  183.1 1.8 collective-permute-start.21
  185.5 1.4 collective-permute-done.17.rest_8_.rest_7_.rest_9_
  187.0 12.6 %collective-permute-done.21.rest_9_.rest_8_.rest_10_ = bf16[320,1024]{1,0:T(8,128)(2,1)S(1)} collective-permute-done((bf16[320,1024]{1,0:T(8,128)(2,1)S(1)}, bf16[320,1024]{1,0:T(8,128)(2,1)S(1)}, u32[]{:S(2)}, u32[]{:S(2)}) %collective-permute-start.21) | collective-permute-done | bytes 655392 | tf_op jit(solution)/shard_map/ppermute | solution.py:745
  200.3 1.3 collective-permute-done.26.rest_17_.rest_16_.rest_18_
  202.6 16.3 %shard_map.301 = (f32[1024,1024]{1,0:T(8,128)}, bf16[1024,1024]{1,0:T(8,128)(2,1)}, bf16[1024,1024]{1,0:T(8,128)(2,1)}, bf16[1024,1024]{1,0:T(8,128)(2,1)}, bf16[1024,1024]{1,0:T(8,128)(2,1)}) custom-call(s32[16]{0:T(128)} %copy-done.81, bf16[1024,512]{1,0:T(8,128)(2,1)} %get-tuple-element.71.rest_0_.o_ref, ...), custom_call_target="tpu_custom_call" | custom-call | flops 1073741824 | bytes 2359296 | tf_op jit(solution)/shard_map/pallas_call | solution.py:448
  218.9 23.2 %shard_map.302 = (bf16[1024,1024]{1,0:T(8,128)(2,1)}, bf16[1024,1024]{1,0:T(8,128)(2,1)}) custom-call(s32[8]{0:T(128)} %pad_add_fusion.win_ref, bf16[1024,1024]{1,0:T(8,128)(2,1)} %get-tuple-element.73.q_ref, bf16[1024,1024]{1,0:T(8,128)(2,1)} %get-tuple-element.74.k_ref, bf16[1024,1024]{1,0:T(8,128)(2,1)} %get-tuple-element.75.v_ref, ...), custom_call_target="tpu_custom_call" | custom-call | flops 2147483648 | bytes 1310720 | tf_op jit(solution)/shard_map/pallas_call | solution.py:127
  242.1 58.1 %shard_map.303 = (bf16[1024,1024]{1,0:T(8,128)(2,1)}, bf16[1024,1024]{1,0:T(8,128)(2,1)}, bf16[1024,4096]{1,0:T(8,128)(2,1)}, bf16[1024,1024]{1,0:T(8,128)(2,1)}...) custom-call(s32[16]{0:T(128)} %copy-done.81, ...), custom_call_target="tpu_custom_call" | custom-call | flops 4831838208 | bytes 4980736 | tf_op jit(solution)/shard_map/pallas_call | solution.py:448
  300.2 31.2 %shard_map.313 = bf16[16,512,1024]{2,1,0:T(8,128)(2,1)} custom-call(bf16[1024,1024]{1,0:T(8,128)(2,1)} %get-tuple-element.110.a_ref, bf16[1024,4096]{1,0:T(8,128)(2,1)} %get-tuple-element.111.du_ref, bf16[1024,4096]{1,0:T(8,128)(2,1)} %get-tuple-element.112.h_ref, bf16[1024,1024]{1,0:T(8,128)(2,1)} %get-tuple-element.113.df_ref), custom_call_target="tpu_custom_call" | custom-call | flops 2147483648 | bytes 6291456 | tf_op jit(solution)/shard_map/pallas_call | solution.py:548
  334.5 39.6 %shard_map.304 = (bf16[1024,1024]{1,0:T(8,128)(2,1)S(1)}, bf16[1024,1024]{1,0:T(8,128)(2,1)S(1)}, bf16[1024,1024]{1,0:T(8,128)(2,1)}) custom-call(s32[8]{0:T(128)S(1)} %copy-done.27, bf16[1024,1024]{1,0:T(8,128)(2,1)} %get-tuple-element.73.q_ref, bf16[1024,1024]{1,0:T(8,128)(2,1)} %get-tuple-element.74.k_ref, bf16[1024,1024]{1,0:T(8,128)(2,1)} %get-tuple-element.75.v_ref, ...), custom_call_target="tpu_custom_call" | custom-call | flops 5368709120 | bytes 2097152 | tf_op jit(solution)/shard_map/pallas_call | solution.py:212
  375.4 1.4 copy-done.1
  376.8 17.7 %shard_map.305 = (bf16[8,512,512]{2,1,0:T(8,128)(2,1)}, bf16[8,512,512]{2,1,0:T(8,128)(2,1)}) custom-call(s32[9]{0:T(128)} %pad_add_fusion.2.rank_ref, bf16[1024,1024]{1,0:T(8,128)(2,1)} %get-tuple-element.76.rest_0_.o_ref, bf16[1024,1024]{1,0:T(8,128)(2,1)} %get-tuple-element.85.rest_1_, bf16[1024,1024]{1,0:T(8,128)(2,1)} %bitcast.36, ...), custom_call_target="tpu_custom_call" | custom-call | flops 1073741824 | bytes 3145728 | tf_op jit(solution)/shard_map/pallas_call | solution.py:499
  394.5 3.5 collective-permute-start.30
  398.0 19.4 %shard_map.306 = (f32[1024,1024]{1,0:T(8,128)}, bf16[1024,1024]{1,0:T(8,128)(2,1)}, bf16[1024,1024]{1,0:T(8,128)(2,1)}, f32[1024,1024]{1,0:T(8,128)}, f32[8,1024]{1,0:T(8,128)}) custom-call(s32[16]{0:T(128)} %copy-done.81, bf16[1024,1024]{1,0:T(8,128)(2,1)} %copy-done, bf16[1024,1024]{1,0:T(8,128)(2,1)} %copy-done.1, ...), custom_call_target="tpu_custom_call" | custom-call | flops 1073741824 | bytes 3407872 | tf_op jit(solution)/shard_map/pallas_call | solution.py:448
  417.5 1.6 copy-done.2
  419.1 3.7 shard_map.307
  422.8 1.3 copy-done.7
  424.3 1.9 collective-permute-start.32
  426.2 20.2 %shard_map.308 = (bf16[1024,512]{1,0:T(8,128)(2,1)S(1)}, bf16[1024,512]{1,0:T(8,128)(2,1)S(1)}, bf16[1024,512]{1,0:T(8,128)(2,1)S(1)}) custom-call(s32[8]{0:T(128)S(1)} %copy-done.26, bf16[1024,1024]{1,0:T(8,128)(2,1)} %get-tuple-element.68.q_ref, bf16[1024,1024]{1,0:T(8,128)(2,1)} %get-tuple-element.69.k_ref, bf16[1024,1024]{1,0:T(8,128)(2,1)} %get-tuple-element.70.v_ref, ...), custom_call_target="tpu_custom_call" | custom-call | flops 2684354560 | bytes 1048576 | tf_op jit(solution)/shard_map/pallas_call | solution.py:212
  451.1 20.3 %shard_map.309 = (bf16[1024,512]{1,0:T(8,128)(2,1)S(1)}, bf16[1024,512]{1,0:T(8,128)(2,1)S(1)}, bf16[1024,512]{1,0:T(8,128)(2,1)S(1)}) custom-call(s32[8]{0:T(128)S(1)} %copy-done.26, bf16[1024,1024]{1,0:T(8,128)(2,1)} %get-tuple-element.68.q_ref, bf16[1024,1024]{1,0:T(8,128)(2,1)} %get-tuple-element.69.k_ref, bf16[1024,1024]{1,0:T(8,128)(2,1)} %get-tuple-element.70.v_ref, ...), custom_call_target="tpu_custom_call" | custom-call | flops 2684354560 | bytes 1048576 | tf_op jit(solution)/shard_map/pallas_call | solution.py:212
  475.4 17.0 %shard_map.310 = (bf16[8,512,512]{2,1,0:T(8,128)(2,1)}, bf16[8,512,512]{2,1,0:T(8,128)(2,1)}) custom-call(s32[9]{0:T(128)} %get-tuple-element.154.rank_ref, bf16[1024,512]{1,0:T(8,128)(2,1)} %get-tuple-element.71.rest_0_.o_ref, bf16[1024,512]{1,0:T(8,128)(2,1)} %get-tuple-element.72.rest_1_.o_ref, bf16[1024,1024]{1,0:T(8,128)(2,1)} %get-tuple-element.102.rest_2_, ...), custom_call_target="tpu_custom_call" | custom-call | flops 1073741824 | bytes 3145728 | tf_op jit(solution)/shard_map/pallas_call | solution.py:499
  492.4 16.3 %shard_map.311 = (f32[1024,1024]{1,0:T(8,128)}, f32[8,1024]{1,0:T(8,128)}) custom-call(s32[16]{0:T(128)} %copy-done.81, bf16[1024,512]{1,0:T(8,128)(2,1)} %copy-done.6, bf16[1024,512]{1,0:T(8,128)(2,1)} %copy-done.16, bf16[1024,512]{1,0:T(8,128)(2,1)} %copy-done.14, bf16[1024,512]{1,0:T(8,128)(2,1)} %copy-done.17, bf16[1024,512]{1,0:T(8,128)(2,1)} %copy-done.15, ...), custom_call_target="tpu_custom_call" | custom-call | flops 805306368 | bytes 2097152 | tf_op jit(solution)/shard_map/pallas_call | solution.py:448
  508.7 2.0 copy-done.28
  510.8 2.5 shard_map.312
  517.2 2.0 shard_map.314
  520.3 10.7 %collective-permute-start.34 = (bf16[512,512]{1,0:T(8,128)(2,1)S(1)}, bf16[512,512]{1,0:T(8,128)(2,1)S(1)}, u32[]{:S(2)}, u32[]{:S(2)}) collective-permute-start(bf16[512,512]{1,0:T(8,128)(2,1)S(1)} %copy-done.24), channel_id=1, source_target_pairs={{4,0},{5,1},{8,4},{9,5},{12,8},{13,9},{14,12},{15,13},{10,14},{11,... | collective-permute-start | bytes 1572872 | tf_op jit(solution)/shard_map/ppermute | solution.py:788
  531.4 1.9 collective-permute-start.37
  533.3 15.6 %collective-permute-done.37 = f32[8,1024]{1,0:T(8,128)S(1)} collective-permute-done((f32[8,1024]{1,0:T(8,128)S(1)}, f32[8,1024]{1,0:T(8,128)S(1)}, u32[]{:S(2)}, u32[]{:S(2)}) %collective-permute-start.37) | collective-permute-done | bytes 32800 | tf_op jit(solution)/shard_map/ppermute | solution.py:836
  549.6 2.0 collective-permute-done.35.rest_3_
  552.4 2.8 shard_map.315
  555.2 3.8 collective-permute-start.39
  559.1 2.3 collective-permute-start.50
  561.9 12.1 %collective-permute-done.41 = f32[8,1024]{1,0:T(8,128)S(1)} collective-permute-done((f32[8,1024]{1,0:T(8,128)S(1)}, f32[8,1024]{1,0:T(8,128)S(1)}, u32[]{:S(2)}, u32[]{:S(2)}) %collective-permute-start.41) | collective-permute-done | bytes 32800 | tf_op jit(solution)/shard_map/ppermute | solution.py:836
  574.0 2.6 collective-permute-start.43
  576.6 3.1 collective-permute-done.43
  581.9 2.8 shard_map.316
  584.7 1.9 collective-permute-start.44
  586.6 2.4 collective-permute-start.45
  589.0 1.9 collective-permute-done.45
  591.0 14.5 %collective-permute-done.44.rest_0_ = bf16[512,512]{1,0:T(8,128)(2,1)S(1)} collective-permute-done((bf16[512,512]{1,0:T(8,128)(2,1)}, bf16[512,512]{1,0:T(8,128)(2,1)S(1)}, u32[]{:S(2)}, u32[]{:S(2)}) %collective-permute-start.44) | collective-permute-done | bytes 524320 | tf_op jit(solution)/shard_map/ppermute | solution.py:788
  606.3 2.1 shard_map.317
  609.6 8.3 %collective-permute-done.46 = bf16[512,512]{1,0:T(8,128)(2,1)S(1)} collective-permute-done((bf16[512,512]{1,0:T(8,128)(2,1)}, bf16[512,512]{1,0:T(8,128)(2,1)S(1)}, u32[]{:S(2)}, u32[]{:S(2)}) %collective-permute-start.46) | collective-permute-done | bytes 524320 | tf_op jit(solution)/shard_map/ppermute | solution.py:788
  617.9 1.5 fusion.1
  619.3 2.1 collective-permute-start.48
  623.6 7.8 %collective-permute-done.48 = bf16[512,512]{1,0:T(8,128)(2,1)S(1)} collective-permute-done((bf16[512,512]{1,0:T(8,128)(2,1)S(1)}, bf16[512,512]{1,0:T(8,128)(2,1)S(1)}, u32[]{:S(2)}, u32[]{:S(2)}) %collective-permute-start.48) | collective-permute-done | bytes 524320 | tf_op jit(solution)/shard_map/ppermute | solution.py:762
  632.4 2.0 collective-permute-start.49
  636.5 2.4 collective-permute-done.49
  (322 shorter events, 54.0 us)
Async XLA Ops:
  7.3 234.9 %all-gather.2.cloned.1.call-start = ((), (), s32[]{:S(2)}) async-start(), calls=%async_computation.2 | async-start | bytes 17301504 | tf_op jit(solution)/shard_map/all_gather | solution.py:892
  8.7 37.9 %copy-start.82 = (s32[1,1024]{1,0:T(1,128)S(1)}, s32[1,1024]{1,0:T(1,128)}, u32[]{:S(2)}) copy-start(s32[1,1024]{1,0:T(1,128)} %param.22) | copy-start | bytes 12292
  8.7 74.8 %copy-start.76 = (bf16[64,1024]{1,0:T(8,128)(2,1)S(1)}, bf16[64,1024]{1,0:T(8,128)(2,1)}, u32[]{:S(2)}) copy-start(bf16[64,1024]{1,0:T(8,128)(2,1)} %param.30) | copy-start | bytes 393220
  9.7 504.0 %reduce-scatter.3.cloned.1.call-start = ((), (), s32[]{:S(2)}) async-start(), calls=%async_computation.3 | async-start | bytes 17825792 | tf_op jit(solution)/shard_map/reduce_scatter | solution.py:961
  9.9 86.8 %copy-start.45 = (bf16[208,1024]{1,0:T(8,128)(2,1)}, bf16[208,1024]{1,0:T(8,128)(2,1)S(1)}, u32[]{:S(2)}) copy-start(bf16[208,1024]{1,0:T(8,128)(2,1)S(1)} %fusion.3.rest_0_.rest_9_) | copy-start | bytes 1277956
  9.9 12.8 %collective-permute-start.3 = (bf16[208,1024]{1,0:T(8,128)(2,1)S(1)}, bf16[208,1024]{1,0:T(8,128)(2,1)S(1)}, u32[]{:S(2)}, u32[]{:S(2)}) collective-permute-start(bf16[208,1024]{1,0:T(8,128)(2,1)S(1)} %fusion.3.rest_0_.rest_9_), channel_id=1, source_target_pairs={{0,4},{1,5},{4,8},{5,9},{8,12},{9,13},{12,14},{13,15},{14,10},{15,... | collective-permute-start | bytes 1277960 | tf_op jit(solution)/shard_map/ppermute | solution.py:724
  13.0 32.6 %collective-permute-start = (bf16[208,1024]{1,0:T(8,128)(2,1)S(1)}, bf16[208,1024]{1,0:T(8,128)(2,1)S(1)}, u32[]{:S(2)}, u32[]{:S(2)}) collective-permute-start(bf16[208,1024]{1,0:T(8,128)(2,1)S(1)} %fusion.3.rest_0_.rest_9_), channel_id=1, source_target_pairs={{4,0},{5,1},{8,4},{9,5},{12,8},{13,9},{14,12},{15,13},{10,14},{11,... | collective-permute-start | bytes 1277960 | tf_op jit(solution)/shard_map/ppermute | solution.py:727
  13.0 71.7 %collective-permute-start.7 = (bf16[208,1024]{1,0:T(8,128)(2,1)S(1)}, bf16[208,1024]{1,0:T(8,128)(2,1)S(1)}, u32[]{:S(2)}, u32[]{:S(2)}) collective-permute-start(bf16[208,1024]{1,0:T(8,128)(2,1)S(1)} %fusion.3.rest_0_.rest_9_), channel_id=1, source_target_pairs={{0,1},{1,0},{2,3},{3,2},{4,5},{5,4},{6,7},{7,6},{8,9},{9,8},{10,11... | collective-permute-start | bytes 1277960 | tf_op jit(solution)/shard_map/ppermute | solution.py:729
  22.8 74.0 %copy-start.46 = (bf16[208,1024]{1,0:T(8,128)(2,1)}, bf16[208,1024]{1,0:T(8,128)(2,1)S(1)}, u32[]{:S(2)}) copy-start(bf16[208,1024]{1,0:T(8,128)(2,1)S(1)} %collective-permute-done.3.rest_7_.rest_16_) | copy-start | bytes 1277956
  22.8 20.3 %collective-permute-start.4 = (bf16[208,1024]{1,0:T(8,128)(2,1)S(1)}, bf16[208,1024]{1,0:T(8,128)(2,1)S(1)}, u32[]{:S(2)}, u32[]{:S(2)}) collective-permute-start(bf16[208,1024]{1,0:T(8,128)(2,1)S(1)} %collective-permute-done.3.rest_7_.rest_16_), channel_id=1, source_target_pairs={{0,4},{1,5},{4,8},{5,9},{8,12},{9,13},{12,14},{13,15},{14,10},{15,... | collective-permute-start | bytes 1277960 | tf_op jit(solution)/shard_map/ppermute | solution.py:724
  43.1 50.9 %copy-start.49 = (bf16[208,1024]{1,0:T(8,128)(2,1)}, bf16[208,1024]{1,0:T(8,128)(2,1)S(1)}, u32[]{:S(2)}) copy-start(bf16[208,1024]{1,0:T(8,128)(2,1)S(1)} %collective-permute-done.4.rest_6_.rest_15_) | copy-start | bytes 1277956
  43.1 13.7 %collective-permute-start.5 = (bf16[208,1024]{1,0:T(8,128)(2,1)S(1)}, bf16[208,1024]{1,0:T(8,128)(2,1)S(1)}, u32[]{:S(2)}, u32[]{:S(2)}) collective-permute-start(bf16[208,1024]{1,0:T(8,128)(2,1)S(1)} %collective-permute-done.4.rest_6_.rest_15_), channel_id=1, source_target_pairs={{0,4},{1,5},{4,8},{5,9},{8,12},{9,13},{12,14},{13,15},{14,10},{15,... | collective-permute-start | bytes 1277960 | tf_op jit(solution)/shard_map/ppermute | solution.py:724
  45.6 48.3 %copy-start.47 = (bf16[208,1024]{1,0:T(8,128)(2,1)}, bf16[208,1024]{1,0:T(8,128)(2,1)S(1)}, u32[]{:S(2)}) copy-start(bf16[208,1024]{1,0:T(8,128)(2,1)S(1)} %collective-permute-done.rest_1_.rest_10_) | copy-start | bytes 1277956
  45.6 22.1 %collective-permute-start.1 = (bf16[208,1024]{1,0:T(8,128)(2,1)S(1)}, bf16[208,1024]{1,0:T(8,128)(2,1)S(1)}, u32[]{:S(2)}, u32[]{:S(2)}) collective-permute-start(bf16[208,1024]{1,0:T(8,128)(2,1)S(1)} %collective-permute-done.rest_1_.rest_10_), channel_id=1, source_target_pairs={{4,0},{5,1},{8,4},{9,5},{12,8},{13,9},{14,12},{15,13},{10,14},{11,... | collective-permute-start | bytes 1277960 | tf_op jit(solution)/shard_map/ppermute | solution.py:727
  56.8 37.3 %copy-start.50 = (bf16[208,1024]{1,0:T(8,128)(2,1)}, bf16[208,1024]{1,0:T(8,128)(2,1)S(1)}, u32[]{:S(2)}) copy-start(bf16[208,1024]{1,0:T(8,128)(2,1)S(1)} %collective-permute-done.5.rest_5_.rest_14_) | copy-start | bytes 1277956
  56.8 26.0 %collective-permute-start.6 = (bf16[208,1024]{1,0:T(8,128)(2,1)S(1)}, bf16[208,1024]{1,0:T(8,128)(2,1)S(1)}, u32[]{:S(2)}, u32[]{:S(2)}) collective-permute-start(bf16[208,1024]{1,0:T(8,128)(2,1)S(1)} %collective-permute-done.5.rest_5_.rest_14_), channel_id=1, source_target_pairs={{0,4},{1,5},{4,8},{5,9},{8,12},{9,13},{12,14},{13,15},{14,10},{15,... | collective-permute-start | bytes 1277960 | tf_op jit(solution)/shard_map/ppermute | solution.py:724
  67.2 18.1 %collective-permute-start.8 = (bf16[208,1024]{1,0:T(8,128)(2,1)S(1)}, bf16[208,1024]{1,0:T(8,128)(2,1)S(1)}, u32[]{:S(2)}, u32[]{:S(2)}) collective-permute-start(bf16[208,1024]{1,0:T(8,128)(2,1)S(1)} %collective-permute-done.rest_1_.rest_10_), channel_id=1, source_target_pairs={{0,1},{1,0},{2,3},{3,2},{4,5},{5,4},{6,7},{7,6},{8,9},{9,8},{10,11... | collective-permute-start | bytes 1277960 | tf_op jit(solution)/shard_map/ppermute | solution.py:729
  67.2 21.5 %collective-permute-start.14 = (bf16[208,1024]{1,0:T(8,128)(2,1)S(1)}, bf16[208,1024]{1,0:T(8,128)(2,1)S(1)}, u32[]{:S(2)}, u32[]{:S(2)}) collective-permute-start(bf16[208,1024]{1,0:T(8,128)(2,1)S(1)} %collective-permute-done.3.rest_7_.rest_16_), channel_id=1, source_target_pairs={{0,1},{1,0},{2,3},{3,2},{4,5},{5,4},{6,7},{7,6},{8,9},{9,8},{10,11... | collective-permute-start | bytes 1277960 | tf_op jit(solution)/shard_map/ppermute | solution.py:729
  67.7 20.9 %collective-permute-start.2 = (bf16[208,1024]{1,0:T(8,128)(2,1)S(1)}, bf16[208,1024]{1,0:T(8,128)(2,1)S(1)}, u32[]{:S(2)}, u32[]{:S(2)}) collective-permute-start(bf16[208,1024]{1,0:T(8,128)(2,1)S(1)} %collective-permute-done.1.rest_2_.rest_11_), channel_id=1, source_target_pairs={{4,0},{5,1},{8,4},{9,5},{12,8},{13,9},{14,12},{15,13},{10,14},{11,... | collective-permute-start | bytes 1277960 | tf_op jit(solution)/shard_map/ppermute | solution.py:727
  82.8 7.2 %collective-permute-start.9 = (bf16[208,1024]{1,0:T(8,128)(2,1)S(1)}, bf16[208,1024]{1,0:T(8,128)(2,1)S(1)}, u32[]{:S(2)}, u32[]{:S(2)}) collective-permute-start(bf16[208,1024]{1,0:T(8,128)(2,1)S(1)} %collective-permute-done.1.rest_2_.rest_11_), channel_id=1, source_target_pairs={{0,1},{1,0},{2,3},{3,2},{4,5},{5,4},{6,7},{7,6},{8,9},{9,8},{10,11... | collective-permute-start | bytes 1277960 | tf_op jit(solution)/shard_map/ppermute | solution.py:729
  83.5 84.4 %copy-start.29 = (bf16[320,1024]{1,0:T(8,128)(2,1)}, bf16[320,1024]{1,0:T(8,128)(2,1)S(1)}, u32[]{:S(2)}) copy-start(bf16[320,1024]{1,0:T(8,128)(2,1)S(1)} %constant_dynamic-update-slice_fusion.rest_5_.rest_4_.rest_6_) | copy-start | bytes 1966084
  84.7 9.2 %collective-permute-start.13 = (bf16[208,1024]{1,0:T(8,128)(2,1)S(1)}, bf16[208,1024]{1,0:T(8,128)(2,1)S(1)}, u32[]{:S(2)}, u32[]{:S(2)}) collective-permute-start(bf16[208,1024]{1,0:T(8,128)(2,1)S(1)} %collective-permute-done.4.rest_6_.rest_15_), channel_id=1, source_target_pairs={{0,1},{1,0},{2,3},{3,2},{4,5},{5,4},{6,7},{7,6},{8,9},{9,8},{10,11... | collective-permute-start | bytes 1277960 | tf_op jit(solution)/shard_map/ppermute | solution.py:729
  85.3 8.8 %collective-permute-start.12 = (bf16[208,1024]{1,0:T(8,128)(2,1)S(1)}, bf16[208,1024]{1,0:T(8,128)(2,1)S(1)}, u32[]{:S(2)}, u32[]{:S(2)}) collective-permute-start(bf16[208,1024]{1,0:T(8,128)(2,1)S(1)} %collective-permute-done.5.rest_5_.rest_14_), channel_id=1, source_target_pairs={{0,1},{1,0},{2,3},{3,2},{4,5},{5,4},{6,7},{7,6},{8,9},{9,8},{10,11... | collective-permute-start | bytes 1277960 | tf_op jit(solution)/shard_map/ppermute | solution.py:729
  88.6 5.5 collective-permute-start.10
  88.7 5.5 collective-permute-start.11
  90.0 35.3 %collective-permute-start.18 = (bf16[320,1024]{1,0:T(8,128)(2,1)}, bf16[320,1024]{1,0:T(8,128)(2,1)S(1)}, u32[]{:S(2)}, u32[]{:S(2)}) collective-permute-start(bf16[320,1024]{1,0:T(8,128)(2,1)} %broadcast_add_fusion.5), channel_id=1, source_target_pairs={{0,4},{1,5},{4,8},{5,9},{8,12},{9,13},{12,14},{13,15},{14,10},{15,... | collective-permute-start | bytes 1966088 | tf_op jit(solution)/shard_map/ppermute | solution.py:745
  94.0 59.0 %collective-permute-start.15 = (bf16[320,1024]{1,0:T(8,128)(2,1)}, bf16[320,1024]{1,0:T(8,128)(2,1)S(1)}, u32[]{:S(2)}, u32[]{:S(2)}) collective-permute-start(bf16[320,1024]{1,0:T(8,128)(2,1)} %broadcast_add_fusion.5), channel_id=1, source_target_pairs={{4,0},{5,1},{8,4},{9,5},{12,8},{13,9},{14,12},{15,13},{10,14},{11,... | collective-permute-start | bytes 1966088 | tf_op jit(solution)/shard_map/ppermute | solution.py:749
  125.3 43.1 %copy-start.30 = (bf16[320,1024]{1,0:T(8,128)(2,1)}, bf16[320,1024]{1,0:T(8,128)(2,1)S(1)}, u32[]{:S(2)}) copy-start(bf16[320,1024]{1,0:T(8,128)(2,1)S(1)} %collective-permute-done.18.rest_12_.rest_11_.rest_13_) | copy-start | bytes 1966084
  125.3 38.3 %collective-permute-start.19 = (bf16[320,1024]{1,0:T(8,128)(2,1)S(1)}, bf16[320,1024]{1,0:T(8,128)(2,1)S(1)}, u32[]{:S(2)}, u32[]{:S(2)}) collective-permute-start(bf16[320,1024]{1,0:T(8,128)(2,1)S(1)} %broadcast_add_fusion.3), channel_id=1, source_target_pairs={{0,4},{1,5},{4,8},{5,9},{8,12},{9,13},{12,14},{13,15},{14,10},{15,... | collective-permute-start | bytes 1966088 | tf_op jit(solution)/shard_map/ppermute | solution.py:745
  153.0 17.1 %collective-permute-start.16 = (bf16[320,1024]{1,0:T(8,128)(2,1)S(1)}, bf16[320,1024]{1,0:T(8,128)(2,1)S(1)}, u32[]{:S(2)}, u32[]{:S(2)}) collective-permute-start(bf16[320,1024]{1,0:T(8,128)(2,1)S(1)} %broadcast_add_fusion.4), channel_id=1, source_target_pairs={{4,0},{5,1},{8,4},{9,5},{12,8},{13,9},{14,12},{15,13},{10,14},{11,... | collective-permute-start | bytes 1966088 | tf_op jit(solution)/shard_map/ppermute | solution.py:749
  163.7 38.9 %copy-start.32 = (bf16[320,1024]{1,0:T(8,128)(2,1)}, bf16[320,1024]{1,0:T(8,128)(2,1)S(1)}, u32[]{:S(2)}) copy-start(bf16[320,1024]{1,0:T(8,128)(2,1)S(1)} %collective-permute-done.19.rest_11_.rest_10_.rest_12_) | copy-start | bytes 1966084
  163.7 19.3 %collective-permute-start.20 = (bf16[320,1024]{1,0:T(8,128)(2,1)S(1)}, bf16[320,1024]{1,0:T(8,128)(2,1)S(1)}, u32[]{:S(2)}, u32[]{:S(2)}) collective-permute-start(bf16[320,1024]{1,0:T(8,128)(2,1)S(1)} %broadcast_add_fusion.1), channel_id=1, source_target_pairs={{0,4},{1,5},{4,8},{5,9},{8,12},{9,13},{12,14},{13,15},{14,10},{15,... | collective-permute-start | bytes 1966088 | tf_op jit(solution)/shard_map/ppermute | solution.py:745
  167.8 17.1 %collective-permute-start.22 = (bf16[320,1024]{1,0:T(8,128)(2,1)S(1)}, bf16[320,1024]{1,0:T(8,128)(2,1)S(1)}, u32[]{:S(2)}, u32[]{:S(2)}) collective-permute-start(bf16[320,1024]{1,0:T(8,128)(2,1)S(1)} %constant_dynamic-update-slice_fusion.rest_5_.rest_4_.rest_6_), channel_id=1, source_target_pairs={{0,1},{1,0},{2,3},{3,2},{4,5},{5,4},{6,7},{7,6},{8,9},{9,8},{10,11... | collective-permute-start | bytes 1966088 | tf_op jit(solution)/shard_map/ppermute | solution.py:754
  167.8 17.1 %collective-permute-start.23 = (bf16[320,1024]{1,0:T(8,128)(2,1)S(1)}, bf16[320,1024]{1,0:T(8,128)(2,1)S(1)}, u32[]{:S(2)}, u32[]{:S(2)}) collective-permute-start(bf16[320,1024]{1,0:T(8,128)(2,1)S(1)} %collective-permute-done.15.rest_6_.rest_5_.rest_7_), channel_id=1, source_target_pairs={{0,1},{1,0},{2,3},{3,2},{4,5},{5,4},{6,7},{7,6},{8,9},{9,8},{10,11... | collective-permute-start | bytes 1966088 | tf_op jit(solution)/shard_map/ppermute | solution.py:754
  168.4 17.1 %collective-permute-start.29 = (bf16[320,1024]{1,0:T(8,128)(2,1)S(1)}, bf16[320,1024]{1,0:T(8,128)(2,1)S(1)}, u32[]{:S(2)}, u32[]{:S(2)}) collective-permute-start(bf16[320,1024]{1,0:T(8,128)(2,1)S(1)} %collective-permute-done.18.rest_12_.rest_11_.rest_13_), channel_id=1, source_target_pairs={{0,1},{1,0},{2,3},{3,2},{4,5},{5,4},{6,7},{7,6},{8,9},{9,8},{10,11... | collective-permute-start | bytes 1966088 | tf_op jit(solution)/shard_map/ppermute | solution.py:754
  170.1 16.8 %collective-permute-start.17 = (bf16[320,1024]{1,0:T(8,128)(2,1)S(1)}, bf16[320,1024]{1,0:T(8,128)(2,1)S(1)}, u32[]{:S(2)}, u32[]{:S(2)}) collective-permute-start(bf16[320,1024]{1,0:T(8,128)(2,1)S(1)} %broadcast_add_fusion.2), channel_id=1, source_target_pairs={{4,0},{5,1},{8,4},{9,5},{12,8},{13,9},{14,12},{15,13},{10,14},{11,... | collective-permute-start | bytes 1966088 | tf_op jit(solution)/shard_map/ppermute | solution.py:749
  183.1 16.5 %collective-permute-start.21 = (bf16[320,1024]{1,0:T(8,128)(2,1)S(1)}, bf16[320,1024]{1,0:T(8,128)(2,1)S(1)}, u32[]{:S(2)}, u32[]{:S(2)}) collective-permute-start(bf16[320,1024]{1,0:T(8,128)(2,1)S(1)} %broadcast_add_fusion), channel_id=1, source_target_pairs={{0,4},{1,5},{4,8},{5,9},{8,12},{9,13},{12,14},{13,15},{14,10},{15,... | collective-permute-start | bytes 1966088 | tf_op jit(solution)/shard_map/ppermute | solution.py:745
  184.9 15.4 %collective-permute-start.28 = (bf16[320,1024]{1,0:T(8,128)(2,1)S(1)}, bf16[320,1024]{1,0:T(8,128)(2,1)S(1)}, u32[]{:S(2)}, u32[]{:S(2)}) collective-permute-start(bf16[320,1024]{1,0:T(8,128)(2,1)S(1)} %collective-permute-done.19.rest_11_.rest_10_.rest_12_), channel_id=1, source_target_pairs={{0,1},{1,0},{2,3},{3,2},{4,5},{5,4},{6,7},{7,6},{8,9},{9,8},{10,11... | collective-permute-start | bytes 1966088 | tf_op jit(solution)/shard_map/ppermute | solution.py:754
  184.9 15.3 %collective-permute-start.24 = (bf16[320,1024]{1,0:T(8,128)(2,1)S(1)}, bf16[320,1024]{1,0:T(8,128)(2,1)S(1)}, u32[]{:S(2)}, u32[]{:S(2)}) collective-permute-start(bf16[320,1024]{1,0:T(8,128)(2,1)S(1)} %collective-permute-done.16.rest_7_.rest_6_.rest_8_), channel_id=1, source_target_pairs={{0,1},{1,0},{2,3},{3,2},{4,5},{5,4},{6,7},{7,6},{8,9},{9,8},{10,11... | collective-permute-start | bytes 1966088 | tf_op jit(solution)/shard_map/ppermute | solution.py:754
  185.4 14.9 %collective-permute-start.27 = (bf16[320,1024]{1,0:T(8,128)(2,1)S(1)}, bf16[320,1024]{1,0:T(8,128)(2,1)S(1)}, u32[]{:S(2)}, u32[]{:S(2)}) collective-permute-start(bf16[320,1024]{1,0:T(8,128)(2,1)S(1)} %collective-permute-done.20.rest_10_.rest_9_.rest_11_), channel_id=1, source_target_pairs={{0,1},{1,0},{2,3},{3,2},{4,5},{5,4},{6,7},{7,6},{8,9},{9,8},{10,11... | collective-permute-start | bytes 1966088 | tf_op jit(solution)/shard_map/ppermute | solution.py:754
  187.0 13.4 %collective-permute-start.25 = (bf16[320,1024]{1,0:T(8,128)(2,1)S(1)}, bf16[320,1024]{1,0:T(8,128)(2,1)S(1)}, u32[]{:S(2)}, u32[]{:S(2)}) collective-permute-start(bf16[320,1024]{1,0:T(8,128)(2,1)S(1)} %collective-permute-done.17.rest_8_.rest_7_.rest_9_), channel_id=1, source_target_pairs={{0,1},{1,0},{2,3},{3,2},{4,5},{5,4},{6,7},{7,6},{8,9},{9,8},{10,11... | collective-permute-start | bytes 1966088 | tf_op jit(solution)/shard_map/ppermute | solution.py:754
  199.6 2.1 collective-permute-start.26
  331.4 300.9 %reduce-scatter.5.cloned.1.call-start = ((), (), s32[]{:S(2)}) async-start(), calls=%async_computation.4 | async-start | bytes 2359296 | tf_op jit(solution)/shard_map/reduce_scatter | solution.py:813
  394.5 23.0 %collective-permute-start.30 = (bf16[8,512,512]{2,1,0:T(8,128)(2,1)}, bf16[8,512,512]{2,1,0:T(8,128)(2,1)}, u32[]{:S(2)}, u32[]{:S(2)}) collective-permute-start(bf16[8,512,512]{2,1,0:T(8,128)(2,1)} %get-tuple-element.90), channel_id=1, source_target_pairs={{0,1},{1,0},{2,3},{3,2},{4,5},{5,4},{6,7},{7,6},{8,9},{9,8},{10,11... | collective-permute-start | bytes 12582920 | tf_op jit(solution)/shard_map/ppermute | solution.py:802
  424.1 26.0 %collective-permute-start.31 = (bf16[4,256,512]{2,1,0:T(8,128)(2,1)S(1)}, bf16[4,256,512]{2,1,0:T(8,128)(2,1)S(1)}, u32[]{:S(2)}, u32[]{:S(2)}) collective-permute-start(bf16[4,256,512]{2,1,0:T(8,128)(2,1)S(1)} %get-tuple-element.95), channel_id=1, source_target_pairs={{0,16},{16,0},{1,17},{17,1},{2,18},{18,2},{3,19},{19,3},{4,20},{20... | collective-permute-start | bytes 3145736 | tf_op jit(solution)/shard_map/ppermute | solution.py:807
  424.3 50.1 %collective-permute-start.32 = (bf16[4,256,512]{2,1,0:T(8,128)(2,1)S(1)}, bf16[4,256,512]{2,1,0:T(8,128)(2,1)S(1)}, u32[]{:S(2)}, u32[]{:S(2)}) collective-permute-start(bf16[4,256,512]{2,1,0:T(8,128)(2,1)S(1)} %get-tuple-element.103), channel_id=1, source_target_pairs={{0,16},{16,0},{1,17},{17,1},{2,18},{18,2},{3,19},{19,3},{4,20},{20... | collective-permute-start | bytes 3145736 | tf_op jit(solution)/shard_map/ppermute | solution.py:807
  492.4 16.3 %collective-permute-start.33 = (bf16[8,512,512]{2,1,0:T(8,128)(2,1)}, bf16[8,512,512]{2,1,0:T(8,128)(2,1)S(1)}, u32[]{:S(2)}, u32[]{:S(2)}) collective-permute-start(bf16[8,512,512]{2,1,0:T(8,128)(2,1)} %get-tuple-element.107), channel_id=1, source_target_pairs={{0,1},{1,0},{2,3},{3,2},{4,5},{5,4},{6,7},{7,6},{8,9},{9,8},{10,11... | collective-permute-start | bytes 12582920 | tf_op jit(solution)/shard_map/ppermute | solution.py:774
  520.3 29.3 %collective-permute-start.34 = (bf16[512,512]{1,0:T(8,128)(2,1)S(1)}, bf16[512,512]{1,0:T(8,128)(2,1)S(1)}, u32[]{:S(2)}, u32[]{:S(2)}) collective-permute-start(bf16[512,512]{1,0:T(8,128)(2,1)S(1)} %copy-done.24), channel_id=1, source_target_pairs={{4,0},{5,1},{8,4},{9,5},{12,8},{13,9},{14,12},{15,13},{10,14},{11,... | collective-permute-start | bytes 1572872 | tf_op jit(solution)/shard_map/ppermute | solution.py:788
  531.1 20.5 %collective-permute-start.35 = (bf16[512,512]{1,0:T(8,128)(2,1)S(1)}, bf16[512,512]{1,0:T(8,128)(2,1)S(1)}, u32[]{:S(2)}, u32[]{:S(2)}) collective-permute-start(bf16[512,512]{1,0:T(8,128)(2,1)S(1)} %copy-done.85), channel_id=1, source_target_pairs={{0,4},{1,5},{4,8},{5,9},{8,12},{9,13},{12,14},{13,15},{14,10},{15,... | collective-permute-start | bytes 1572872 | tf_op jit(solution)/shard_map/ppermute | solution.py:790
  531.1 2.2 collective-permute-start.36
  531.4 17.6 %collective-permute-start.37 = (f32[8,1024]{1,0:T(8,128)S(1)}, f32[8,1024]{1,0:T(8,128)S(1)}, u32[]{:S(2)}, u32[]{:S(2)}) collective-permute-start(f32[8,1024]{1,0:T(8,128)S(1)} %add_add_fusion.2), channel_id=1, source_target_pairs={{0,2},{1,3},{2,0},{3,1},{4,6},{5,7},{6,4},{7,5},{8,10},{9,11},{10,... | collective-permute-start | bytes 98312 | tf_op jit(solution)/shard_map/ppermute | solution.py:836
  533.2 15.7 %collective-permute-start.38 = (f32[8,1024]{1,0:T(8,128)S(1)}, f32[8,1024]{1,0:T(8,128)S(1)}, u32[]{:S(2)}, u32[]{:S(2)}) collective-permute-start(f32[8,1024]{1,0:T(8,128)S(1)} %add_add_fusion.2), channel_id=1, source_target_pairs={{0,3},{1,2},{2,1},{3,0},{4,7},{5,6},{6,5},{7,4},{8,11},{9,10},{10,... | collective-permute-start | bytes 98312 | tf_op jit(solution)/shard_map/ppermute | solution.py:836
  555.2 25.1 %collective-permute-start.39 = (bf16[512,512]{1,0:T(8,128)(2,1)}, bf16[512,512]{1,0:T(8,128)(2,1)S(1)}, u32[]{:S(2)}, u32[]{:S(2)}) collective-permute-start(bf16[512,512]{1,0:T(8,128)(2,1)} %get-tuple-element.117.rest_6_), channel_id=1, source_target_pairs={{4,0},{5,1},{8,4},{9,5},{12,8},{13,9},{14,12},{15,13},{10,14},{11,... | collective-permute-start | bytes 1572872 | tf_op jit(solution)/shard_map/ppermute | solution.py:788
  559.0 21.3 %collective-permute-start.40 = (bf16[512,512]{1,0:T(8,128)(2,1)}, bf16[512,512]{1,0:T(8,128)(2,1)S(1)}, u32[]{:S(2)}, u32[]{:S(2)}) collective-permute-start(bf16[512,512]{1,0:T(8,128)(2,1)} %get-tuple-element.118), channel_id=1, source_target_pairs={{0,4},{1,5},{4,8},{5,9},{8,12},{9,13},{12,14},{13,15},{14,10},{15,... | collective-permute-start | bytes 1572872 | tf_op jit(solution)/shard_map/ppermute | solution.py:790
  559.1 50.1 %collective-permute-start.50 = (bf16[512,1024]{1,0:T(8,128)(2,1)S(1)}, bf16[512,1024]{1,0:T(8,128)(2,1)S(1)}, u32[]{:S(2)}, u32[]{:S(2)}) collective-permute-start(bf16[512,1024]{1,0:T(8,128)(2,1)S(1)} %copy-done.20), channel_id=1, source_target_pairs={{0,16},{16,0},{1,17},{17,1},{2,18},{18,2},{3,19},{19,3},{4,20},{20... | collective-permute-start | bytes 3145736 | tf_op jit(solution)/shard_map/ppermute | solution.py:762
  561.4 12.7 %collective-permute-start.41 = (f32[8,1024]{1,0:T(8,128)S(1)}, f32[8,1024]{1,0:T(8,128)S(1)}, u32[]{:S(2)}, u32[]{:S(2)}) collective-permute-start(f32[8,1024]{1,0:T(8,128)S(1)} %copy-done.66), channel_id=1, source_target_pairs={{0,4},{1,5},{2,6},{3,7},{4,0},{5,1},{6,2},{7,3},{8,12},{9,13},{10,... | collective-permute-start | bytes 98312 | tf_op jit(solution)/shard_map/ppermute | solution.py:836
  561.9 14.7 %collective-permute-start.42 = (f32[8,1024]{1,0:T(8,128)S(1)}, f32[8,1024]{1,0:T(8,128)S(1)}, u32[]{:S(2)}, u32[]{:S(2)}) collective-permute-start(f32[8,1024]{1,0:T(8,128)S(1)} %copy-done.66), channel_id=1, source_target_pairs={{0,8},{1,9},{2,10},{3,11},{4,12},{5,13},{6,14},{7,15},{8,0},{9,1},... | collective-permute-start | bytes 98312 | tf_op jit(solution)/shard_map/ppermute | solution.py:836
  574.0 5.7 collective-permute-start.43
  584.7 20.8 %collective-permute-start.44 = (bf16[512,512]{1,0:T(8,128)(2,1)}, bf16[512,512]{1,0:T(8,128)(2,1)S(1)}, u32[]{:S(2)}, u32[]{:S(2)}) collective-permute-start(bf16[512,512]{1,0:T(8,128)(2,1)} %get-tuple-element.119.rest_3_), channel_id=1, source_target_pairs={{4,0},{5,1},{8,4},{9,5},{12,8},{13,9},{14,12},{15,13},{10,14},{11,... | collective-permute-start | bytes 1572872 | tf_op jit(solution)/shard_map/ppermute | solution.py:788
  586.6 4.3 collective-permute-start.45
  591.0 18.6 %collective-permute-start.47 = (bf16[512,512]{1,0:T(8,128)(2,1)}, bf16[512,512]{1,0:T(8,128)(2,1)S(1)}, u32[]{:S(2)}, u32[]{:S(2)}) collective-permute-start(bf16[512,512]{1,0:T(8,128)(2,1)} %get-tuple-element.120), channel_id=1, source_target_pairs={{0,4},{1,5},{4,8},{5,9},{8,12},{9,13},{12,14},{13,15},{14,10},{15,... | collective-permute-start | bytes 1572872 | tf_op jit(solution)/shard_map/ppermute | solution.py:790
  608.5 9.4 %collective-permute-start.46 = (bf16[512,512]{1,0:T(8,128)(2,1)}, bf16[512,512]{1,0:T(8,128)(2,1)S(1)}, u32[]{:S(2)}, u32[]{:S(2)}) collective-permute-start(bf16[512,512]{1,0:T(8,128)(2,1)} %shard_map.317), channel_id=1, source_target_pairs={{4,0},{5,1},{8,4},{9,5},{12,8},{13,9},{14,12},{15,13},{10,14},{11,... | collective-permute-start | bytes 1572872 | tf_op jit(solution)/shard_map/ppermute | solution.py:788
  619.3 12.1 %collective-permute-start.48 = (bf16[512,512]{1,0:T(8,128)(2,1)S(1)}, bf16[512,512]{1,0:T(8,128)(2,1)S(1)}, u32[]{:S(2)}, u32[]{:S(2)}) collective-permute-start(bf16[512,512]{1,0:T(8,128)(2,1)S(1)} %fusion.1), channel_id=1, source_target_pairs={{0,16},{16,0},{1,17},{17,1},{2,18},{18,2},{3,19},{19,3},{4,20},{20... | collective-permute-start | bytes 1572872 | tf_op jit(solution)/shard_map/ppermute | solution.py:762
  632.4 6.6 %collective-permute-start.49 = (bf16[256,512]{1,0:T(8,128)(2,1)}, bf16[256,512]{1,0:T(8,128)(2,1)S(1)}, u32[]{:S(2)}, u32[]{:S(2)}) collective-permute-start(bf16[256,512]{1,0:T(8,128)(2,1)} %reduce-scatter.5.cloned.1.call-done), channel_id=1, source_target_pairs={{0,16},{16,0},{1,17},{17,1},{2,18},{18,2},{3,19},{19,3},{4,20},{20... | collective-permute-start | bytes 786440 | tf_op jit(solution)/shard_map/ppermute | solution.py:817
  (76 other events, 577.1 us)
Sparse Core Ops, SparseCore 0:
  11.0 156.1 all-gather.1
  331.6 182.1 reduce-scatter.2
  519.4 86.1 reduce-scatter.4

commit v4 on v3

--- a/solution.py
+++ b/solution.py
@@ -65,6 +65,7 @@
         ka[2*g+1] = jnp.where(first, kx_ref[...], kp)
     row = lax.broadcasted_iota(jnp.int32, (128, 1), 0)
     rpart = row % 64
+    zero = jnp.zeros((1, 128), jnp.bfloat16)
 
     def one(i, W):
         rows = pl.ds(pl.multiple_of(i * bq, bq), bq)
@@ -90,18 +91,19 @@
             l = jnp.sum(p, axis=0, keepdims=True)
             inv = 1.0 / l
             if norm: p = p * inv
-            o = lax.dot_general(p.astype(jnp.bfloat16), v_ref[win, g*128:(g+1)*128], TN, preferred_element_type=jnp.float32)
-            outs.append(o); invs.append(inv)
+            vw = v_ref[win, g*128:(g+1)*128]
+            vw = jnp.where(first, vw, zero) if h % 2 == 0 else jnp.where(first, zero, vw)
+            outs.append(lax.dot_general(vw, p.astype(jnp.bfloat16), TN, preferred_element_type=jnp.float32)); invs.append(inv)
             neg = -(m + jnp.log(l))
             hi = neg.astype(jnp.bfloat16).astype(jnp.float32)
             mid = (neg - hi).astype(jnp.bfloat16).astype(jnp.float32)
             lo = neg - hi - mid
             lses.append((hi, mid, lo))
         for g in range(hp):
-            o = jnp.where(first, outs[2*g], outs[2*g+1])
+            o = outs[2*g] + outs[2*g+1]
             if not norm:
-                t = jnp.where(row < 64, invs[2*g], invs[2*g+1])
-                o = o * jnp.transpose(t)
+                o = o * jnp.where(row < 64, invs[2*g], invs[2*g+1])
+            o = jnp.transpose(o)
             o_ref[rows, g*128:(g+1)*128] = o.astype(jnp.bfloat16)
             a, b = lses[2*g], lses[2*g+1]
             e = jnp.where(row < 64, jnp.where(rpart == 8, b[0], jnp.where(rpart == 9, b[1], b[2])), jnp.where(rpart == 8, a[0], jnp.where(rpart == 9, a[1], a[2])))
@@ -117,7 +119,7 @@
 
     lax.fori_loop(0, nq, step, 0)
 
-def attend_forward(q, k, v, qx, kx, win, causal, pairs, after=(), bq=256, bk=256, hp=2):
+def attend_forward(q, k, v, qx, kx, win, causal, pairs, after=(), bq=256, bk=256, hp=4):
     L, N = q.shape[0], k.shape[0]
     w = 128 * hp
     start, number = pairs[0] // hp, (pairs[1] - pairs[0]) // hp
@@ -141,7 +143,7 @@
     )(win, q, k, v, qx, kx, *after)
 
 
-def attend_backward_kernel(bq, bk, causal, win_ref, q_ref, k_ref, v_ref, o_ref, do_ref, qe_ref, kx_ref, *rest):
+def attend_backward_kernel(bq, bk, causal, hp, win_ref, q_ref, k_ref, v_ref, o_ref, do_ref, qe_ref, kx_ref, *rest):
     dq_ref, dk_ref, dv_ref, ka, va, dka, dva = rest[-7:]
     L, N = q_ref.shape[0], k_ref.shape[0]
     nq = L // bq
@@ -149,10 +151,12 @@
     first = lane < 64
     part = lane % 64
     ones = jnp.broadcast_to(jnp.where(part < 3, 1.0, 0.0).astype(jnp.bfloat16), (N, 128))
-    ka[0] = jnp.where(first, k_ref[...], kx_ref[...])
-    ka[1] = jnp.where(first, kx_ref[...], k_ref[...])
-    va[0] = jnp.where(first, v_ref[...], ones)
-    va[1] = jnp.where(first, ones, v_ref[...])
+    for g in range(hp):
+        c = slice(g*128,(g+1)*128)
+        ka[2*g] = jnp.where(first, k_ref[:, c], kx_ref[...])
+        ka[2*g+1] = jnp.where(first, kx_ref[...], k_ref[:, c])
+        va[2*g] = jnp.where(first, v_ref[:, c], ones)
+        va[2*g+1] = jnp.where(first, ones, v_ref[:, c])
     dka[...] = jnp.zeros_like(dka)
     dva[...] = jnp.zeros_like(dva)
     zero = jnp.zeros((1, 128), jnp.bfloat16)
@@ -160,35 +164,46 @@
     def one(i, W):
         rows = pl.ds(pl.multiple_of(i * bq, bq), bq)
         win = pl.ds(pl.multiple_of(win_ref[i], 16), W)
-        qb, xb, dob = q_ref[rows, :], qe_ref[rows, :], do_ref[rows, :]
-        prod = dob.astype(jnp.float32) * o_ref[rows, :].astype(jnp.float32)
-        ps, dss = [], []
-        for h in range(2):
-            mine = first if h == 0 else jnp.logical_not(first)
-            neg = -jnp.sum(jnp.where(mine, prod, 0.0), axis=1, keepdims=True)
-            hi = neg.astype(jnp.bfloat16).astype(jnp.float32)
-            mid = (neg - hi).astype(jnp.bfloat16).astype(jnp.float32)
-            lo = neg - hi - mid
-            de = jnp.where(part == 0, hi, jnp.where(part == 1, mid, jnp.where(part == 2, lo, 0.0))).astype(jnp.bfloat16)
-            qa = jnp.where(mine, qb, xb)
-            da = jnp.where(mine, dob, de)
-            s = lax.dot_general(ka[h, win, :], qa, NT, preferred_element_type=jnp.float32)
-            if causal:
-                tri = lax.broadcasted_iota(jnp.int32, (bq, bq), 0) <= lax.broadcasted_iota(jnp.int32, (bq, bq), 1)
-                d = jnp.where(tri, s[W - bq:, :], -BIG)
-                s = d if W == bq else jnp.concatenate([s[: W - bq, :], d], axis=0)
-            p = jnp.exp(s)
-            dp = lax.dot_general(va[h, win, :], da, NT, preferred_element_type=jnp.float32)
-            dss.append((p * dp).astype(jnp.bfloat16))
-            ps.append(p.astype(jnp.bfloat16))
-        docat = jnp.concatenate([jnp.where(first, dob, zero), jnp.where(first, zero, dob)], axis=0)
-        qcat = jnp.concatenate([jnp.where(first, qb, zero), jnp.where(first, zero, qb)], axis=0)
-        dva[win, :] += jnp.dot(jnp.concatenate(ps, axis=1), docat, preferred_element_type=jnp.float32)
-        dka[win, :] += jnp.dot(jnp.concatenate(dss, axis=1), qcat, preferred_element_type=jnp.float32)
-        kw = k_ref[win, :]
-        dq0 = lax.dot_general(dss[0], kw, TN, preferred_element_type=jnp.float32)
-        dq1 = lax.dot_general(dss[1], kw, TN, preferred_element_type=jnp.float32)
-        dq_ref[rows, :] = (jnp.where(first, dq0, dq1) * 0.125).astype(jnp.bfloat16)
+        S = []
+        for g in range(hp):
+            c = slice(g*128,(g+1)*128)
+            qb, xb, dob = q_ref[rows, c], qe_ref[rows, c], do_ref[rows, c]
+            prod = dob.astype(jnp.float32) * o_ref[rows, c].astype(jnp.float32)
+            for h in range(2):
+                mine = first if h == 0 else jnp.logical_not(first)
+                neg = -jnp.sum(jnp.where(mine, prod, 0.0), axis=1, keepdims=True)
+                hi = neg.astype(jnp.bfloat16).astype(jnp.float32)
+                mid = (neg - hi).astype(jnp.bfloat16).astype(jnp.float32)
+                lo = neg - hi - mid
+                de = jnp.where(part == 0, hi, jnp.where(part == 1, mid, jnp.where(part == 2, lo, 0.0))).astype(jnp.bfloat16)
+                qa = jnp.where(mine, qb, xb)
+                da = jnp.where(mine, dob, de)
+                s = lax.dot_general(ka[2*g+h, win, :], qa, NT, preferred_element_type=jnp.float32)
+                dp = lax.dot_general(va[2*g+h, win, :], da, NT, preferred_element_type=jnp.float32)
+                S.append((s, dp))
+        for g in range(hp):
+            c = slice(g*128,(g+1)*128)
+            qb, dob = q_ref[rows, c], do_ref[rows, c]
+            ps, dss = [], []
+            for h in range(2):
+                s, dp = S[2*g+h]
+                if causal:
+                    tri = lax.broadcasted_iota(jnp.int32, (bq, bq), 0) <= lax.broadcasted_iota(jnp.int32, (bq, bq), 1)
+                    d = jnp.where(tri, s[W - bq:, :], -BIG)
+                    s = d if W == bq else jnp.concatenate([s[: W - bq, :], d], axis=0)
+                p = jnp.exp(s)
+                dss.append((p * dp).astype(jnp.bfloat16))
+                ps.append(p.astype(jnp.bfloat16))
+            docat = jnp.concatenate([jnp.where(first, dob, zero), jnp.where(first, zero, dob)], axis=0)
+            qcat = jnp.concatenate([jnp.where(first, qb, zero), jnp.where(first, zero, qb)], axis=0)
+            dva[win, c] += jnp.dot(jnp.concatenate(ps, axis=1), docat, preferred_element_type=jnp.float32)
+            dka[win, c] += jnp.dot(jnp.concatenate(dss, axis=1), qcat, preferred_element_type=jnp.float32)
+            kw = k_ref[win, c]
+            k0, k1 = jnp.where(first, kw, zero), jnp.where(first, zero, kw)
+            turned = lax.dot_general(k0, dss[0], TN, preferred_element_type=jnp.float32)
+            turned = turned + lax.dot_general(k1, dss[1], TN, preferred_element_type=jnp.float32)
+            dq = jnp.transpose(turned)
+            dq_ref[rows, c] = (dq * 0.125).astype(jnp.bfloat16)
 
     def step(i, c):
         for j in range(1, N // bk + 1):
@@ -201,29 +216,29 @@
     dk_ref[...] = dka[...].astype(jnp.bfloat16)
     dv_ref[...] = dva[...].astype(jnp.bfloat16)
 
-
-def attend_backward(q, k, v, o, do, qe, kx, win, causal, pairs, base=0, after=(), bq=256, bk=256):
+def attend_backward(q, k, v, o, do, qe, kx, win, causal, pairs, base=0, after=(), bq=256, bk=256, hp=2):
     L, N = q.shape[0], k.shape[0]
-    start, number = pairs[0], pairs[1] - pairs[0]
-    col = lambda n: pl.BlockSpec((n, 128), lambda p, _: (0, start + p))
-    own = lambda n: pl.BlockSpec((n, 128), lambda p, _: (0, p))
-    held = pl.BlockSpec((L, 128), lambda p, _: (0, start - base + p))
+    w = 128 * hp
+    start, number, base = pairs[0] // hp, (pairs[1] - pairs[0]) // hp, base // hp
+    col = lambda n: pl.BlockSpec((n, w), lambda p, _: (0, start + p))
+    own = lambda n: pl.BlockSpec((n, w), lambda p, _: (0, p))
+    held = pl.BlockSpec((L, w), lambda p, _: (0, start - base + p))
     fix = lambda n: pl.BlockSpec((n, 128), lambda p, _: (0, 0))
     return pl.pallas_call(
-        functools.partial(attend_backward_kernel, bq, bk, causal),
+        functools.partial(attend_backward_kernel, bq, bk, causal, hp),
         grid_spec=pltpu.PrefetchScalarGridSpec(
             num_scalar_prefetch=1,
             grid=(number,),
             in_specs=[col(L), col(N), col(N), held, col(L), held, fix(N)]
             + [pl.BlockSpec(memory_space=pl.ANY)] * len(after),
             out_specs=[own(L), own(N), own(N)],
-            scratch_shapes=[pltpu.VMEM((2, N, 128), jnp.bfloat16)] * 2 + [pltpu.VMEM((N, 128), jnp.float32)] * 2,
+            scratch_shapes=[pltpu.VMEM((2 * hp, N, 128), jnp.bfloat16)] * 2 + [pltpu.VMEM((N, w), jnp.float32)] * 2,
         ),
-        out_shape=[jax.ShapeDtypeStruct((L, number * 128), jnp.bfloat16)]
-        + [jax.ShapeDtypeStruct((N, number * 128), jnp.bfloat16)] * 2,
-        compiler_params=pltpu.CompilerParams(vmem_limit_bytes=48 << 20),
+        out_shape=[jax.ShapeDtypeStruct((L, number * w), jnp.bfloat16)]
+        + [jax.ShapeDtypeStruct((N, number * w), jnp.bfloat16)] * 2,
+        compiler_params=pltpu.CompilerParams(vmem_limit_bytes=58 << 20),
         cost_estimate=estimate(
-            flops=COST * 5 * 2 * L * N * number * 128, bytes_accessed=16 * L * number * 128, transcendentals=0
+            flops=COST * 5 * 2 * L * N * number * w, bytes_accessed=16 * L * number * w, transcendentals=0
         ),
     )(win, q, k, v, o, do, qe, kx, *after)
 
@@ -381,20 +396,18 @@
     do_ref[...] = low(mm_back(dc, wc[...]))
 
 
-def fourth_kernel(plans, n_refs, n_g, order_ref, *rest):
-    dq_refs, dk_refs, dv_refs = (rest[i * n_g : (i + 1) * n_g] for i in range(3))
-    (r_ref, dr_ref, norm_ref), rest = rest[3 * n_g : 3 * n_g + 3], rest[3 * n_g + 3 :]
-    refs, (dx_ref, dc_ref, do_ref, de_ref, term_ref, w, sem) = rest[:n_refs], rest[-7:]
+def fourth_kernel(plans, n_refs, order_ref, dq_ref, r_ref, dr_ref, norm_ref, *rest):
+    refs, (dx_ref, dc_ref, do_ref, term_ref, w, sem) = rest[:n_refs], rest[-6:]
 
     @pl.when(pl.program_id(0) == 0)
     def _():
-        for i in range(4):
+        for i in range(2):
             fetch(plans[i], refs, order_ref, w.at[i], sem.at[i])
-        for i in range(4):
+        for i in range(2):
             arrived(w.at[i], sem.at[i])
         term_ref[...] = jnp.zeros_like(term_ref)
 
-    da = mm_back(joined(dq_refs), w[1])
+    da = mm_back(dq_ref[...], w[1])
     unit, scale = normed(r_ref[...])
     term_rows(term_ref, 1, da * unit)
     term_rows(term_ref, 5, da)
@@ -403,7 +416,19 @@
     dc = low(dx)
     dc_ref[...] = dc
     do_ref[...] = low(mm_back(dc, w[0]))
-    de_ref[...] = mm_back(joined(dk_refs), w[2]) + mm_back(joined(dv_refs), w[3])
+
+
+def enc_kernel(plans, n_refs, order_ref, dk_ref, dv_ref, norm_ref, *rest):
+    refs, (de_ref, w, sem) = rest[:n_refs], rest[-3:]
+
+    @pl.when(pl.program_id(0) == 0)
+    def _():
+        for i in range(2):
+            fetch(plans[i], refs, order_ref, w.at[i], sem.at[i])
+        for i in range(2):
+            arrived(w.at[i], sem.at[i])
+
+    de_ref[...] = mm_back(dk_ref[...], w[0]) + mm_back(dv_ref[...], w[1])
 
 
 def fifth_kernel(plans, n_refs, n_g, order_ref, *rest):
@@ -463,13 +488,20 @@
     )(order, *row_inputs, norms, *piece_refs)
 
 
-def term_kernel(names, chips, n_left, n_right, rank_ref, *rest):
+def term_kernel(names, chips, n_left, n_right, n_extra, rank_ref, *rest):
     parts = len(names)
+    extra, rest = rest[:n_extra], rest[n_extra:]
     flat, rest = rest[: sum(n_left)], rest[sum(n_left) :]
     lefts = [flat[sum(n_left[:i]) : sum(n_left[: i + 1])] for i in range(len(n_left))]
     rights = [rest[sum(n_right[:i]) : sum(n_right[: i + 1])] for i in range(parts)]
     mine_ref, other_ref, turned = rest[-3:]
-    rows = mine_ref.shape[1]
+    rows = turned.shape[0] // (2 * chips)
+
+    def deal(chip, at, number, one, two):
+        core = rank_ref[chips]
+        mine_ref[rank_ref[chip], at : at + number] = jnp.where(core == 0, one, two)
+        other_ref[rank_ref[chip], at : at + number] = jnp.where(core == 0, two, one)
+
     for i in range(parts):
 
         @pl.when(pl.program_id(0) == i)
@@ -477,42 +509,50 @@
             if i == 0 or names[i] != names[i - 1]:
                 turned[...] = jnp.transpose(joined(lefts[names[i]]))
             total = low(mm(turned[...], joined(rights[i])))
-            core = rank_ref[chips]
             for chip in range(chips):
                 one = total[2 * chip * rows : (2 * chip + 1) * rows]
                 two = total[(2 * chip + 1) * rows : (2 * chip + 2) * rows]
-                mine_ref[rank_ref[chip]] = jnp.where(core == 0, one, two)
-                other_ref[rank_ref[chip]] = jnp.where(core == 0, two, one)
-
-
-def term_sets(rank, lefts, parts, count, after=()):
+                deal(chip, i * rows if extra else 0, rows, one, two)
+            if extra and i == 0:
+                terms = extra[0][...] + extra[1][...] + extra[2][...]
+                empty = jnp.zeros((8, 512 - rows), jnp.float32)
+                for chip in range(chips):
+                    one, two = (
+                        low(jnp.concatenate([jnp.concatenate([terms[:, s * rows : (s + 1) * rows], empty], axis=1), jnp.zeros((24, 512), jnp.float32)], axis=0))
+                        for s in (2 * chip, 2 * chip + 1)
+                    )
+                    deal(chip, parts * rows, 32, one, two)
+
+
+def term_sets(rank, lefts, parts, count, after=(), extra=()):
     total, depth = sum(x.shape[1] for x in lefts[0]), lefts[0][0].shape[0]
     flat = [x for left in lefts for x in left]
     rows = total // count
     chips = count // 2
     number = len(parts)
+    all_rows = number * rows + (32 if extra else 0)
     rights, specs = [], []
     for _, given in parts:
         for x, c in given:
             rights.append(x)
             specs.append(pl.BlockSpec((depth, 512 // len(given)), lambda n, _, c=c: (0, c)))
     return pl.pallas_call(
-        functools.partial(term_kernel, [p[0] for p in parts], chips, [len(left) for left in lefts], [len(p[1]) for p in parts]),
+        functools.partial(term_kernel, [p[0] for p in parts], chips, [len(left) for left in lefts], [len(p[1]) for p in parts], len(extra)),
         grid_spec=pltpu.PrefetchScalarGridSpec(
             num_scalar_prefetch=1,
             grid=(number,),
-            in_specs=[pl.BlockSpec(x.shape, lambda n, _: (0, 0)) for x in flat]
+            in_specs=[pl.BlockSpec(x.shape, lambda n, _: (0, 0)) for x in [*extra, *flat]]
             + specs
             + [pl.BlockSpec(memory_space=pl.ANY)] * len(after),
-            out_specs=[pl.BlockSpec((chips, rows, 512), lambda n, _: (0, n, 0))] * 2,
+            out_specs=[pl.BlockSpec((chips, all_rows, 512), lambda n, _: (0, 0, 0)) if extra else pl.BlockSpec((chips, rows, 512), lambda n, _: (0, n, 0))] * 2,
             scratch_shapes=[pltpu.VMEM((total, depth), jnp.bfloat16)],
         ),
-        out_shape=[jax.ShapeDtypeStruct((chips, number * rows, 512), jnp.bfloat16)] * 2,
+        out_shape=[jax.ShapeDtypeStruct((chips, all_rows, 512), jnp.bfloat16)] * 2,
         compiler_params=pltpu.CompilerParams(vmem_limit_bytes=58 << 20),
         cost_estimate=estimate(
             flops=2 * number * total * 512 * depth, bytes_accessed=6 * number * total * 512, transcendentals=0
         ),
-    )(rank, *flat, *rights, *after)
+    )(rank, *extra, *flat, *rights, *after)
 
 
 def ffn_term_kernel(parts, a_ref, du_ref, h_ref, df_ref, *rest):
@@ -563,78 +603,35 @@
     )(a, du, h, df)
 
 
-def halve_kernel(split, rep_ref, mine_ref, came_ref, *rest):
-    keep_ref, soon_ref, late_ref = rest[-3:]
+def halve_kernel(rep_ref, mine_ref, came_ref, *rest):
+    keep_ref, send_ref = rest[-2:]
     total = low(mine_ref[...].astype(jnp.float32) + came_ref[...].astype(jnp.float32))
     half = total.shape[1] // 2
     one, two = total[:, :half], total[:, half:]
     keep_ref[...] = jnp.where(rep_ref[0] == 0, one, two)
-    send = jnp.where(rep_ref[0] == 0, two, one)
-
-    @pl.when(pl.program_id(0) < split)
-    def _():
-        soon_ref[...] = send
-
-    @pl.when(pl.program_id(0) >= split)
-    def _():
-        late_ref[...] = send
-
-
-def halve(rep, mine, came, split, after=()):
+    send_ref[...] = jnp.where(rep_ref[0] == 0, two, one)
+
+
+def halve(rep, mine, came, after=()):
     chips, rows, width = mine.shape
-    pairs = chips // 2
     spec = pl.BlockSpec((2, rows, width), lambda i, _: (i, 0, 0))
-    block = (2, rows // 2, width)
-    half = rows // 2
+    out = pl.BlockSpec((2, rows // 2, width), lambda i, _: (i, 0, 0))
     return pl.pallas_call(
-        functools.partial(halve_kernel, split),
+        halve_kernel,
         grid_spec=pltpu.PrefetchScalarGridSpec(
             num_scalar_prefetch=1,
-            grid=(pairs,),
+            grid=(chips // 2,),
             in_specs=[spec, spec] + [pl.BlockSpec(memory_space=pl.ANY)] * len(after),
-            out_specs=[
-                pl.BlockSpec(block, lambda i, _: (i, 0, 0)),
-                pl.BlockSpec(block, lambda i, _: (jnp.minimum(i, split - 1), 0, 0)),
-                pl.BlockSpec(block, lambda i, _: (jnp.maximum(i - split, 0), 0, 0)),
-            ],
+            out_specs=[out, out],
         ),
-        out_shape=[
-            jax.ShapeDtypeStruct((chips, half, width), jnp.bfloat16),
-            jax.ShapeDtypeStruct((2 * split, half, width), jnp.bfloat16),
-            jax.ShapeDtypeStruct((chips - 2 * split, half, width), jnp.bfloat16),
-        ],
+        out_shape=[jax.ShapeDtypeStruct((chips, rows // 2, width), jnp.bfloat16)] * 2,
         compiler_params=pltpu.CompilerParams(vmem_limit_bytes=32 << 20),
         cost_estimate=estimate(flops=2 * mine.size, bytes_accessed=6 * mine.size, transcendentals=0),
     )(rep, mine, came, *after)
 
 
-def pair_kernel(split, one_ref, soon_ref, late_ref, *rest):
-    two = jnp.where(pl.program_id(0) < split, soon_ref[...], late_ref[...])
-    rest[-1][...] = low(one_ref[...].astype(jnp.float32) + two.astype(jnp.float32))
-
-
-def pair_sum(one, soon, late, after=()):
-    chips, rows, width = one.shape
-    split = soon.shape[0] // 2
-    block = (2, rows, width)
-    spec = pl.BlockSpec(block, lambda i: (i, 0, 0))
-    return pl.pallas_call(
-        functools.partial(pair_kernel, split),
-        grid=(chips // 2,),
-        in_specs=[
-            spec,
-            pl.BlockSpec(block, lambda i: (jnp.minimum(i, split - 1), 0, 0)),
-            pl.BlockSpec(block, lambda i: (jnp.maximum(i - split, 0), 0, 0)),
-        ]
-        + [pl.BlockSpec(memory_space=pl.ANY)] * len(after),
-        out_specs=spec,
-        out_shape=jax.ShapeDtypeStruct(one.shape, jnp.bfloat16),
-        compiler_params=pltpu.CompilerParams(vmem_limit_bytes=32 << 20),
-        cost_estimate=estimate(flops=one.size, bytes_accessed=6 * one.size, transcendentals=0),
-    )(one, soon, late, *after)
-
-
-def hop_kernel(first, second, *rest):
+def hop_kernel(first, second, carried, *rest):
+    rest = rest[: len(rest) - carried]
     if first:
         mine_up, came_up, mine_down, came_down = rest[:4]
         up = mine_up[0].astype(jnp.float32) + came_up[0].astype(jnp.float32)
@@ -653,7 +650,7 @@
     rest[-1][...] = low(down)
 
 
-def hop(mine, came, up, down, up_at, down_at, after=()):
+def hop(mine, came, up, down, up_at, down_at, after=(), carry=()):
     rows, width = mine.shape[1:]
     blocks = 2 if rows % 32 == 0 else 1
     part = rows // blocks
@@ -676,13 +673,15 @@
         specs += [pick(down_at)] * 2
     number = 1 if down_at is None else 2
     return pl.pallas_call(
-        functools.partial(hop_kernel, up is None, down_at is not None),
+        functools.partial(hop_kernel, up is None, down_at is not None, len(carry)),
         grid=(blocks,),
-        in_specs=specs + [pl.BlockSpec(memory_space=pl.ANY)] * len(after),
-        out_specs=[flat] * number,
-        out_shape=[jax.ShapeDtypeStruct((rows, width), jnp.bfloat16)] * number,
+        in_specs=specs + [pl.BlockSpec(memory_space=pl.ANY)] * (len(after) + len(carry)),
+        out_specs=[flat] * number + [pl.BlockSpec(memory_space=pl.ANY)] * len(carry),
+        out_shape=[jax.ShapeDtypeStruct((rows, width), jnp.bfloat16)] * number
+        + [jax.ShapeDtypeStruct(x.shape, x.dtype) for x in carry],
+        input_output_aliases={len(args) + len(after) + i: number + i for i in range(len(carry))},
         cost_estimate=estimate(flops=4 * rows * width, bytes_accessed=16 * rows * width, transcendentals=0),
-    )(*args, *after)
+    )(*args, *after, *carry)
 
 
 def ring_walk(chips):
@@ -736,19 +735,14 @@
         self.pieces = [piece] + [None] * (self.chips - 1)
         self.step = 0
 
-    def hop(self, after):
-        def held(part):
-            return part + after[:1, :1] * 0
-
+    def hop(self, *after):
         last, half = self.step, self.chips // 2
+        upward, downward = self.pieces[-last % self.chips], self.pieces[last]
+        held = sum(low(a[:1, :1]) for a in after) * 0
         self.step += 1
-        up = lax.ppermute(held(self.pieces[-last % self.chips]), "shard", self.up)
-        self.pieces[self.chips - self.step] = up
-        if self.step == half:
-            return [up]
-        down = lax.ppermute(held(self.pieces[last]), "shard", self.down)
-        self.pieces[self.step] = down
-        return [up, down]
+        self.pieces[self.chips - self.step] = lax.ppermute(upward + held, "shard", self.up)
+        if self.step < half:
+            self.pieces[self.step] = lax.ppermute(downward + held, "shard", self.down)
 
     def finish(self):
         return self.pieces + [lax.ppermute(p, "shard", self.swap) for p in self.pieces]
@@ -764,27 +758,27 @@
 
 
 class RingSum:
-    def __init__(self, mine, other, count, flip=False):
-        self.up, self.down, swap = ring_moves(count)
+    def __init__(self, mine, came, count, flip=False):
+        self.up, self.down, _ = ring_moves(count)
         self.chips = count // 2
         self.sign = 1
         if flip:
             self.up, self.down, self.sign = self.down, self.up, -1
-        self.mine = mine
-        self.came = lax.ppermute(other, "shard", swap)
+        self.mine, self.came = mine, came
         self.step = self.chips // 2
         self.upward = self.downward = None
 
     def at(self, distance):
         return (self.sign * distance) % self.chips
 
-    def hop(self, after=()):
+    def hop(self, after=(), carry=()):
         half = self.chips // 2
         down_at = 1 - self.step if self.step > 1 else None
         sums = hop(
             self.mine, self.came, self.upward, self.downward if down_at is not None else None,
-            self.at(self.step), None if down_at is None else self.at(down_at), after,
+            self.at(self.step), None if down_at is None else self.at(down_at), after, carry,
         )
+        self.carried = sums[len(sums) - len(carry) :]
         self.upward = lax.ppermute(sums[0], "shard", self.up)
         if down_at is not None:
             self.downward = lax.ppermute(sums[1], "shard", self.down)
@@ -792,55 +786,25 @@
         return [sums[0]]
 
     def finish(self):
-        owned = add_low(self.mine[0], self.came[0], self.upward, self.downward)
-        return over_rep(owned)
-
-
-class HalfSum:
-    def __init__(self, rep, mine, other, count):
-        self.rep, self.count, self.mine = rep, count, mine
-        self.came = lax.ppermute(other, "shard", ring_moves(count)[2])
-
-    def over_rep(self, split, after=()):
-        swap = [(0, 1), (1, 0)]
-        self.keep, soon, late = halve(self.rep, self.mine, self.came, split, after)
-        self.soon, self.late = lax.ppermute(soon, "rep", swap), lax.ppermute(late, "rep", swap)
-        return [self.keep]
-
-    def over_chips(self, after=()):
-        both = pair_sum(self.keep, self.soon, self.late, after).reshape(-1, self.keep.shape[2])
-        groups = [list(range(core, self.count, 2)) for core in range(2)]
-        self.owned = lax.psum_scatter(both, "shard", scatter_dimension=0, axis_index_groups=groups, tiled=True)
-        return [both]
-
-    def finish(self):
-        partner = lax.ppermute(self.owned, "rep", [(0, 1), (1, 0)])
-        first = self.rep[0] == 0
-        return jnp.concatenate(
-            [jnp.where(first, self.owned, partner), jnp.where(first, partner, self.owned)], axis=0
-        ).astype(jnp.float32)
+        return add_low(self.mine[0], self.came[0], self.upward, self.downward)
+
+
+def over_cores(other, count):
+    return lax.ppermute(other, "shard", ring_moves(count)[2])
+
+
+def swap_reps(part):
+    return lax.ppermute(part, "rep", [(0, 1), (1, 0)])
+
+
+def both_halves(rep, owned):
+    partner = swap_reps(owned)
+    first = rep[0] == 0
+    return jnp.concatenate([jnp.where(first, owned, partner), jnp.where(first, partner, owned)], axis=0).astype(jnp.float32)
 
 
 def scatter_sum(term):
     return over_rep(lax.psum_scatter(low(term), "shard", scatter_dimension=0, tiled=True))
-
-
-class TotalSum:
-    def __init__(self, values_in, count):
-        self.value, self.count, self.step = values_in, count, 1
-
-    def phase(self):
-        if self.step < self.count:
-            radix = min(4, self.count // self.step)
-            came = [
-                lax.ppermute(self.value, "shard", [(i, i ^ (k * self.step)) for i in range(self.count)])
-                for k in range(1, radix)
-            ]
-            self.step *= radix
-        else:
-            came = [lax.ppermute(self.value, "rep", [(0, 1), (1, 0)])]
-        self.value = self.value + sum(came[1:], came[0])
-        return [self.value]
 
 
 def weight_term(left, right):
@@ -881,14 +845,19 @@
 
     norm_piece = jnp.concatenate([norm_gains, norm_biases], axis=0)
     in_parts = [ffn_in[:, i * width : (i + 1) * width] for i in range(parts)]
+    unit_extra, enc_extra = key_extras(unit_ids[0]), key_extras(enc_ids[0])
+    query_extra = query_extras(unit_ids[0])
+    self_windows = windows(unit_ids[0], unit_ids[0], 256, 256, True)
+    cross_windows = windows(unit_ids[0], enc_ids[0], 256, 256, False)
     if ring:
         order, rank = ring_tables(count)
         norm_row = jnp.pad(norm_piece.reshape(1, -1), ((0, 15), (0, width - 8 * own_width)))
+        rep = lax.axis_index("rep").astype(jnp.int32).reshape(1)
+        piece_b = jnp.concatenate([self_o, cross_q, cross_k, cross_v, cross_o], axis=0)
+        half_c = jnp.where(rep[0] == 0, jnp.concatenate(in_parts, axis=0), ffn_out)
         set_a = gather_pieces(jnp.concatenate([self_q, self_k, self_v, norm_row], axis=0), count)
-        ring_b = RingGather(jnp.concatenate([self_o, cross_q, cross_k, cross_v, cross_o], axis=0), count)
+        ring_b = RingGather(piece_b, count)
         ring_b.hop(set_a[count // 4])
-        rep = lax.axis_index("rep").astype(jnp.int32).reshape(1)
-        half_c = jnp.where(rep[0] == 0, jnp.concatenate(in_parts, axis=0), ffn_out)
         set_c = [lax.all_gather(half_c, ("rep", "shard"), axis=0, tiled=True)]
         norm_rows = jnp.concatenate([p[3 * own : 3 * own + 1, : 8 * own_width] for p in set_a], axis=0)
         place = (jnp.arange(count, dtype=jnp.int32)[:, None] == order[None, :]).astype(bf16)
@@ -913,10 +882,6 @@
     sems = pltpu.SemaphoreType.DMA
     square = 2 * row_count * width * width
 
-    unit_extra, enc_extra = key_extras(unit_ids[0]), key_extras(enc_ids[0])
-    query_extra = query_extras(unit_ids[0])
-    self_windows = windows(unit_ids[0], unit_ids[0], 256, 256, True)
-    cross_windows = windows(unit_ids[0], enc_ids[0], 256, 256, False)
     a1, q1, k1, v1 = by_rows(
         functools.partial(first_kernel, plan_a, len(set_a)), order, [x], norms, set_a,
         [(width, bf16)] * 4, False,
@@ -929,7 +894,7 @@
         ring_b.hop(o1_low)
         o1_high, log1_high = attend_forward(*self_args, (pairs // 2, pairs), [o1_low])
         ring_b.hop(o1_high)
-        ring_b.hop(o1_high)
+        ring_b.hop()
         set_b = ring_b.finish()
     else:
         o1_low, log1_low = attend_forward(*self_args, (0, pairs // 2))
@@ -956,17 +921,23 @@
 
     cross_args = (q2, k2, v2, o2, do2, log2, enc_extra, cross_windows, False)
     if ring:
-        plain = jnp.concatenate([jnp.arange(count // 2, dtype=jnp.int32), rank[-1:]])
         ffn_set = ffn_terms(a3, du, h, df, count)
         ffn_set = lax.psum_scatter(ffn_set.reshape(-1, width), "shard", scatter_dimension=0, tiled=True)
     else:
         grad_in, grad_out = scatter_sum(weight_term(a3, du)), scatter_sum(weight_term(h, df))
     dq2, dk2, dv2 = attend_backward(*cross_args, (0, pairs))
-    fourth = functools.partial(
-        by_rows, functools.partial(fourth_kernel, plan_b[:4], len(set_b), 1), order, [dq2, dk2, dv2, r1, dr2], norms, set_b,
-        [(width, f32), (width, bf16), (width, bf16), (width, f32)], True,
-        [pltpu.VMEM((4, width, width), bf16), sems((4,))], 4 * square,
+    dr1, dc1, do1, terms_two = by_rows(
+        functools.partial(fourth_kernel, plan_b[:2], len(set_b)), order, [dq2, r1, dr2], norms, set_b,
+        [(width, f32), (width, bf16), (width, bf16)], True,
+        [pltpu.VMEM((2, width, width), bf16), sems((2,))], 2 * square,
     )
+
+    def enc_backward(after):
+        return by_rows(
+            functools.partial(enc_kernel, plan_b[2:4], len(set_b)), order, [dk2, dv2], norms, set_b,
+            [(width, f32)], False,
+            [pltpu.VMEM((2, width, width), bf16), sems((2,))], 2 * square, after,
+        )[0]
 
     half = pairs // 2
 
@@ -985,33 +956,34 @@
         )
 
     if ring:
-        sums_b = HalfSum(
-            rep,
-            *term_sets(
-                plain, [(o2,), (a2,), (enc,)],
-                [(i, [(g, c)]) for i, g in ((0, dc2), (1, dq2), (2, dk2), (2, dv2)) for c in range(2)], count,
-            ),
-            count,
+        groups = [self_backward(0, [])]
+        groups.append(self_backward(1, [groups[0][0]]))
+        mine, other = term_sets(
+            rank, [tuple(o1), (a1,)],
+            [(0, [(dc1, c)]) for c in range(2)] + [(1, [(g[i], 0)]) for i in range(3) for g in groups], count,
         )
-        dr1, dc1, do1, grad_enc, terms_two = fourth([sums_b.mine])
-        groups = [self_backward(0, sums_b.over_rep(2, [dc1]))]
-        groups.append(self_backward(1, [groups[0][0], sums_b.soon]))
-        sums_a = RingSum(
-            *term_sets(
-                rank, [tuple(o1), (a1,)],
-                [(0, [(dc1, c)]) for c in range(2)] + [(1, [(g[i], 0)]) for i in range(3) for g in groups], count, [sums_b.late],
-            ),
-            count, True,
+        sums_a = RingSum(mine, over_cores(other, count), count, True)
+        grad_x, terms_one = fifth(groups, [mine])
+        last = sums_a.hop([grad_x])
+        mine, other = term_sets(
+            rank, [(o2,), (a2,), (enc,)],
+            [(i, [(g, c)]) for i, g in ((0, dc2), (1, dq2), (2, dk2), (2, dv2)) for c in range(2)], count, last,
+            [terms_one, terms_two, terms_three],
         )
-        grad_x, terms_one = fifth(groups, [sums_a.mine])
-        norm_sum = TotalSum(terms_one + terms_two + terms_three, count)
-        last = sums_b.over_chips(sums_a.hop([grad_x]) + [ffn_set])
-        for _ in range(count // 4 - 1):
-            last = sums_a.hop(last + norm_sum.phase())
-        ffn_set = over_rep(ffn_set)
+        last = sums_a.hop([mine], [other])
+        came = over_cores(sums_a.carried[0], count)
+        grad_enc = enc_backward(last)
+        keep, send = halve(rep, mine, came, [grad_enc])
+        sums_b = RingSum(keep, swap_reps(send), count)
+        last = sums_a.hop(sums_a.hop([keep]))
+        ffn_set = over_rep(ffn_set + last[0][:1, :1] * 0)
+        last = sums_b.hop(sums_b.hop(sums_b.hop(last)))
+        sums_b.hop(last + [ffn_set])
+        grad_a, grad_b = over_rep(sums_a.finish()), both_halves(rep, sums_b.finish())
         grad_in = jnp.concatenate([ffn_set[i * own : (i + 1) * own] for i in range(parts)], axis=1)
         grad_out = ffn_set[parts * own :]
-        grad_a, grad_b = sums_a.finish(), sums_b.finish()
+
+        norm_sum = grad_b[8 * own : 8 * own + 8, :own_width]
 
         def columns(array, places):
             return jnp.concatenate([array[i * own : (i + 1) * own] for i in places], axis=1)
@@ -1019,22 +991,18 @@
         grad_co, grad_cq, grad_ck, grad_cv = (columns(grad_b, (2 * w, 2 * w + 1)) for w in range(4))
         grad_so, grad_sq, grad_sk, grad_sv = (columns(grad_a, (2 * w, 2 * w + 1)) for w in range(4))
     else:
-        dr1, dc1, do1, grad_enc, terms_two = fourth()
+        grad_enc = enc_backward(())
         groups = [self_backward(i, ()) for i in range(2)]
         dq1, dk1, dv1 = (jnp.concatenate([g[i] for g in groups], axis=1) for i in range(3))
         grad_x, terms_one = fifth(groups, ())
-        norm_sum = TotalSum(terms_one + terms_two + terms_three, count)
-        while norm_sum.step < count:
-            norm_sum.phase()
-        norm_sum.phase()
+        norm_sum = lax.psum(terms_one + terms_two + terms_three, ("rep", "shard"))
+        norm_sum = lax.dynamic_slice_in_dim(norm_sum, lax.axis_index("shard") * own_width, own_width, 1)
         grad_co, grad_cq, grad_ck, grad_cv, grad_so, grad_sq, grad_sk, grad_sv = (
             scatter_sum(weight_term(a, b))
             for a, b in (
                 (o2, dc2), (a2, dq2), (enc, dk2), (enc, dv2), (jnp.concatenate(o1, axis=1), dc1), (a1, dq1), (a1, dk1), (a1, dv1)
             )
         )
-    norm_sum = norm_sum.value
-    norm_sum = lax.dynamic_slice_in_dim(norm_sum, lax.axis_index("shard") * own_width, own_width, 1)
     return (
         out.reshape(tokens.shape),
         grad_x.reshape(tokens.shape),

time: 656 us -> 631 us (0.962)
  waiting for transfers between devices: 165 us -> 143 us
  local copies, waits for them, and re-layouts: 36.3 us -> 22.6 us
  starting transfers between devices: 78 us -> 85.9 us
    ppermute x19 -> x11, waiting for transfers between devices: 75.2 us -> 36 us  [the longest x4 29.3 us: hop(): lax.ppermute(upward + held, 'shard', self.up)]
    ppermute x4 -> x8, waiting for transfers between devices: 22.8 us -> 43.7 us  [hop(): self.upward = lax.ppermute(sums[0], 'shard', self.up)]
    unnamed x179 -> x129, local copies, waits for them, and re-layouts: 26.5 us -> 12.9 us
    ppermute x3 -> x6, starting transfers between devices: 0.01 us -> 12.3 us  [hop(): self.downward = lax.ppermute(sums[1], 'shard', self.down)]
    pallas_call x5 -> x4, Pallas kernels: 85.9 us -> 74.1 us  [the longest x3 69.3 us: attend_backward(): pl.pallas_call(functools.partial(attend_backward_kernel, bq, bk, causal,...]
    pallas_call x4 -> x8, Pallas kernels: 10.3 us -> 18.7 us  [hop(): pl.pallas_call(functools.partial(hop_kernel, up is None, down_at is not N...]
    pallas_call x3, Pallas kernels: 48.7 us -> 42 us  [attend_forward(): pl.pallas_call(functools.partial(attend_forward_kernel, bq, bk, causal, h...]
    pallas_call x5 -> x6, Pallas kernels: 124 us -> 130 us  [by_rows(): pl.pallas_call(kernel, grid_spec=pltpu.PrefetchScalarGridSpec(num_scalar_...]
  transfers between devices with their start and end apart: 54 -> 52, of which waited for: 22 -> 21; matrix products, arithmetic and copies ran while one was open for 4% -> 4% of each run, Pallas kernels for 37% -> 39%
where the time goes in v4:
time: 631 us; the launch traced here: 625 us
  Pallas kernels  333 us (53%)
  waiting for transfers between devices  143 us (23%)
  starting transfers between devices  85.9 us (14%)
  local copies, waits for them, and re-layouts  22.6 us (4%)
  other arithmetic  21.9 us (3%)
  between operations  17.9 us (3%)
    pallas_call x6, Pallas kernels, by_rows(): pl.pallas_call(kernel, grid_spec=pltpu.PrefetchScalarGridSpec(num_scalar_...  130 us
    pallas_call x3, Pallas kernels, attend_backward(): pl.pallas_call(functools.partial(attend_backward_kernel, bq, bk, causal,...  69.3 us
    ppermute x4, waiting for transfers between devices, gather_pieces(): upward = lax.ppermute(upward, 'shard', up)  52.5 us
    ppermute x8, waiting for transfers between devices, hop(): self.upward = lax.ppermute(sums[0], 'shard', self.up)  43.7 us
    pallas_call x3, Pallas kernels, attend_forward(): pl.pallas_call(functools.partial(attend_forward_kernel, bq, bk, causal, h...  42 us
    pallas_call x2, Pallas kernels, term_sets(): pl.pallas_call(functools.partial(term_kernel, [p[0] for p in parts], chip...  37.7 us
    pallas_call x1, Pallas kernels, ffn_terms(): pl.pallas_call(functools.partial(ffn_term_kernel, parts), grid=(per, 2 *...  31.1 us
    ppermute x4, waiting for transfers between devices, hop(): lax.ppermute(upward + held, 'shard', self.up)  29.3 us
  transfers between devices with their start and end apart: 52, of which 21 were waited for; matrix products, arithmetic and copies ran while one was open for 4% of the time, Pallas kernels for 39%

profile of v4, /device:TPU:0, one launch (start us, length us, event | category | flops | bytes accessed | tf_op | source)
XLA Modules:
  0.0 625.3 jit_solution(7986284229362828995)
XLA Ops:
  9.9 3.1 collective-permute-start.3
  14.6 8.2 %collective-permute-done.3.rest_7_.rest_16_ = bf16[208,1024]{1,0:T(8,128)(2,1)S(1)} collective-permute-done((bf16[208,1024]{1,0:T(8,128)(2,1)S(1)}, bf16[208,1024]{1,0:T(8,128)(2,1)S(1)}, u32[]{:S(2)}, u32[]{:S(2)}) %collective-permute-start.3) | collective-permute-done | bytes 426016 | tf_op jit(solution)/shard_map/ppermute | solution.py:723
  22.8 1.8 collective-permute-start.4
  24.7 18.4 %collective-permute-done.4.rest_6_.rest_15_ = bf16[208,1024]{1,0:T(8,128)(2,1)S(1)} collective-permute-done((bf16[208,1024]{1,0:T(8,128)(2,1)S(1)}, bf16[208,1024]{1,0:T(8,128)(2,1)S(1)}, u32[]{:S(2)}, u32[]{:S(2)}) %collective-permute-start.4) | collective-permute-done | bytes 426016 | tf_op jit(solution)/shard_map/ppermute | solution.py:723
  43.1 2.5 collective-permute-start.5
  46.8 10.7 %collective-permute-done.5.rest_5_.rest_14_ = bf16[208,1024]{1,0:T(8,128)(2,1)S(1)} collective-permute-done((bf16[208,1024]{1,0:T(8,128)(2,1)S(1)}, bf16[208,1024]{1,0:T(8,128)(2,1)S(1)}, u32[]{:S(2)}, u32[]{:S(2)}) %collective-permute-start.5) | collective-permute-done | bytes 426016 | tf_op jit(solution)/shard_map/ppermute | solution.py:723
  57.6 9.3 %collective-permute-start.6 = (bf16[208,1024]{1,0:T(8,128)(2,1)S(1)}, bf16[208,1024]{1,0:T(8,128)(2,1)S(1)}, u32[]{:S(2)}, u32[]{:S(2)}) collective-permute-start(bf16[208,1024]{1,0:T(8,128)(2,1)S(1)} %collective-permute-done.5.rest_5_.rest_14_), channel_id=1, source_target_pairs={{0,4},{1,5},{4,8},{5,9},{8,12},{9,13},{12,14},{13,15},{14,10},{15,... | collective-permute-start | bytes 1277960 | tf_op jit(solution)/shard_map/ppermute | solution.py:723
  68.4 15.1 %collective-permute-done.6.rest_4_.rest_13_ = bf16[208,1024]{1,0:T(8,128)(2,1)S(1)} collective-permute-done((bf16[208,1024]{1,0:T(8,128)(2,1)S(1)}, bf16[208,1024]{1,0:T(8,128)(2,1)S(1)}, u32[]{:S(2)}, u32[]{:S(2)}) %collective-permute-start.6) | collective-permute-done | bytes 426016 | tf_op jit(solution)/shard_map/ppermute | solution.py:723
  86.0 3.1 collective-permute-done.2.rest_3_.rest_12_
  90.6 2.1 collective-permute-start.18
  97.6 13.9 %shard_map.298 = (bf16[1024,1024]{1,0:T(8,128)(2,1)}, bf16[1024,1024]{1,0:T(8,128)(2,1)}, bf16[1024,1024]{1,0:T(8,128)(2,1)}, bf16[1024,1024]{1,0:T(8,128)(2,1)}) custom-call(s32[16]{0:T(128)} %copy-done.57, bf16[1024,1024]{1,0:T(8,128)(2,1)} %bitcast.38, f32[8,1024]{1,0:T(8,128)} %reshape.101.norm_ref.rest_4_.rest_3_.rest_8_, bf16[208,1024]{1,0:T(8,128)(2,1)} %copy-done.22, ...), custom_call_target="tpu_custom_call" | custom-call | flops 805306368 | bytes 1310720 | tf_op jit(solution)/shard_map/pallas_call | solution.py:473
  111.5 11.6 %shard_map.299 = (bf16[1024,512]{1,0:T(8,128)(2,1)}, bf16[1024,512]{1,0:T(8,128)(2,1)}) custom-call(s32[8]{0:T(128)} %pad_add_fusion.1.win_ref, bf16[1024,1024]{1,0:T(8,128)(2,1)} %get-tuple-element.73.q_ref, bf16[1024,1024]{1,0:T(8,128)(2,1)} %get-tuple-element.74.k_ref, bf16[1024,1024]{1,0:T(8,128)(2,1)} %get-tuple-element.75.v_ref, ...), custom_call_target="tpu_custom_call" | custom-call | flops 1073741824 | bytes 655360 | tf_op jit(solution)/shard_map/pallas_call | solution.py:129
  125.0 13.7 %collective-permute-start.19 = (bf16[320,1024]{1,0:T(8,128)(2,1)S(1)}, bf16[320,1024]{1,0:T(8,128)(2,1)S(1)}, u32[]{:S(2)}, u32[]{:S(2)}) collective-permute-start(bf16[320,1024]{1,0:T(8,128)(2,1)S(1)} %broadcast_add_fusion.3), channel_id=1, source_target_pairs={{0,4},{1,5},{4,8},{5,9},{8,12},{9,13},{12,14},{13,15},{14,10},{15,... | collective-permute-start | bytes 1966088 | tf_op jit(solution)/shard_map/ppermute | solution.py:743
  138.7 11.7 %shard_map.300 = (bf16[1024,512]{1,0:T(8,128)(2,1)}, bf16[1024,512]{1,0:T(8,128)(2,1)}) custom-call(s32[8]{0:T(128)} %pad_add_fusion.1.win_ref, bf16[1024,1024]{1,0:T(8,128)(2,1)} %get-tuple-element.73.q_ref, bf16[1024,1024]{1,0:T(8,128)(2,1)} %get-tuple-element.74.k_ref, bf16[1024,1024]{1,0:T(8,128)(2,1)} %get-tuple-element.75.v_ref, ...), custom_call_target="tpu_custom_call" | custom-call | flops 1073741824 | bytes 655360 | tf_op jit(solution)/shard_map/pallas_call | solution.py:129
  152.4 6.0 collective-permute-done.19.rest_11_.rest_10_.rest_6_
  158.4 9.7 %collective-permute-start.20 = (bf16[320,1024]{1,0:T(8,128)(2,1)S(1)}, bf16[320,1024]{1,0:T(8,128)(2,1)S(1)}, u32[]{:S(2)}, u32[]{:S(2)}) collective-permute-start(bf16[320,1024]{1,0:T(8,128)(2,1)S(1)} %broadcast_add_fusion.1), channel_id=1, source_target_pairs={{0,4},{1,5},{4,8},{5,9},{8,12},{9,13},{12,14},{13,15},{14,10},{15,... | collective-permute-start | bytes 1966088 | tf_op jit(solution)/shard_map/ppermute | solution.py:743
  169.8 12.2 %collective-permute-done.20.rest_10_.rest_9_.rest_5_ = bf16[320,1024]{1,0:T(8,128)(2,1)S(1)} collective-permute-done((bf16[320,1024]{1,0:T(8,128)(2,1)S(1)}, bf16[320,1024]{1,0:T(8,128)(2,1)S(1)}, u32[]{:S(2)}, u32[]{:S(2)}) %collective-permute-start.20) | collective-permute-done | bytes 655392 | tf_op jit(solution)/shard_map/ppermute | solution.py:743
  182.0 2.9 collective-permute-start.21
  186.6 11.2 %collective-permute-done.21.rest_9_.rest_8_.rest_4_ = bf16[320,1024]{1,0:T(8,128)(2,1)S(1)} collective-permute-done((bf16[320,1024]{1,0:T(8,128)(2,1)S(1)}, bf16[320,1024]{1,0:T(8,128)(2,1)S(1)}, u32[]{:S(2)}, u32[]{:S(2)}) %collective-permute-start.21) | collective-permute-done | bytes 655392 | tf_op jit(solution)/shard_map/ppermute | solution.py:743
  198.6 1.4 collective-permute-done.26.rest_17_.rest_16_.rest_12_
  200.8 16.4 %shard_map.301 = (f32[1024,1024]{1,0:T(8,128)}, bf16[1024,1024]{1,0:T(8,128)(2,1)}, bf16[1024,1024]{1,0:T(8,128)(2,1)}, bf16[1024,1024]{1,0:T(8,128)(2,1)}, bf16[1024,1024]{1,0:T(8,128)(2,1)}) custom-call(s32[16]{0:T(128)} %copy-done.57, bf16[1024,512]{1,0:T(8,128)(2,1)} %get-tuple-element.76.rest_0_.o_ref, ...), custom_call_target="tpu_custom_call" | custom-call | flops 1073741824 | bytes 2359296 | tf_op jit(solution)/shard_map/pallas_call | solution.py:473
  217.2 18.6 %shard_map.302 = (bf16[1024,1024]{1,0:T(8,128)(2,1)}, bf16[1024,1024]{1,0:T(8,128)(2,1)}) custom-call(s32[8]{0:T(128)} %pad_add_fusion.win_ref, bf16[1024,1024]{1,0:T(8,128)(2,1)} %get-tuple-element.78.q_ref, bf16[1024,1024]{1,0:T(8,128)(2,1)} %get-tuple-element.79.k_ref, bf16[1024,1024]{1,0:T(8,128)(2,1)} %get-tuple-element.80.v_ref, ...), custom_call_target="tpu_custom_call" | custom-call | flops 2147483648 | bytes 1310720 | tf_op jit(solution)/shard_map/pallas_call | solution.py:129
  235.8 58.1 %shard_map.303 = (bf16[1024,1024]{1,0:T(8,128)(2,1)}, bf16[1024,1024]{1,0:T(8,128)(2,1)}, bf16[1024,4096]{1,0:T(8,128)(2,1)}, bf16[1024,1024]{1,0:T(8,128)(2,1)}...) custom-call(s32[16]{0:T(128)} %copy-done.57, ...), custom_call_target="tpu_custom_call" | custom-call | flops 4831838208 | bytes 4980736 | tf_op jit(solution)/shard_map/pallas_call | solution.py:473
  293.9 31.1 %shard_map.320 = bf16[16,512,1024]{2,1,0:T(8,128)(2,1)} custom-call(bf16[1024,1024]{1,0:T(8,128)(2,1)} %get-tuple-element.126.a_ref, bf16[1024,4096]{1,0:T(8,128)(2,1)} %get-tuple-element.127.du_ref, bf16[1024,4096]{1,0:T(8,128)(2,1)} %get-tuple-element.128.h_ref, bf16[1024,1024]{1,0:T(8,128)(2,1)} %get-tuple-element.129.df_ref), custom_call_target="tpu_custom_call" | custom-call | flops 2147483648 | bytes 6291456 | tf_op jit(solution)/shard_map/pallas_call | solution.py:588
  326.3 31.2 %shard_map.304 = (bf16[1024,1024]{1,0:T(8,128)(2,1)}, bf16[1024,1024]{1,0:T(8,128)(2,1)}, bf16[1024,1024]{1,0:T(8,128)(2,1)}) custom-call(s32[8]{0:T(128)} %pad_add_fusion.win_ref, bf16[1024,1024]{1,0:T(8,128)(2,1)} %get-tuple-element.78.q_ref, bf16[1024,1024]{1,0:T(8,128)(2,1)} %get-tuple-element.79.k_ref, bf16[1024,1024]{1,0:T(8,128)(2,1)} %get-tuple-element.80.v_ref, ...), custom_call_target="tpu_custom_call" | custom-call | flops 5368709120 | bytes 2097152 | tf_op jit(solution)/shard_map/pallas_call | solution.py:227
  357.5 14.3 %shard_map.305 = (f32[1024,1024]{1,0:T(8,128)}, bf16[1024,1024]{1,0:T(8,128)(2,1)}, bf16[1024,1024]{1,0:T(8,128)(2,1)}, f32[8,1024]{1,0:T(8,128)}) custom-call(s32[16]{0:T(128)} %copy-done.57, bf16[1024,1024]{1,0:T(8,128)(2,1)} %get-tuple-element.86.dq_ref.rest_8_.rest_9_, f32[1024,1024]{1,0:T(8,128)} %get-tuple-element.82.rest_1_.r_ref, ...), custom_call_target="tpu_custom_call" | custom-call | flops 536870912 | bytes 2359296 | tf_op jit(solution)/shard_map/pallas_call | solution.py:473
  371.7 19.3 %shard_map.306 = (bf16[1024,512]{1,0:T(8,128)(2,1)}, bf16[1024,512]{1,0:T(8,128)(2,1)}, bf16[1024,512]{1,0:T(8,128)(2,1)}) custom-call(s32[8]{0:T(128)} %pad_add_fusion.1.win_ref, bf16[1024,1024]{1,0:T(8,128)(2,1)} %get-tuple-element.73.q_ref, bf16[1024,1024]{1,0:T(8,128)(2,1)} %get-tuple-element.74.k_ref, bf16[1024,1024]{1,0:T(8,128)(2,1)} %get-tuple-element.75.v_ref, ...), custom_call_target="tpu_custom_call" | custom-call | flops 2684354560 | bytes 1048576 | tf_op jit(solution)/shard_map/pallas_call | solution.py:227
  391.1 18.8 %shard_map.307 = (bf16[1024,512]{1,0:T(8,128)(2,1)}, bf16[1024,512]{1,0:T(8,128)(2,1)}, bf16[1024,512]{1,0:T(8,128)(2,1)}) custom-call(s32[8]{0:T(128)} %pad_add_fusion.1.win_ref, bf16[1024,1024]{1,0:T(8,128)(2,1)} %get-tuple-element.73.q_ref, bf16[1024,1024]{1,0:T(8,128)(2,1)} %get-tuple-element.74.k_ref, bf16[1024,1024]{1,0:T(8,128)(2,1)} %get-tuple-element.75.v_ref, ...), custom_call_target="tpu_custom_call" | custom-call | flops 2684354560 | bytes 1048576 | tf_op jit(solution)/shard_map/pallas_call | solution.py:227
  409.8 17.3 %shard_map.308 = (bf16[8,512,512]{2,1,0:T(8,128)(2,1)}, bf16[8,512,512]{2,1,0:T(8,128)(2,1)}) custom-call(s32[9]{0:T(128)} %dynamic-slice_bitcast_fusion.rank_ref, bf16[1024,512]{1,0:T(8,128)(2,1)} %get-tuple-element.76.rest_0_.o_ref, bf16[1024,512]{1,0:T(8,128)(2,1)} %get-tuple-element.77.rest_1_.o_ref, bf16[1024,1024]{1,0:T(8,128)(2,1)} %get-tuple-element.98.rest_2_, ...), custom_call_target="tpu_custom_call" | custom-call | flops 1073741824 | bytes 3145728 | tf_op jit(solution)/shard_map/pallas_call | solution.py:539
  427.2 16.0 %shard_map.309 = (f32[1024,1024]{1,0:T(8,128)}, f32[8,1024]{1,0:T(8,128)}) custom-call(s32[16]{0:T(128)} %copy-done.57, bf16[1024,512]{1,0:T(8,128)(2,1)} %get-tuple-element.90.rest_0_.rest_5_, bf16[1024,512]{1,0:T(8,128)(2,1)} %get-tuple-element.92.rest_6_.rest_1_, bf16[1024,512]{1,0:T(8,128)(2,1)} %get-tuple-element.93.rest_7_.rest_2_, ...), custom_call_target="tpu_custom_call" | custom-call | flops 805306368 | bytes 2097152 | tf_op jit(solution)/shard_map/pallas_call | solution.py:473
  443.2 2.4 shard_map.310
  445.6 5.6 collective-permute-start.32
  451.2 20.4 %shard_map.311 = (bf16[8,544,512]{2,1,0:T(8,128)(2,1)}, bf16[8,544,512]{2,1,0:T(8,128)(2,1)}) custom-call(s32[9]{0:T(128)} %dynamic-slice_bitcast_fusion.rank_ref, f32[8,1024]{1,0:T(8,128)} %get-tuple-element.107.rest_0_, f32[8,1024]{1,0:T(8,128)} %get-tuple-element.108.rest_1_, f32[8,1024]{1,0:T(8,128)} %get-tuple-element.109.rest_2_, ...), custom_call_target="tpu_custom_call" | custom-call | flops 1073741824 | bytes 3145728 | tf_op jit(solution)/shard_map/pallas_call | solution.py:539
  472.6 2.8 shard_map.312
  475.6 1.8 collective-permute-start.34
  477.6 11.2 %shard_map.313.rest_0_ = f32[1024,1024]{1,0:T(8,128)} custom-call(s32[16]{0:T(128)} %copy-done.57, bf16[1024,1024]{1,0:T(8,128)(2,1)} %get-tuple-element.102.rest_10_.rest_11_.dk_ref, bf16[1024,1024]{1,0:T(8,128)(2,1)} %get-tuple-element.103.rest_12_.rest_13_.dv_ref, f32[8,1024]{1,0:T(8,128)} %reshape.101.norm_ref.rest_4_.rest_3_.rest_8_, ...), custom_call_target="tpu_custom_call" | custom-call | flops 536870912 | bytes 1048576 | tf_op jit(solution)/shard_map/pallas_call | solution.py:473
  488.8 2.2 copy-done.2
  491.0 4.9 shard_map.314
  495.9 1.4 copy-done
  497.2 7.2 %collective-permute-start.40 = (bf16[8,272,512]{2,1,0:T(8,128)(2,1)}, bf16[8,272,512]{2,1,0:T(8,128)(2,1)S(1)}, u32[]{:S(2)}, u32[]{:S(2)}) collective-permute-start(bf16[8,272,512]{2,1,0:T(8,128)(2,1)} %get-tuple-element.120), channel_id=1, source_target_pairs={{0,16},{16,0},{1,17},{17,1},{2,18},{18,2},{3,19},{19,3},{4,20},{20... | collective-permute-start | bytes 6684680 | tf_op jit(solution)/shard_map/ppermute | solution.py:797
  504.4 10.7 %collective-permute-done.33.rest_0_ = bf16[512,512]{1,0:T(8,128)(2,1)S(1)} collective-permute-done((bf16[512,512]{1,0:T(8,128)(2,1)}, bf16[512,512]{1,0:T(8,128)(2,1)S(1)}, u32[]{:S(2)}, u32[]{:S(2)}) %collective-permute-start.33) | collective-permute-done | bytes 524320 | tf_op jit(solution)/shard_map/ppermute | solution.py:782
  515.9 2.8 shard_map.315
  518.7 8.4 %collective-permute-start.36 = (bf16[512,512]{1,0:T(8,128)(2,1)}, bf16[512,512]{1,0:T(8,128)(2,1)S(1)}, u32[]{:S(2)}, u32[]{:S(2)}) collective-permute-start(bf16[512,512]{1,0:T(8,128)(2,1)} %get-tuple-element.118.rest_3_), channel_id=1, source_target_pairs={{4,0},{5,1},{8,4},{9,5},{12,8},{13,9},{14,12},{15,13},{10,14},{11,... | collective-permute-start | bytes 1572872 | tf_op jit(solution)/shard_map/ppermute | solution.py:782
  527.2 11.6 %collective-permute-done.36.rest_0_ = bf16[512,512]{1,0:T(8,128)(2,1)S(1)} collective-permute-done((bf16[512,512]{1,0:T(8,128)(2,1)}, bf16[512,512]{1,0:T(8,128)(2,1)S(1)}, u32[]{:S(2)}, u32[]{:S(2)}) %collective-permute-start.36) | collective-permute-done | bytes 524320 | tf_op jit(solution)/shard_map/ppermute | solution.py:782
  539.5 2.1 shard_map.316.rest_4_
  541.7 2.4 collective-permute-start.37
  544.1 10.7 %collective-permute-done.37 = bf16[512,512]{1,0:T(8,128)(2,1)S(1)} collective-permute-done((bf16[512,512]{1,0:T(8,128)(2,1)}, bf16[512,512]{1,0:T(8,128)(2,1)S(1)}, u32[]{:S(2)}, u32[]{:S(2)}) %collective-permute-start.37) | collective-permute-done | bytes 524320 | tf_op jit(solution)/shard_map/ppermute | solution.py:782
  554.8 1.5 fusion.1
  558.2 2.3 broadcast_add_fusion
  560.5 2.0 collective-permute-start.46
  562.5 1.4 copy-done.3
  563.9 2.1 shard_map.317
  566.0 2.4 collective-permute-start.42
  568.3 2.9 collective-permute-done.39
  572.7 2.4 collective-permute-done.41.rest_0_
  575.8 2.3 shard_map.318
  582.3 2.6 collective-permute-done.44.rest_3_
  586.7 2.3 shard_map.319
  588.9 1.4 collective-permute-start.48
  591.0 3.0 convert_add_fusion.rest_4_
  593.9 3.2 collective-permute-done.45.rest_0_
  597.8 1.9 shard_map.321
  602.6 4.0 collective-permute-done.47
  609.0 5.5 collective-permute-done.49
  (265 shorter events, 46.2 us)
Async XLA Ops:
  7.3 228.6 %all-gather.2.cloned.1.call-start = ((), (), s32[]{:S(2)}) async-start(), calls=%async_computation.1 | async-start | bytes 17301504 | tf_op jit(solution)/shard_map/all_gather | solution.py:861
  8.6 36.9 %copy-start.54 = (bf16[64,1024]{1,0:T(8,128)(2,1)S(1)}, bf16[64,1024]{1,0:T(8,128)(2,1)}, u32[]{:S(2)}) copy-start(bf16[64,1024]{1,0:T(8,128)(2,1)} %param.29) | copy-start | bytes 393220
  8.7 38.0 %copy-start.58 = (s32[1,1024]{1,0:T(1,128)S(1)}, s32[1,1024]{1,0:T(1,128)}, u32[]{:S(2)}) copy-start(s32[1,1024]{1,0:T(1,128)} %param.22) | copy-start | bytes 12292
  8.7 75.4 %copy-start.55 = (bf16[64,1024]{1,0:T(8,128)(2,1)S(1)}, bf16[64,1024]{1,0:T(8,128)(2,1)}, u32[]{:S(2)}) copy-start(bf16[64,1024]{1,0:T(8,128)(2,1)} %param.30) | copy-start | bytes 393220
  9.7 548.5 %reduce-scatter.2.cloned.1.call-start = ((), (), s32[]{:S(2)}) async-start(), calls=%async_computation.2 | async-start | bytes 17825792 | tf_op jit(solution)/shard_map/reduce_scatter | solution.py:925
  9.9 87.6 %copy-start.22 = (bf16[208,1024]{1,0:T(8,128)(2,1)}, bf16[208,1024]{1,0:T(8,128)(2,1)S(1)}, u32[]{:S(2)}) copy-start(bf16[208,1024]{1,0:T(8,128)(2,1)S(1)} %fusion.5.rest_0_.rest_9_) | copy-start | bytes 1277956
  9.9 12.8 %collective-permute-start.3 = (bf16[208,1024]{1,0:T(8,128)(2,1)S(1)}, bf16[208,1024]{1,0:T(8,128)(2,1)S(1)}, u32[]{:S(2)}, u32[]{:S(2)}) collective-permute-start(bf16[208,1024]{1,0:T(8,128)(2,1)S(1)} %fusion.5.rest_0_.rest_9_), channel_id=1, source_target_pairs={{0,4},{1,5},{4,8},{5,9},{8,12},{9,13},{12,14},{13,15},{14,10},{15,... | collective-permute-start | bytes 1277960 | tf_op jit(solution)/shard_map/ppermute | solution.py:723
  13.0 72.3 %collective-permute-start.7 = (bf16[208,1024]{1,0:T(8,128)(2,1)S(1)}, bf16[208,1024]{1,0:T(8,128)(2,1)S(1)}, u32[]{:S(2)}, u32[]{:S(2)}) collective-permute-start(bf16[208,1024]{1,0:T(8,128)(2,1)S(1)} %fusion.5.rest_0_.rest_9_), channel_id=1, source_target_pairs={{0,1},{1,0},{2,3},{3,2},{4,5},{5,4},{6,7},{7,6},{8,9},{9,8},{10,11... | collective-permute-start | bytes 1277960 | tf_op jit(solution)/shard_map/ppermute | solution.py:728
  13.0 32.6 %collective-permute-start = (bf16[208,1024]{1,0:T(8,128)(2,1)S(1)}, bf16[208,1024]{1,0:T(8,128)(2,1)S(1)}, u32[]{:S(2)}, u32[]{:S(2)}) collective-permute-start(bf16[208,1024]{1,0:T(8,128)(2,1)S(1)} %fusion.5.rest_0_.rest_9_), channel_id=1, source_target_pairs={{4,0},{5,1},{8,4},{9,5},{12,8},{13,9},{14,12},{15,13},{10,14},{11,... | collective-permute-start | bytes 1277960 | tf_op jit(solution)/shard_map/ppermute | solution.py:726
  22.8 74.8 %copy-start.23 = (bf16[208,1024]{1,0:T(8,128)(2,1)}, bf16[208,1024]{1,0:T(8,128)(2,1)S(1)}, u32[]{:S(2)}) copy-start(bf16[208,1024]{1,0:T(8,128)(2,1)S(1)} %collective-permute-done.3.rest_7_.rest_16_) | copy-start | bytes 1277956
  22.8 20.3 %collective-permute-start.4 = (bf16[208,1024]{1,0:T(8,128)(2,1)S(1)}, bf16[208,1024]{1,0:T(8,128)(2,1)S(1)}, u32[]{:S(2)}, u32[]{:S(2)}) collective-permute-start(bf16[208,1024]{1,0:T(8,128)(2,1)S(1)} %collective-permute-done.3.rest_7_.rest_16_), channel_id=1, source_target_pairs={{0,4},{1,5},{4,8},{5,9},{8,12},{9,13},{12,14},{13,15},{14,10},{15,... | collective-permute-start | bytes 1277960 | tf_op jit(solution)/shard_map/ppermute | solution.py:723
  43.1 51.5 %copy-start.26 = (bf16[208,1024]{1,0:T(8,128)(2,1)}, bf16[208,1024]{1,0:T(8,128)(2,1)S(1)}, u32[]{:S(2)}) copy-start(bf16[208,1024]{1,0:T(8,128)(2,1)S(1)} %collective-permute-done.4.rest_6_.rest_15_) | copy-start | bytes 1277956
  43.1 14.5 %collective-permute-start.5 = (bf16[208,1024]{1,0:T(8,128)(2,1)S(1)}, bf16[208,1024]{1,0:T(8,128)(2,1)S(1)}, u32[]{:S(2)}, u32[]{:S(2)}) collective-permute-start(bf16[208,1024]{1,0:T(8,128)(2,1)S(1)} %collective-permute-done.4.rest_6_.rest_15_), channel_id=1, source_target_pairs={{0,4},{1,5},{4,8},{5,9},{8,12},{9,13},{12,14},{13,15},{14,10},{15,... | collective-permute-start | bytes 1277960 | tf_op jit(solution)/shard_map/ppermute | solution.py:723
  45.6 49.0 %copy-start.25 = (bf16[208,1024]{1,0:T(8,128)(2,1)}, bf16[208,1024]{1,0:T(8,128)(2,1)S(1)}, u32[]{:S(2)}) copy-start(bf16[208,1024]{1,0:T(8,128)(2,1)S(1)} %collective-permute-done.rest_1_.rest_10_) | copy-start | bytes 1277956
  45.6 22.7 %collective-permute-start.1 = (bf16[208,1024]{1,0:T(8,128)(2,1)S(1)}, bf16[208,1024]{1,0:T(8,128)(2,1)S(1)}, u32[]{:S(2)}, u32[]{:S(2)}) collective-permute-start(bf16[208,1024]{1,0:T(8,128)(2,1)S(1)} %collective-permute-done.rest_1_.rest_10_), channel_id=1, source_target_pairs={{4,0},{5,1},{8,4},{9,5},{12,8},{13,9},{14,12},{15,13},{10,14},{11,... | collective-permute-start | bytes 1277960 | tf_op jit(solution)/shard_map/ppermute | solution.py:726
  57.6 37.3 %copy-start.27 = (bf16[208,1024]{1,0:T(8,128)(2,1)}, bf16[208,1024]{1,0:T(8,128)(2,1)S(1)}, u32[]{:S(2)}) copy-start(bf16[208,1024]{1,0:T(8,128)(2,1)S(1)} %collective-permute-done.5.rest_5_.rest_14_) | copy-start | bytes 1277956
  57.6 25.8 %collective-permute-start.6 = (bf16[208,1024]{1,0:T(8,128)(2,1)S(1)}, bf16[208,1024]{1,0:T(8,128)(2,1)S(1)}, u32[]{:S(2)}, u32[]{:S(2)}) collective-permute-start(bf16[208,1024]{1,0:T(8,128)(2,1)S(1)} %collective-permute-done.5.rest_5_.rest_14_), channel_id=1, source_target_pairs={{0,4},{1,5},{4,8},{5,9},{8,12},{9,13},{12,14},{13,15},{14,10},{15,... | collective-permute-start | bytes 1277960 | tf_op jit(solution)/shard_map/ppermute | solution.py:723
  67.8 18.2 %collective-permute-start.14 = (bf16[208,1024]{1,0:T(8,128)(2,1)S(1)}, bf16[208,1024]{1,0:T(8,128)(2,1)S(1)}, u32[]{:S(2)}, u32[]{:S(2)}) collective-permute-start(bf16[208,1024]{1,0:T(8,128)(2,1)S(1)} %collective-permute-done.3.rest_7_.rest_16_), channel_id=1, source_target_pairs={{0,1},{1,0},{2,3},{3,2},{4,5},{5,4},{6,7},{7,6},{8,9},{9,8},{10,11... | collective-permute-start | bytes 1277960 | tf_op jit(solution)/shard_map/ppermute | solution.py:728
  67.8 21.4 %collective-permute-start.8 = (bf16[208,1024]{1,0:T(8,128)(2,1)S(1)}, bf16[208,1024]{1,0:T(8,128)(2,1)S(1)}, u32[]{:S(2)}, u32[]{:S(2)}) collective-permute-start(bf16[208,1024]{1,0:T(8,128)(2,1)S(1)} %collective-permute-done.rest_1_.rest_10_), channel_id=1, source_target_pairs={{0,1},{1,0},{2,3},{3,2},{4,5},{5,4},{6,7},{7,6},{8,9},{9,8},{10,11... | collective-permute-start | bytes 1277960 | tf_op jit(solution)/shard_map/ppermute | solution.py:728
  68.3 20.9 %collective-permute-start.2 = (bf16[208,1024]{1,0:T(8,128)(2,1)S(1)}, bf16[208,1024]{1,0:T(8,128)(2,1)S(1)}, u32[]{:S(2)}, u32[]{:S(2)}) collective-permute-start(bf16[208,1024]{1,0:T(8,128)(2,1)S(1)} %collective-permute-done.1.rest_2_.rest_11_), channel_id=1, source_target_pairs={{4,0},{5,1},{8,4},{9,5},{12,8},{13,9},{14,12},{15,13},{10,14},{11,... | collective-permute-start | bytes 1277960 | tf_op jit(solution)/shard_map/ppermute | solution.py:726
  83.4 7.2 %collective-permute-start.13 = (bf16[208,1024]{1,0:T(8,128)(2,1)S(1)}, bf16[208,1024]{1,0:T(8,128)(2,1)S(1)}, u32[]{:S(2)}, u32[]{:S(2)}) collective-permute-start(bf16[208,1024]{1,0:T(8,128)(2,1)S(1)} %collective-permute-done.4.rest_6_.rest_15_), channel_id=1, source_target_pairs={{0,1},{1,0},{2,3},{3,2},{4,5},{5,4},{6,7},{7,6},{8,9},{9,8},{10,11... | collective-permute-start | bytes 1277960 | tf_op jit(solution)/shard_map/ppermute | solution.py:728
  84.1 84.0 %copy-start.5 = (bf16[320,1024]{1,0:T(8,128)(2,1)}, bf16[320,1024]{1,0:T(8,128)(2,1)S(1)}, u32[]{:S(2)}) copy-start(bf16[320,1024]{1,0:T(8,128)(2,1)S(1)} %constant_dynamic-update-slice_fusion.rest_5_.rest_4_.rest_0_) | copy-start | bytes 1966084
  85.4 9.2 %collective-permute-start.9 = (bf16[208,1024]{1,0:T(8,128)(2,1)S(1)}, bf16[208,1024]{1,0:T(8,128)(2,1)S(1)}, u32[]{:S(2)}, u32[]{:S(2)}) collective-permute-start(bf16[208,1024]{1,0:T(8,128)(2,1)S(1)} %collective-permute-done.1.rest_2_.rest_11_), channel_id=1, source_target_pairs={{0,1},{1,0},{2,3},{3,2},{4,5},{5,4},{6,7},{7,6},{8,9},{9,8},{10,11... | collective-permute-start | bytes 1277960 | tf_op jit(solution)/shard_map/ppermute | solution.py:728
  86.0 8.9 %collective-permute-start.12 = (bf16[208,1024]{1,0:T(8,128)(2,1)S(1)}, bf16[208,1024]{1,0:T(8,128)(2,1)S(1)}, u32[]{:S(2)}, u32[]{:S(2)}) collective-permute-start(bf16[208,1024]{1,0:T(8,128)(2,1)S(1)} %collective-permute-done.5.rest_5_.rest_14_), channel_id=1, source_target_pairs={{0,1},{1,0},{2,3},{3,2},{4,5},{5,4},{6,7},{7,6},{8,9},{9,8},{10,11... | collective-permute-start | bytes 1277960 | tf_op jit(solution)/shard_map/ppermute | solution.py:728
  89.2 5.7 collective-permute-start.10
  89.2 5.7 collective-permute-start.11
  90.6 34.4 %collective-permute-start.18 = (bf16[320,1024]{1,0:T(8,128)(2,1)}, bf16[320,1024]{1,0:T(8,128)(2,1)S(1)}, u32[]{:S(2)}, u32[]{:S(2)}) collective-permute-start(bf16[320,1024]{1,0:T(8,128)(2,1)} %broadcast_add_fusion.5), channel_id=1, source_target_pairs={{0,4},{1,5},{4,8},{5,9},{8,12},{9,13},{12,14},{13,15},{14,10},{15,... | collective-permute-start | bytes 1966088 | tf_op jit(solution)/shard_map/ppermute | solution.py:743
  94.6 57.6 %collective-permute-start.15 = (bf16[320,1024]{1,0:T(8,128)(2,1)}, bf16[320,1024]{1,0:T(8,128)(2,1)S(1)}, u32[]{:S(2)}, u32[]{:S(2)}) collective-permute-start(bf16[320,1024]{1,0:T(8,128)(2,1)} %broadcast_add_fusion.5), channel_id=1, source_target_pairs={{4,0},{5,1},{8,4},{9,5},{12,8},{13,9},{14,12},{15,13},{10,14},{11,... | collective-permute-start | bytes 1966088 | tf_op jit(solution)/shard_map/ppermute | solution.py:745
  125.0 43.1 %copy-start.6 = (bf16[320,1024]{1,0:T(8,128)(2,1)}, bf16[320,1024]{1,0:T(8,128)(2,1)S(1)}, u32[]{:S(2)}) copy-start(bf16[320,1024]{1,0:T(8,128)(2,1)S(1)} %collective-permute-done.18.rest_12_.rest_11_.rest_7_) | copy-start | bytes 1966084
  125.0 33.3 %collective-permute-start.19 = (bf16[320,1024]{1,0:T(8,128)(2,1)S(1)}, bf16[320,1024]{1,0:T(8,128)(2,1)S(1)}, u32[]{:S(2)}, u32[]{:S(2)}) collective-permute-start(bf16[320,1024]{1,0:T(8,128)(2,1)S(1)} %broadcast_add_fusion.3), channel_id=1, source_target_pairs={{0,4},{1,5},{4,8},{5,9},{8,12},{9,13},{12,14},{13,15},{14,10},{15,... | collective-permute-start | bytes 1966088 | tf_op jit(solution)/shard_map/ppermute | solution.py:743
  152.3 48.5 %copy-start.7 = (bf16[320,1024]{1,0:T(8,128)(2,1)}, bf16[320,1024]{1,0:T(8,128)(2,1)S(1)}, u32[]{:S(2)}) copy-start(bf16[320,1024]{1,0:T(8,128)(2,1)S(1)} %collective-permute-done.15.rest_6_.rest_5_.rest_1_) | copy-start | bytes 1966084
  152.3 16.4 %collective-permute-start.16 = (bf16[320,1024]{1,0:T(8,128)(2,1)S(1)}, bf16[320,1024]{1,0:T(8,128)(2,1)S(1)}, u32[]{:S(2)}, u32[]{:S(2)}) collective-permute-start(bf16[320,1024]{1,0:T(8,128)(2,1)S(1)} %broadcast_add_fusion.4), channel_id=1, source_target_pairs={{4,0},{5,1},{8,4},{9,5},{12,8},{13,9},{14,12},{15,13},{10,14},{11,... | collective-permute-start | bytes 1966088 | tf_op jit(solution)/shard_map/ppermute | solution.py:745
  158.4 42.4 %copy-start.8 = (bf16[320,1024]{1,0:T(8,128)(2,1)}, bf16[320,1024]{1,0:T(8,128)(2,1)S(1)}, u32[]{:S(2)}) copy-start(bf16[320,1024]{1,0:T(8,128)(2,1)S(1)} %collective-permute-done.19.rest_11_.rest_10_.rest_6_) | copy-start | bytes 1966084
  158.4 23.6 %collective-permute-start.20 = (bf16[320,1024]{1,0:T(8,128)(2,1)S(1)}, bf16[320,1024]{1,0:T(8,128)(2,1)S(1)}, u32[]{:S(2)}, u32[]{:S(2)}) collective-permute-start(bf16[320,1024]{1,0:T(8,128)(2,1)S(1)} %broadcast_add_fusion.1), channel_id=1, source_target_pairs={{0,4},{1,5},{4,8},{5,9},{8,12},{9,13},{12,14},{13,15},{14,10},{15,... | collective-permute-start | bytes 1966088 | tf_op jit(solution)/shard_map/ppermute | solution.py:743
  168.1 16.7 %collective-permute-start.22 = (bf16[320,1024]{1,0:T(8,128)(2,1)S(1)}, bf16[320,1024]{1,0:T(8,128)(2,1)S(1)}, u32[]{:S(2)}, u32[]{:S(2)}) collective-permute-start(bf16[320,1024]{1,0:T(8,128)(2,1)S(1)} %constant_dynamic-update-slice_fusion.rest_5_.rest_4_.rest_0_), channel_id=1, source_target_pairs={{0,1},{1,0},{2,3},{3,2},{4,5},{5,4},{6,7},{7,6},{8,9},{9,8},{10,11... | collective-permute-start | bytes 1966088 | tf_op jit(solution)/shard_map/ppermute | solution.py:748
  168.1 16.7 %collective-permute-start.29 = (bf16[320,1024]{1,0:T(8,128)(2,1)S(1)}, bf16[320,1024]{1,0:T(8,128)(2,1)S(1)}, u32[]{:S(2)}, u32[]{:S(2)}) collective-permute-start(bf16[320,1024]{1,0:T(8,128)(2,1)S(1)} %collective-permute-done.18.rest_12_.rest_11_.rest_7_), channel_id=1, source_target_pairs={{0,1},{1,0},{2,3},{3,2},{4,5},{5,4},{6,7},{7,6},{8,9},{9,8},{10,11... | collective-permute-start | bytes 1966088 | tf_op jit(solution)/shard_map/ppermute | solution.py:748
  168.6 16.7 %collective-permute-start.23 = (bf16[320,1024]{1,0:T(8,128)(2,1)S(1)}, bf16[320,1024]{1,0:T(8,128)(2,1)S(1)}, u32[]{:S(2)}, u32[]{:S(2)}) collective-permute-start(bf16[320,1024]{1,0:T(8,128)(2,1)S(1)} %collective-permute-done.15.rest_6_.rest_5_.rest_1_), channel_id=1, source_target_pairs={{0,1},{1,0},{2,3},{3,2},{4,5},{5,4},{6,7},{7,6},{8,9},{9,8},{10,11... | collective-permute-start | bytes 1966088 | tf_op jit(solution)/shard_map/ppermute | solution.py:748
  168.8 17.9 %collective-permute-start.17 = (bf16[320,1024]{1,0:T(8,128)(2,1)S(1)}, bf16[320,1024]{1,0:T(8,128)(2,1)S(1)}, u32[]{:S(2)}, u32[]{:S(2)}) collective-permute-start(bf16[320,1024]{1,0:T(8,128)(2,1)S(1)} %broadcast_add_fusion.2), channel_id=1, source_target_pairs={{4,0},{5,1},{8,4},{9,5},{12,8},{13,9},{14,12},{15,13},{10,14},{11,... | collective-permute-start | bytes 1966088 | tf_op jit(solution)/shard_map/ppermute | solution.py:745
  182.0 15.8 %collective-permute-start.21 = (bf16[320,1024]{1,0:T(8,128)(2,1)S(1)}, bf16[320,1024]{1,0:T(8,128)(2,1)S(1)}, u32[]{:S(2)}, u32[]{:S(2)}) collective-permute-start(bf16[320,1024]{1,0:T(8,128)(2,1)S(1)} %collective-permute-done.20.rest_10_.rest_9_.rest_5_), channel_id=1, source_target_pairs={{0,4},{1,5},{4,8},{5,9},{8,12},{9,13},{12,14},{13,15},{14,10},{15,... | collective-permute-start | bytes 1966088 | tf_op jit(solution)/shard_map/ppermute | solution.py:743
  184.8 13.6 %collective-permute-start.24 = (bf16[320,1024]{1,0:T(8,128)(2,1)S(1)}, bf16[320,1024]{1,0:T(8,128)(2,1)S(1)}, u32[]{:S(2)}, u32[]{:S(2)}) collective-permute-start(bf16[320,1024]{1,0:T(8,128)(2,1)S(1)} %collective-permute-done.16.rest_7_.rest_6_.rest_2_), channel_id=1, source_target_pairs={{0,1},{1,0},{2,3},{3,2},{4,5},{5,4},{6,7},{7,6},{8,9},{9,8},{10,11... | collective-permute-start | bytes 1966088 | tf_op jit(solution)/shard_map/ppermute | solution.py:748
  184.9 13.6 %collective-permute-start.28 = (bf16[320,1024]{1,0:T(8,128)(2,1)S(1)}, bf16[320,1024]{1,0:T(8,128)(2,1)S(1)}, u32[]{:S(2)}, u32[]{:S(2)}) collective-permute-start(bf16[320,1024]{1,0:T(8,128)(2,1)S(1)} %collective-permute-done.19.rest_11_.rest_10_.rest_6_), channel_id=1, source_target_pairs={{0,1},{1,0},{2,3},{3,2},{4,5},{5,4},{6,7},{7,6},{8,9},{9,8},{10,11... | collective-permute-start | bytes 1966088 | tf_op jit(solution)/shard_map/ppermute | solution.py:748
  185.4 13.2 %collective-permute-start.27 = (bf16[320,1024]{1,0:T(8,128)(2,1)S(1)}, bf16[320,1024]{1,0:T(8,128)(2,1)S(1)}, u32[]{:S(2)}, u32[]{:S(2)}) collective-permute-start(bf16[320,1024]{1,0:T(8,128)(2,1)S(1)} %collective-permute-done.20.rest_10_.rest_9_.rest_5_), channel_id=1, source_target_pairs={{0,1},{1,0},{2,3},{3,2},{4,5},{5,4},{6,7},{7,6},{8,9},{9,8},{10,11... | collective-permute-start | bytes 1966088 | tf_op jit(solution)/shard_map/ppermute | solution.py:748
  186.6 11.9 %collective-permute-start.25 = (bf16[320,1024]{1,0:T(8,128)(2,1)S(1)}, bf16[320,1024]{1,0:T(8,128)(2,1)S(1)}, u32[]{:S(2)}, u32[]{:S(2)}) collective-permute-start(bf16[320,1024]{1,0:T(8,128)(2,1)S(1)} %collective-permute-done.17.rest_8_.rest_7_.rest_3_), channel_id=1, source_target_pairs={{0,1},{1,0},{2,3},{3,2},{4,5},{5,4},{6,7},{7,6},{8,9},{9,8},{10,11... | collective-permute-start | bytes 1966088 | tf_op jit(solution)/shard_map/ppermute | solution.py:748
  197.8 2.1 collective-permute-start.26
  427.1 16.1 %collective-permute-start.30 = (bf16[8,512,512]{2,1,0:T(8,128)(2,1)}, bf16[8,512,512]{2,1,0:T(8,128)(2,1)}, u32[]{:S(2)}, u32[]{:S(2)}) collective-permute-start(bf16[8,512,512]{2,1,0:T(8,128)(2,1)} %get-tuple-element.104), channel_id=1, source_target_pairs={{0,1},{1,0},{2,3},{3,2},{4,5},{5,4},{6,7},{7,6},{8,9},{9,8},{10,11... | collective-permute-start | bytes 12582920 | tf_op jit(solution)/shard_map/ppermute | solution.py:793
  445.6 26.0 %collective-permute-start.32 = (bf16[512,512]{1,0:T(8,128)(2,1)}, bf16[512,512]{1,0:T(8,128)(2,1)S(1)}, u32[]{:S(2)}, u32[]{:S(2)}) collective-permute-start(bf16[512,512]{1,0:T(8,128)(2,1)} %get-tuple-element.106), channel_id=1, source_target_pairs={{0,4},{1,5},{4,8},{5,9},{8,12},{9,13},{12,14},{13,15},{14,10},{15,... | collective-permute-start | bytes 1572872 | tf_op jit(solution)/shard_map/ppermute | solution.py:784
  451.2 20.4 %collective-permute-start.31 = (bf16[512,512]{1,0:T(8,128)(2,1)}, bf16[512,512]{1,0:T(8,128)(2,1)S(1)}, u32[]{:S(2)}, u32[]{:S(2)}) collective-permute-start(bf16[512,512]{1,0:T(8,128)(2,1)} %get-tuple-element.105.rest_14_), channel_id=1, source_target_pairs={{4,0},{5,1},{8,4},{9,5},{12,8},{13,9},{14,12},{15,13},{10,14},{11,... | collective-permute-start | bytes 1572872 | tf_op jit(solution)/shard_map/ppermute | solution.py:782
  475.4 13.4 %collective-permute-start.35 = (bf16[8,544,512]{2,1,0:T(8,128)(2,1)}, bf16[8,544,512]{2,1,0:T(8,128)(2,1)}, u32[]{:S(2)}, u32[]{:S(2)}) collective-permute-start(bf16[8,544,512]{2,1,0:T(8,128)(2,1)} %get-tuple-element.116), channel_id=1, source_target_pairs={{0,1},{1,0},{2,3},{3,2},{4,5},{5,4},{6,7},{7,6},{8,9},{9,8},{10,11... | collective-permute-start | bytes 13369352 | tf_op jit(solution)/shard_map/ppermute | solution.py:793
  475.6 28.8 %collective-permute-start.34 = (bf16[512,512]{1,0:T(8,128)(2,1)}, bf16[512,512]{1,0:T(8,128)(2,1)S(1)}, u32[]{:S(2)}, u32[]{:S(2)}) collective-permute-start(bf16[512,512]{1,0:T(8,128)(2,1)} %get-tuple-element.115), channel_id=1, source_target_pairs={{0,4},{1,5},{4,8},{5,9},{8,12},{9,13},{12,14},{13,15},{14,10},{15,... | collective-permute-start | bytes 1572872 | tf_op jit(solution)/shard_map/ppermute | solution.py:784
  477.4 37.7 %collective-permute-start.33 = (bf16[512,512]{1,0:T(8,128)(2,1)}, bf16[512,512]{1,0:T(8,128)(2,1)S(1)}, u32[]{:S(2)}, u32[]{:S(2)}) collective-permute-start(bf16[512,512]{1,0:T(8,128)(2,1)} %get-tuple-element.114.rest_16_), channel_id=1, source_target_pairs={{4,0},{5,1},{8,4},{9,5},{12,8},{13,9},{14,12},{15,13},{10,14},{11,... | collective-permute-start | bytes 1572872 | tf_op jit(solution)/shard_map/ppermute | solution.py:782
  497.2 65.3 %collective-permute-start.40 = (bf16[8,272,512]{2,1,0:T(8,128)(2,1)}, bf16[8,272,512]{2,1,0:T(8,128)(2,1)S(1)}, u32[]{:S(2)}, u32[]{:S(2)}) collective-permute-start(bf16[8,272,512]{2,1,0:T(8,128)(2,1)} %get-tuple-element.120), channel_id=1, source_target_pairs={{0,16},{16,0},{1,17},{17,1},{2,18},{18,2},{3,19},{19,3},{4,20},{20... | collective-permute-start | bytes 6684680 | tf_op jit(solution)/shard_map/ppermute | solution.py:797
  518.7 20.0 %collective-permute-start.36 = (bf16[512,512]{1,0:T(8,128)(2,1)}, bf16[512,512]{1,0:T(8,128)(2,1)S(1)}, u32[]{:S(2)}, u32[]{:S(2)}) collective-permute-start(bf16[512,512]{1,0:T(8,128)(2,1)} %get-tuple-element.118.rest_3_), channel_id=1, source_target_pairs={{4,0},{5,1},{8,4},{9,5},{12,8},{13,9},{14,12},{15,13},{10,14},{11,... | collective-permute-start | bytes 1572872 | tf_op jit(solution)/shard_map/ppermute | solution.py:782
  527.2 16.9 %collective-permute-start.38 = (bf16[512,512]{1,0:T(8,128)(2,1)}, bf16[512,512]{1,0:T(8,128)(2,1)S(1)}, u32[]{:S(2)}, u32[]{:S(2)}) collective-permute-start(bf16[512,512]{1,0:T(8,128)(2,1)} %get-tuple-element.119), channel_id=1, source_target_pairs={{0,4},{1,5},{4,8},{5,9},{8,12},{9,13},{12,14},{13,15},{14,10},{15,... | collective-permute-start | bytes 1572872 | tf_op jit(solution)/shard_map/ppermute | solution.py:784
  541.7 13.1 %collective-permute-start.37 = (bf16[512,512]{1,0:T(8,128)(2,1)}, bf16[512,512]{1,0:T(8,128)(2,1)S(1)}, u32[]{:S(2)}, u32[]{:S(2)}) collective-permute-start(bf16[512,512]{1,0:T(8,128)(2,1)} %shard_map.316.rest_4_), channel_id=1, source_target_pairs={{4,0},{5,1},{8,4},{9,5},{12,8},{13,9},{14,12},{15,13},{10,14},{11,... | collective-permute-start | bytes 1572872 | tf_op jit(solution)/shard_map/ppermute | solution.py:782
  556.3 14.9 %collective-permute-start.39 = (bf16[512,512]{1,0:T(8,128)(2,1)S(1)}, bf16[512,512]{1,0:T(8,128)(2,1)S(1)}, u32[]{:S(2)}, u32[]{:S(2)}) collective-permute-start(bf16[512,512]{1,0:T(8,128)(2,1)S(1)} %fusion.1), channel_id=1, source_target_pairs={{0,16},{16,0},{1,17},{17,1},{2,18},{18,2},{3,19},{19,3},{4,20},{20... | collective-permute-start | bytes 1572872 | tf_op jit(solution)/shard_map/ppermute | solution.py:756
  560.5 30.5 %collective-permute-start.46 = (bf16[512,1024]{1,0:T(8,128)(2,1)}, bf16[512,1024]{1,0:T(8,128)(2,1)}, u32[]{:S(2)}, u32[]{:S(2)}) collective-permute-start(bf16[512,1024]{1,0:T(8,128)(2,1)} %broadcast_add_fusion), channel_id=1, source_target_pairs={{0,16},{16,0},{1,17},{17,1},{2,18},{18,2},{3,19},{19,3},{4,20},{20... | collective-permute-start | bytes 3145736 | tf_op jit(solution)/shard_map/ppermute | solution.py:756
  566.0 6.8 %collective-permute-start.42 = (bf16[272,512]{1,0:T(8,128)(2,1)}, bf16[272,512]{1,0:T(8,128)(2,1)S(1)}, u32[]{:S(2)}, u32[]{:S(2)}) collective-permute-start(bf16[272,512]{1,0:T(8,128)(2,1)} %get-tuple-element.122), channel_id=1, source_target_pairs={{4,0},{5,1},{8,4},{9,5},{12,8},{13,9},{14,12},{15,13},{10,14},{11,... | collective-permute-start | bytes 835592 | tf_op jit(solution)/shard_map/ppermute | solution.py:784
  568.3 6.8 %collective-permute-start.41 = (bf16[272,512]{1,0:T(8,128)(2,1)}, bf16[272,512]{1,0:T(8,128)(2,1)S(1)}, u32[]{:S(2)}, u32[]{:S(2)}) collective-permute-start(bf16[272,512]{1,0:T(8,128)(2,1)} %get-tuple-element.121.rest_6_), channel_id=1, source_target_pairs={{0,4},{1,5},{4,8},{5,9},{8,12},{9,13},{12,14},{13,15},{14,10},{15,... | collective-permute-start | bytes 835592 | tf_op jit(solution)/shard_map/ppermute | solution.py:782
  578.1 6.8 %collective-permute-start.44 = (bf16[272,512]{1,0:T(8,128)(2,1)}, bf16[272,512]{1,0:T(8,128)(2,1)S(1)}, u32[]{:S(2)}, u32[]{:S(2)}) collective-permute-start(bf16[272,512]{1,0:T(8,128)(2,1)} %get-tuple-element.124), channel_id=1, source_target_pairs={{4,0},{5,1},{8,4},{9,5},{12,8},{13,9},{14,12},{15,13},{10,14},{11,... | collective-permute-start | bytes 835592 | tf_op jit(solution)/shard_map/ppermute | solution.py:784
  579.2 6.8 %collective-permute-start.43 = (bf16[272,512]{1,0:T(8,128)(2,1)}, bf16[272,512]{1,0:T(8,128)(2,1)S(1)}, u32[]{:S(2)}, u32[]{:S(2)}) collective-permute-start(bf16[272,512]{1,0:T(8,128)(2,1)} %get-tuple-element.123.rest_6_), channel_id=1, source_target_pairs={{0,4},{1,5},{4,8},{5,9},{8,12},{9,13},{12,14},{13,15},{14,10},{15,... | collective-permute-start | bytes 835592 | tf_op jit(solution)/shard_map/ppermute | solution.py:782
  588.9 13.7 %collective-permute-start.48 = (bf16[272,512]{1,0:T(8,128)(2,1)}, bf16[272,512]{1,0:T(8,128)(2,1)S(1)}, u32[]{:S(2)}, u32[]{:S(2)}) collective-permute-start(bf16[272,512]{1,0:T(8,128)(2,1)} %get-tuple-element.130), channel_id=1, source_target_pairs={{4,0},{5,1},{8,4},{9,5},{12,8},{13,9},{14,12},{15,13},{10,14},{11,... | collective-permute-start | bytes 835592 | tf_op jit(solution)/shard_map/ppermute | solution.py:784
  590.4 6.8 %collective-permute-start.45 = (bf16[272,512]{1,0:T(8,128)(2,1)}, bf16[272,512]{1,0:T(8,128)(2,1)S(1)}, u32[]{:S(2)}, u32[]{:S(2)}) collective-permute-start(bf16[272,512]{1,0:T(8,128)(2,1)} %get-tuple-element.125.rest_3_), channel_id=1, source_target_pairs={{0,4},{1,5},{4,8},{5,9},{8,12},{9,13},{12,14},{13,15},{14,10},{15,... | collective-permute-start | bytes 835592 | tf_op jit(solution)/shard_map/ppermute | solution.py:782
  599.8 6.9 %collective-permute-start.47 = (bf16[272,512]{1,0:T(8,128)(2,1)}, bf16[272,512]{1,0:T(8,128)(2,1)S(1)}, u32[]{:S(2)}, u32[]{:S(2)}) collective-permute-start(bf16[272,512]{1,0:T(8,128)(2,1)} %shard_map.321), channel_id=1, source_target_pairs={{0,4},{1,5},{4,8},{5,9},{8,12},{9,13},{12,14},{13,15},{14,10},{15,... | collective-permute-start | bytes 835592 | tf_op jit(solution)/shard_map/ppermute | solution.py:782
  607.9 6.6 %collective-permute-start.49 = (bf16[272,512]{1,0:T(8,128)(2,1)S(1)}, bf16[272,512]{1,0:T(8,128)(2,1)S(1)}, u32[]{:S(2)}, u32[]{:S(2)}) collective-permute-start(bf16[272,512]{1,0:T(8,128)(2,1)S(1)} %fusion.4), channel_id=1, source_target_pairs={{0,16},{16,0},{1,17},{17,1},{2,18},{18,2},{3,19},{19,3},{4,20},{20... | collective-permute-start | bytes 835592 | tf_op jit(solution)/shard_map/ppermute | solution.py:797
  (49 other events, 334.9 us)
Sparse Core Ops, SparseCore 0:
  11.5 155.2 all-gather.1
  325.2 201.5 reduce-scatter.1

commit v5 on v4

--- a/solution.py
+++ b/solution.py
@@ -555,52 +555,39 @@
     )(rank, *extra, *flat, *rights, *after)
 
 
-def ffn_term_kernel(parts, a_ref, du_ref, h_ref, df_ref, *rest):
-    out_ref = rest[-1]
-    step = pl.program_id(1)
-    width = a_ref.shape[1]
-    rows_in = width // out_ref.shape[0]
-    rows_out = parts * rows_in
-    owners = width // rows_out
-
-    def deal(total, rows, first, at):
-        for i in range(width // rows):
-            out_ref[first + i, pl.ds(at, rows)] = total[i * rows : (i + 1) * rows]
-
-    for i in range(parts):
-
-        @pl.when(step == i)
-        def _():
-            total = low(lax.dot_general(a_ref[...], du_ref[...], TN, preferred_element_type=jnp.float32))
-            deal(total, rows_in, 0, i * rows_in)
-
-        @pl.when(step == parts + i)
-        def _():
-            total = low(lax.dot_general(h_ref[...], df_ref[...], TN, preferred_element_type=jnp.float32))
-            deal(total, rows_out, i * owners, parts * rows_in)
-
-
-def ffn_terms(a, du, h, df, count, block=512):
+def ffn_term_kernel(left_ref, right_ref, *rest):
+    total = lax.dot_general(left_ref[...], right_ref[...], TN, preferred_element_type=jnp.float32)
+    rest[-1][...] = low(total).reshape(rest[-1].shape)
+
+
+def ffn_terms(a, du, h, df, count):
     depth, width = a.shape
     parts = du.shape[1] // width
-    rows = (parts * width + h.shape[1]) // count
-    per = width // block
+    rows_in, rows_out = width // count, parts * width // count
+    out_shape = jax.ShapeDtypeStruct((count, parts * rows_in + rows_out, width), jnp.bfloat16)
+    whole = pl.BlockSpec((depth, width), lambda n: (0, 0))
+    part = pl.BlockSpec((depth, width), lambda n: (0, n))
+    params = pltpu.CompilerParams(vmem_limit_bytes=58 << 20)
+    cost = estimate(flops=2 * parts * depth * width * width, bytes_accessed=6 * parts * width * width, transcendentals=0)
+    terms = pl.pallas_call(
+        ffn_term_kernel,
+        grid=(parts,),
+        in_specs=[whole, part],
+        out_specs=pl.BlockSpec((count, rows_in, width), lambda n: (0, n, 0)),
+        out_shape=out_shape,
+        compiler_params=params,
+        cost_estimate=cost,
+    )(a, du)
     return pl.pallas_call(
-        functools.partial(ffn_term_kernel, parts),
-        grid=(per, 2 * parts),
-        in_specs=[
-            pl.BlockSpec((depth, width), lambda n, s: (0, 0)),
-            pl.BlockSpec((depth, block), lambda n, s: (0, jnp.minimum(s, parts - 1) * per + n)),
-            pl.BlockSpec((depth, width), lambda n, s: (0, jnp.maximum(s - parts, 0))),
-            pl.BlockSpec((depth, block), lambda n, s: (0, n)),
-        ],
-        out_specs=pl.BlockSpec((count, rows, block), lambda n, s: (0, 0, n)),
-        out_shape=jax.ShapeDtypeStruct((count, rows, width), jnp.bfloat16),
-        compiler_params=pltpu.CompilerParams(vmem_limit_bytes=58 << 20),
-        cost_estimate=estimate(
-            flops=4 * parts * depth * width * width, bytes_accessed=12 * parts * width * width, transcendentals=0
-        ),
-    )(a, du, h, df)
+        ffn_term_kernel,
+        grid=(parts,),
+        in_specs=[part, whole, pl.BlockSpec(memory_space=pl.ANY)],
+        out_specs=pl.BlockSpec((width // rows_out, rows_out, width), lambda n: (n, 1, 0)),
+        out_shape=out_shape,
+        input_output_aliases={2: 0},
+        compiler_params=params,
+        cost_estimate=cost,
+    )(h, df, terms)
 
 
 def halve_kernel(rep_ref, mine_ref, came_ref, *rest):

time: 631 us -> 626 us (level)
  waiting for transfers between devices: 143 us -> 151 us
  starting transfers between devices: 85.9 us -> 78.4 us
    ppermute x8, starting transfers between devices: 13.6 us -> 5.69 us  [hop(): self.upward = lax.ppermute(sums[0], 'shard', self.up)]
    pallas_call x1 -> x2, Pallas kernels: 31.1 us -> 26.4 us  [the longest x1 13.3 us: ffn_terms(): pl.pallas_call(ffn_term_kernel, grid=(parts,), in_specs=[part, whole, pl....]
  transfers between devices with their start and end apart: 52 -> 52, of which waited for: 21 -> 24; matrix products, arithmetic and copies ran while one was open for 4% -> 4% of each run, Pallas kernels for 39% -> 39%
where the time goes in v5:
time: 626 us; the launch traced here: 620 us
  Pallas kernels  328 us (52%)
  waiting for transfers between devices  151 us (24%)
  starting transfers between devices  78.4 us (13%)
  local copies, waits for them, and re-layouts  23.1 us (4%)
  other arithmetic  21.9 us (3%)
  between operations  17.9 us (3%)
    pallas_call x6, Pallas kernels, by_rows(): pl.pallas_call(kernel, grid_spec=pltpu.PrefetchScalarGridSpec(num_scalar_...  129 us
    pallas_call x3, Pallas kernels, attend_backward(): pl.pallas_call(functools.partial(attend_backward_kernel, bq, bk, causal,...  69.3 us
    ppermute x4, waiting for transfers between devices, gather_pieces(): upward = lax.ppermute(upward, 'shard', up)  52.5 us
    ppermute x8, waiting for transfers between devices, hop(): self.upward = lax.ppermute(sums[0], 'shard', self.up)  46.3 us
    pallas_call x3, Pallas kernels, attend_forward(): pl.pallas_call(functools.partial(attend_forward_kernel, bq, bk, causal, h...  42 us
    pallas_call x2, Pallas kernels, term_sets(): pl.pallas_call(functools.partial(term_kernel, [p[0] for p in parts], chip...  37.6 us
    ppermute x4, waiting for transfers between devices, hop(): lax.ppermute(upward + held, 'shard', self.up)  29.3 us
    ppermute x4, starting transfers between devices, hop(): lax.ppermute(upward + held, 'shard', self.up)  28.4 us
  transfers between devices with their start and end apart: 52, of which 24 were waited for; matrix products, arithmetic and copies ran while one was open for 4% of the time, Pallas kernels for 39%

profile of v5, /device:TPU:0, one launch (start us, length us, event | category | flops | bytes accessed | tf_op | source)
XLA Modules:
  0.0 620.0 jit_solution(17001674353899798506)
XLA Ops:
  9.9 3.1 collective-permute-start.3
  14.6 8.2 %collective-permute-done.3.rest_7_.rest_16_ = bf16[208,1024]{1,0:T(8,128)(2,1)S(1)} collective-permute-done((bf16[208,1024]{1,0:T(8,128)(2,1)S(1)}, bf16[208,1024]{1,0:T(8,128)(2,1)S(1)}, u32[]{:S(2)}, u32[]{:S(2)}) %collective-permute-start.3) | collective-permute-done | bytes 426016 | tf_op jit(solution)/shard_map/ppermute | solution.py:710
  22.8 1.8 collective-permute-start.4
  24.7 18.4 %collective-permute-done.4.rest_6_.rest_15_ = bf16[208,1024]{1,0:T(8,128)(2,1)S(1)} collective-permute-done((bf16[208,1024]{1,0:T(8,128)(2,1)S(1)}, bf16[208,1024]{1,0:T(8,128)(2,1)S(1)}, u32[]{:S(2)}, u32[]{:S(2)}) %collective-permute-start.4) | collective-permute-done | bytes 426016 | tf_op jit(solution)/shard_map/ppermute | solution.py:710
  43.1 2.5 collective-permute-start.5
  46.8 10.7 %collective-permute-done.5.rest_5_.rest_14_ = bf16[208,1024]{1,0:T(8,128)(2,1)S(1)} collective-permute-done((bf16[208,1024]{1,0:T(8,128)(2,1)S(1)}, bf16[208,1024]{1,0:T(8,128)(2,1)S(1)}, u32[]{:S(2)}, u32[]{:S(2)}) %collective-permute-start.5) | collective-permute-done | bytes 426016 | tf_op jit(solution)/shard_map/ppermute | solution.py:710
  57.6 9.3 %collective-permute-start.6 = (bf16[208,1024]{1,0:T(8,128)(2,1)S(1)}, bf16[208,1024]{1,0:T(8,128)(2,1)S(1)}, u32[]{:S(2)}, u32[]{:S(2)}) collective-permute-start(bf16[208,1024]{1,0:T(8,128)(2,1)S(1)} %collective-permute-done.5.rest_5_.rest_14_), channel_id=1, source_target_pairs={{0,4},{1,5},{4,8},{5,9},{8,12},{9,13},{12,14},{13,15},{14,10},{15,... | collective-permute-start | bytes 1277960 | tf_op jit(solution)/shard_map/ppermute | solution.py:710
  68.4 15.1 %collective-permute-done.6.rest_4_.rest_13_ = bf16[208,1024]{1,0:T(8,128)(2,1)S(1)} collective-permute-done((bf16[208,1024]{1,0:T(8,128)(2,1)S(1)}, bf16[208,1024]{1,0:T(8,128)(2,1)S(1)}, u32[]{:S(2)}, u32[]{:S(2)}) %collective-permute-start.6) | collective-permute-done | bytes 426016 | tf_op jit(solution)/shard_map/ppermute | solution.py:710
  86.0 3.1 collective-permute-done.2.rest_3_.rest_12_
  90.6 2.1 collective-permute-start.18
  97.6 13.9 %shard_map.298 = (bf16[1024,1024]{1,0:T(8,128)(2,1)}, bf16[1024,1024]{1,0:T(8,128)(2,1)}, bf16[1024,1024]{1,0:T(8,128)(2,1)}, bf16[1024,1024]{1,0:T(8,128)(2,1)}) custom-call(s32[16]{0:T(128)} %copy-done.57, bf16[1024,1024]{1,0:T(8,128)(2,1)} %bitcast.38, f32[8,1024]{1,0:T(8,128)} %reshape.101.norm_ref.rest_4_.rest_3_.rest_8_, bf16[208,1024]{1,0:T(8,128)(2,1)} %copy-done.22, ...), custom_call_target="tpu_custom_call" | custom-call | flops 805306368 | bytes 1310720 | tf_op jit(solution)/shard_map/pallas_call | solution.py:473
  111.5 11.6 %shard_map.299 = (bf16[1024,512]{1,0:T(8,128)(2,1)}, bf16[1024,512]{1,0:T(8,128)(2,1)}) custom-call(s32[8]{0:T(128)} %pad_add_fusion.1.win_ref, bf16[1024,1024]{1,0:T(8,128)(2,1)} %get-tuple-element.73.q_ref, bf16[1024,1024]{1,0:T(8,128)(2,1)} %get-tuple-element.74.k_ref, bf16[1024,1024]{1,0:T(8,128)(2,1)} %get-tuple-element.75.v_ref, ...), custom_call_target="tpu_custom_call" | custom-call | flops 1073741824 | bytes 655360 | tf_op jit(solution)/shard_map/pallas_call | solution.py:129
  125.0 13.7 %collective-permute-start.19 = (bf16[320,1024]{1,0:T(8,128)(2,1)S(1)}, bf16[320,1024]{1,0:T(8,128)(2,1)S(1)}, u32[]{:S(2)}, u32[]{:S(2)}) collective-permute-start(bf16[320,1024]{1,0:T(8,128)(2,1)S(1)} %broadcast_add_fusion.3), channel_id=1, source_target_pairs={{0,4},{1,5},{4,8},{5,9},{8,12},{9,13},{12,14},{13,15},{14,10},{15,... | collective-permute-start | bytes 1966088 | tf_op jit(solution)/shard_map/ppermute | solution.py:730
  138.7 11.7 %shard_map.300 = (bf16[1024,512]{1,0:T(8,128)(2,1)}, bf16[1024,512]{1,0:T(8,128)(2,1)}) custom-call(s32[8]{0:T(128)} %pad_add_fusion.1.win_ref, bf16[1024,1024]{1,0:T(8,128)(2,1)} %get-tuple-element.73.q_ref, bf16[1024,1024]{1,0:T(8,128)(2,1)} %get-tuple-element.74.k_ref, bf16[1024,1024]{1,0:T(8,128)(2,1)} %get-tuple-element.75.v_ref, ...), custom_call_target="tpu_custom_call" | custom-call | flops 1073741824 | bytes 655360 | tf_op jit(solution)/shard_map/pallas_call | solution.py:129
  152.4 5.9 collective-permute-done.19.rest_11_.rest_10_.rest_6_
  158.3 9.8 %collective-permute-start.20 = (bf16[320,1024]{1,0:T(8,128)(2,1)S(1)}, bf16[320,1024]{1,0:T(8,128)(2,1)S(1)}, u32[]{:S(2)}, u32[]{:S(2)}) collective-permute-start(bf16[320,1024]{1,0:T(8,128)(2,1)S(1)} %broadcast_add_fusion.1), channel_id=1, source_target_pairs={{0,4},{1,5},{4,8},{5,9},{8,12},{9,13},{12,14},{13,15},{14,10},{15,... | collective-permute-start | bytes 1966088 | tf_op jit(solution)/shard_map/ppermute | solution.py:730
  169.8 12.2 %collective-permute-done.20.rest_10_.rest_9_.rest_5_ = bf16[320,1024]{1,0:T(8,128)(2,1)S(1)} collective-permute-done((bf16[320,1024]{1,0:T(8,128)(2,1)S(1)}, bf16[320,1024]{1,0:T(8,128)(2,1)S(1)}, u32[]{:S(2)}, u32[]{:S(2)}) %collective-permute-start.20) | collective-permute-done | bytes 655392 | tf_op jit(solution)/shard_map/ppermute | solution.py:730
  182.0 2.9 collective-permute-start.21
  186.6 11.2 %collective-permute-done.21.rest_9_.rest_8_.rest_4_ = bf16[320,1024]{1,0:T(8,128)(2,1)S(1)} collective-permute-done((bf16[320,1024]{1,0:T(8,128)(2,1)S(1)}, bf16[320,1024]{1,0:T(8,128)(2,1)S(1)}, u32[]{:S(2)}, u32[]{:S(2)}) %collective-permute-start.21) | collective-permute-done | bytes 655392 | tf_op jit(solution)/shard_map/ppermute | solution.py:730
  200.8 16.4 %shard_map.301 = (f32[1024,1024]{1,0:T(8,128)}, bf16[1024,1024]{1,0:T(8,128)(2,1)}, bf16[1024,1024]{1,0:T(8,128)(2,1)}, bf16[1024,1024]{1,0:T(8,128)(2,1)}, bf16[1024,1024]{1,0:T(8,128)(2,1)}) custom-call(s32[16]{0:T(128)} %copy-done.57, bf16[1024,512]{1,0:T(8,128)(2,1)} %get-tuple-element.76.rest_0_.o_ref, ...), custom_call_target="tpu_custom_call" | custom-call | flops 1073741824 | bytes 2359296 | tf_op jit(solution)/shard_map/pallas_call | solution.py:473
  217.2 18.6 %shard_map.302 = (bf16[1024,1024]{1,0:T(8,128)(2,1)}, bf16[1024,1024]{1,0:T(8,128)(2,1)}) custom-call(s32[8]{0:T(128)} %pad_add_fusion.win_ref, bf16[1024,1024]{1,0:T(8,128)(2,1)} %get-tuple-element.78.q_ref, bf16[1024,1024]{1,0:T(8,128)(2,1)} %get-tuple-element.79.k_ref, bf16[1024,1024]{1,0:T(8,128)(2,1)} %get-tuple-element.80.v_ref, ...), custom_call_target="tpu_custom_call" | custom-call | flops 2147483648 | bytes 1310720 | tf_op jit(solution)/shard_map/pallas_call | solution.py:129
  235.9 58.1 %shard_map.303 = (bf16[1024,1024]{1,0:T(8,128)(2,1)}, bf16[1024,1024]{1,0:T(8,128)(2,1)}, bf16[1024,4096]{1,0:T(8,128)(2,1)}, bf16[1024,1024]{1,0:T(8,128)(2,1)}...) custom-call(s32[16]{0:T(128)} %copy-done.57, ...), custom_call_target="tpu_custom_call" | custom-call | flops 4831838208 | bytes 4980736 | tf_op jit(solution)/shard_map/pallas_call | solution.py:473
  293.9 13.1 %shard_map.320.rest_0_ = bf16[16,512,1024]{2,1,0:T(8,128)(2,1)} custom-call(bf16[1024,1024]{1,0:T(8,128)(2,1)} %get-tuple-element.128.left_ref, bf16[1024,4096]{1,0:T(8,128)(2,1)} %get-tuple-element.129.right_ref), custom_call_target="tpu_custom_call" | custom-call | flops 1073741824 | bytes 3145728 | tf_op jit(solution)/shard_map/pallas_call | solution.py:572
  307.0 13.3 %shard_map.321 = bf16[16,512,1024]{2,1,0:T(8,128)(2,1)} custom-call(bf16[1024,4096]{1,0:T(8,128)(2,1)} %get-tuple-element.126.left_ref, bf16[1024,1024]{1,0:T(8,128)(2,1)} %get-tuple-element.127.right_ref, bf16[16,512,1024]{2,1,0:T(8,128)(2,1)} %shard_map.320.rest_0_), custom_call_target="tpu_custom_call", output_to_operand_aliasing={{}: (2, {})} | custom-call | flops 1073741824 | bytes 3145728 | tf_op jit(solution)/shard_map/pallas_call | solution.py:581
  321.5 31.1 %shard_map.304 = (bf16[1024,1024]{1,0:T(8,128)(2,1)}, bf16[1024,1024]{1,0:T(8,128)(2,1)}, bf16[1024,1024]{1,0:T(8,128)(2,1)}) custom-call(s32[8]{0:T(128)} %pad_add_fusion.win_ref, bf16[1024,1024]{1,0:T(8,128)(2,1)} %get-tuple-element.78.q_ref, bf16[1024,1024]{1,0:T(8,128)(2,1)} %get-tuple-element.79.k_ref, bf16[1024,1024]{1,0:T(8,128)(2,1)} %get-tuple-element.80.v_ref, ...), custom_call_target="tpu_custom_call" | custom-call | flops 5368709120 | bytes 2097152 | tf_op jit(solution)/shard_map/pallas_call | solution.py:227
  352.6 13.7 %shard_map.305 = (f32[1024,1024]{1,0:T(8,128)}, bf16[1024,1024]{1,0:T(8,128)(2,1)}, bf16[1024,1024]{1,0:T(8,128)(2,1)}, f32[8,1024]{1,0:T(8,128)}) custom-call(s32[16]{0:T(128)} %copy-done.57, bf16[1024,1024]{1,0:T(8,128)(2,1)} %get-tuple-element.86.dq_ref.rest_8_.rest_9_, f32[1024,1024]{1,0:T(8,128)} %get-tuple-element.82.rest_1_.r_ref, ...), custom_call_target="tpu_custom_call" | custom-call | flops 536870912 | bytes 2359296 | tf_op jit(solution)/shard_map/pallas_call | solution.py:473
  366.3 19.3 %shard_map.306 = (bf16[1024,512]{1,0:T(8,128)(2,1)}, bf16[1024,512]{1,0:T(8,128)(2,1)}, bf16[1024,512]{1,0:T(8,128)(2,1)}) custom-call(s32[8]{0:T(128)} %pad_add_fusion.1.win_ref, bf16[1024,1024]{1,0:T(8,128)(2,1)} %get-tuple-element.73.q_ref, bf16[1024,1024]{1,0:T(8,128)(2,1)} %get-tuple-element.74.k_ref, bf16[1024,1024]{1,0:T(8,128)(2,1)} %get-tuple-element.75.v_ref, ...), custom_call_target="tpu_custom_call" | custom-call | flops 2684354560 | bytes 1048576 | tf_op jit(solution)/shard_map/pallas_call | solution.py:227
  385.6 18.9 %shard_map.307 = (bf16[1024,512]{1,0:T(8,128)(2,1)}, bf16[1024,512]{1,0:T(8,128)(2,1)}, bf16[1024,512]{1,0:T(8,128)(2,1)}) custom-call(s32[8]{0:T(128)} %pad_add_fusion.1.win_ref, bf16[1024,1024]{1,0:T(8,128)(2,1)} %get-tuple-element.73.q_ref, bf16[1024,1024]{1,0:T(8,128)(2,1)} %get-tuple-element.74.k_ref, bf16[1024,1024]{1,0:T(8,128)(2,1)} %get-tuple-element.75.v_ref, ...), custom_call_target="tpu_custom_call" | custom-call | flops 2684354560 | bytes 1048576 | tf_op jit(solution)/shard_map/pallas_call | solution.py:227
  404.5 17.2 %shard_map.308 = (bf16[8,512,512]{2,1,0:T(8,128)(2,1)}, bf16[8,512,512]{2,1,0:T(8,128)(2,1)}) custom-call(s32[9]{0:T(128)} %dynamic-slice_bitcast_fusion.rank_ref, bf16[1024,512]{1,0:T(8,128)(2,1)} %get-tuple-element.76.rest_0_.o_ref, bf16[1024,512]{1,0:T(8,128)(2,1)} %get-tuple-element.77.rest_1_.o_ref, bf16[1024,1024]{1,0:T(8,128)(2,1)} %get-tuple-element.98.rest_2_, ...), custom_call_target="tpu_custom_call" | custom-call | flops 1073741824 | bytes 3145728 | tf_op jit(solution)/shard_map/pallas_call | solution.py:539
  421.7 5.6 collective-permute-start.30
  427.3 15.9 %shard_map.309 = (f32[1024,1024]{1,0:T(8,128)}, f32[8,1024]{1,0:T(8,128)}) custom-call(s32[16]{0:T(128)} %copy-done.57, bf16[1024,512]{1,0:T(8,128)(2,1)} %get-tuple-element.90.rest_0_.rest_5_, bf16[1024,512]{1,0:T(8,128)(2,1)} %get-tuple-element.92.rest_6_.rest_1_, bf16[1024,512]{1,0:T(8,128)(2,1)} %get-tuple-element.93.rest_7_.rest_2_, ...), custom_call_target="tpu_custom_call" | custom-call | flops 805306368 | bytes 2097152 | tf_op jit(solution)/shard_map/pallas_call | solution.py:473
  443.2 2.5 shard_map.310
  445.7 5.6 collective-permute-start.32
  451.3 20.4 %shard_map.311 = (bf16[8,544,512]{2,1,0:T(8,128)(2,1)}, bf16[8,544,512]{2,1,0:T(8,128)(2,1)}) custom-call(s32[9]{0:T(128)} %dynamic-slice_bitcast_fusion.rank_ref, f32[8,1024]{1,0:T(8,128)} %get-tuple-element.107.rest_0_, f32[8,1024]{1,0:T(8,128)} %get-tuple-element.108.rest_1_, f32[8,1024]{1,0:T(8,128)} %get-tuple-element.109.rest_2_, ...), custom_call_target="tpu_custom_call" | custom-call | flops 1073741824 | bytes 3145728 | tf_op jit(solution)/shard_map/pallas_call | solution.py:539
  472.7 2.7 shard_map.312
  475.4 2.5 collective-permute-start.34
  477.9 11.1 %shard_map.313.rest_0_ = f32[1024,1024]{1,0:T(8,128)} custom-call(s32[16]{0:T(128)} %copy-done.57, bf16[1024,1024]{1,0:T(8,128)(2,1)} %get-tuple-element.102.rest_10_.rest_11_.dk_ref, bf16[1024,1024]{1,0:T(8,128)(2,1)} %get-tuple-element.103.rest_12_.rest_13_.dv_ref, f32[8,1024]{1,0:T(8,128)} %reshape.101.norm_ref.rest_4_.rest_3_.rest_8_, ...), custom_call_target="tpu_custom_call" | custom-call | flops 536870912 | bytes 1048576 | tf_op jit(solution)/shard_map/pallas_call | solution.py:473
  489.0 2.2 copy-done.2
  491.2 4.8 shard_map.314
  497.4 1.6 collective-permute-start.40
  499.0 2.5 collective-permute-done.34.rest_3_
  501.5 14.1 %collective-permute-done.33.rest_0_ = bf16[512,512]{1,0:T(8,128)(2,1)S(1)} collective-permute-done((bf16[512,512]{1,0:T(8,128)(2,1)}, bf16[512,512]{1,0:T(8,128)(2,1)S(1)}, u32[]{:S(2)}, u32[]{:S(2)}) %collective-permute-start.33) | collective-permute-done | bytes 524320 | tf_op jit(solution)/shard_map/ppermute | solution.py:769
  516.5 2.8 shard_map.315
  519.3 2.0 collective-permute-start.38
  521.3 13.2 %collective-permute-done.36.rest_0_ = bf16[512,512]{1,0:T(8,128)(2,1)S(1)} collective-permute-done((bf16[512,512]{1,0:T(8,128)(2,1)}, bf16[512,512]{1,0:T(8,128)(2,1)S(1)}, u32[]{:S(2)}, u32[]{:S(2)}) %collective-permute-start.36) | collective-permute-done | bytes 524320 | tf_op jit(solution)/shard_map/ppermute | solution.py:769
  535.3 2.1 shard_map.316.rest_4_
  537.5 14.1 %collective-permute-done.37 = bf16[512,512]{1,0:T(8,128)(2,1)S(1)} collective-permute-done((bf16[512,512]{1,0:T(8,128)(2,1)}, bf16[512,512]{1,0:T(8,128)(2,1)S(1)}, u32[]{:S(2)}, u32[]{:S(2)}) %collective-permute-start.37) | collective-permute-done | bytes 524320 | tf_op jit(solution)/shard_map/ppermute | solution.py:769
  551.5 1.5 fusion.1
  555.0 2.3 broadcast_add_fusion
  557.2 2.0 collective-permute-start.46
  560.6 2.1 shard_map.317
  563.0 1.7 collective-permute-start.41
  564.7 3.2 collective-permute-done.39
  568.2 1.9 collective-permute-done.42.rest_3_
  571.5 2.3 shard_map.318
  574.4 1.4 collective-permute-start.43
  578.0 2.6 collective-permute-done.44.rest_3_
  582.0 2.3 shard_map.319
  586.3 2.3 collective-permute-done.46
  588.7 3.0 convert_add_fusion.rest_4_
  592.5 1.9 shard_map.322
  597.6 3.7 collective-permute-done.47
  602.5 1.7 collective-permute-start.49
  605.2 3.9 collective-permute-done.49
  (266 shorter events, 49.7 us)
Async XLA Ops:
  7.3 228.6 %all-gather.2.cloned.1.call-start = ((), (), s32[]{:S(2)}) async-start(), calls=%async_computation.1 | async-start | bytes 17301504 | tf_op jit(solution)/shard_map/all_gather | solution.py:848
  8.6 36.9 %copy-start.54 = (bf16[64,1024]{1,0:T(8,128)(2,1)S(1)}, bf16[64,1024]{1,0:T(8,128)(2,1)}, u32[]{:S(2)}) copy-start(bf16[64,1024]{1,0:T(8,128)(2,1)} %param.29) | copy-start | bytes 393220
  8.7 38.0 %copy-start.58 = (s32[1,1024]{1,0:T(1,128)S(1)}, s32[1,1024]{1,0:T(1,128)}, u32[]{:S(2)}) copy-start(s32[1,1024]{1,0:T(1,128)} %param.22) | copy-start | bytes 12292
  8.7 75.4 %copy-start.55 = (bf16[64,1024]{1,0:T(8,128)(2,1)S(1)}, bf16[64,1024]{1,0:T(8,128)(2,1)}, u32[]{:S(2)}) copy-start(bf16[64,1024]{1,0:T(8,128)(2,1)} %param.30) | copy-start | bytes 393220
  9.7 545.2 %reduce-scatter.2.cloned.1.call-start = ((), (), s32[]{:S(2)}) async-start(), calls=%async_computation.2 | async-start | bytes 17825792 | tf_op jit(solution)/shard_map/reduce_scatter | solution.py:912
  9.9 87.6 %copy-start.22 = (bf16[208,1024]{1,0:T(8,128)(2,1)}, bf16[208,1024]{1,0:T(8,128)(2,1)S(1)}, u32[]{:S(2)}) copy-start(bf16[208,1024]{1,0:T(8,128)(2,1)S(1)} %fusion.5.rest_0_.rest_9_) | copy-start | bytes 1277956
  9.9 12.8 %collective-permute-start.3 = (bf16[208,1024]{1,0:T(8,128)(2,1)S(1)}, bf16[208,1024]{1,0:T(8,128)(2,1)S(1)}, u32[]{:S(2)}, u32[]{:S(2)}) collective-permute-start(bf16[208,1024]{1,0:T(8,128)(2,1)S(1)} %fusion.5.rest_0_.rest_9_), channel_id=1, source_target_pairs={{0,4},{1,5},{4,8},{5,9},{8,12},{9,13},{12,14},{13,15},{14,10},{15,... | collective-permute-start | bytes 1277960 | tf_op jit(solution)/shard_map/ppermute | solution.py:710
  13.0 72.3 %collective-permute-start.7 = (bf16[208,1024]{1,0:T(8,128)(2,1)S(1)}, bf16[208,1024]{1,0:T(8,128)(2,1)S(1)}, u32[]{:S(2)}, u32[]{:S(2)}) collective-permute-start(bf16[208,1024]{1,0:T(8,128)(2,1)S(1)} %fusion.5.rest_0_.rest_9_), channel_id=1, source_target_pairs={{0,1},{1,0},{2,3},{3,2},{4,5},{5,4},{6,7},{7,6},{8,9},{9,8},{10,11... | collective-permute-start | bytes 1277960 | tf_op jit(solution)/shard_map/ppermute | solution.py:715
  13.0 32.6 %collective-permute-start = (bf16[208,1024]{1,0:T(8,128)(2,1)S(1)}, bf16[208,1024]{1,0:T(8,128)(2,1)S(1)}, u32[]{:S(2)}, u32[]{:S(2)}) collective-permute-start(bf16[208,1024]{1,0:T(8,128)(2,1)S(1)} %fusion.5.rest_0_.rest_9_), channel_id=1, source_target_pairs={{4,0},{5,1},{8,4},{9,5},{12,8},{13,9},{14,12},{15,13},{10,14},{11,... | collective-permute-start | bytes 1277960 | tf_op jit(solution)/shard_map/ppermute | solution.py:713
  22.8 74.8 %copy-start.23 = (bf16[208,1024]{1,0:T(8,128)(2,1)}, bf16[208,1024]{1,0:T(8,128)(2,1)S(1)}, u32[]{:S(2)}) copy-start(bf16[208,1024]{1,0:T(8,128)(2,1)S(1)} %collective-permute-done.3.rest_7_.rest_16_) | copy-start | bytes 1277956
  22.8 20.3 %collective-permute-start.4 = (bf16[208,1024]{1,0:T(8,128)(2,1)S(1)}, bf16[208,1024]{1,0:T(8,128)(2,1)S(1)}, u32[]{:S(2)}, u32[]{:S(2)}) collective-permute-start(bf16[208,1024]{1,0:T(8,128)(2,1)S(1)} %collective-permute-done.3.rest_7_.rest_16_), channel_id=1, source_target_pairs={{0,4},{1,5},{4,8},{5,9},{8,12},{9,13},{12,14},{13,15},{14,10},{15,... | collective-permute-start | bytes 1277960 | tf_op jit(solution)/shard_map/ppermute | solution.py:710
  43.1 51.5 %copy-start.26 = (bf16[208,1024]{1,0:T(8,128)(2,1)}, bf16[208,1024]{1,0:T(8,128)(2,1)S(1)}, u32[]{:S(2)}) copy-start(bf16[208,1024]{1,0:T(8,128)(2,1)S(1)} %collective-permute-done.4.rest_6_.rest_15_) | copy-start | bytes 1277956
  43.1 14.5 %collective-permute-start.5 = (bf16[208,1024]{1,0:T(8,128)(2,1)S(1)}, bf16[208,1024]{1,0:T(8,128)(2,1)S(1)}, u32[]{:S(2)}, u32[]{:S(2)}) collective-permute-start(bf16[208,1024]{1,0:T(8,128)(2,1)S(1)} %collective-permute-done.4.rest_6_.rest_15_), channel_id=1, source_target_pairs={{0,4},{1,5},{4,8},{5,9},{8,12},{9,13},{12,14},{13,15},{14,10},{15,... | collective-permute-start | bytes 1277960 | tf_op jit(solution)/shard_map/ppermute | solution.py:710
  45.6 49.0 %copy-start.25 = (bf16[208,1024]{1,0:T(8,128)(2,1)}, bf16[208,1024]{1,0:T(8,128)(2,1)S(1)}, u32[]{:S(2)}) copy-start(bf16[208,1024]{1,0:T(8,128)(2,1)S(1)} %collective-permute-done.rest_1_.rest_10_) | copy-start | bytes 1277956
  45.6 22.7 %collective-permute-start.1 = (bf16[208,1024]{1,0:T(8,128)(2,1)S(1)}, bf16[208,1024]{1,0:T(8,128)(2,1)S(1)}, u32[]{:S(2)}, u32[]{:S(2)}) collective-permute-start(bf16[208,1024]{1,0:T(8,128)(2,1)S(1)} %collective-permute-done.rest_1_.rest_10_), channel_id=1, source_target_pairs={{4,0},{5,1},{8,4},{9,5},{12,8},{13,9},{14,12},{15,13},{10,14},{11,... | collective-permute-start | bytes 1277960 | tf_op jit(solution)/shard_map/ppermute | solution.py:713
  57.6 37.3 %copy-start.27 = (bf16[208,1024]{1,0:T(8,128)(2,1)}, bf16[208,1024]{1,0:T(8,128)(2,1)S(1)}, u32[]{:S(2)}) copy-start(bf16[208,1024]{1,0:T(8,128)(2,1)S(1)} %collective-permute-done.5.rest_5_.rest_14_) | copy-start | bytes 1277956
  57.6 25.8 %collective-permute-start.6 = (bf16[208,1024]{1,0:T(8,128)(2,1)S(1)}, bf16[208,1024]{1,0:T(8,128)(2,1)S(1)}, u32[]{:S(2)}, u32[]{:S(2)}) collective-permute-start(bf16[208,1024]{1,0:T(8,128)(2,1)S(1)} %collective-permute-done.5.rest_5_.rest_14_), channel_id=1, source_target_pairs={{0,4},{1,5},{4,8},{5,9},{8,12},{9,13},{12,14},{13,15},{14,10},{15,... | collective-permute-start | bytes 1277960 | tf_op jit(solution)/shard_map/ppermute | solution.py:710
  67.8 18.2 %collective-permute-start.14 = (bf16[208,1024]{1,0:T(8,128)(2,1)S(1)}, bf16[208,1024]{1,0:T(8,128)(2,1)S(1)}, u32[]{:S(2)}, u32[]{:S(2)}) collective-permute-start(bf16[208,1024]{1,0:T(8,128)(2,1)S(1)} %collective-permute-done.3.rest_7_.rest_16_), channel_id=1, source_target_pairs={{0,1},{1,0},{2,3},{3,2},{4,5},{5,4},{6,7},{7,6},{8,9},{9,8},{10,11... | collective-permute-start | bytes 1277960 | tf_op jit(solution)/shard_map/ppermute | solution.py:715
  67.8 21.4 %collective-permute-start.8 = (bf16[208,1024]{1,0:T(8,128)(2,1)S(1)}, bf16[208,1024]{1,0:T(8,128)(2,1)S(1)}, u32[]{:S(2)}, u32[]{:S(2)}) collective-permute-start(bf16[208,1024]{1,0:T(8,128)(2,1)S(1)} %collective-permute-done.rest_1_.rest_10_), channel_id=1, source_target_pairs={{0,1},{1,0},{2,3},{3,2},{4,5},{5,4},{6,7},{7,6},{8,9},{9,8},{10,11... | collective-permute-start | bytes 1277960 | tf_op jit(solution)/shard_map/ppermute | solution.py:715
  68.3 20.9 %collective-permute-start.2 = (bf16[208,1024]{1,0:T(8,128)(2,1)S(1)}, bf16[208,1024]{1,0:T(8,128)(2,1)S(1)}, u32[]{:S(2)}, u32[]{:S(2)}) collective-permute-start(bf16[208,1024]{1,0:T(8,128)(2,1)S(1)} %collective-permute-done.1.rest_2_.rest_11_), channel_id=1, source_target_pairs={{4,0},{5,1},{8,4},{9,5},{12,8},{13,9},{14,12},{15,13},{10,14},{11,... | collective-permute-start | bytes 1277960 | tf_op jit(solution)/shard_map/ppermute | solution.py:713
  83.4 7.2 %collective-permute-start.13 = (bf16[208,1024]{1,0:T(8,128)(2,1)S(1)}, bf16[208,1024]{1,0:T(8,128)(2,1)S(1)}, u32[]{:S(2)}, u32[]{:S(2)}) collective-permute-start(bf16[208,1024]{1,0:T(8,128)(2,1)S(1)} %collective-permute-done.4.rest_6_.rest_15_), channel_id=1, source_target_pairs={{0,1},{1,0},{2,3},{3,2},{4,5},{5,4},{6,7},{7,6},{8,9},{9,8},{10,11... | collective-permute-start | bytes 1277960 | tf_op jit(solution)/shard_map/ppermute | solution.py:715
  84.1 84.0 %copy-start.5 = (bf16[320,1024]{1,0:T(8,128)(2,1)}, bf16[320,1024]{1,0:T(8,128)(2,1)S(1)}, u32[]{:S(2)}) copy-start(bf16[320,1024]{1,0:T(8,128)(2,1)S(1)} %constant_dynamic-update-slice_fusion.rest_5_.rest_4_.rest_0_) | copy-start | bytes 1966084
  85.4 9.2 %collective-permute-start.9 = (bf16[208,1024]{1,0:T(8,128)(2,1)S(1)}, bf16[208,1024]{1,0:T(8,128)(2,1)S(1)}, u32[]{:S(2)}, u32[]{:S(2)}) collective-permute-start(bf16[208,1024]{1,0:T(8,128)(2,1)S(1)} %collective-permute-done.1.rest_2_.rest_11_), channel_id=1, source_target_pairs={{0,1},{1,0},{2,3},{3,2},{4,5},{5,4},{6,7},{7,6},{8,9},{9,8},{10,11... | collective-permute-start | bytes 1277960 | tf_op jit(solution)/shard_map/ppermute | solution.py:715
  86.0 8.9 %collective-permute-start.12 = (bf16[208,1024]{1,0:T(8,128)(2,1)S(1)}, bf16[208,1024]{1,0:T(8,128)(2,1)S(1)}, u32[]{:S(2)}, u32[]{:S(2)}) collective-permute-start(bf16[208,1024]{1,0:T(8,128)(2,1)S(1)} %collective-permute-done.5.rest_5_.rest_14_), channel_id=1, source_target_pairs={{0,1},{1,0},{2,3},{3,2},{4,5},{5,4},{6,7},{7,6},{8,9},{9,8},{10,11... | collective-permute-start | bytes 1277960 | tf_op jit(solution)/shard_map/ppermute | solution.py:715
  89.2 5.7 collective-permute-start.10
  89.2 5.7 collective-permute-start.11
  90.6 34.4 %collective-permute-start.18 = (bf16[320,1024]{1,0:T(8,128)(2,1)}, bf16[320,1024]{1,0:T(8,128)(2,1)S(1)}, u32[]{:S(2)}, u32[]{:S(2)}) collective-permute-start(bf16[320,1024]{1,0:T(8,128)(2,1)} %broadcast_add_fusion.5), channel_id=1, source_target_pairs={{0,4},{1,5},{4,8},{5,9},{8,12},{9,13},{12,14},{13,15},{14,10},{15,... | collective-permute-start | bytes 1966088 | tf_op jit(solution)/shard_map/ppermute | solution.py:730
  94.6 57.6 %collective-permute-start.15 = (bf16[320,1024]{1,0:T(8,128)(2,1)}, bf16[320,1024]{1,0:T(8,128)(2,1)S(1)}, u32[]{:S(2)}, u32[]{:S(2)}) collective-permute-start(bf16[320,1024]{1,0:T(8,128)(2,1)} %broadcast_add_fusion.5), channel_id=1, source_target_pairs={{4,0},{5,1},{8,4},{9,5},{12,8},{13,9},{14,12},{15,13},{10,14},{11,... | collective-permute-start | bytes 1966088 | tf_op jit(solution)/shard_map/ppermute | solution.py:732
  125.0 43.1 %copy-start.6 = (bf16[320,1024]{1,0:T(8,128)(2,1)}, bf16[320,1024]{1,0:T(8,128)(2,1)S(1)}, u32[]{:S(2)}) copy-start(bf16[320,1024]{1,0:T(8,128)(2,1)S(1)} %collective-permute-done.18.rest_12_.rest_11_.rest_7_) | copy-start | bytes 1966084
  125.0 33.3 %collective-permute-start.19 = (bf16[320,1024]{1,0:T(8,128)(2,1)S(1)}, bf16[320,1024]{1,0:T(8,128)(2,1)S(1)}, u32[]{:S(2)}, u32[]{:S(2)}) collective-permute-start(bf16[320,1024]{1,0:T(8,128)(2,1)S(1)} %broadcast_add_fusion.3), channel_id=1, source_target_pairs={{0,4},{1,5},{4,8},{5,9},{8,12},{9,13},{12,14},{13,15},{14,10},{15,... | collective-permute-start | bytes 1966088 | tf_op jit(solution)/shard_map/ppermute | solution.py:730
  152.3 48.5 %copy-start.7 = (bf16[320,1024]{1,0:T(8,128)(2,1)}, bf16[320,1024]{1,0:T(8,128)(2,1)S(1)}, u32[]{:S(2)}) copy-start(bf16[320,1024]{1,0:T(8,128)(2,1)S(1)} %collective-permute-done.15.rest_6_.rest_5_.rest_1_) | copy-start | bytes 1966084
  152.3 16.8 %collective-permute-start.16 = (bf16[320,1024]{1,0:T(8,128)(2,1)S(1)}, bf16[320,1024]{1,0:T(8,128)(2,1)S(1)}, u32[]{:S(2)}, u32[]{:S(2)}) collective-permute-start(bf16[320,1024]{1,0:T(8,128)(2,1)S(1)} %broadcast_add_fusion.4), channel_id=1, source_target_pairs={{4,0},{5,1},{8,4},{9,5},{12,8},{13,9},{14,12},{15,13},{10,14},{11,... | collective-permute-start | bytes 1966088 | tf_op jit(solution)/shard_map/ppermute | solution.py:732
  158.3 42.5 %copy-start.8 = (bf16[320,1024]{1,0:T(8,128)(2,1)}, bf16[320,1024]{1,0:T(8,128)(2,1)S(1)}, u32[]{:S(2)}) copy-start(bf16[320,1024]{1,0:T(8,128)(2,1)S(1)} %collective-permute-done.19.rest_11_.rest_10_.rest_6_) | copy-start | bytes 1966084
  158.3 23.6 %collective-permute-start.20 = (bf16[320,1024]{1,0:T(8,128)(2,1)S(1)}, bf16[320,1024]{1,0:T(8,128)(2,1)S(1)}, u32[]{:S(2)}, u32[]{:S(2)}) collective-permute-start(bf16[320,1024]{1,0:T(8,128)(2,1)S(1)} %broadcast_add_fusion.1), channel_id=1, source_target_pairs={{0,4},{1,5},{4,8},{5,9},{8,12},{9,13},{12,14},{13,15},{14,10},{15,... | collective-permute-start | bytes 1966088 | tf_op jit(solution)/shard_map/ppermute | solution.py:730
  168.1 16.7 %collective-permute-start.22 = (bf16[320,1024]{1,0:T(8,128)(2,1)S(1)}, bf16[320,1024]{1,0:T(8,128)(2,1)S(1)}, u32[]{:S(2)}, u32[]{:S(2)}) collective-permute-start(bf16[320,1024]{1,0:T(8,128)(2,1)S(1)} %constant_dynamic-update-slice_fusion.rest_5_.rest_4_.rest_0_), channel_id=1, source_target_pairs={{0,1},{1,0},{2,3},{3,2},{4,5},{5,4},{6,7},{7,6},{8,9},{9,8},{10,11... | collective-permute-start | bytes 1966088 | tf_op jit(solution)/shard_map/ppermute | solution.py:735
  168.1 16.7 %collective-permute-start.29 = (bf16[320,1024]{1,0:T(8,128)(2,1)S(1)}, bf16[320,1024]{1,0:T(8,128)(2,1)S(1)}, u32[]{:S(2)}, u32[]{:S(2)}) collective-permute-start(bf16[320,1024]{1,0:T(8,128)(2,1)S(1)} %collective-permute-done.18.rest_12_.rest_11_.rest_7_), channel_id=1, source_target_pairs={{0,1},{1,0},{2,3},{3,2},{4,5},{5,4},{6,7},{7,6},{8,9},{9,8},{10,11... | collective-permute-start | bytes 1966088 | tf_op jit(solution)/shard_map/ppermute | solution.py:735
  168.6 16.7 %collective-permute-start.23 = (bf16[320,1024]{1,0:T(8,128)(2,1)S(1)}, bf16[320,1024]{1,0:T(8,128)(2,1)S(1)}, u32[]{:S(2)}, u32[]{:S(2)}) collective-permute-start(bf16[320,1024]{1,0:T(8,128)(2,1)S(1)} %collective-permute-done.15.rest_6_.rest_5_.rest_1_), channel_id=1, source_target_pairs={{0,1},{1,0},{2,3},{3,2},{4,5},{5,4},{6,7},{7,6},{8,9},{9,8},{10,11... | collective-permute-start | bytes 1966088 | tf_op jit(solution)/shard_map/ppermute | solution.py:735
  169.2 17.4 %collective-permute-start.17 = (bf16[320,1024]{1,0:T(8,128)(2,1)S(1)}, bf16[320,1024]{1,0:T(8,128)(2,1)S(1)}, u32[]{:S(2)}, u32[]{:S(2)}) collective-permute-start(bf16[320,1024]{1,0:T(8,128)(2,1)S(1)} %broadcast_add_fusion.2), channel_id=1, source_target_pairs={{4,0},{5,1},{8,4},{9,5},{12,8},{13,9},{14,12},{15,13},{10,14},{11,... | collective-permute-start | bytes 1966088 | tf_op jit(solution)/shard_map/ppermute | solution.py:732
  182.0 15.8 %collective-permute-start.21 = (bf16[320,1024]{1,0:T(8,128)(2,1)S(1)}, bf16[320,1024]{1,0:T(8,128)(2,1)S(1)}, u32[]{:S(2)}, u32[]{:S(2)}) collective-permute-start(bf16[320,1024]{1,0:T(8,128)(2,1)S(1)} %collective-permute-done.20.rest_10_.rest_9_.rest_5_), channel_id=1, source_target_pairs={{0,4},{1,5},{4,8},{5,9},{8,12},{9,13},{12,14},{13,15},{14,10},{15,... | collective-permute-start | bytes 1966088 | tf_op jit(solution)/shard_map/ppermute | solution.py:730
  184.8 13.6 %collective-permute-start.24 = (bf16[320,1024]{1,0:T(8,128)(2,1)S(1)}, bf16[320,1024]{1,0:T(8,128)(2,1)S(1)}, u32[]{:S(2)}, u32[]{:S(2)}) collective-permute-start(bf16[320,1024]{1,0:T(8,128)(2,1)S(1)} %collective-permute-done.16.rest_7_.rest_6_.rest_2_), channel_id=1, source_target_pairs={{0,1},{1,0},{2,3},{3,2},{4,5},{5,4},{6,7},{7,6},{8,9},{9,8},{10,11... | collective-permute-start | bytes 1966088 | tf_op jit(solution)/shard_map/ppermute | solution.py:735
  184.9 13.6 %collective-permute-start.28 = (bf16[320,1024]{1,0:T(8,128)(2,1)S(1)}, bf16[320,1024]{1,0:T(8,128)(2,1)S(1)}, u32[]{:S(2)}, u32[]{:S(2)}) collective-permute-start(bf16[320,1024]{1,0:T(8,128)(2,1)S(1)} %collective-permute-done.19.rest_11_.rest_10_.rest_6_), channel_id=1, source_target_pairs={{0,1},{1,0},{2,3},{3,2},{4,5},{5,4},{6,7},{7,6},{8,9},{9,8},{10,11... | collective-permute-start | bytes 1966088 | tf_op jit(solution)/shard_map/ppermute | solution.py:735
  185.4 13.2 %collective-permute-start.27 = (bf16[320,1024]{1,0:T(8,128)(2,1)S(1)}, bf16[320,1024]{1,0:T(8,128)(2,1)S(1)}, u32[]{:S(2)}, u32[]{:S(2)}) collective-permute-start(bf16[320,1024]{1,0:T(8,128)(2,1)S(1)} %collective-permute-done.20.rest_10_.rest_9_.rest_5_), channel_id=1, source_target_pairs={{0,1},{1,0},{2,3},{3,2},{4,5},{5,4},{6,7},{7,6},{8,9},{9,8},{10,11... | collective-permute-start | bytes 1966088 | tf_op jit(solution)/shard_map/ppermute | solution.py:735
  186.6 11.9 %collective-permute-start.25 = (bf16[320,1024]{1,0:T(8,128)(2,1)S(1)}, bf16[320,1024]{1,0:T(8,128)(2,1)S(1)}, u32[]{:S(2)}, u32[]{:S(2)}) collective-permute-start(bf16[320,1024]{1,0:T(8,128)(2,1)S(1)} %collective-permute-done.17.rest_8_.rest_7_.rest_3_), channel_id=1, source_target_pairs={{0,1},{1,0},{2,3},{3,2},{4,5},{5,4},{6,7},{7,6},{8,9},{9,8},{10,11... | collective-permute-start | bytes 1966088 | tf_op jit(solution)/shard_map/ppermute | solution.py:735
  197.8 2.1 collective-permute-start.26
  421.7 21.5 %collective-permute-start.30 = (bf16[8,512,512]{2,1,0:T(8,128)(2,1)}, bf16[8,512,512]{2,1,0:T(8,128)(2,1)}, u32[]{:S(2)}, u32[]{:S(2)}) collective-permute-start(bf16[8,512,512]{2,1,0:T(8,128)(2,1)} %get-tuple-element.104), channel_id=1, source_target_pairs={{0,1},{1,0},{2,3},{3,2},{4,5},{5,4},{6,7},{7,6},{8,9},{9,8},{10,11... | collective-permute-start | bytes 12582920 | tf_op jit(solution)/shard_map/ppermute | solution.py:780
  445.7 26.0 %collective-permute-start.32 = (bf16[512,512]{1,0:T(8,128)(2,1)}, bf16[512,512]{1,0:T(8,128)(2,1)S(1)}, u32[]{:S(2)}, u32[]{:S(2)}) collective-permute-start(bf16[512,512]{1,0:T(8,128)(2,1)} %get-tuple-element.106), channel_id=1, source_target_pairs={{0,4},{1,5},{4,8},{5,9},{8,12},{9,13},{12,14},{13,15},{14,10},{15,... | collective-permute-start | bytes 1572872 | tf_op jit(solution)/shard_map/ppermute | solution.py:771
  451.3 20.4 %collective-permute-start.31 = (bf16[512,512]{1,0:T(8,128)(2,1)}, bf16[512,512]{1,0:T(8,128)(2,1)S(1)}, u32[]{:S(2)}, u32[]{:S(2)}) collective-permute-start(bf16[512,512]{1,0:T(8,128)(2,1)} %get-tuple-element.105.rest_14_), channel_id=1, source_target_pairs={{4,0},{5,1},{8,4},{9,5},{12,8},{13,9},{14,12},{15,13},{10,14},{11,... | collective-permute-start | bytes 1572872 | tf_op jit(solution)/shard_map/ppermute | solution.py:769
  475.4 13.6 %collective-permute-start.35 = (bf16[8,544,512]{2,1,0:T(8,128)(2,1)}, bf16[8,544,512]{2,1,0:T(8,128)(2,1)}, u32[]{:S(2)}, u32[]{:S(2)}) collective-permute-start(bf16[8,544,512]{2,1,0:T(8,128)(2,1)} %get-tuple-element.116), channel_id=1, source_target_pairs={{0,1},{1,0},{2,3},{3,2},{4,5},{5,4},{6,7},{7,6},{8,9},{9,8},{10,11... | collective-permute-start | bytes 13369352 | tf_op jit(solution)/shard_map/ppermute | solution.py:780
  475.4 26.1 %collective-permute-start.34 = (bf16[512,512]{1,0:T(8,128)(2,1)}, bf16[512,512]{1,0:T(8,128)(2,1)S(1)}, u32[]{:S(2)}, u32[]{:S(2)}) collective-permute-start(bf16[512,512]{1,0:T(8,128)(2,1)} %get-tuple-element.115), channel_id=1, source_target_pairs={{0,4},{1,5},{4,8},{5,9},{8,12},{9,13},{12,14},{13,15},{14,10},{15,... | collective-permute-start | bytes 1572872 | tf_op jit(solution)/shard_map/ppermute | solution.py:771
  477.9 37.8 %collective-permute-start.33 = (bf16[512,512]{1,0:T(8,128)(2,1)}, bf16[512,512]{1,0:T(8,128)(2,1)S(1)}, u32[]{:S(2)}, u32[]{:S(2)}) collective-permute-start(bf16[512,512]{1,0:T(8,128)(2,1)} %get-tuple-element.114.rest_16_), channel_id=1, source_target_pairs={{4,0},{5,1},{8,4},{9,5},{12,8},{13,9},{14,12},{15,13},{10,14},{11,... | collective-permute-start | bytes 1572872 | tf_op jit(solution)/shard_map/ppermute | solution.py:769
  497.4 61.8 %collective-permute-start.40 = (bf16[8,272,512]{2,1,0:T(8,128)(2,1)}, bf16[8,272,512]{2,1,0:T(8,128)(2,1)S(1)}, u32[]{:S(2)}, u32[]{:S(2)}) collective-permute-start(bf16[8,272,512]{2,1,0:T(8,128)(2,1)} %get-tuple-element.120), channel_id=1, source_target_pairs={{0,16},{16,0},{1,17},{17,1},{2,18},{18,2},{3,19},{19,3},{4,20},{20... | collective-permute-start | bytes 6684680 | tf_op jit(solution)/shard_map/ppermute | solution.py:784
  519.3 15.2 %collective-permute-start.36 = (bf16[512,512]{1,0:T(8,128)(2,1)}, bf16[512,512]{1,0:T(8,128)(2,1)S(1)}, u32[]{:S(2)}, u32[]{:S(2)}) collective-permute-start(bf16[512,512]{1,0:T(8,128)(2,1)} %get-tuple-element.118.rest_3_), channel_id=1, source_target_pairs={{4,0},{5,1},{8,4},{9,5},{12,8},{13,9},{14,12},{15,13},{10,14},{11,... | collective-permute-start | bytes 1572872 | tf_op jit(solution)/shard_map/ppermute | solution.py:769
  519.3 18.2 %collective-permute-start.38 = (bf16[512,512]{1,0:T(8,128)(2,1)}, bf16[512,512]{1,0:T(8,128)(2,1)S(1)}, u32[]{:S(2)}, u32[]{:S(2)}) collective-permute-start(bf16[512,512]{1,0:T(8,128)(2,1)} %get-tuple-element.119), channel_id=1, source_target_pairs={{0,4},{1,5},{4,8},{5,9},{8,12},{9,13},{12,14},{13,15},{14,10},{15,... | collective-permute-start | bytes 1572872 | tf_op jit(solution)/shard_map/ppermute | solution.py:771
  537.4 14.1 %collective-permute-start.37 = (bf16[512,512]{1,0:T(8,128)(2,1)}, bf16[512,512]{1,0:T(8,128)(2,1)S(1)}, u32[]{:S(2)}, u32[]{:S(2)}) collective-permute-start(bf16[512,512]{1,0:T(8,128)(2,1)} %shard_map.316.rest_4_), channel_id=1, source_target_pairs={{4,0},{5,1},{8,4},{9,5},{12,8},{13,9},{14,12},{15,13},{10,14},{11,... | collective-permute-start | bytes 1572872 | tf_op jit(solution)/shard_map/ppermute | solution.py:769
  553.0 14.9 %collective-permute-start.39 = (bf16[512,512]{1,0:T(8,128)(2,1)S(1)}, bf16[512,512]{1,0:T(8,128)(2,1)S(1)}, u32[]{:S(2)}, u32[]{:S(2)}) collective-permute-start(bf16[512,512]{1,0:T(8,128)(2,1)S(1)} %fusion.1), channel_id=1, source_target_pairs={{0,16},{16,0},{1,17},{17,1},{2,18},{18,2},{3,19},{19,3},{4,20},{20... | collective-permute-start | bytes 1572872 | tf_op jit(solution)/shard_map/ppermute | solution.py:743
  557.2 31.4 %collective-permute-start.46 = (bf16[512,1024]{1,0:T(8,128)(2,1)}, bf16[512,1024]{1,0:T(8,128)(2,1)}, u32[]{:S(2)}, u32[]{:S(2)}) collective-permute-start(bf16[512,1024]{1,0:T(8,128)(2,1)} %broadcast_add_fusion), channel_id=1, source_target_pairs={{0,16},{16,0},{1,17},{17,1},{2,18},{18,2},{3,19},{19,3},{4,20},{20... | collective-permute-start | bytes 3145736 | tf_op jit(solution)/shard_map/ppermute | solution.py:743
  562.7 7.4 %collective-permute-start.42 = (bf16[272,512]{1,0:T(8,128)(2,1)}, bf16[272,512]{1,0:T(8,128)(2,1)S(1)}, u32[]{:S(2)}, u32[]{:S(2)}) collective-permute-start(bf16[272,512]{1,0:T(8,128)(2,1)} %get-tuple-element.122), channel_id=1, source_target_pairs={{4,0},{5,1},{8,4},{9,5},{12,8},{13,9},{14,12},{15,13},{10,14},{11,... | collective-permute-start | bytes 835592 | tf_op jit(solution)/shard_map/ppermute | solution.py:771
  563.0 7.4 %collective-permute-start.41 = (bf16[272,512]{1,0:T(8,128)(2,1)}, bf16[272,512]{1,0:T(8,128)(2,1)S(1)}, u32[]{:S(2)}, u32[]{:S(2)}) collective-permute-start(bf16[272,512]{1,0:T(8,128)(2,1)} %get-tuple-element.121.rest_6_), channel_id=1, source_target_pairs={{0,4},{1,5},{4,8},{5,9},{8,12},{9,13},{12,14},{13,15},{14,10},{15,... | collective-permute-start | bytes 835592 | tf_op jit(solution)/shard_map/ppermute | solution.py:769
  573.8 6.8 %collective-permute-start.44 = (bf16[272,512]{1,0:T(8,128)(2,1)}, bf16[272,512]{1,0:T(8,128)(2,1)S(1)}, u32[]{:S(2)}, u32[]{:S(2)}) collective-permute-start(bf16[272,512]{1,0:T(8,128)(2,1)} %get-tuple-element.124), channel_id=1, source_target_pairs={{4,0},{5,1},{8,4},{9,5},{12,8},{13,9},{14,12},{15,13},{10,14},{11,... | collective-permute-start | bytes 835592 | tf_op jit(solution)/shard_map/ppermute | solution.py:771
  574.4 6.8 %collective-permute-start.43 = (bf16[272,512]{1,0:T(8,128)(2,1)}, bf16[272,512]{1,0:T(8,128)(2,1)S(1)}, u32[]{:S(2)}, u32[]{:S(2)}) collective-permute-start(bf16[272,512]{1,0:T(8,128)(2,1)} %get-tuple-element.123.rest_6_), channel_id=1, source_target_pairs={{0,4},{1,5},{4,8},{5,9},{8,12},{9,13},{12,14},{13,15},{14,10},{15,... | collective-permute-start | bytes 835592 | tf_op jit(solution)/shard_map/ppermute | solution.py:769
  584.3 13.3 %collective-permute-start.48 = (bf16[272,512]{1,0:T(8,128)(2,1)}, bf16[272,512]{1,0:T(8,128)(2,1)S(1)}, u32[]{:S(2)}, u32[]{:S(2)}) collective-permute-start(bf16[272,512]{1,0:T(8,128)(2,1)} %get-tuple-element.130), channel_id=1, source_target_pairs={{4,0},{5,1},{8,4},{9,5},{12,8},{13,9},{14,12},{15,13},{10,14},{11,... | collective-permute-start | bytes 835592 | tf_op jit(solution)/shard_map/ppermute | solution.py:771
  585.1 6.8 %collective-permute-start.45 = (bf16[272,512]{1,0:T(8,128)(2,1)}, bf16[272,512]{1,0:T(8,128)(2,1)S(1)}, u32[]{:S(2)}, u32[]{:S(2)}) collective-permute-start(bf16[272,512]{1,0:T(8,128)(2,1)} %get-tuple-element.125.rest_3_), channel_id=1, source_target_pairs={{0,4},{1,5},{4,8},{5,9},{8,12},{9,13},{12,14},{13,15},{14,10},{15,... | collective-permute-start | bytes 835592 | tf_op jit(solution)/shard_map/ppermute | solution.py:769
  594.5 6.9 %collective-permute-start.47 = (bf16[272,512]{1,0:T(8,128)(2,1)}, bf16[272,512]{1,0:T(8,128)(2,1)S(1)}, u32[]{:S(2)}, u32[]{:S(2)}) collective-permute-start(bf16[272,512]{1,0:T(8,128)(2,1)} %shard_map.322), channel_id=1, source_target_pairs={{0,4},{1,5},{4,8},{5,9},{8,12},{9,13},{12,14},{13,15},{14,10},{15,... | collective-permute-start | bytes 835592 | tf_op jit(solution)/shard_map/ppermute | solution.py:769
  602.5 6.6 %collective-permute-start.49 = (bf16[272,512]{1,0:T(8,128)(2,1)S(1)}, bf16[272,512]{1,0:T(8,128)(2,1)S(1)}, u32[]{:S(2)}, u32[]{:S(2)}) collective-permute-start(bf16[272,512]{1,0:T(8,128)(2,1)S(1)} %fusion.4), channel_id=1, source_target_pairs={{0,16},{16,0},{1,17},{17,1},{2,18},{18,2},{3,19},{19,3},{4,20},{20... | collective-permute-start | bytes 835592 | tf_op jit(solution)/shard_map/ppermute | solution.py:784
  (49 other events, 335.1 us)
Sparse Core Ops, SparseCore 0:
  11.5 155.2 all-gather.1
  320.4 205.0 reduce-scatter.1

commit v6 on v5

--- a/solution.py
+++ b/solution.py
@@ -111,7 +111,7 @@
             qe_ref[rows, g*128:(g+1)*128] = jnp.where(part < 8, xb.astype(jnp.float32), e).astype(jnp.bfloat16)
 
     def step(i, c):
-        for j in range(1, N // bk + 1):
+        for j in range(bq // bk if causal else 1, N // bk + 1):
             @pl.when(win_ref[nq + i] == j)
             def _():
                 one(i, j * bk)
@@ -119,7 +119,7 @@
 
     lax.fori_loop(0, nq, step, 0)
 
-def attend_forward(q, k, v, qx, kx, win, causal, pairs, after=(), bq=256, bk=256, hp=4):
+def attend_forward(q, k, v, qx, kx, win, causal, pairs, after=(), bq=256, bk=128, hp=4):
     L, N = q.shape[0], k.shape[0]
     w = 128 * hp
     start, number = pairs[0] // hp, (pairs[1] - pairs[0]) // hp
@@ -206,7 +206,7 @@
             dq_ref[rows, c] = (dq * 0.125).astype(jnp.bfloat16)
 
     def step(i, c):
-        for j in range(1, N // bk + 1):
+        for j in range(bq // bk if causal else 1, N // bk + 1):
             @pl.when(win_ref[nq + i] == j)
             def _():
                 one(i, j * bk)
@@ -216,7 +216,7 @@
     dk_ref[...] = dka[...].astype(jnp.bfloat16)
     dv_ref[...] = dva[...].astype(jnp.bfloat16)
 
-def attend_backward(q, k, v, o, do, qe, kx, win, causal, pairs, base=0, after=(), bq=256, bk=256, hp=2):
+def attend_backward(q, k, v, o, do, qe, kx, win, causal, pairs, base=0, after=(), bq=256, bk=128, hp=2):
     L, N = q.shape[0], k.shape[0]
     w = 128 * hp
     start, number, base = pairs[0] // hp, (pairs[1] - pairs[0]) // hp, base // hp
@@ -834,8 +834,8 @@
     in_parts = [ffn_in[:, i * width : (i + 1) * width] for i in range(parts)]
     unit_extra, enc_extra = key_extras(unit_ids[0]), key_extras(enc_ids[0])
     query_extra = query_extras(unit_ids[0])
-    self_windows = windows(unit_ids[0], unit_ids[0], 256, 256, True)
-    cross_windows = windows(unit_ids[0], enc_ids[0], 256, 256, False)
+    self_windows = windows(unit_ids[0], unit_ids[0], 256, 128, True)
+    cross_windows = windows(unit_ids[0], enc_ids[0], 256, 128, False)
     if ring:
         order, rank = ring_tables(count)
         norm_row = jnp.pad(norm_piece.reshape(1, -1), ((0, 15), (0, width - 8 * own_width)))

time: 626 us -> 624 us (level)
    ppermute x4, waiting for transfers between devices: 29.3 us -> 16.3 us  [hop(): lax.ppermute(upward + held, 'shard', self.up)]
    ppermute x6, starting transfers between devices: 11.7 us -> 2.24 us  [hop(): self.downward = lax.ppermute(sums[1], 'shard', self.down)]
    ppermute x3, waiting for transfers between devices: 1.65 us -> 10.1 us  [hop(): self.pieces[self.step] = lax.ppermute(downward + held, 'shard', self.down)]
    ppermute x8, starting transfers between devices: 5.69 us -> 12.1 us  [hop(): self.upward = lax.ppermute(sums[0], 'shard', self.up)]
  transfers between devices with their start and end apart: 52 -> 52, of which waited for: 24 -> 24; matrix products, arithmetic and copies ran while one was open for 4% -> 4% of each run, Pallas kernels for 39% -> 40%
where the time goes in v6:
time: 624 us; the launch traced here: 616 us
  Pallas kernels  332 us (53%)
  waiting for transfers between devices  148 us (24%)
  starting transfers between devices  73.7 us (12%)
  local copies, waits for them, and re-layouts  23.1 us (4%)
  other arithmetic  21.9 us (4%)
  between operations  17.9 us (3%)
    pallas_call x6, Pallas kernels, by_rows(): pl.pallas_call(kernel, grid_spec=pltpu.PrefetchScalarGridSpec(num_scalar_...  129 us
    pallas_call x3, Pallas kernels, attend_backward(): pl.pallas_call(functools.partial(attend_backward_kernel, bq, bk, causal,...  67.7 us
    ppermute x4, waiting for transfers between devices, gather_pieces(): upward = lax.ppermute(upward, 'shard', up)  52.5 us
    pallas_call x3, Pallas kernels, attend_forward(): pl.pallas_call(functools.partial(attend_forward_kernel, bq, bk, causal, h...  48 us
    ppermute x8, waiting for transfers between devices, hop(): self.upward = lax.ppermute(sums[0], 'shard', self.up)  47.7 us
    pallas_call x2, Pallas kernels, term_sets(): pl.pallas_call(functools.partial(term_kernel, [p[0] for p in parts], chip...  37.4 us
    ppermute x4, starting transfers between devices, hop(): lax.ppermute(upward + held, 'shard', self.up)  28.9 us
    pallas_call x8, Pallas kernels, hop(): pl.pallas_call(functools.partial(hop_kernel, up is None, down_at is not N...  18.8 us
  transfers between devices with their start and end apart: 52, of which 24 were waited for; matrix products, arithmetic and copies ran while one was open for 4% of the time, Pallas kernels for 40%

profile of v6, /device:TPU:0, one launch (start us, length us, event | category | flops | bytes accessed | tf_op | source)
XLA Modules:
  0.0 616.3 jit_solution(14856311298230309583)
XLA Ops:
  9.9 3.1 collective-permute-start.3
  14.6 8.2 %collective-permute-done.3.rest_7_.rest_16_ = bf16[208,1024]{1,0:T(8,128)(2,1)S(1)} collective-permute-done((bf16[208,1024]{1,0:T(8,128)(2,1)S(1)}, bf16[208,1024]{1,0:T(8,128)(2,1)S(1)}, u32[]{:S(2)}, u32[]{:S(2)}) %collective-permute-start.3) | collective-permute-done | bytes 426016 | tf_op jit(solution)/shard_map/ppermute | solution.py:710
  22.8 1.8 collective-permute-start.4
  24.7 18.4 %collective-permute-done.4.rest_6_.rest_15_ = bf16[208,1024]{1,0:T(8,128)(2,1)S(1)} collective-permute-done((bf16[208,1024]{1,0:T(8,128)(2,1)S(1)}, bf16[208,1024]{1,0:T(8,128)(2,1)S(1)}, u32[]{:S(2)}, u32[]{:S(2)}) %collective-permute-start.4) | collective-permute-done | bytes 426016 | tf_op jit(solution)/shard_map/ppermute | solution.py:710
  43.1 2.5 collective-permute-start.5
  46.8 10.7 %collective-permute-done.5.rest_5_.rest_14_ = bf16[208,1024]{1,0:T(8,128)(2,1)S(1)} collective-permute-done((bf16[208,1024]{1,0:T(8,128)(2,1)S(1)}, bf16[208,1024]{1,0:T(8,128)(2,1)S(1)}, u32[]{:S(2)}, u32[]{:S(2)}) %collective-permute-start.5) | collective-permute-done | bytes 426016 | tf_op jit(solution)/shard_map/ppermute | solution.py:710
  57.6 9.3 %collective-permute-start.6 = (bf16[208,1024]{1,0:T(8,128)(2,1)S(1)}, bf16[208,1024]{1,0:T(8,128)(2,1)S(1)}, u32[]{:S(2)}, u32[]{:S(2)}) collective-permute-start(bf16[208,1024]{1,0:T(8,128)(2,1)S(1)} %collective-permute-done.5.rest_5_.rest_14_), channel_id=1, source_target_pairs={{0,4},{1,5},{4,8},{5,9},{8,12},{9,13},{12,14},{13,15},{14,10},{15,... | collective-permute-start | bytes 1277960 | tf_op jit(solution)/shard_map/ppermute | solution.py:710
  68.4 15.1 %collective-permute-done.6.rest_4_.rest_13_ = bf16[208,1024]{1,0:T(8,128)(2,1)S(1)} collective-permute-done((bf16[208,1024]{1,0:T(8,128)(2,1)S(1)}, bf16[208,1024]{1,0:T(8,128)(2,1)S(1)}, u32[]{:S(2)}, u32[]{:S(2)}) %collective-permute-start.6) | collective-permute-done | bytes 426016 | tf_op jit(solution)/shard_map/ppermute | solution.py:710
  86.0 3.1 collective-permute-done.2.rest_3_.rest_12_
  90.6 2.1 collective-permute-start.18
  97.3 13.9 %shard_map.298 = (bf16[1024,1024]{1,0:T(8,128)(2,1)}, bf16[1024,1024]{1,0:T(8,128)(2,1)}, bf16[1024,1024]{1,0:T(8,128)(2,1)}, bf16[1024,1024]{1,0:T(8,128)(2,1)}) custom-call(s32[16]{0:T(128)} %copy-done.57, bf16[1024,1024]{1,0:T(8,128)(2,1)} %bitcast.38, f32[8,1024]{1,0:T(8,128)} %reshape.101.norm_ref.rest_4_.rest_3_.rest_8_, bf16[208,1024]{1,0:T(8,128)(2,1)} %copy-done.22, ...), custom_call_target="tpu_custom_call" | custom-call | flops 805306368 | bytes 1310720 | tf_op jit(solution)/shard_map/pallas_call | solution.py:473
  111.2 10.9 %shard_map.299 = (bf16[1024,512]{1,0:T(8,128)(2,1)}, bf16[1024,512]{1,0:T(8,128)(2,1)}) custom-call(s32[8]{0:T(128)} %pad_add_fusion.1.win_ref, bf16[1024,1024]{1,0:T(8,128)(2,1)} %get-tuple-element.73.q_ref, bf16[1024,1024]{1,0:T(8,128)(2,1)} %get-tuple-element.74.k_ref, bf16[1024,1024]{1,0:T(8,128)(2,1)} %get-tuple-element.75.v_ref, ...), custom_call_target="tpu_custom_call" | custom-call | flops 1073741824 | bytes 655360 | tf_op jit(solution)/shard_map/pallas_call | solution.py:129
  124.0 14.5 %collective-permute-start.19 = (bf16[320,1024]{1,0:T(8,128)(2,1)S(1)}, bf16[320,1024]{1,0:T(8,128)(2,1)S(1)}, u32[]{:S(2)}, u32[]{:S(2)}) collective-permute-start(bf16[320,1024]{1,0:T(8,128)(2,1)S(1)} %broadcast_add_fusion.3), channel_id=1, source_target_pairs={{0,4},{1,5},{4,8},{5,9},{8,12},{9,13},{12,14},{13,15},{14,10},{15,... | collective-permute-start | bytes 1966088 | tf_op jit(solution)/shard_map/ppermute | solution.py:730
  138.5 16.8 %shard_map.300 = (bf16[1024,512]{1,0:T(8,128)(2,1)}, bf16[1024,512]{1,0:T(8,128)(2,1)}) custom-call(s32[8]{0:T(128)} %pad_add_fusion.1.win_ref, bf16[1024,1024]{1,0:T(8,128)(2,1)} %get-tuple-element.73.q_ref, bf16[1024,1024]{1,0:T(8,128)(2,1)} %get-tuple-element.74.k_ref, bf16[1024,1024]{1,0:T(8,128)(2,1)} %get-tuple-element.75.v_ref, ...), custom_call_target="tpu_custom_call" | custom-call | flops 1073741824 | bytes 655360 | tf_op jit(solution)/shard_map/pallas_call | solution.py:129
  158.3 9.8 %collective-permute-start.20 = (bf16[320,1024]{1,0:T(8,128)(2,1)S(1)}, bf16[320,1024]{1,0:T(8,128)(2,1)S(1)}, u32[]{:S(2)}, u32[]{:S(2)}) collective-permute-start(bf16[320,1024]{1,0:T(8,128)(2,1)S(1)} %broadcast_add_fusion.1), channel_id=1, source_target_pairs={{0,4},{1,5},{4,8},{5,9},{8,12},{9,13},{12,14},{13,15},{14,10},{15,... | collective-permute-start | bytes 1966088 | tf_op jit(solution)/shard_map/ppermute | solution.py:730
  168.7 5.4 collective-permute-done.16.rest_7_.rest_6_.rest_2_
  174.2 7.8 %collective-permute-done.20.rest_10_.rest_9_.rest_5_ = bf16[320,1024]{1,0:T(8,128)(2,1)S(1)} collective-permute-done((bf16[320,1024]{1,0:T(8,128)(2,1)S(1)}, bf16[320,1024]{1,0:T(8,128)(2,1)S(1)}, u32[]{:S(2)}, u32[]{:S(2)}) %collective-permute-start.20) | collective-permute-done | bytes 655392 | tf_op jit(solution)/shard_map/ppermute | solution.py:730
  182.0 2.5 collective-permute-start.21
  185.1 4.7 collective-permute-done.17.rest_8_.rest_7_.rest_3_
  189.8 7.7 %collective-permute-done.21.rest_9_.rest_8_.rest_4_ = bf16[320,1024]{1,0:T(8,128)(2,1)S(1)} collective-permute-done((bf16[320,1024]{1,0:T(8,128)(2,1)S(1)}, bf16[320,1024]{1,0:T(8,128)(2,1)S(1)}, u32[]{:S(2)}, u32[]{:S(2)}) %collective-permute-start.21) | collective-permute-done | bytes 655392 | tf_op jit(solution)/shard_map/ppermute | solution.py:730
  198.2 1.3 collective-permute-done.26.rest_17_.rest_16_.rest_12_
  200.5 16.3 %shard_map.301 = (f32[1024,1024]{1,0:T(8,128)}, bf16[1024,1024]{1,0:T(8,128)(2,1)}, bf16[1024,1024]{1,0:T(8,128)(2,1)}, bf16[1024,1024]{1,0:T(8,128)(2,1)}, bf16[1024,1024]{1,0:T(8,128)(2,1)}) custom-call(s32[16]{0:T(128)} %copy-done.57, bf16[1024,512]{1,0:T(8,128)(2,1)} %get-tuple-element.76.rest_0_.o_ref, ...), custom_call_target="tpu_custom_call" | custom-call | flops 1073741824 | bytes 2359296 | tf_op jit(solution)/shard_map/pallas_call | solution.py:473
  216.8 20.3 %shard_map.302 = (bf16[1024,1024]{1,0:T(8,128)(2,1)}, bf16[1024,1024]{1,0:T(8,128)(2,1)}) custom-call(s32[8]{0:T(128)} %pad_add_fusion.win_ref, bf16[1024,1024]{1,0:T(8,128)(2,1)} %get-tuple-element.78.q_ref, bf16[1024,1024]{1,0:T(8,128)(2,1)} %get-tuple-element.79.k_ref, bf16[1024,1024]{1,0:T(8,128)(2,1)} %get-tuple-element.80.v_ref, ...), custom_call_target="tpu_custom_call" | custom-call | flops 2147483648 | bytes 1310720 | tf_op jit(solution)/shard_map/pallas_call | solution.py:129
  237.1 57.9 %shard_map.303 = (bf16[1024,1024]{1,0:T(8,128)(2,1)}, bf16[1024,1024]{1,0:T(8,128)(2,1)}, bf16[1024,4096]{1,0:T(8,128)(2,1)}, bf16[1024,1024]{1,0:T(8,128)(2,1)}...) custom-call(s32[16]{0:T(128)} %copy-done.57, ...), custom_call_target="tpu_custom_call" | custom-call | flops 4831838208 | bytes 4980736 | tf_op jit(solution)/shard_map/pallas_call | solution.py:473
  295.1 13.1 %shard_map.320.rest_0_ = bf16[16,512,1024]{2,1,0:T(8,128)(2,1)} custom-call(bf16[1024,1024]{1,0:T(8,128)(2,1)} %get-tuple-element.128.left_ref, bf16[1024,4096]{1,0:T(8,128)(2,1)} %get-tuple-element.129.right_ref), custom_call_target="tpu_custom_call" | custom-call | flops 1073741824 | bytes 3145728 | tf_op jit(solution)/shard_map/pallas_call | solution.py:572
  308.1 13.1 %shard_map.321 = bf16[16,512,1024]{2,1,0:T(8,128)(2,1)} custom-call(bf16[1024,4096]{1,0:T(8,128)(2,1)} %get-tuple-element.126.left_ref, bf16[1024,1024]{1,0:T(8,128)(2,1)} %get-tuple-element.127.right_ref, bf16[16,512,1024]{2,1,0:T(8,128)(2,1)} %shard_map.320.rest_0_), custom_call_target="tpu_custom_call", output_to_operand_aliasing={{}: (2, {})} | custom-call | flops 1073741824 | bytes 3145728 | tf_op jit(solution)/shard_map/pallas_call | solution.py:581
  322.4 33.1 %shard_map.304 = (bf16[1024,1024]{1,0:T(8,128)(2,1)}, bf16[1024,1024]{1,0:T(8,128)(2,1)}, bf16[1024,1024]{1,0:T(8,128)(2,1)}) custom-call(s32[8]{0:T(128)} %pad_add_fusion.win_ref, bf16[1024,1024]{1,0:T(8,128)(2,1)} %get-tuple-element.78.q_ref, bf16[1024,1024]{1,0:T(8,128)(2,1)} %get-tuple-element.79.k_ref, bf16[1024,1024]{1,0:T(8,128)(2,1)} %get-tuple-element.80.v_ref, ...), custom_call_target="tpu_custom_call" | custom-call | flops 5368709120 | bytes 2097152 | tf_op jit(solution)/shard_map/pallas_call | solution.py:227
  355.5 13.3 %shard_map.305 = (f32[1024,1024]{1,0:T(8,128)}, bf16[1024,1024]{1,0:T(8,128)(2,1)}, bf16[1024,1024]{1,0:T(8,128)(2,1)}, f32[8,1024]{1,0:T(8,128)}) custom-call(s32[16]{0:T(128)} %copy-done.57, bf16[1024,1024]{1,0:T(8,128)(2,1)} %get-tuple-element.86.dq_ref.rest_8_.rest_9_, f32[1024,1024]{1,0:T(8,128)} %get-tuple-element.82.rest_1_.r_ref, ...), custom_call_target="tpu_custom_call" | custom-call | flops 536870912 | bytes 2359296 | tf_op jit(solution)/shard_map/pallas_call | solution.py:473
  368.8 17.2 %shard_map.306 = (bf16[1024,512]{1,0:T(8,128)(2,1)}, bf16[1024,512]{1,0:T(8,128)(2,1)}, bf16[1024,512]{1,0:T(8,128)(2,1)}) custom-call(s32[8]{0:T(128)} %pad_add_fusion.1.win_ref, bf16[1024,1024]{1,0:T(8,128)(2,1)} %get-tuple-element.73.q_ref, bf16[1024,1024]{1,0:T(8,128)(2,1)} %get-tuple-element.74.k_ref, bf16[1024,1024]{1,0:T(8,128)(2,1)} %get-tuple-element.75.v_ref, ...), custom_call_target="tpu_custom_call" | custom-call | flops 2684354560 | bytes 1048576 | tf_op jit(solution)/shard_map/pallas_call | solution.py:227
  386.0 17.5 %shard_map.307 = (bf16[1024,512]{1,0:T(8,128)(2,1)}, bf16[1024,512]{1,0:T(8,128)(2,1)}, bf16[1024,512]{1,0:T(8,128)(2,1)}) custom-call(s32[8]{0:T(128)} %pad_add_fusion.1.win_ref, bf16[1024,1024]{1,0:T(8,128)(2,1)} %get-tuple-element.73.q_ref, bf16[1024,1024]{1,0:T(8,128)(2,1)} %get-tuple-element.74.k_ref, bf16[1024,1024]{1,0:T(8,128)(2,1)} %get-tuple-element.75.v_ref, ...), custom_call_target="tpu_custom_call" | custom-call | flops 2684354560 | bytes 1048576 | tf_op jit(solution)/shard_map/pallas_call | solution.py:227
  403.5 17.0 %shard_map.308 = (bf16[8,512,512]{2,1,0:T(8,128)(2,1)}, bf16[8,512,512]{2,1,0:T(8,128)(2,1)}) custom-call(s32[9]{0:T(128)} %dynamic-slice_bitcast_fusion.rank_ref, bf16[1024,512]{1,0:T(8,128)(2,1)} %get-tuple-element.76.rest_0_.o_ref, bf16[1024,512]{1,0:T(8,128)(2,1)} %get-tuple-element.77.rest_1_.o_ref, bf16[1024,1024]{1,0:T(8,128)(2,1)} %get-tuple-element.98.rest_2_, ...), custom_call_target="tpu_custom_call" | custom-call | flops 1073741824 | bytes 3145728 | tf_op jit(solution)/shard_map/pallas_call | solution.py:539
  420.5 7.4 %collective-permute-start.30 = (bf16[8,512,512]{2,1,0:T(8,128)(2,1)}, bf16[8,512,512]{2,1,0:T(8,128)(2,1)}, u32[]{:S(2)}, u32[]{:S(2)}) collective-permute-start(bf16[8,512,512]{2,1,0:T(8,128)(2,1)} %get-tuple-element.104), channel_id=1, source_target_pairs={{0,1},{1,0},{2,3},{3,2},{4,5},{5,4},{6,7},{7,6},{8,9},{9,8},{10,11... | collective-permute-start | bytes 12582920 | tf_op jit(solution)/shard_map/ppermute | solution.py:780
  427.9 16.0 %shard_map.309 = (f32[1024,1024]{1,0:T(8,128)}, f32[8,1024]{1,0:T(8,128)}) custom-call(s32[16]{0:T(128)} %copy-done.57, bf16[1024,512]{1,0:T(8,128)(2,1)} %get-tuple-element.90.rest_0_.rest_5_, bf16[1024,512]{1,0:T(8,128)(2,1)} %get-tuple-element.92.rest_6_.rest_1_, bf16[1024,512]{1,0:T(8,128)(2,1)} %get-tuple-element.93.rest_7_.rest_2_, ...), custom_call_target="tpu_custom_call" | custom-call | flops 805306368 | bytes 2097152 | tf_op jit(solution)/shard_map/pallas_call | solution.py:473
  443.9 2.4 shard_map.310
  446.3 2.0 collective-permute-start.31
  448.4 20.3 %shard_map.311 = (bf16[8,544,512]{2,1,0:T(8,128)(2,1)}, bf16[8,544,512]{2,1,0:T(8,128)(2,1)}) custom-call(s32[9]{0:T(128)} %dynamic-slice_bitcast_fusion.rank_ref, f32[8,1024]{1,0:T(8,128)} %get-tuple-element.107.rest_0_, f32[8,1024]{1,0:T(8,128)} %get-tuple-element.108.rest_1_, f32[8,1024]{1,0:T(8,128)} %get-tuple-element.109.rest_2_, ...), custom_call_target="tpu_custom_call" | custom-call | flops 1073741824 | bytes 3145728 | tf_op jit(solution)/shard_map/pallas_call | solution.py:539
  469.7 2.7 shard_map.312
  472.5 2.0 collective-permute-start.33
  474.5 11.8 %shard_map.313.rest_0_ = f32[1024,1024]{1,0:T(8,128)} custom-call(s32[16]{0:T(128)} %copy-done.57, bf16[1024,1024]{1,0:T(8,128)(2,1)} %get-tuple-element.102.rest_10_.rest_11_.dk_ref, bf16[1024,1024]{1,0:T(8,128)(2,1)} %get-tuple-element.103.rest_12_.rest_13_.dv_ref, f32[8,1024]{1,0:T(8,128)} %reshape.101.norm_ref.rest_4_.rest_3_.rest_8_, ...), custom_call_target="tpu_custom_call" | custom-call | flops 536870912 | bytes 1048576 | tf_op jit(solution)/shard_map/pallas_call | solution.py:473
  486.4 2.2 copy-done.2
  488.6 4.8 shard_map.314
  493.4 1.4 copy-done
  494.7 2.0 collective-permute-done.34.rest_3_
  496.8 9.8 %collective-permute-done.33.rest_0_ = bf16[512,512]{1,0:T(8,128)(2,1)S(1)} collective-permute-done((bf16[512,512]{1,0:T(8,128)(2,1)}, bf16[512,512]{1,0:T(8,128)(2,1)S(1)}, u32[]{:S(2)}, u32[]{:S(2)}) %collective-permute-start.33) | collective-permute-done | bytes 524320 | tf_op jit(solution)/shard_map/ppermute | solution.py:769
  507.4 2.8 shard_map.315
  510.2 2.9 collective-permute-start.36
  513.1 18.8 %collective-permute-done.36.rest_0_ = bf16[512,512]{1,0:T(8,128)(2,1)S(1)} collective-permute-done((bf16[512,512]{1,0:T(8,128)(2,1)}, bf16[512,512]{1,0:T(8,128)(2,1)S(1)}, u32[]{:S(2)}, u32[]{:S(2)}) %collective-permute-start.36) | collective-permute-done | bytes 524320 | tf_op jit(solution)/shard_map/ppermute | solution.py:769
  532.7 2.1 shard_map.316.rest_4_
  534.9 13.4 %collective-permute-done.37 = bf16[512,512]{1,0:T(8,128)(2,1)S(1)} collective-permute-done((bf16[512,512]{1,0:T(8,128)(2,1)}, bf16[512,512]{1,0:T(8,128)(2,1)S(1)}, u32[]{:S(2)}, u32[]{:S(2)}) %collective-permute-start.37) | collective-permute-done | bytes 524320 | tf_op jit(solution)/shard_map/ppermute | solution.py:769
  548.3 1.5 fusion.1
  551.7 2.3 broadcast_add_fusion
  554.0 2.0 collective-permute-start.46
  556.0 1.4 copy-done.3
  557.4 2.1 shard_map.317
  559.8 1.7 collective-permute-start.41
  561.5 3.2 collective-permute-done.39
  567.7 2.3 shard_map.318
  574.2 2.6 collective-permute-done.44.rest_3_
  578.6 2.3 shard_map.319
  582.9 1.9 collective-permute-done.46
  584.7 3.0 convert_add_fusion.rest_4_
  589.0 1.9 shard_map.322
  594.2 3.6 collective-permute-done.47
  600.0 5.5 collective-permute-done.49
  (266 shorter events, 47.9 us)
Async XLA Ops:
  7.3 229.9 %all-gather.2.cloned.1.call-start = ((), (), s32[]{:S(2)}) async-start(), calls=%async_computation.1 | async-start | bytes 17301504 | tf_op jit(solution)/shard_map/all_gather | solution.py:848
  8.6 36.9 %copy-start.54 = (bf16[64,1024]{1,0:T(8,128)(2,1)S(1)}, bf16[64,1024]{1,0:T(8,128)(2,1)}, u32[]{:S(2)}) copy-start(bf16[64,1024]{1,0:T(8,128)(2,1)} %param.29) | copy-start | bytes 393220
  8.7 38.0 %copy-start.58 = (s32[1,1024]{1,0:T(1,128)S(1)}, s32[1,1024]{1,0:T(1,128)}, u32[]{:S(2)}) copy-start(s32[1,1024]{1,0:T(1,128)} %param.22) | copy-start | bytes 12292
  8.7 75.4 %copy-start.55 = (bf16[64,1024]{1,0:T(8,128)(2,1)S(1)}, bf16[64,1024]{1,0:T(8,128)(2,1)}, u32[]{:S(2)}) copy-start(bf16[64,1024]{1,0:T(8,128)(2,1)} %param.30) | copy-start | bytes 393220
  9.7 542.0 %reduce-scatter.2.cloned.1.call-start = ((), (), s32[]{:S(2)}) async-start(), calls=%async_computation.2 | async-start | bytes 17825792 | tf_op jit(solution)/shard_map/reduce_scatter | solution.py:912
  9.9 87.4 %copy-start.22 = (bf16[208,1024]{1,0:T(8,128)(2,1)}, bf16[208,1024]{1,0:T(8,128)(2,1)S(1)}, u32[]{:S(2)}) copy-start(bf16[208,1024]{1,0:T(8,128)(2,1)S(1)} %fusion.5.rest_0_.rest_9_) | copy-start | bytes 1277956
  9.9 12.8 %collective-permute-start.3 = (bf16[208,1024]{1,0:T(8,128)(2,1)S(1)}, bf16[208,1024]{1,0:T(8,128)(2,1)S(1)}, u32[]{:S(2)}, u32[]{:S(2)}) collective-permute-start(bf16[208,1024]{1,0:T(8,128)(2,1)S(1)} %fusion.5.rest_0_.rest_9_), channel_id=1, source_target_pairs={{0,4},{1,5},{4,8},{5,9},{8,12},{9,13},{12,14},{13,15},{14,10},{15,... | collective-permute-start | bytes 1277960 | tf_op jit(solution)/shard_map/ppermute | solution.py:710
  13.0 72.3 %collective-permute-start.7 = (bf16[208,1024]{1,0:T(8,128)(2,1)S(1)}, bf16[208,1024]{1,0:T(8,128)(2,1)S(1)}, u32[]{:S(2)}, u32[]{:S(2)}) collective-permute-start(bf16[208,1024]{1,0:T(8,128)(2,1)S(1)} %fusion.5.rest_0_.rest_9_), channel_id=1, source_target_pairs={{0,1},{1,0},{2,3},{3,2},{4,5},{5,4},{6,7},{7,6},{8,9},{9,8},{10,11... | collective-permute-start | bytes 1277960 | tf_op jit(solution)/shard_map/ppermute | solution.py:715
  13.0 32.6 %collective-permute-start = (bf16[208,1024]{1,0:T(8,128)(2,1)S(1)}, bf16[208,1024]{1,0:T(8,128)(2,1)S(1)}, u32[]{:S(2)}, u32[]{:S(2)}) collective-permute-start(bf16[208,1024]{1,0:T(8,128)(2,1)S(1)} %fusion.5.rest_0_.rest_9_), channel_id=1, source_target_pairs={{4,0},{5,1},{8,4},{9,5},{12,8},{13,9},{14,12},{15,13},{10,14},{11,... | collective-permute-start | bytes 1277960 | tf_op jit(solution)/shard_map/ppermute | solution.py:713
  22.8 74.6 %copy-start.23 = (bf16[208,1024]{1,0:T(8,128)(2,1)}, bf16[208,1024]{1,0:T(8,128)(2,1)S(1)}, u32[]{:S(2)}) copy-start(bf16[208,1024]{1,0:T(8,128)(2,1)S(1)} %collective-permute-done.3.rest_7_.rest_16_) | copy-start | bytes 1277956
  22.8 20.3 %collective-permute-start.4 = (bf16[208,1024]{1,0:T(8,128)(2,1)S(1)}, bf16[208,1024]{1,0:T(8,128)(2,1)S(1)}, u32[]{:S(2)}, u32[]{:S(2)}) collective-permute-start(bf16[208,1024]{1,0:T(8,128)(2,1)S(1)} %collective-permute-done.3.rest_7_.rest_16_), channel_id=1, source_target_pairs={{0,4},{1,5},{4,8},{5,9},{8,12},{9,13},{12,14},{13,15},{14,10},{15,... | collective-permute-start | bytes 1277960 | tf_op jit(solution)/shard_map/ppermute | solution.py:710
  43.1 51.5 %copy-start.26 = (bf16[208,1024]{1,0:T(8,128)(2,1)}, bf16[208,1024]{1,0:T(8,128)(2,1)S(1)}, u32[]{:S(2)}) copy-start(bf16[208,1024]{1,0:T(8,128)(2,1)S(1)} %collective-permute-done.4.rest_6_.rest_15_) | copy-start | bytes 1277956
  43.1 14.5 %collective-permute-start.5 = (bf16[208,1024]{1,0:T(8,128)(2,1)S(1)}, bf16[208,1024]{1,0:T(8,128)(2,1)S(1)}, u32[]{:S(2)}, u32[]{:S(2)}) collective-permute-start(bf16[208,1024]{1,0:T(8,128)(2,1)S(1)} %collective-permute-done.4.rest_6_.rest_15_), channel_id=1, source_target_pairs={{0,4},{1,5},{4,8},{5,9},{8,12},{9,13},{12,14},{13,15},{14,10},{15,... | collective-permute-start | bytes 1277960 | tf_op jit(solution)/shard_map/ppermute | solution.py:710
  45.6 48.9 %copy-start.25 = (bf16[208,1024]{1,0:T(8,128)(2,1)}, bf16[208,1024]{1,0:T(8,128)(2,1)S(1)}, u32[]{:S(2)}) copy-start(bf16[208,1024]{1,0:T(8,128)(2,1)S(1)} %collective-permute-done.rest_1_.rest_10_) | copy-start | bytes 1277956
  45.6 22.7 %collective-permute-start.1 = (bf16[208,1024]{1,0:T(8,128)(2,1)S(1)}, bf16[208,1024]{1,0:T(8,128)(2,1)S(1)}, u32[]{:S(2)}, u32[]{:S(2)}) collective-permute-start(bf16[208,1024]{1,0:T(8,128)(2,1)S(1)} %collective-permute-done.rest_1_.rest_10_), channel_id=1, source_target_pairs={{4,0},{5,1},{8,4},{9,5},{12,8},{13,9},{14,12},{15,13},{10,14},{11,... | collective-permute-start | bytes 1277960 | tf_op jit(solution)/shard_map/ppermute | solution.py:713
  57.6 37.1 %copy-start.27 = (bf16[208,1024]{1,0:T(8,128)(2,1)}, bf16[208,1024]{1,0:T(8,128)(2,1)S(1)}, u32[]{:S(2)}) copy-start(bf16[208,1024]{1,0:T(8,128)(2,1)S(1)} %collective-permute-done.5.rest_5_.rest_14_) | copy-start | bytes 1277956
  57.6 25.8 %collective-permute-start.6 = (bf16[208,1024]{1,0:T(8,128)(2,1)S(1)}, bf16[208,1024]{1,0:T(8,128)(2,1)S(1)}, u32[]{:S(2)}, u32[]{:S(2)}) collective-permute-start(bf16[208,1024]{1,0:T(8,128)(2,1)S(1)} %collective-permute-done.5.rest_5_.rest_14_), channel_id=1, source_target_pairs={{0,4},{1,5},{4,8},{5,9},{8,12},{9,13},{12,14},{13,15},{14,10},{15,... | collective-permute-start | bytes 1277960 | tf_op jit(solution)/shard_map/ppermute | solution.py:710
  67.8 18.1 %collective-permute-start.14 = (bf16[208,1024]{1,0:T(8,128)(2,1)S(1)}, bf16[208,1024]{1,0:T(8,128)(2,1)S(1)}, u32[]{:S(2)}, u32[]{:S(2)}) collective-permute-start(bf16[208,1024]{1,0:T(8,128)(2,1)S(1)} %collective-permute-done.3.rest_7_.rest_16_), channel_id=1, source_target_pairs={{0,1},{1,0},{2,3},{3,2},{4,5},{5,4},{6,7},{7,6},{8,9},{9,8},{10,11... | collective-permute-start | bytes 1277960 | tf_op jit(solution)/shard_map/ppermute | solution.py:715
  67.8 21.4 %collective-permute-start.8 = (bf16[208,1024]{1,0:T(8,128)(2,1)S(1)}, bf16[208,1024]{1,0:T(8,128)(2,1)S(1)}, u32[]{:S(2)}, u32[]{:S(2)}) collective-permute-start(bf16[208,1024]{1,0:T(8,128)(2,1)S(1)} %collective-permute-done.rest_1_.rest_10_), channel_id=1, source_target_pairs={{0,1},{1,0},{2,3},{3,2},{4,5},{5,4},{6,7},{7,6},{8,9},{9,8},{10,11... | collective-permute-start | bytes 1277960 | tf_op jit(solution)/shard_map/ppermute | solution.py:715
  68.3 20.9 %collective-permute-start.2 = (bf16[208,1024]{1,0:T(8,128)(2,1)S(1)}, bf16[208,1024]{1,0:T(8,128)(2,1)S(1)}, u32[]{:S(2)}, u32[]{:S(2)}) collective-permute-start(bf16[208,1024]{1,0:T(8,128)(2,1)S(1)} %collective-permute-done.1.rest_2_.rest_11_), channel_id=1, source_target_pairs={{4,0},{5,1},{8,4},{9,5},{12,8},{13,9},{14,12},{15,13},{10,14},{11,... | collective-permute-start | bytes 1277960 | tf_op jit(solution)/shard_map/ppermute | solution.py:713
  83.4 7.2 %collective-permute-start.13 = (bf16[208,1024]{1,0:T(8,128)(2,1)S(1)}, bf16[208,1024]{1,0:T(8,128)(2,1)S(1)}, u32[]{:S(2)}, u32[]{:S(2)}) collective-permute-start(bf16[208,1024]{1,0:T(8,128)(2,1)S(1)} %collective-permute-done.4.rest_6_.rest_15_), channel_id=1, source_target_pairs={{0,1},{1,0},{2,3},{3,2},{4,5},{5,4},{6,7},{7,6},{8,9},{9,8},{10,11... | collective-permute-start | bytes 1277960 | tf_op jit(solution)/shard_map/ppermute | solution.py:715
  84.1 84.0 %copy-start.5 = (bf16[320,1024]{1,0:T(8,128)(2,1)}, bf16[320,1024]{1,0:T(8,128)(2,1)S(1)}, u32[]{:S(2)}) copy-start(bf16[320,1024]{1,0:T(8,128)(2,1)S(1)} %constant_dynamic-update-slice_fusion.rest_5_.rest_4_.rest_0_) | copy-start | bytes 1966084
  85.4 9.1 %collective-permute-start.9 = (bf16[208,1024]{1,0:T(8,128)(2,1)S(1)}, bf16[208,1024]{1,0:T(8,128)(2,1)S(1)}, u32[]{:S(2)}, u32[]{:S(2)}) collective-permute-start(bf16[208,1024]{1,0:T(8,128)(2,1)S(1)} %collective-permute-done.1.rest_2_.rest_11_), channel_id=1, source_target_pairs={{0,1},{1,0},{2,3},{3,2},{4,5},{5,4},{6,7},{7,6},{8,9},{9,8},{10,11... | collective-permute-start | bytes 1277960 | tf_op jit(solution)/shard_map/ppermute | solution.py:715
  86.0 8.7 %collective-permute-start.12 = (bf16[208,1024]{1,0:T(8,128)(2,1)S(1)}, bf16[208,1024]{1,0:T(8,128)(2,1)S(1)}, u32[]{:S(2)}, u32[]{:S(2)}) collective-permute-start(bf16[208,1024]{1,0:T(8,128)(2,1)S(1)} %collective-permute-done.5.rest_5_.rest_14_), channel_id=1, source_target_pairs={{0,1},{1,0},{2,3},{3,2},{4,5},{5,4},{6,7},{7,6},{8,9},{9,8},{10,11... | collective-permute-start | bytes 1277960 | tf_op jit(solution)/shard_map/ppermute | solution.py:715
  89.2 5.5 collective-permute-start.10
  89.2 5.5 collective-permute-start.11
  90.6 33.3 %collective-permute-start.18 = (bf16[320,1024]{1,0:T(8,128)(2,1)}, bf16[320,1024]{1,0:T(8,128)(2,1)S(1)}, u32[]{:S(2)}, u32[]{:S(2)}) collective-permute-start(bf16[320,1024]{1,0:T(8,128)(2,1)} %broadcast_add_fusion.5), channel_id=1, source_target_pairs={{0,4},{1,5},{4,8},{5,9},{8,12},{9,13},{12,14},{13,15},{14,10},{15,... | collective-permute-start | bytes 1966088 | tf_op jit(solution)/shard_map/ppermute | solution.py:730
  94.6 62.6 %collective-permute-start.15 = (bf16[320,1024]{1,0:T(8,128)(2,1)}, bf16[320,1024]{1,0:T(8,128)(2,1)S(1)}, u32[]{:S(2)}, u32[]{:S(2)}) collective-permute-start(bf16[320,1024]{1,0:T(8,128)(2,1)} %broadcast_add_fusion.5), channel_id=1, source_target_pairs={{4,0},{5,1},{8,4},{9,5},{12,8},{13,9},{14,12},{15,13},{10,14},{11,... | collective-permute-start | bytes 1966088 | tf_op jit(solution)/shard_map/ppermute | solution.py:732
  124.0 44.2 %copy-start.6 = (bf16[320,1024]{1,0:T(8,128)(2,1)}, bf16[320,1024]{1,0:T(8,128)(2,1)S(1)}, u32[]{:S(2)}) copy-start(bf16[320,1024]{1,0:T(8,128)(2,1)S(1)} %collective-permute-done.18.rest_12_.rest_11_.rest_7_) | copy-start | bytes 1966084
  124.0 34.2 %collective-permute-start.19 = (bf16[320,1024]{1,0:T(8,128)(2,1)S(1)}, bf16[320,1024]{1,0:T(8,128)(2,1)S(1)}, u32[]{:S(2)}, u32[]{:S(2)}) collective-permute-start(bf16[320,1024]{1,0:T(8,128)(2,1)S(1)} %broadcast_add_fusion.3), channel_id=1, source_target_pairs={{0,4},{1,5},{4,8},{5,9},{8,12},{9,13},{12,14},{13,15},{14,10},{15,... | collective-permute-start | bytes 1966088 | tf_op jit(solution)/shard_map/ppermute | solution.py:730
  157.2 43.2 %copy-start.7 = (bf16[320,1024]{1,0:T(8,128)(2,1)}, bf16[320,1024]{1,0:T(8,128)(2,1)S(1)}, u32[]{:S(2)}) copy-start(bf16[320,1024]{1,0:T(8,128)(2,1)S(1)} %collective-permute-done.15.rest_6_.rest_5_.rest_1_) | copy-start | bytes 1966084
  157.3 16.9 %collective-permute-start.16 = (bf16[320,1024]{1,0:T(8,128)(2,1)S(1)}, bf16[320,1024]{1,0:T(8,128)(2,1)S(1)}, u32[]{:S(2)}, u32[]{:S(2)}) collective-permute-start(bf16[320,1024]{1,0:T(8,128)(2,1)S(1)} %broadcast_add_fusion.4), channel_id=1, source_target_pairs={{4,0},{5,1},{8,4},{9,5},{12,8},{13,9},{14,12},{15,13},{10,14},{11,... | collective-permute-start | bytes 1966088 | tf_op jit(solution)/shard_map/ppermute | solution.py:732
  158.2 42.2 %copy-start.8 = (bf16[320,1024]{1,0:T(8,128)(2,1)}, bf16[320,1024]{1,0:T(8,128)(2,1)S(1)}, u32[]{:S(2)}) copy-start(bf16[320,1024]{1,0:T(8,128)(2,1)S(1)} %collective-permute-done.19.rest_11_.rest_10_.rest_6_) | copy-start | bytes 1966084
  158.3 23.7 %collective-permute-start.20 = (bf16[320,1024]{1,0:T(8,128)(2,1)S(1)}, bf16[320,1024]{1,0:T(8,128)(2,1)S(1)}, u32[]{:S(2)}, u32[]{:S(2)}) collective-permute-start(bf16[320,1024]{1,0:T(8,128)(2,1)S(1)} %broadcast_add_fusion.1), channel_id=1, source_target_pairs={{0,4},{1,5},{4,8},{5,9},{8,12},{9,13},{12,14},{13,15},{14,10},{15,... | collective-permute-start | bytes 1966088 | tf_op jit(solution)/shard_map/ppermute | solution.py:730
  168.1 16.4 %collective-permute-start.22 = (bf16[320,1024]{1,0:T(8,128)(2,1)S(1)}, bf16[320,1024]{1,0:T(8,128)(2,1)S(1)}, u32[]{:S(2)}, u32[]{:S(2)}) collective-permute-start(bf16[320,1024]{1,0:T(8,128)(2,1)S(1)} %constant_dynamic-update-slice_fusion.rest_5_.rest_4_.rest_0_), channel_id=1, source_target_pairs={{0,1},{1,0},{2,3},{3,2},{4,5},{5,4},{6,7},{7,6},{8,9},{9,8},{10,11... | collective-permute-start | bytes 1966088 | tf_op jit(solution)/shard_map/ppermute | solution.py:735
  168.1 16.4 %collective-permute-start.29 = (bf16[320,1024]{1,0:T(8,128)(2,1)S(1)}, bf16[320,1024]{1,0:T(8,128)(2,1)S(1)}, u32[]{:S(2)}, u32[]{:S(2)}) collective-permute-start(bf16[320,1024]{1,0:T(8,128)(2,1)S(1)} %collective-permute-done.18.rest_12_.rest_11_.rest_7_), channel_id=1, source_target_pairs={{0,1},{1,0},{2,3},{3,2},{4,5},{5,4},{6,7},{7,6},{8,9},{9,8},{10,11... | collective-permute-start | bytes 1966088 | tf_op jit(solution)/shard_map/ppermute | solution.py:735
  168.6 16.4 %collective-permute-start.23 = (bf16[320,1024]{1,0:T(8,128)(2,1)S(1)}, bf16[320,1024]{1,0:T(8,128)(2,1)S(1)}, u32[]{:S(2)}, u32[]{:S(2)}) collective-permute-start(bf16[320,1024]{1,0:T(8,128)(2,1)S(1)} %collective-permute-done.15.rest_6_.rest_5_.rest_1_), channel_id=1, source_target_pairs={{0,1},{1,0},{2,3},{3,2},{4,5},{5,4},{6,7},{7,6},{8,9},{9,8},{10,11... | collective-permute-start | bytes 1966088 | tf_op jit(solution)/shard_map/ppermute | solution.py:735
  174.2 15.6 %collective-permute-start.17 = (bf16[320,1024]{1,0:T(8,128)(2,1)S(1)}, bf16[320,1024]{1,0:T(8,128)(2,1)S(1)}, u32[]{:S(2)}, u32[]{:S(2)}) collective-permute-start(bf16[320,1024]{1,0:T(8,128)(2,1)S(1)} %broadcast_add_fusion.2), channel_id=1, source_target_pairs={{4,0},{5,1},{8,4},{9,5},{12,8},{13,9},{14,12},{15,13},{10,14},{11,... | collective-permute-start | bytes 1966088 | tf_op jit(solution)/shard_map/ppermute | solution.py:732
  182.0 15.5 %collective-permute-start.21 = (bf16[320,1024]{1,0:T(8,128)(2,1)S(1)}, bf16[320,1024]{1,0:T(8,128)(2,1)S(1)}, u32[]{:S(2)}, u32[]{:S(2)}) collective-permute-start(bf16[320,1024]{1,0:T(8,128)(2,1)S(1)} %collective-permute-done.20.rest_10_.rest_9_.rest_5_), channel_id=1, source_target_pairs={{0,4},{1,5},{4,8},{5,9},{8,12},{9,13},{12,14},{13,15},{14,10},{15,... | collective-permute-start | bytes 1966088 | tf_op jit(solution)/shard_map/ppermute | solution.py:730
  184.5 13.7 %collective-permute-start.24 = (bf16[320,1024]{1,0:T(8,128)(2,1)S(1)}, bf16[320,1024]{1,0:T(8,128)(2,1)S(1)}, u32[]{:S(2)}, u32[]{:S(2)}) collective-permute-start(bf16[320,1024]{1,0:T(8,128)(2,1)S(1)} %collective-permute-done.16.rest_7_.rest_6_.rest_2_), channel_id=1, source_target_pairs={{0,1},{1,0},{2,3},{3,2},{4,5},{5,4},{6,7},{7,6},{8,9},{9,8},{10,11... | collective-permute-start | bytes 1966088 | tf_op jit(solution)/shard_map/ppermute | solution.py:735
  184.5 13.6 %collective-permute-start.28 = (bf16[320,1024]{1,0:T(8,128)(2,1)S(1)}, bf16[320,1024]{1,0:T(8,128)(2,1)S(1)}, u32[]{:S(2)}, u32[]{:S(2)}) collective-permute-start(bf16[320,1024]{1,0:T(8,128)(2,1)S(1)} %collective-permute-done.19.rest_11_.rest_10_.rest_6_), channel_id=1, source_target_pairs={{0,1},{1,0},{2,3},{3,2},{4,5},{5,4},{6,7},{7,6},{8,9},{9,8},{10,11... | collective-permute-start | bytes 1966088 | tf_op jit(solution)/shard_map/ppermute | solution.py:735
  185.0 13.2 %collective-permute-start.27 = (bf16[320,1024]{1,0:T(8,128)(2,1)S(1)}, bf16[320,1024]{1,0:T(8,128)(2,1)S(1)}, u32[]{:S(2)}, u32[]{:S(2)}) collective-permute-start(bf16[320,1024]{1,0:T(8,128)(2,1)S(1)} %collective-permute-done.20.rest_10_.rest_9_.rest_5_), channel_id=1, source_target_pairs={{0,1},{1,0},{2,3},{3,2},{4,5},{5,4},{6,7},{7,6},{8,9},{9,8},{10,11... | collective-permute-start | bytes 1966088 | tf_op jit(solution)/shard_map/ppermute | solution.py:735
  189.8 8.4 %collective-permute-start.25 = (bf16[320,1024]{1,0:T(8,128)(2,1)S(1)}, bf16[320,1024]{1,0:T(8,128)(2,1)S(1)}, u32[]{:S(2)}, u32[]{:S(2)}) collective-permute-start(bf16[320,1024]{1,0:T(8,128)(2,1)S(1)} %collective-permute-done.17.rest_8_.rest_7_.rest_3_), channel_id=1, source_target_pairs={{0,1},{1,0},{2,3},{3,2},{4,5},{5,4},{6,7},{7,6},{8,9},{9,8},{10,11... | collective-permute-start | bytes 1966088 | tf_op jit(solution)/shard_map/ppermute | solution.py:735
  197.5 2.1 collective-permute-start.26
  420.5 23.4 %collective-permute-start.30 = (bf16[8,512,512]{2,1,0:T(8,128)(2,1)}, bf16[8,512,512]{2,1,0:T(8,128)(2,1)}, u32[]{:S(2)}, u32[]{:S(2)}) collective-permute-start(bf16[8,512,512]{2,1,0:T(8,128)(2,1)} %get-tuple-element.104), channel_id=1, source_target_pairs={{0,1},{1,0},{2,3},{3,2},{4,5},{5,4},{6,7},{7,6},{8,9},{9,8},{10,11... | collective-permute-start | bytes 12582920 | tf_op jit(solution)/shard_map/ppermute | solution.py:780
  446.3 22.4 %collective-permute-start.32 = (bf16[512,512]{1,0:T(8,128)(2,1)}, bf16[512,512]{1,0:T(8,128)(2,1)S(1)}, u32[]{:S(2)}, u32[]{:S(2)}) collective-permute-start(bf16[512,512]{1,0:T(8,128)(2,1)} %get-tuple-element.106), channel_id=1, source_target_pairs={{0,4},{1,5},{4,8},{5,9},{8,12},{9,13},{12,14},{13,15},{14,10},{15,... | collective-permute-start | bytes 1572872 | tf_op jit(solution)/shard_map/ppermute | solution.py:771
  446.3 22.4 %collective-permute-start.31 = (bf16[512,512]{1,0:T(8,128)(2,1)}, bf16[512,512]{1,0:T(8,128)(2,1)S(1)}, u32[]{:S(2)}, u32[]{:S(2)}) collective-permute-start(bf16[512,512]{1,0:T(8,128)(2,1)} %get-tuple-element.105.rest_14_), channel_id=1, source_target_pairs={{4,0},{5,1},{8,4},{9,5},{12,8},{13,9},{14,12},{15,13},{10,14},{11,... | collective-permute-start | bytes 1572872 | tf_op jit(solution)/shard_map/ppermute | solution.py:769
  472.4 13.9 %collective-permute-start.35 = (bf16[8,544,512]{2,1,0:T(8,128)(2,1)}, bf16[8,544,512]{2,1,0:T(8,128)(2,1)}, u32[]{:S(2)}, u32[]{:S(2)}) collective-permute-start(bf16[8,544,512]{2,1,0:T(8,128)(2,1)} %get-tuple-element.116), channel_id=1, source_target_pairs={{0,1},{1,0},{2,3},{3,2},{4,5},{5,4},{6,7},{7,6},{8,9},{9,8},{10,11... | collective-permute-start | bytes 13369352 | tf_op jit(solution)/shard_map/ppermute | solution.py:780
  472.4 24.4 %collective-permute-start.34 = (bf16[512,512]{1,0:T(8,128)(2,1)}, bf16[512,512]{1,0:T(8,128)(2,1)S(1)}, u32[]{:S(2)}, u32[]{:S(2)}) collective-permute-start(bf16[512,512]{1,0:T(8,128)(2,1)} %get-tuple-element.115), channel_id=1, source_target_pairs={{0,4},{1,5},{4,8},{5,9},{8,12},{9,13},{12,14},{13,15},{14,10},{15,... | collective-permute-start | bytes 1572872 | tf_op jit(solution)/shard_map/ppermute | solution.py:771
  472.5 34.0 %collective-permute-start.33 = (bf16[512,512]{1,0:T(8,128)(2,1)}, bf16[512,512]{1,0:T(8,128)(2,1)S(1)}, u32[]{:S(2)}, u32[]{:S(2)}) collective-permute-start(bf16[512,512]{1,0:T(8,128)(2,1)} %get-tuple-element.114.rest_16_), channel_id=1, source_target_pairs={{4,0},{5,1},{8,4},{9,5},{12,8},{13,9},{14,12},{15,13},{10,14},{11,... | collective-permute-start | bytes 1572872 | tf_op jit(solution)/shard_map/ppermute | solution.py:769
  494.7 61.3 %collective-permute-start.40 = (bf16[8,272,512]{2,1,0:T(8,128)(2,1)}, bf16[8,272,512]{2,1,0:T(8,128)(2,1)S(1)}, u32[]{:S(2)}, u32[]{:S(2)}) collective-permute-start(bf16[8,272,512]{2,1,0:T(8,128)(2,1)} %get-tuple-element.120), channel_id=1, source_target_pairs={{0,16},{16,0},{1,17},{17,1},{2,18},{18,2},{3,19},{19,3},{4,20},{20... | collective-permute-start | bytes 6684680 | tf_op jit(solution)/shard_map/ppermute | solution.py:784
  510.2 21.7 %collective-permute-start.36 = (bf16[512,512]{1,0:T(8,128)(2,1)}, bf16[512,512]{1,0:T(8,128)(2,1)S(1)}, u32[]{:S(2)}, u32[]{:S(2)}) collective-permute-start(bf16[512,512]{1,0:T(8,128)(2,1)} %get-tuple-element.118.rest_3_), channel_id=1, source_target_pairs={{4,0},{5,1},{8,4},{9,5},{12,8},{13,9},{14,12},{15,13},{10,14},{11,... | collective-permute-start | bytes 1572872 | tf_op jit(solution)/shard_map/ppermute | solution.py:769
  513.1 21.8 %collective-permute-start.38 = (bf16[512,512]{1,0:T(8,128)(2,1)}, bf16[512,512]{1,0:T(8,128)(2,1)S(1)}, u32[]{:S(2)}, u32[]{:S(2)}) collective-permute-start(bf16[512,512]{1,0:T(8,128)(2,1)} %get-tuple-element.119), channel_id=1, source_target_pairs={{0,4},{1,5},{4,8},{5,9},{8,12},{9,13},{12,14},{13,15},{14,10},{15,... | collective-permute-start | bytes 1572872 | tf_op jit(solution)/shard_map/ppermute | solution.py:771
  534.8 13.5 %collective-permute-start.37 = (bf16[512,512]{1,0:T(8,128)(2,1)}, bf16[512,512]{1,0:T(8,128)(2,1)S(1)}, u32[]{:S(2)}, u32[]{:S(2)}) collective-permute-start(bf16[512,512]{1,0:T(8,128)(2,1)} %shard_map.316.rest_4_), channel_id=1, source_target_pairs={{4,0},{5,1},{8,4},{9,5},{12,8},{13,9},{14,12},{15,13},{10,14},{11,... | collective-permute-start | bytes 1572872 | tf_op jit(solution)/shard_map/ppermute | solution.py:769
  549.8 14.9 %collective-permute-start.39 = (bf16[512,512]{1,0:T(8,128)(2,1)S(1)}, bf16[512,512]{1,0:T(8,128)(2,1)S(1)}, u32[]{:S(2)}, u32[]{:S(2)}) collective-permute-start(bf16[512,512]{1,0:T(8,128)(2,1)S(1)} %fusion.1), channel_id=1, source_target_pairs={{0,16},{16,0},{1,17},{17,1},{2,18},{18,2},{3,19},{19,3},{4,20},{20... | collective-permute-start | bytes 1572872 | tf_op jit(solution)/shard_map/ppermute | solution.py:743
  554.0 30.7 %collective-permute-start.46 = (bf16[512,1024]{1,0:T(8,128)(2,1)}, bf16[512,1024]{1,0:T(8,128)(2,1)}, u32[]{:S(2)}, u32[]{:S(2)}) collective-permute-start(bf16[512,1024]{1,0:T(8,128)(2,1)} %broadcast_add_fusion), channel_id=1, source_target_pairs={{0,16},{16,0},{1,17},{17,1},{2,18},{18,2},{3,19},{19,3},{4,20},{20... | collective-permute-start | bytes 3145736 | tf_op jit(solution)/shard_map/ppermute | solution.py:743
  559.5 6.8 %collective-permute-start.42 = (bf16[272,512]{1,0:T(8,128)(2,1)}, bf16[272,512]{1,0:T(8,128)(2,1)S(1)}, u32[]{:S(2)}, u32[]{:S(2)}) collective-permute-start(bf16[272,512]{1,0:T(8,128)(2,1)} %get-tuple-element.122), channel_id=1, source_target_pairs={{4,0},{5,1},{8,4},{9,5},{12,8},{13,9},{14,12},{15,13},{10,14},{11,... | collective-permute-start | bytes 835592 | tf_op jit(solution)/shard_map/ppermute | solution.py:771
  559.8 6.8 %collective-permute-start.41 = (bf16[272,512]{1,0:T(8,128)(2,1)}, bf16[272,512]{1,0:T(8,128)(2,1)S(1)}, u32[]{:S(2)}, u32[]{:S(2)}) collective-permute-start(bf16[272,512]{1,0:T(8,128)(2,1)} %get-tuple-element.121.rest_6_), channel_id=1, source_target_pairs={{0,4},{1,5},{4,8},{5,9},{8,12},{9,13},{12,14},{13,15},{14,10},{15,... | collective-permute-start | bytes 835592 | tf_op jit(solution)/shard_map/ppermute | solution.py:769
  570.0 6.8 %collective-permute-start.44 = (bf16[272,512]{1,0:T(8,128)(2,1)}, bf16[272,512]{1,0:T(8,128)(2,1)S(1)}, u32[]{:S(2)}, u32[]{:S(2)}) collective-permute-start(bf16[272,512]{1,0:T(8,128)(2,1)} %get-tuple-element.124), channel_id=1, source_target_pairs={{4,0},{5,1},{8,4},{9,5},{12,8},{13,9},{14,12},{15,13},{10,14},{11,... | collective-permute-start | bytes 835592 | tf_op jit(solution)/shard_map/ppermute | solution.py:771
  571.1 6.8 %collective-permute-start.43 = (bf16[272,512]{1,0:T(8,128)(2,1)}, bf16[272,512]{1,0:T(8,128)(2,1)S(1)}, u32[]{:S(2)}, u32[]{:S(2)}) collective-permute-start(bf16[272,512]{1,0:T(8,128)(2,1)} %get-tuple-element.123.rest_6_), channel_id=1, source_target_pairs={{0,4},{1,5},{4,8},{5,9},{8,12},{9,13},{12,14},{13,15},{14,10},{15,... | collective-permute-start | bytes 835592 | tf_op jit(solution)/shard_map/ppermute | solution.py:769
  580.9 13.3 %collective-permute-start.48 = (bf16[272,512]{1,0:T(8,128)(2,1)}, bf16[272,512]{1,0:T(8,128)(2,1)S(1)}, u32[]{:S(2)}, u32[]{:S(2)}) collective-permute-start(bf16[272,512]{1,0:T(8,128)(2,1)} %get-tuple-element.130), channel_id=1, source_target_pairs={{4,0},{5,1},{8,4},{9,5},{12,8},{13,9},{14,12},{15,13},{10,14},{11,... | collective-permute-start | bytes 835592 | tf_op jit(solution)/shard_map/ppermute | solution.py:771
  581.6 6.8 %collective-permute-start.45 = (bf16[272,512]{1,0:T(8,128)(2,1)}, bf16[272,512]{1,0:T(8,128)(2,1)S(1)}, u32[]{:S(2)}, u32[]{:S(2)}) collective-permute-start(bf16[272,512]{1,0:T(8,128)(2,1)} %get-tuple-element.125.rest_3_), channel_id=1, source_target_pairs={{0,4},{1,5},{4,8},{5,9},{8,12},{9,13},{12,14},{13,15},{14,10},{15,... | collective-permute-start | bytes 835592 | tf_op jit(solution)/shard_map/ppermute | solution.py:769
  591.0 6.8 %collective-permute-start.47 = (bf16[272,512]{1,0:T(8,128)(2,1)}, bf16[272,512]{1,0:T(8,128)(2,1)S(1)}, u32[]{:S(2)}, u32[]{:S(2)}) collective-permute-start(bf16[272,512]{1,0:T(8,128)(2,1)} %shard_map.322), channel_id=1, source_target_pairs={{0,4},{1,5},{4,8},{5,9},{8,12},{9,13},{12,14},{13,15},{14,10},{15,... | collective-permute-start | bytes 835592 | tf_op jit(solution)/shard_map/ppermute | solution.py:769
  598.9 6.6 %collective-permute-start.49 = (bf16[272,512]{1,0:T(8,128)(2,1)S(1)}, bf16[272,512]{1,0:T(8,128)(2,1)S(1)}, u32[]{:S(2)}, u32[]{:S(2)}) collective-permute-start(bf16[272,512]{1,0:T(8,128)(2,1)S(1)} %fusion.4), channel_id=1, source_target_pairs={{0,16},{16,0},{1,17},{17,1},{2,18},{18,2},{3,19},{19,3},{4,20},{20... | collective-permute-start | bytes 835592 | tf_op jit(solution)/shard_map/ppermute | solution.py:784
  (49 other events, 321.4 us)
Sparse Core Ops, SparseCore 0:
  11.5 155.6 all-gather.1
  321.4 205.1 reduce-scatter.1
